TPU v7x, 32 devices: a whole 2x2x4 slice. The times are simulated.
32 devices in a mesh: node: 4 (over y, x), gx: 4 (over z), gy: 2 (over core).
Axes of the slice: x: 2, y: 2, z: 4, core: 2. Of those that a mesh axis runs over, the one named last changes fastest.
Arguments:
- initial: float32 [5, 48, 32, 128], P(None, 'gx', 'gy'), may hold values from -8 to 50, as said below
- guesses: float32 [4, 5, 48, 32, 128], P('node', None, 'gx', 'gy'), may hold values from -8 to 50, as said below
Outputs:
- node_states: float32 [4, 5, 48, 32, 128], P('node', None, 'gx', 'gy')
Inputs may be any that keep to these rules, and one draw needn't show every extreme that they name: `initial`: each cell holds density, three momenta and total energy of a gas with ratio of heats 1.4: density 0.5 to 2.5, pressure 0.3 to 9, velocity components at most 3 in magnitude. `guesses`: each cell of each node holds density, three momenta and total energy of a gas with ratio of heats 1.4: density 0.5 to 2.5, pressure 0.3 to 9, velocity components at most 3 in magnitude.
All inputs are finite; a program needn't handle non-finite values.
Results may differ from a plain program's by a relative error of at most 0.0001.
Values sent between devices are 32-bit elements; how exact they have to be, the bound alone decides.
No kernel may reach another device: no remote copies, remote signals or barrier semaphores. Data moves between devices by JAX's collectives and lax.ppermute only.
A program may use at most 64 MiB of HBM per device.

v0:
```python
import jax
import jax.numpy as jnp
from jax import lax
from jax.sharding import PartitionSpec as P

SWEEPS = 2


heat_ratio = 1.4
step_size = 0.025
density_floor = 0.5
pressure_floor = 0.25
epsilon = 1e-06
radau_weights = [
    [0.112999479323156, -0.040309220723522, 0.025802377420336, -0.009904676507266],
    [0.2343839957474, 0.206892573935359, -0.047857128048541, 0.016047422806516],
    [0.21668178462325, 0.406123263867373, 0.189036518170056, -0.024182104899833],
    [0.220462211176768, 0.388193468843172, 0.32884431998006, 0.0625],
]


def padded_2(cells, sides, width):
    for axis, dim in sides:
        count = lax.axis_size(axis)
        head = lax.slice_in_dim(cells, 0, width, axis=dim)
        tail = lax.slice_in_dim(cells, cells.shape[dim] - width, cells.shape[dim], axis=dim)
        cells = jnp.concatenate(
            [
                lax.ppermute(tail, axis, [(i, (i + 1) % count) for i in range(count)]),
                cells,
                lax.ppermute(head, axis, [((i + 1) % count, i) for i in range(count)]),
            ],
            axis=dim,
        )
    return cells


def primitives(fields):
    density = jnp.maximum(fields[0], density_floor)
    velocity = fields[1:4] / density
    pressure = jnp.maximum(
        0.4 * (fields[4] - 0.5 * jnp.sum(fields[1:4] * velocity, axis=0)), pressure_floor
    )
    return (density, velocity, pressure)


def local_speeds(fields):
    density, velocity, pressure = primitives(fields)
    sound = jnp.sqrt(heat_ratio * pressure / density)
    return tuple((jnp.max(jnp.abs(velocity[direction]) + sound) for direction in range(3)))


def reconstruct(first, second, third, fourth, fifth):
    cand_zero = (2.0 * first - 7.0 * second + 11.0 * third) / 6.0
    cand_one = (-second + 5.0 * third + 2.0 * fourth) / 6.0
    cand_two = (2.0 * third + 5.0 * fourth - fifth) / 6.0
    smooth_zero = (
        13.0 / 12.0 * (first - 2.0 * second + third) ** 2
        + 0.25 * (first - 4.0 * second + 3.0 * third) ** 2
    )
    smooth_one = 13.0 / 12.0 * (second - 2.0 * third + fourth) ** 2 + 0.25 * (second - fourth) ** 2
    smooth_two = (
        13.0 / 12.0 * (third - 2.0 * fourth + fifth) ** 2
        + 0.25 * (3.0 * third - 4.0 * fourth + fifth) ** 2
    )
    weight_zero = 0.1 / (epsilon + smooth_zero) ** 2
    weight_one = 0.6 / (epsilon + smooth_one) ** 2
    weight_two = 0.3 / (epsilon + smooth_two) ** 2
    return (weight_zero * cand_zero + weight_one * cand_one + weight_two * cand_two) / (
        weight_zero + weight_one + weight_two
    )


def flux_along(extended, spatial_axis, alpha):
    direction = spatial_axis - 1
    density, velocity, pressure = primitives(extended)
    speed = velocity[direction]
    components = [
        extended[direction + 1],
        extended[1] * speed,
        extended[2] * speed,
        extended[3] * speed,
        (extended[4] + pressure) * speed,
    ]
    components[direction + 1] = components[direction + 1] + pressure
    fluxes = jnp.stack(components)
    right_going = 0.5 * (fluxes + alpha * extended)
    left_going = 0.5 * (fluxes - alpha * extended)
    length = extended.shape[spatial_axis] - 6

    def window(values, begin):
        return lax.slice_in_dim(values, begin, begin + length + 1, axis=spatial_axis)

    interface = reconstruct(
        window(right_going, 0),
        window(right_going, 1),
        window(right_going, 2),
        window(right_going, 3),
        window(right_going, 4),
    )
    interface = interface + reconstruct(
        window(left_going, 5),
        window(left_going, 4),
        window(left_going, 3),
        window(left_going, 2),
        window(left_going, 1),
    )
    return lax.slice_in_dim(interface, 0, length, axis=spatial_axis) - lax.slice_in_dim(
        interface, 1, length + 1, axis=spatial_axis
    )


def wrapped_depth(fields):
    return jnp.concatenate([fields[:, :, :, -3:], fields, fields[:, :, :, :3]], axis=3)


def evaluate(fields):
    alphas = lax.pmax(local_speeds(fields), ("gx", "gy"))
    padded = padded_2(fields, (("gx", 1), ("gy", 2)), 3)
    along_depth = flux_along(wrapped_depth(fields), 3, alphas[2])
    along_first = flux_along(padded[:, :, 3:-3, :], 1, alphas[0])
    along_second = flux_along(padded[:, 3:-3, :, :], 2, alphas[1])
    return along_first + along_second + along_depth


def local(initial, guesses):
    weights_table = jnp.array(radau_weights, jnp.float32)
    node_index = lax.axis_index("node")
    current = guesses[0]
    for sweep_index in range(SWEEPS):
        rate = evaluate(current)
        own_row = lax.dynamic_index_in_dim(weights_table, node_index, 0, keepdims=False)
        combined = jnp.sum(
            own_row[:, None, None, None, None]
            * lax.all_gather(rate[None], "node", axis=0, tiled=True),
            axis=0,
        )
        current = initial + step_size * combined
    return current[None]


def solution(mesh):
    placed = (P(None, "gx", "gy", None), P("node", None, "gx", "gy", None))
    return jax.shard_map(
        local,
        mesh=mesh,
        in_specs=placed,
        out_specs=P("node", None, "gx", "gy", None),
        check_vma=False,
    )
```

profile of v0, /device:TPU:0, one launch (start us, length us, event | category | flops | bytes accessed | tf_op | source)
XLA Modules:
  0.0 159.4 jit_solution(2291142398562544692)
XLA Ops:
  6.5 1.0 fusion.69
  7.6 3.1 %collective-permute-start = (f32[5,3,16,128]{3,2,1,0:T(8,128)S(1)}, f32[5,3,16,128]{3,2,1,0:T(8,128)S(1)}, u32[]{:S(2)}, u32[]{:S(2)}) collective-permute-start(f32[5,3,16,128]{3,2,1,0:T(8,128)S(1)} %get-tuple-element.71), channel_id=1, source_target_pairs={{0,2},{2,4},{4,6},{6,0},{1,3},{3,5},{5,7},{7,1},{8,10},{10,12},{12... | collective-permute-start | bytes 368648 | tf_op jit(solution)/shard_map/ppermute | solution.py:29
  10.7 2.1 %collective-permute-start.1 = (f32[5,3,16,128]{3,2,1,0:T(8,128)S(1)}, f32[5,3,16,128]{3,2,1,0:T(8,128)S(1)}, u32[]{:S(2)}, u32[]{:S(2)}) collective-permute-start(f32[5,3,16,128]{3,2,1,0:T(8,128)S(1)} %get-tuple-element.72), channel_id=1, source_target_pairs={{2,0},{4,2},{6,4},{0,6},{3,1},{5,3},{7,5},{1,7},{10,8},{12,10},{14... | collective-permute-start | bytes 368648 | tf_op jit(solution)/shard_map/ppermute | solution.py:31
  12.7 0.9 maximum_bitcast_fusion
  13.7 0.2 fusion.70
  13.9 0.4 pad_maximum_fusion.2
  14.4 0.1 multiply_reduce_fusion.3
  14.6 0.1 add_dynamic-update-slice_fusion.1
  14.7 0.1 multiply_dynamic-update-slice_fusion.1
  14.7 0.8 fusion.59
  15.5 15.1 %all-reduce.1 = (f32[]{:T(128)}, f32[]{:T(128)}, f32[]{:T(128)}) all-reduce(f32[]{:T(128)} %get-tuple-element.9, f32[]{:T(128)} %get-tuple-element.10, f32[]{:T(128)} %get-tuple-element.8), channel_id=1, replica_groups=mesh['node'=4,'gx'=4,'gy'=2] {'gx','gy'}, use_global_device_ids=true, to_apply=%region_9.0 | all-reduce | flops 3 | bytes 24 | tf_op jit(solution)/shard_map/pmax | solution.py:118
  30.6 0.9 add_multiply_fusion.1
  31.5 5.0 %divide_add_fusion.1 = f32[5,12,16,129]{3,2,1,0:T(8,128)S(1)} fusion(f32[5,12,16,134]{3,2,1,0:T(8,128)S(1)} %get-tuple-element.44, f32[5,12,16,134]{3,2,1,0:T(8,128)S(1)} %get-tuple-element.43), kind=kLoop, calls=%fused_computation.9 | loop fusion | flops 15975360 | bytes 5448960 | tf_op jit(solution)/shard_map/add | solution.py:101
  36.5 0.0 collective-permute-done.1
  36.5 0.1 pad_maximum_fusion.4
  36.6 0.1 fusion.66
  36.7 0.1 multiply_reduce_fusion.7
  36.9 0.1 collective-permute-start.2
  37.0 0.5 collective-permute-start.3
  37.5 0.8 add_multiply_fusion.5
  38.3 2.4 %divide_add_fusion.5 = f32[5,13,16,128]{3,2,1,0:T(8,128)S(1)} fusion(f32[5,18,16,128]{3,2,1,0:T(8,128)S(1)} %get-tuple-element.52, f32[5,18,16,128]{3,2,1,0:T(8,128)S(1)} %get-tuple-element.51), kind=kLoop, calls=%fused_computation.31 | loop fusion | flops 17172480 | bytes 5857280 | tf_op jit(solution)/shard_map/add | solution.py:101
  40.7 0.0 collective-permute-done.2
  40.8 0.1 constant_dynamic-update-slice_fusion
  40.8 0.2 pad_maximum_fusion
  41.0 0.1 multiply_reduce_fusion.6
  41.1 0.1 add_dynamic-update-slice_fusion.4
  41.3 0.8 add_multiply_fusion.4
  42.0 3.8 %divide_add_fusion.3 = f32[5,12,17,128]{3,2,1,0:T(8,128)S(1)} fusion(f32[5,12,22,128]{3,2,1,0:T(8,128)S(1)} %get-tuple-element.48, f32[5,12,22,128]{3,2,1,0:T(8,128)S(1)} %get-tuple-element.47), kind=kLoop, calls=%fused_computation.21 | loop fusion | flops 16842240 | bytes 5744640 | tf_op jit(solution)/shard_map/add | solution.py:101
  45.8 1.0 fusion.2
  46.8 0.0 all-gather.5.cloned.1.call-update
  46.9 0.0 all-gather.7.cloned.1.call-start
  46.9 0.7 dynamic-slice_bitcast_fusion
  47.6 31.8 %all-gather.5.cloned.1.call-done = f32[20,12,16,128]{3,2,1,0:T(8,128)} async-done(((f32[5,12,16,128]{3,2,1,0:T(8,128)}), f32[20,12,16,128]{3,2,1,0:T(8,128)}) %all-gather.5.cloned.1.call-update) | async-done | bytes 1966096 | tf_op jit(solution)/shard_map/all_gather | solution.py:135
  79.5 1.9 %multiply_reduce_fusion.1 = f32[5,12,16,128]{3,2,1,0:T(8,128)S(1)} fusion(f32[4,5,12,16,128]{4,3,2,1,0:T(8,128)} %bitcast.165, f32[4]{0:T(128)S(1)} %dynamic-slice_bitcast_fusion), kind=kLoop, calls=%fused_computation.1 | loop fusion | flops 860160 | bytes 2457616 | tf_op jit(solution)/shard_map/reduce_sum | solution.py:133
  81.3 0.1 multiply_add_fusion
  81.5 0.2 fusion.68
  81.7 1.5 collective-permute-start.4
  83.2 2.3 %collective-permute-start.5 = (f32[5,3,16,128]{3,2,1,0:T(8,128)S(1)}, f32[5,3,16,128]{3,2,1,0:T(8,128)S(1)}, u32[]{:S(2)}, u32[]{:S(2)}) collective-permute-start(f32[5,3,16,128]{3,2,1,0:T(8,128)S(1)} %get-tuple-element.68), channel_id=1, source_target_pairs={{2,0},{4,2},{6,4},{0,6},{3,1},{5,3},{7,5},{1,7},{10,8},{12,10},{14... | collective-permute-start | bytes 368648 | tf_op jit(solution)/shard_map/ppermute | solution.py:31
  85.6 0.4 pad_maximum_fusion.3
  86.1 0.1 multiply_reduce_fusion.2
  86.3 0.1 add_dynamic-update-slice_fusion
  86.3 0.1 multiply_dynamic-update-slice_fusion
  86.4 0.8 fusion.49
  87.2 14.9 %all-reduce = (f32[]{:T(128)}, f32[]{:T(128)}, f32[]{:T(128)}) all-reduce(f32[]{:T(128)} %get-tuple-element.6, f32[]{:T(128)} %get-tuple-element.7, f32[]{:T(128)} %get-tuple-element.5), channel_id=1, replica_groups=mesh['node'=4,'gx'=4,'gy'=2] {'gx','gy'}, use_global_device_ids=true, to_apply=%region_20.21 | all-reduce | flops 3 | bytes 24 | tf_op jit(solution)/shard_map/pmax | solution.py:118
  102.0 0.9 add_multiply_fusion
  103.0 5.0 %divide_add_fusion = f32[5,12,16,129]{3,2,1,0:T(8,128)S(1)} fusion(f32[5,12,16,134]{3,2,1,0:T(8,128)S(1)} %get-tuple-element.42, f32[5,12,16,134]{3,2,1,0:T(8,128)S(1)} %get-tuple-element.41), kind=kLoop, calls=%fused_computation.6 | loop fusion | flops 15975360 | bytes 5448960 | tf_op jit(solution)/shard_map/add | solution.py:101
  108.0 0.1 pad_maximum_fusion.5
  108.1 0.1 fusion.65
  108.1 0.1 multiply_reduce_fusion.5
  108.4 0.1 collective-permute-start.6
  108.4 0.5 collective-permute-start.7
  108.9 0.8 add_multiply_fusion.3
  109.7 2.4 %divide_add_fusion.4 = f32[5,13,16,128]{3,2,1,0:T(8,128)S(1)} fusion(f32[5,18,16,128]{3,2,1,0:T(8,128)S(1)} %get-tuple-element.50, f32[5,18,16,128]{3,2,1,0:T(8,128)S(1)} %get-tuple-element.49), kind=kLoop, calls=%fused_computation.30 | loop fusion | flops 17172480 | bytes 5857280 | tf_op jit(solution)/shard_map/add | solution.py:101
  112.2 0.2 pad_maximum_fusion.1
  112.4 0.1 constant_dynamic-update-slice_fusion.1
  112.4 0.1 multiply_reduce_fusion.4
  112.5 0.1 add_dynamic-update-slice_fusion.2
  112.7 0.8 add_multiply_fusion.2
  113.5 3.8 %divide_add_fusion.2 = f32[5,12,17,128]{3,2,1,0:T(8,128)S(1)} fusion(f32[5,12,22,128]{3,2,1,0:T(8,128)S(1)} %get-tuple-element.46, f32[5,12,22,128]{3,2,1,0:T(8,128)S(1)} %get-tuple-element.45), kind=kLoop, calls=%fused_computation.16 | loop fusion | flops 16842240 | bytes 5744640 | tf_op jit(solution)/shard_map/add | solution.py:101
  117.3 1.0 fusion
  118.3 0.0 all-gather.7.cloned.1.call-update
  118.3 31.6 %all-gather.7.cloned.1.call-done = f32[20,12,16,128]{3,2,1,0:T(8,128)} async-done(((f32[5,12,16,128]{3,2,1,0:T(8,128)}), f32[20,12,16,128]{3,2,1,0:T(8,128)}) %all-gather.7.cloned.1.call-update) | async-done | bytes 1966096 | tf_op jit(solution)/shard_map/all_gather | solution.py:135
  149.9 1.8 %multiply_reduce_fusion = f32[5,12,16,128]{3,2,1,0:T(8,128)S(1)} fusion(f32[4,5,12,16,128]{4,3,2,1,0:T(8,128)} %bitcast.166, f32[4]{0:T(128)S(1)} %dynamic-slice_bitcast_fusion), kind=kLoop, calls=%fused_computation | loop fusion | flops 860160 | bytes 2457616 | tf_op jit(solution)/shard_map/reduce_sum | solution.py:133
  151.7 0.8 add_bitcast_fusion
  (37 shorter events, 0.8 us)
Async XLA Ops:
  6.5 7.1 %copy-start = (f32[1,5,12,16,128]{4,3,2,1,0:T(8,128)S(1)}, f32[1,5,12,16,128]{4,3,2,1,0:T(8,128)}, u32[]{:S(2)}) copy-start(f32[1,5,12,16,128]{4,3,2,1,0:T(8,128)} %param.4) | copy-start | bytes 1474564
  6.5 72.9 %all-gather.5.cloned.1.call-start = ((), (), s32[]{:S(2)}) async-start(), calls=%async_computation | async-start | bytes 2457600 | tf_op jit(solution)/shard_map/all_gather | solution.py:135
  7.6 29.0 %collective-permute-start = (f32[5,3,16,128]{3,2,1,0:T(8,128)S(1)}, f32[5,3,16,128]{3,2,1,0:T(8,128)S(1)}, u32[]{:S(2)}, u32[]{:S(2)}) collective-permute-start(f32[5,3,16,128]{3,2,1,0:T(8,128)S(1)} %get-tuple-element.71), channel_id=1, source_target_pairs={{0,2},{2,4},{4,6},{6,0},{1,3},{3,5},{5,7},{7,1},{8,10},{10,12},{12... | collective-permute-start | bytes 368648 | tf_op jit(solution)/shard_map/ppermute | solution.py:29
  10.7 25.9 %collective-permute-start.1 = (f32[5,3,16,128]{3,2,1,0:T(8,128)S(1)}, f32[5,3,16,128]{3,2,1,0:T(8,128)S(1)}, u32[]{:S(2)}, u32[]{:S(2)}) collective-permute-start(f32[5,3,16,128]{3,2,1,0:T(8,128)S(1)} %get-tuple-element.72), channel_id=1, source_target_pairs={{2,0},{4,2},{6,4},{0,6},{3,1},{5,3},{7,5},{1,7},{10,8},{12,10},{14... | collective-permute-start | bytes 368648 | tf_op jit(solution)/shard_map/ppermute | solution.py:31
  36.9 3.8 %collective-permute-start.2 = (f32[5,18,3,128]{3,2,1,0:T(4,128)S(1)}, f32[5,18,3,128]{3,2,1,0:T(4,128)S(1)}, u32[]{:S(2)}, u32[]{:S(2)}) collective-permute-start(f32[5,18,3,128]{3,2,1,0:T(4,128)S(1)} %get-tuple-element.65), channel_id=1, source_target_pairs={{0,1},{1,0},{2,3},{3,2},{4,5},{5,4},{6,7},{7,6},{8,9},{9,8},{10,11... | collective-permute-start | bytes 414728 | tf_op jit(solution)/shard_map/ppermute | solution.py:29
  37.0 3.7 %collective-permute-start.3 = (f32[5,18,3,128]{3,2,1,0:T(4,128)S(1)}, f32[5,18,3,128]{3,2,1,0:T(4,128)S(1)}, u32[]{:S(2)}, u32[]{:S(2)}) collective-permute-start(f32[5,18,3,128]{3,2,1,0:T(4,128)S(1)} %get-tuple-element.66), channel_id=1, source_target_pairs={{1,0},{0,1},{3,2},{2,3},{5,4},{4,5},{7,6},{6,7},{9,8},{8,9},{11,10... | collective-permute-start | bytes 414728 | tf_op jit(solution)/shard_map/ppermute | solution.py:31
  46.9 103.1 %all-gather.7.cloned.1.call-start = ((), (), s32[]{:S(2)}) async-start(), calls=%async_computation.1 | async-start | bytes 2457600 | tf_op jit(solution)/shard_map/all_gather | solution.py:135
  79.5 1.9 %copy-start.1 = (f32[5,12,16,128]{3,2,1,0:T(8,128)S(1)}, f32[5,12,16,128]{3,2,1,0:T(8,128)}, u32[]{:S(2)}) copy-start(f32[5,12,16,128]{3,2,1,0:T(8,128)} %param.3) | copy-start | bytes 1474564
  81.7 26.3 %collective-permute-start.4 = (f32[5,3,16,128]{3,2,1,0:T(8,128)S(1)}, f32[5,3,16,128]{3,2,1,0:T(8,128)S(1)}, u32[]{:S(2)}, u32[]{:S(2)}) collective-permute-start(f32[5,3,16,128]{3,2,1,0:T(8,128)S(1)} %get-tuple-element.67), channel_id=1, source_target_pairs={{0,2},{2,4},{4,6},{6,0},{1,3},{3,5},{5,7},{7,1},{8,10},{10,12},{12... | collective-permute-start | bytes 368648 | tf_op jit(solution)/shard_map/ppermute | solution.py:29
  83.2 24.8 %collective-permute-start.5 = (f32[5,3,16,128]{3,2,1,0:T(8,128)S(1)}, f32[5,3,16,128]{3,2,1,0:T(8,128)S(1)}, u32[]{:S(2)}, u32[]{:S(2)}) collective-permute-start(f32[5,3,16,128]{3,2,1,0:T(8,128)S(1)} %get-tuple-element.68), channel_id=1, source_target_pairs={{2,0},{4,2},{6,4},{0,6},{3,1},{5,3},{7,5},{1,7},{10,8},{12,10},{14... | collective-permute-start | bytes 368648 | tf_op jit(solution)/shard_map/ppermute | solution.py:31
  108.4 3.8 %collective-permute-start.6 = (f32[5,18,3,128]{3,2,1,0:T(4,128)S(1)}, f32[5,18,3,128]{3,2,1,0:T(4,128)S(1)}, u32[]{:S(2)}, u32[]{:S(2)}) collective-permute-start(f32[5,18,3,128]{3,2,1,0:T(4,128)S(1)} %get-tuple-element.61), channel_id=1, source_target_pairs={{0,1},{1,0},{2,3},{3,2},{4,5},{5,4},{6,7},{7,6},{8,9},{9,8},{10,11... | collective-permute-start | bytes 414728 | tf_op jit(solution)/shard_map/ppermute | solution.py:29
  108.4 3.7 %collective-permute-start.7 = (f32[5,18,3,128]{3,2,1,0:T(4,128)S(1)}, f32[5,18,3,128]{3,2,1,0:T(4,128)S(1)}, u32[]{:S(2)}, u32[]{:S(2)}) collective-permute-start(f32[5,18,3,128]{3,2,1,0:T(4,128)S(1)} %get-tuple-element.62), channel_id=1, source_target_pairs={{1,0},{0,1},{3,2},{2,3},{5,4},{4,5},{7,6},{6,7},{9,8},{8,9},{11,10... | collective-permute-start | bytes 414728 | tf_op jit(solution)/shard_map/ppermute | solution.py:31
Sparse Core Ops, SparseCore 0:
  47.0 32.4 all-gather.4
  118.4 31.4 all-gather.6
where the time goes:
time: 160 us; the launch traced here: 159 us
  waiting for transfers between devices  63.5 us (40%)
  other arithmetic  39.5 us (25%)
  blocking collectives  30 us (19%)
  between operations  13.9 us (9%)
  starting transfers between devices  10.2 us (6%)
  local copies, waits for them, and re-layouts  2.27 us (1%)
    all_gather x2, waiting for transfers between devices, local(): lax.all_gather(rate[None], 'node', axis=0, tiled=True)  63.5 us
    pmax x2, blocking collectives, evaluate(): alphas = lax.pmax(local_speeds(fields), ('gx', 'gy'))  30 us
    add x6, other arithmetic, flux_along(): interface + reconstruct(window(left_going, 5), window(left_going, 4), win...  22.3 us
    ppermute x4, starting transfers between devices, padded_2(): lax.ppermute(head, axis, [((i + 1) % count, i) for i in range(count)])  5.42 us
    mul x6, other arithmetic, flux_along(): right_going = 0.5 * (fluxes + alpha * extended)  5.04 us
    ppermute x4, starting transfers between devices, padded_2(): lax.ppermute(tail, axis, [(i, (i + 1) % count) for i in range(count)])  4.75 us
    reduce_sum x2, other arithmetic, local(): jnp.sum(own_row[:, None, None, None, None] * lax.all_gather(rate[None], '...  3.7 us
  transfers between devices with their start and end apart: 10, of which 2 were waited for; matrix products, arithmetic and copies ran while one was open for 15% of the time, Pallas kernels for 0%

commit v1 on v0

v1 whole, which is shorter than its diff:
```python
import functools

import jax
import jax.numpy as jnp
from jax import lax
from jax.experimental import pallas as pl
from jax.experimental.pallas import tpu as pltpu
from jax.sharding import PartitionSpec as P

SWEEPS = 2
HALO = 3
COMPONENTS = 5

heat_ratio = 1.4
step_size = 0.025
density_floor = 0.5
pressure_floor = 0.25
epsilon = 1e-06
radau_weights = [
    [0.112999479323156, -0.040309220723522, 0.025802377420336, -0.009904676507266],
    [0.2343839957474, 0.206892573935359, -0.047857128048541, 0.016047422806516],
    [0.21668178462325, 0.406123263867373, 0.189036518170056, -0.024182104899833],
    [0.220462211176768, 0.388193468843172, 0.32884431998006, 0.0625],
]


def reciprocal(value):
    return pl.reciprocal(value, approx=True)


def primitives(fields):
    inverse = 1.0 / jnp.maximum(fields[0], density_floor)
    velocity = [fields[k] * inverse for k in (1, 2, 3)]
    energy = fields[1] * velocity[0] + fields[2] * velocity[1] + fields[3] * velocity[2]
    pressure = jnp.maximum(0.4 * (fields[4] - 0.5 * energy), pressure_floor)
    return inverse, velocity, pressure


def signal_speeds(fields):
    inverse, velocity, pressure = primitives(fields)
    sound = jnp.sqrt(heat_ratio * pressure * inverse)
    return [jnp.abs(v) + sound for v in velocity]


def half_fluxes(half, speed, half_pressure, direction):
    flux = [half[direction + 1]] + [half[k] * speed for k in (1, 2, 3)]
    flux.append((half[4] + half_pressure) * speed)
    flux[direction + 1] = flux[direction + 1] + half_pressure
    return flux


def splits(fields, alphas, directions=(0, 1, 2)):
    _, velocity, pressure = primitives(fields)
    half = [0.5 * field for field in fields]
    half_pressure = 0.5 * pressure
    out = []
    for direction in directions:
        flux = half_fluxes(half, velocity[direction], half_pressure, direction)
        signal = [alphas[direction] * value for value in half]
        out.append(
            ([f + s for f, s in zip(flux, signal)], [f - s for f, s in zip(flux, signal)])
        )
    return out


def cell_terms(below, above):
    second = above - below
    both = below + above
    square = second * second
    middle = 0.25 * (both * both) + ((13.0 / 12.0) * square + epsilon)
    outer = middle + square
    cross = both * second
    return second, outer + cross, middle, outer - cross


def correction(first, middle, last, third_first, third_last):
    ratio_first = middle * reciprocal(first)
    ratio_last = middle * reciprocal(last)
    weight_first = ratio_first * ratio_first
    weight_last = 1.5 * (ratio_last * ratio_last)
    total = (6.0 + weight_first) + (weight_last + weight_last)
    return (weight_first * third_first + weight_last * third_last) * reciprocal(total)


def stream(load, store, count):
    plus, minus, centre = {}, {}, {}
    terms_plus, terms_minus, third_plus, third_minus, interface = {}, {}, {}, {}, {}
    differences_plus, differences_minus = {}, {}
    plus[0], minus[0] = load(0)
    for j in range(1, count + 2 * HALO):
        plus[j], minus[j] = load(j)
        differences_plus[j] = plus[j] - plus[j - 1]
        differences_minus[j] = minus[j] - minus[j - 1]
        cell = j - 1
        if cell < 1:
            continue
        terms_plus[cell] = cell_terms(differences_plus[cell], differences_plus[j])
        terms_minus[cell] = cell_terms(differences_minus[cell], differences_minus[j])
        if 2 <= cell <= count + 3:
            centre[cell] = 6.0 * (plus[cell] + minus[cell]) - (
                terms_plus[cell][0] + terms_minus[cell][0]
            )
        if cell < 2:
            continue
        third_plus[cell] = terms_plus[cell][0] - terms_plus[cell - 1][0]
        third_minus[cell] = terms_minus[cell][0] - terms_minus[cell - 1][0]
        if cell < 4:
            continue
        at = cell - 2
        right = correction(
            terms_plus[at - 1][1], terms_plus[at][2], terms_plus[at + 1][3], third_plus[at], third_plus[at + 1]
        )
        left = correction(
            terms_minus[at + 2][3], terms_minus[at + 1][2], terms_minus[at][1],
            third_minus[at + 2], third_minus[at + 1],
        )
        interface[at] = (third_plus[at + 1] - third_minus[at + 1]) - 4.0 * (right - left)
        if at >= 3:
            store(at - 3, (centre[at - 1] - centre[at + 1]) + (interface[at - 1] - interface[at]))


def rolled(plus, minus):
    size = plus.shape[-1]

    def nxt(value, by=1):
        return pltpu.roll(value, size - by, value.ndim - 1)

    def prev(value):
        return pltpu.roll(value, 1, value.ndim - 1)

    above = nxt(plus) - plus
    second_plus, first_p, middle_p, last_p = cell_terms(prev(above), above)
    above = nxt(minus) - minus
    second_minus, first_m, middle_m, last_m = cell_terms(prev(above), above)
    centre = 6.0 * (plus + minus) - (second_plus + second_minus)
    third_plus = nxt(second_plus) - second_plus
    third_minus = nxt(second_minus) - second_minus
    right = correction(prev(first_p), middle_p, nxt(last_p), prev(third_plus), third_plus)
    left = correction(nxt(last_m, 2), nxt(middle_m), first_m, nxt(third_minus), third_minus)
    interface = (third_plus - third_minus) - 4.0 * (right - left)
    return (prev(centre) - nxt(centre)) + (prev(interface) - interface)


def rhs_kernel(u_ref, xlo_ref, xhi_ref, yh_ref, al_ref, out_ref, xp, xm, yp, ym, fy):
    comps, nx, ny, nz = u_ref.shape
    rows = yh_ref.shape[1]
    every = range(comps)
    alphas = [al_ref[k : k + 1, :] for k in range(3)]

    def own(i, carry):
        fields = [u_ref[c, i] for c in every]
        along_x, along_y, along_z = splits(fields, alphas)
        for c in every:
            xp[i + HALO, c * ny : (c + 1) * ny, :] = along_x[0][c]
            xm[i + HALO, c * ny : (c + 1) * ny, :] = along_x[1][c]
            for t in range(0, ny, 8):
                at = pl.ds((HALO + t) * rows + c * nx + i, 8, stride=rows)
                yp[at, :] = along_y[0][c][t : t + 8]
                ym[at, :] = along_y[1][c][t : t + 8]
            out_ref[c, i] = rolled(along_z[0][c], along_z[1][c])
        return carry

    lax.fori_loop(0, nx, own, 0)

    for ref, start in ((xlo_ref, 0), (xhi_ref, nx + HALO)):

        def ghost_x(i, carry, ref=ref, start=start):
            ((p, m),) = splits([ref[c, i] for c in every], alphas, (0,))
            for c in every:
                xp[start + i, c * ny : (c + 1) * ny, :] = p[c]
                xm[start + i, c * ny : (c + 1) * ny, :] = m[c]
            return carry

        lax.fori_loop(0, HALO, ghost_x, 0)

    def ghost_y(i, carry):
        row = jnp.where(i < HALO, i, i + ny) * rows
        ((p, m),) = splits([yh_ref[i, c * nx : (c + 1) * nx, :] for c in every], alphas, (1,))
        for c in every:
            yp[pl.ds(row + c * nx, nx), :] = p[c]
            ym[pl.ds(row + c * nx, nx), :] = m[c]
        return carry

    lax.fori_loop(0, 2 * HALO, ghost_y, 0)

    def along_second(b, carry):
        first = pl.multiple_of(b * 8, 8)

        def load(j):
            return yp[pl.ds(j * rows + first, 8), :], ym[pl.ds(j * rows + first, 8), :]

        def store(i, value):
            fy[pl.ds(i * rows + first, 8), :] = value

        stream(load, store, ny)
        return carry

    lax.fori_loop(0, rows // 8, along_second, 0)

    for c in every:

        def along_first(b, carry, c=c):
            first = pl.multiple_of(b * 8, 8)

            def load(j):
                at = pl.ds(c * ny + first, 8)
                return xp[j, at, :], xm[j, at, :]

            def store(i, value):
                cross = fy[pl.ds(first * rows + c * nx + i, 8, stride=rows), :]
                here = pl.ds(first, 8)
                out_ref[c, i, here, :] = out_ref[c, i, here, :] + value + cross

            stream(load, store, nx)
            return carry

        lax.fori_loop(0, ny // 8, along_first, 0)


def right_hand_side(fields, lower, upper, sides, alphas):
    comps, nx, ny, nz = fields.shape
    rows = sides.shape[1]
    vmem = pl.BlockSpec(memory_space=pltpu.VMEM)
    return pl.pallas_call(
        rhs_kernel,
        out_shape=jax.ShapeDtypeStruct(fields.shape, jnp.float32),
        in_specs=[vmem] * 5,
        out_specs=vmem,
        scratch_shapes=[
            pltpu.VMEM((nx + 2 * HALO, comps * ny, nz), jnp.float32),
            pltpu.VMEM((nx + 2 * HALO, comps * ny, nz), jnp.float32),
            pltpu.VMEM(((ny + 2 * HALO) * rows, nz), jnp.float32),
            pltpu.VMEM(((ny + 2 * HALO) * rows, nz), jnp.float32),
            pltpu.VMEM((ny * rows, nz), jnp.float32),
        ],
        compiler_params=pltpu.CompilerParams(vmem_limit_bytes=24 * 1024 * 1024),
        cost_estimate=pl.CostEstimate(flops=30_000_000, bytes_accessed=1_500_000, transcendentals=0),
        name="right_hand_side",
    )(fields, lower, upper, sides, alphas)


def shifted(value, axis, by):
    count = lax.axis_size(axis)
    return lax.ppermute(value, axis, [(i, (i + by) % count) for i in range(count)])


def local_speeds(fields):
    return jnp.stack([jnp.max(s) for s in signal_speeds([fields[c] for c in range(COMPONENTS)])])


def evaluate(fields):
    comps, nx, ny, nz = fields.shape
    speeds = lax.pmax(local_speeds(fields), ("gx", "gy"))
    alphas = jnp.broadcast_to(jnp.pad(speeds, (0, 5))[:, None], (8, nz))
    lower = shifted(fields[:, -HALO:], "gx", 1)
    upper = shifted(fields[:, :HALO], "gx", -1)
    leading = jnp.moveaxis(fields, 2, 0).reshape(ny, comps * nx, nz)
    pad = -(comps * nx) % 8
    leading = jnp.pad(leading, ((0, 0), (0, pad), (0, 0)))
    sides = jnp.concatenate([shifted(leading[-HALO:], "gy", 1), shifted(leading[:HALO], "gy", -1)])
    return right_hand_side(fields, lower, upper, sides, alphas)


def local(initial, guesses):
    weights_table = jnp.array(radau_weights, jnp.float32) * (step_size / 12.0)
    node_index = lax.axis_index("node")
    current = guesses[0]
    for sweep_index in range(SWEEPS):
        rate = evaluate(current)
        own_row = lax.dynamic_index_in_dim(weights_table, node_index, 0, keepdims=False)
        gathered = lax.all_gather(rate[None], "node", axis=0, tiled=True)
        current = initial + jnp.sum(own_row[:, None, None, None, None] * gathered, axis=0)
    return current[None]


def solution(mesh):
    return jax.shard_map(
        local,
        mesh=mesh,
        in_specs=(P(None, "gx", "gy", None), P("node", None, "gx", "gy", None)),
        out_specs=P("node", None, "gx", "gy", None),
        check_vma=False,
    )
```

time: 160 us -> 153 us (0.956)
  other arithmetic: 39.5 us -> 10.1 us
  Pallas kernels: 0 us -> 18.7 us
  blocking collectives: 30 us -> 34.1 us
    add x9 -> x1, other arithmetic: 24.4 us -> 0.07 us  [local(): initial + jnp.sum(own_row[:, None, None, None, None] * gathered, axis=0)]
    pallas_call x0 -> x2, Pallas kernels: none -> 18.7 us  [right_hand_side(): pl.pallas_call(rhs_kernel, out_shape=jax.ShapeDtypeStruct(fields.shape, j...]
    mul x6 -> x0, other arithmetic: 5.04 us -> none  [flux_along(): right_going = 0.5 * (fluxes + alpha * extended)]
    pmax x2, blocking collectives: 30 us -> 34.1 us  [evaluate(): speeds = lax.pmax(local_speeds(fields), ('gx', 'gy'))]
    another operation x6 -> x2, other arithmetic: 0.26 us -> 3.93 us  [local_speeds(): jnp.stack([jnp.max(s) for s in signal_speeds([fields[c] for c in range(CO...]
    reduce_sum x10 -> x2, other arithmetic: 4.27 us -> 3.66 us  [local(): jnp.sum(own_row[:, None, None, None, None] * gathered, axis=0)]
  transfers between devices with their start and end apart: 10 -> 10, of which waited for: 2 -> 2; matrix products, arithmetic and copies ran while one was open for 15% -> 4% of each run, Pallas kernels for 0% -> 0%
where the time goes in v1:
time: 153 us
  waiting for transfers between devices  63.5 us (42%)
  blocking collectives  34.1 us (22%)
  Pallas kernels  18.7 us (12%)
  between operations  13.5 us (9%)
  other arithmetic  10.1 us (7%)
  starting transfers between devices  9.67 us (6%)
  local copies, waits for them, and re-layouts  3.29 us (2%)
    all_gather x2, waiting for transfers between devices, local(): gathered = lax.all_gather(rate[None], 'node', axis=0, tiled=True)  63.5 us
    pmax x2, blocking collectives, evaluate(): speeds = lax.pmax(local_speeds(fields), ('gx', 'gy'))  34.1 us
    pallas_call x2, Pallas kernels, right_hand_side(): pl.pallas_call(rhs_kernel, out_shape=jax.ShapeDtypeStruct(fields.shape, j...  18.7 us
    ppermute x8, starting transfers between devices, shifted(): lax.ppermute(value, axis, [(i, (i + by) % count) for i in range(count)])  9.62 us
    another operation x2, other arithmetic, local_speeds(): jnp.stack([jnp.max(s) for s in signal_speeds([fields[c] for c in range(CO...  3.93 us
    reduce_sum x2, other arithmetic, local(): jnp.sum(own_row[:, None, None, None, None] * gathered, axis=0)  3.66 us
  transfers between devices with their start and end apart: 10, of which 2 were waited for; matrix products, arithmetic and copies ran while one was open for 4% of the time, Pallas kernels for 0%

profile of v1, /device:TPU:0, one launch (start us, length us, event | category | flops | bytes accessed | tf_op | source)
XLA Modules:
  0.0 152.9 jit_solution(16802202158250544490)
XLA Ops:
  6.5 0.0 copy-start
  6.5 0.0 all-gather.5.cloned.1.call-start
  6.5 1.0 fusion.27
  7.6 5.1 %collective-permute-start.1 = (f32[5,3,16,128]{3,2,1,0:T(8,128)S(1)}, f32[5,3,16,128]{3,2,1,0:T(8,128)S(1)}, u32[]{:S(2)}, u32[]{:S(2)}) collective-permute-start(f32[5,3,16,128]{3,2,1,0:T(8,128)S(1)} %get-tuple-element.17), channel_id=1, source_target_pairs={{0,6},{2,0},{4,2},{6,4},{1,7},{3,1},{5,3},{7,5},{8,14},{10,8},{12,... | collective-permute-start | bytes 368648 | tf_op jit(solution)/shard_map/ppermute | solution.py:244
  12.7 0.0 collective-permute-start
  12.7 1.2 copy.8
  13.9 0.1 collective-permute-start.2
  14.0 0.5 collective-permute-start.3
  14.5 0.0 copy-done
  14.5 0.8 add_reduce_fusion.3
  15.3 2.0 %pad_maximum_fusion.2 = f32[3]{0:T(128)S(1)} fusion(f32[1]{0:T(128)} %bitcast.11, f32[1]{0:T(128)} %bitcast.10, f32[1]{0:T(128)} %bitcast.9), kind=kLoop, calls=%fused_computation.51 | loop fusion | flops 6 | bytes 24 | tf_op jit(solution)/shard_map/stack | solution.py:248
  17.2 17.1 %pmax.14 = f32[3]{0:T(128)S(1)} all-reduce(f32[3]{0:T(128)S(1)} %pad_maximum_fusion.2), channel_id=1, replica_groups=mesh['node'=4,'gx'=4,'gy'=2] {'gx','gy'}, use_global_device_ids=true, to_apply=%region_3.0 | all-reduce | flops 3 | bytes 24 | tf_op jit(solution)/shard_map/pmax | solution.py:253
  34.3 0.0 collective-permute-done.2
  34.3 0.0 collective-permute-done.3
  34.3 0.0 collective-permute-done.1.xhi_ref
  34.3 0.0 collective-permute-done.xlo_ref
  34.4 0.1 broadcast_in_dim.10.al_ref
  34.4 0.0 copy-start.1
  34.4 9.3 %right_hand_side.2 = f32[5,12,16,128]{3,2,1,0:T(8,128)} custom-call(f32[5,12,16,128]{3,2,1,0:T(8,128)S(1)} %bitcast.155, f32[5,3,16,128]{3,2,1,0:T(8,128)S(1)} %collective-permute-done.xlo_ref, f32[5,3,16,128]{3,2,1,0:T(8,128)S(1)} %collective-permute-done.1.xhi_ref, f32[6,64,128]{2,1,0:T(8,128)S(1)} %pad_maximum_fusion.yh_ref, ...), custom_call_target="tpu_custom_call" | custom-call | flops 30000000 | bytes 1500000 | tf_op jit(solution)/shard_map/right_hand_side/pallas_call | solution.py:224
  43.8 0.0 all-gather.5.cloned.1.call-update
  43.8 0.0 all-gather.7.cloned.1.call-start
  43.8 0.7 dynamic-slice_bitcast_fusion
  44.5 31.8 %all-gather.5.cloned.1.call-done = f32[20,12,16,128]{3,2,1,0:T(8,128)} async-done(((f32[5,12,16,128]{3,2,1,0:T(8,128)}), f32[20,12,16,128]{3,2,1,0:T(8,128)}) %all-gather.5.cloned.1.call-update) | async-done | bytes 1966096 | tf_op jit(solution)/shard_map/all_gather | solution.py:271
  76.4 1.8 %multiply_reduce_fusion.1 = f32[5,12,16,128]{3,2,1,0:T(8,128)S(1)} fusion(f32[4,5,12,16,128]{4,3,2,1,0:T(8,128)} %bitcast.156, f32[4]{0:T(128)S(1)} %dynamic-slice_bitcast_fusion), kind=kLoop, calls=%fused_computation.1 | loop fusion | flops 860160 | bytes 2457616 | tf_op jit(solution)/shard_map/reduce_sum | solution.py:272
  78.2 0.0 copy-done.1
  78.2 0.1 add.55.u_ref
  78.3 0.8 add_reduce_fusion.2
  79.1 3.4 %collective-permute-start.5 = (f32[5,3,16,128]{3,2,1,0:T(8,128)S(1)}, f32[5,3,16,128]{3,2,1,0:T(8,128)S(1)}, u32[]{:S(2)}, u32[]{:S(2)}) collective-permute-start(f32[5,3,16,128]{3,2,1,0:T(8,128)S(1)} %get-tuple-element.15), channel_id=1, source_target_pairs={{0,6},{2,0},{4,2},{6,4},{1,7},{3,1},{5,3},{7,5},{8,14},{10,8},{12,... | collective-permute-start | bytes 368648 | tf_op jit(solution)/shard_map/ppermute | solution.py:244
  82.5 0.0 collective-permute-start.4
  82.5 0.2 copy.9
  82.7 0.1 collective-permute-start.6
  82.8 0.5 collective-permute-start.7
  83.3 2.0 %pad_maximum_fusion.3 = f32[3]{0:T(128)S(1)} fusion(f32[1]{0:T(128)} %bitcast.22, f32[1]{0:T(128)} %bitcast.21, f32[1]{0:T(128)} %bitcast.20), kind=kLoop, calls=%fused_computation.52 | loop fusion | flops 6 | bytes 24 | tf_op jit(solution)/shard_map/stack | solution.py:248
  85.2 17.1 %pmax.15 = f32[3]{0:T(128)S(1)} all-reduce(f32[3]{0:T(128)S(1)} %pad_maximum_fusion.3), channel_id=1, replica_groups=mesh['node'=4,'gx'=4,'gy'=2] {'gx','gy'}, use_global_device_ids=true, to_apply=%region_8.9 | all-reduce | flops 3 | bytes 24 | tf_op jit(solution)/shard_map/pmax | solution.py:253
  102.3 0.0 collective-permute-done.6
  102.3 0.0 collective-permute-done.7
  102.3 0.0 collective-permute-done.5.xhi_ref
  102.3 0.0 collective-permute-done.4.xlo_ref
  102.4 0.1 broadcast_in_dim.12.al_ref
  102.4 9.3 %right_hand_side.3 = f32[5,12,16,128]{3,2,1,0:T(8,128)} custom-call(f32[5,12,16,128]{3,2,1,0:T(8,128)S(1)} %add.55.u_ref, f32[5,3,16,128]{3,2,1,0:T(8,128)S(1)} %collective-permute-done.4.xlo_ref, f32[5,3,16,128]{3,2,1,0:T(8,128)S(1)} %collective-permute-done.5.xhi_ref, f32[6,64,128]{2,1,0:T(8,128)S(1)} %pad_maximum_fusion.1.yh_ref, ...), custom_call_target="tpu_custom_call" | custom-call | flops 30000000 | bytes 1500000 | tf_op jit(solution)/shard_map/right_hand_side/pallas_call | solution.py:224
  111.8 0.0 all-gather.7.cloned.1.call-update
  111.8 31.6 %all-gather.7.cloned.1.call-done = f32[20,12,16,128]{3,2,1,0:T(8,128)} async-done(((f32[5,12,16,128]{3,2,1,0:T(8,128)}), f32[20,12,16,128]{3,2,1,0:T(8,128)}) %all-gather.7.cloned.1.call-update) | async-done | bytes 1966096 | tf_op jit(solution)/shard_map/all_gather | solution.py:271
  143.4 1.8 %multiply_reduce_fusion = f32[5,12,16,128]{3,2,1,0:T(8,128)S(1)} fusion(f32[4,5,12,16,128]{4,3,2,1,0:T(8,128)} %bitcast.157, f32[4]{0:T(128)S(1)} %dynamic-slice_bitcast_fusion), kind=kLoop, calls=%fused_computation | loop fusion | flops 860160 | bytes 2457616 | tf_op jit(solution)/shard_map/reduce_sum | solution.py:272
  145.2 0.8 add_bitcast_fusion
  (7 shorter events, 0.1 us)
Async XLA Ops:
  6.5 7.9 %copy-start = (f32[1,5,12,16,128]{4,3,2,1,0:T(8,128)S(1)}, f32[1,5,12,16,128]{4,3,2,1,0:T(8,128)}, u32[]{:S(2)}) copy-start(f32[1,5,12,16,128]{4,3,2,1,0:T(8,128)} %param.4) | copy-start | bytes 1474564
  6.5 69.8 %all-gather.5.cloned.1.call-start = ((), (), s32[]{:S(2)}) async-start(), calls=%async_computation | async-start | bytes 2457600 | tf_op jit(solution)/shard_map/all_gather | solution.py:271
  7.6 26.8 %collective-permute-start.1 = (f32[5,3,16,128]{3,2,1,0:T(8,128)S(1)}, f32[5,3,16,128]{3,2,1,0:T(8,128)S(1)}, u32[]{:S(2)}, u32[]{:S(2)}) collective-permute-start(f32[5,3,16,128]{3,2,1,0:T(8,128)S(1)} %get-tuple-element.17), channel_id=1, source_target_pairs={{0,6},{2,0},{4,2},{6,4},{1,7},{3,1},{5,3},{7,5},{8,14},{10,8},{12,... | collective-permute-start | bytes 368648 | tf_op jit(solution)/shard_map/ppermute | solution.py:244
  12.7 21.7 %collective-permute-start = (f32[5,3,16,128]{3,2,1,0:T(8,128)S(1)}, f32[5,3,16,128]{3,2,1,0:T(8,128)S(1)}, u32[]{:S(2)}, u32[]{:S(2)}) collective-permute-start(f32[5,3,16,128]{3,2,1,0:T(8,128)S(1)} %get-tuple-element.18), channel_id=1, source_target_pairs={{0,2},{2,4},{4,6},{6,0},{1,3},{3,5},{5,7},{7,1},{8,10},{10,12},{12... | collective-permute-start | bytes 368648 | tf_op jit(solution)/shard_map/ppermute | solution.py:244
  13.9 20.4 %collective-permute-start.2 = (f32[3,64,128]{2,1,0:T(8,128)S(1)}, f32[3,64,128]{2,1,0:T(8,128)S(1)}, u32[]{:S(2)}, u32[]{:S(2)}) collective-permute-start(f32[3,64,128]{2,1,0:T(8,128)S(1)} %get-tuple-element.13), channel_id=1, source_target_pairs={{0,1},{1,0},{2,3},{3,2},{4,5},{5,4},{6,7},{7,6},{8,9},{9,8},{10,11... | collective-permute-start | bytes 294920 | tf_op jit(solution)/shard_map/ppermute | solution.py:244
  14.0 20.3 %collective-permute-start.3 = (f32[3,64,128]{2,1,0:T(8,128)S(1)}, f32[3,64,128]{2,1,0:T(8,128)S(1)}, u32[]{:S(2)}, u32[]{:S(2)}) collective-permute-start(f32[3,64,128]{2,1,0:T(8,128)S(1)} %get-tuple-element.14), channel_id=1, source_target_pairs={{0,1},{1,0},{2,3},{3,2},{4,5},{5,4},{6,7},{7,6},{8,9},{9,8},{10,11... | collective-permute-start | bytes 294920 | tf_op jit(solution)/shard_map/ppermute | solution.py:244
  34.4 43.8 %copy-start.1 = (f32[5,12,16,128]{3,2,1,0:T(8,128)S(1)}, f32[5,12,16,128]{3,2,1,0:T(8,128)}, u32[]{:S(2)}) copy-start(f32[5,12,16,128]{3,2,1,0:T(8,128)} %param.3) | copy-start | bytes 1474564
  43.8 99.6 %all-gather.7.cloned.1.call-start = ((), (), s32[]{:S(2)}) async-start(), calls=%async_computation.1 | async-start | bytes 2457600 | tf_op jit(solution)/shard_map/all_gather | solution.py:271
  79.1 23.2 %collective-permute-start.5 = (f32[5,3,16,128]{3,2,1,0:T(8,128)S(1)}, f32[5,3,16,128]{3,2,1,0:T(8,128)S(1)}, u32[]{:S(2)}, u32[]{:S(2)}) collective-permute-start(f32[5,3,16,128]{3,2,1,0:T(8,128)S(1)} %get-tuple-element.15), channel_id=1, source_target_pairs={{0,6},{2,0},{4,2},{6,4},{1,7},{3,1},{5,3},{7,5},{8,14},{10,8},{12,... | collective-permute-start | bytes 368648 | tf_op jit(solution)/shard_map/ppermute | solution.py:244
  82.5 19.9 %collective-permute-start.4 = (f32[5,3,16,128]{3,2,1,0:T(8,128)S(1)}, f32[5,3,16,128]{3,2,1,0:T(8,128)S(1)}, u32[]{:S(2)}, u32[]{:S(2)}) collective-permute-start(f32[5,3,16,128]{3,2,1,0:T(8,128)S(1)} %get-tuple-element.16), channel_id=1, source_target_pairs={{0,2},{2,4},{4,6},{6,0},{1,3},{3,5},{5,7},{7,1},{8,10},{10,12},{12... | collective-permute-start | bytes 368648 | tf_op jit(solution)/shard_map/ppermute | solution.py:244
  82.7 19.6 %collective-permute-start.6 = (f32[3,64,128]{2,1,0:T(8,128)S(1)}, f32[3,64,128]{2,1,0:T(8,128)S(1)}, u32[]{:S(2)}, u32[]{:S(2)}) collective-permute-start(f32[3,64,128]{2,1,0:T(8,128)S(1)} %get-tuple-element.11), channel_id=1, source_target_pairs={{0,1},{1,0},{2,3},{3,2},{4,5},{5,4},{6,7},{7,6},{8,9},{9,8},{10,11... | collective-permute-start | bytes 294920 | tf_op jit(solution)/shard_map/ppermute | solution.py:244
  82.8 19.5 %collective-permute-start.7 = (f32[3,64,128]{2,1,0:T(8,128)S(1)}, f32[3,64,128]{2,1,0:T(8,128)S(1)}, u32[]{:S(2)}, u32[]{:S(2)}) collective-permute-start(f32[3,64,128]{2,1,0:T(8,128)S(1)} %get-tuple-element.12), channel_id=1, source_target_pairs={{0,1},{1,0},{2,3},{3,2},{4,5},{5,4},{6,7},{7,6},{8,9},{9,8},{10,11... | collective-permute-start | bytes 294920 | tf_op jit(solution)/shard_map/ppermute | solution.py:244
Sparse Core Ops, SparseCore 0:
  43.9 32.4 all-gather.4
  111.9 31.4 all-gather.6

commit v2 on v1

--- a/solution.py
+++ b/solution.py
@@ -10,6 +10,7 @@
 SWEEPS = 2
 HALO = 3
 COMPONENTS = 5
+TILE = 8
 
 heat_ratio = 1.4
 step_size = 0.025
@@ -141,31 +142,178 @@
     return (prev(centre) - nxt(centre)) + (prev(interface) - interface)
 
 
-def rhs_kernel(u_ref, xlo_ref, xhi_ref, yh_ref, al_ref, out_ref, xp, xm, yp, ym, fy):
-    comps, nx, ny, nz = u_ref.shape
-    rows = yh_ref.shape[1]
+def lane_index(shape):
+    return lax.broadcasted_iota(jnp.int32, shape, len(shape) - 1)
+
+
+def turned(value, by):
+    size = value.shape[-1]
+    if isinstance(by, int):
+        by = by % size
+        return value if by == 0 else pltpu.roll(value, by, value.ndim - 1)
+    return pltpu.roll(value, lax.rem(by + 4 * size, size), value.ndim - 1)
+
+
+def merged(pieces, slot):
+    out = pieces[0]
+    for number, piece in enumerate(pieces[1:], 1):
+        out = jnp.where(slot == number, piece, out)
+    return out
+
+
+def node_weights(me, count):
+    def picked(row, column):
+        values = [radau_weights[n ^ row][n ^ column] * (step_size / 12.0) for n in range(count)]
+        out = jnp.float32(values[0])
+        for n in range(1, count):
+            out = jnp.where(me == n, jnp.float32(values[n]), out)
+        return out
+
+    return [[picked(row, column) for column in range(count)] for row in range(count)]
+
+
+class Windows:
+    def __init__(self, nx, nz, nodes):
+        self.nodes = nodes
+        self.width = nz // nodes
+        self.pitch = self.width + 8
+        self.slots = nz // self.pitch
+        assert nx % self.slots == 0 and nz % nodes == 0
+        self.rows = nx // self.slots
+
+    def slot(self, shape):
+        return lane_index(shape) // self.pitch
+
+    def group(self, shape):
+        return lane_index(shape) // self.width
+
+    def cut(self, values, quarter):
+        pieces = [
+            turned(value, self.pitch * s + HALO - self.width * quarter) for s, value in enumerate(values)
+        ]
+        return merged(pieces, self.slot(values[0].shape))
+
+    def joined(self, values, s):
+        pieces = [
+            turned(value, self.width * k - self.pitch * s - HALO) for k, value in enumerate(values)
+        ]
+        return merged(pieces, self.group(values[0].shape))
+
+
+def write_edges(read, nx, ny, comps, lo_ref, hi_ref, side_ref):
+    rows = side_ref.shape[1] // (2 * HALO)
+    for c in range(comps):
+        for i in range(HALO):
+            lo_ref[0, pl.ds((c * HALO + i) * ny, ny), :] = read(c, i)
+            hi_ref[0, pl.ds((c * HALO + i) * ny, ny), :] = read(c, nx - HALO + i)
+
+    def side(i, carry):
+        for c in range(comps):
+            value = read(c, i)
+            side_ref[0, pl.ds(c * nx + i, HALO, stride=rows), :] = value[ny - HALO :]
+            side_ref[0, pl.ds(HALO * rows + c * nx + i, HALO, stride=rows), :] = value[:HALO]
+        return carry
+
+    lax.fori_loop(0, nx, side, 0)
+
+
+def speed_rows(read, nx, ny, nz, comps):
+    def step(i, best):
+        speeds = signal_speeds([read(c, i) for c in range(comps)])
+        return tuple(jnp.maximum(b, s) for b, s in zip(best, speeds))
+
+    best = lax.fori_loop(0, nx, step, tuple(jnp.zeros((ny, nz), jnp.float32) for _ in range(3)))
+    return [jnp.max(b, axis=0, keepdims=True) for b in best]
+
+
+def alpha_tile(rows, group):
+    nz = rows[0].shape[-1]
+    tile = jnp.concatenate(rows + [jnp.zeros((TILE - 3, nz), jnp.float32)], axis=0)
+    lane = lane_index(tile.shape)
+    by = 1
+    while by < group:
+        other = jnp.where((lane & by) != 0, turned(tile, by), turned(tile, -by))
+        tile = jnp.maximum(tile, other)
+        by *= 2
+    return tile
+
+
+def open_kernel(u_ref, lo_ref, hi_ref, side_ref, al_ref):
+    comps, nx, ny, nz = u_ref.shape[1:]
+
+    def read(c, i):
+        return u_ref[0, c, i]
+
+    write_edges(read, nx, ny, comps, lo_ref, hi_ref, side_ref)
+    tile = alpha_tile(speed_rows(read, nx, ny, nz, comps), nz)
+    al_ref[...] = tile
+    lo_ref[0, pl.ds(comps * HALO * ny, TILE), :] = tile
+    hi_ref[0, pl.ds(comps * HALO * ny, TILE), :] = tile
+
+
+def blend_kernel(init_ref, *refs):
+    comps, nx, ny, nz = init_ref.shape
+    nodes = len(refs) - 6
+    parts, (win_ref, nat_ref, lo_ref, hi_ref, side_ref, al_ref) = refs[:nodes], refs[nodes:]
+    windows = Windows(nx, nz, nodes)
+    me = lax.axis_index("node")
+    weights = node_weights(me, nodes)
+
+    def step(c, carry):
+        for r in range(windows.rows):
+            at = pl.ds(pl.multiple_of((c * windows.rows + r) * ny, ny), ny)
+            start = windows.cut([init_ref[c, s * windows.rows + r] for s in range(windows.slots)], me)
+            rates = [part[at, :] for part in parts]
+            states = []
+            for k in range(nodes):
+                value = start
+                for j in range(nodes):
+                    value = value + weights[k][j] * rates[j]
+                win_ref[k, at, :] = value
+                states.append(value)
+            for s in range(windows.slots):
+                nat_ref[c, s * windows.rows + r] = windows.joined(states, s)
+        return carry
+
+    lax.fori_loop(0, comps, step, 0)
+
+    def read(c, i):
+        return nat_ref[c, i]
+
+    write_edges(read, nx, ny, comps, lo_ref, hi_ref, side_ref)
+    tile = alpha_tile(speed_rows(read, nx, ny, nz, comps), windows.width)
+    al_ref[...] = tile
+    lo_ref[0, pl.ds(comps * HALO * ny, TILE), :] = tile
+    hi_ref[0, pl.ds(comps * HALO * ny, TILE), :] = tile
+
+
+def along_grid(u, alphas, lo_ref, hi_ref, side_ref, out_ref, scratch, depth):
+    xp, xm, yp, ym, fy = scratch
+    comps, nx, ny, nz = out_ref.shape
+    rows = yp.shape[0] // (ny + 2 * HALO)
     every = range(comps)
-    alphas = [al_ref[k : k + 1, :] for k in range(3)]
 
     def own(i, carry):
-        fields = [u_ref[c, i] for c in every]
-        along_x, along_y, along_z = splits(fields, alphas)
+        split = splits([u(c, i) for c in every], alphas, (0, 1, 2) if depth else (0, 1))
+        along_x, along_y = split[:2]
         for c in every:
             xp[i + HALO, c * ny : (c + 1) * ny, :] = along_x[0][c]
             xm[i + HALO, c * ny : (c + 1) * ny, :] = along_x[1][c]
-            for t in range(0, ny, 8):
-                at = pl.ds((HALO + t) * rows + c * nx + i, 8, stride=rows)
-                yp[at, :] = along_y[0][c][t : t + 8]
-                ym[at, :] = along_y[1][c][t : t + 8]
-            out_ref[c, i] = rolled(along_z[0][c], along_z[1][c])
+            for t in range(0, ny, TILE):
+                at = pl.ds((HALO + t) * rows + c * nx + i, TILE, stride=rows)
+                yp[at, :] = along_y[0][c][t : t + TILE]
+                ym[at, :] = along_y[1][c][t : t + TILE]
+            if depth:
+                out_ref[c, i] = rolled(split[2][0][c], split[2][1][c])
         return carry
 
     lax.fori_loop(0, nx, own, 0)
 
-    for ref, start in ((xlo_ref, 0), (xhi_ref, nx + HALO)):
+    for ref, start in ((lo_ref, 0), (hi_ref, nx + HALO)):
 
         def ghost_x(i, carry, ref=ref, start=start):
-            ((p, m),) = splits([ref[c, i] for c in every], alphas, (0,))
+            fields = [ref[0, pl.ds(pl.multiple_of((c * HALO + i) * ny, ny), ny), :] for c in every]
+            ((p, m),) = splits(fields, alphas, (0,))
             for c in every:
                 xp[start + i, c * ny : (c + 1) * ny, :] = p[c]
                 xm[start + i, c * ny : (c + 1) * ny, :] = m[c]
@@ -175,7 +323,7 @@
 
     def ghost_y(i, carry):
         row = jnp.where(i < HALO, i, i + ny) * rows
-        ((p, m),) = splits([yh_ref[i, c * nx : (c + 1) * nx, :] for c in every], alphas, (1,))
+        ((p, m),) = splits([side_ref[0, pl.ds(i * rows + c * nx, nx), :] for c in every], alphas, (1,))
         for c in every:
             yp[pl.ds(row + c * nx, nx), :] = p[c]
             ym[pl.ds(row + c * nx, nx), :] = m[c]
@@ -184,59 +332,156 @@
     lax.fori_loop(0, 2 * HALO, ghost_y, 0)
 
     def along_second(b, carry):
-        first = pl.multiple_of(b * 8, 8)
+        first = pl.multiple_of(b * TILE, TILE)
 
         def load(j):
-            return yp[pl.ds(j * rows + first, 8), :], ym[pl.ds(j * rows + first, 8), :]
+            at = pl.ds(j * rows + first, TILE)
+            return yp[at, :], ym[at, :]
 
         def store(i, value):
-            fy[pl.ds(i * rows + first, 8), :] = value
+            fy[pl.ds(i * rows + first, TILE), :] = value
 
         stream(load, store, ny)
         return carry
 
-    lax.fori_loop(0, rows // 8, along_second, 0)
+    lax.fori_loop(0, rows // TILE, along_second, 0)
 
     for c in every:
 
         def along_first(b, carry, c=c):
-            first = pl.multiple_of(b * 8, 8)
+            first = pl.multiple_of(b * TILE, TILE)
 
             def load(j):
-                at = pl.ds(c * ny + first, 8)
+                at = pl.ds(c * ny + first, TILE)
                 return xp[j, at, :], xm[j, at, :]
 
             def store(i, value):
-                cross = fy[pl.ds(first * rows + c * nx + i, 8, stride=rows), :]
-                here = pl.ds(first, 8)
+                cross = fy[pl.ds(first * rows + c * nx + i, TILE, stride=rows), :]
+                here = pl.ds(first, TILE)
                 out_ref[c, i, here, :] = out_ref[c, i, here, :] + value + cross
 
             stream(load, store, nx)
             return carry
 
-        lax.fori_loop(0, ny // 8, along_first, 0)
-
-
-def right_hand_side(fields, lower, upper, sides, alphas):
-    comps, nx, ny, nz = fields.shape
-    rows = sides.shape[1]
+        lax.fori_loop(0, ny // TILE, along_first, 0)
+
+
+def first_kernel(u_ref, lo_ref, hi_ref, side_ref, al_ref, other_ref, *refs):
+    nodes = len(refs) - 6
+    parts, rate, scratch = refs[:nodes], refs[nodes], refs[nodes + 1 :]
+    comps, nx, ny, nz = u_ref.shape[1:]
+    tile = jnp.maximum(al_ref[...], other_ref[...])
+    alphas = [tile[k : k + 1, :] for k in range(3)]
+    along_grid(lambda c, i: u_ref[0, c, i], alphas, lo_ref, hi_ref, side_ref, rate, scratch, True)
+    windows = Windows(nx, nz, nodes)
+    me = lax.axis_index("node")
+
+    def cut(c, carry):
+        for r in range(windows.rows):
+            values = [rate[c, s * windows.rows + r] for s in range(windows.slots)]
+            at = pl.ds(pl.multiple_of((c * windows.rows + r) * ny, ny), ny)
+            for k in range(nodes):
+                parts[k][at, :] = windows.cut(values, me ^ k)
+        return carry
+
+    lax.fori_loop(0, comps, cut, 0)
+
+
+def second_kernel(init_ref, nat_ref, win_ref, lo_ref, hi_ref, side_ref, *refs):
+    nodes = win_ref.shape[0]
+    tiles, outs, (rate, deep), scratch = refs[:nodes], refs[nodes : 2 * nodes], refs[2 * nodes : 2 * nodes + 2], refs[2 * nodes + 2 :]
+    comps, nx, ny, nz = nat_ref.shape
+    every = range(comps)
+    windows = Windows(nx, nz, nodes)
+    me = lax.axis_index("node")
+    group = windows.group((TILE, nz))
+    tile = tiles[0][...]
+    for k in range(1, nodes):
+        value = tiles[k][...]
+        tile = jnp.maximum(tile, merged([turned(value, windows.width * (g - (g ^ k))) for g in range(nodes)], group))
+    alphas = [tile[k : k + 1, :] for k in range(3)]
+
+    for k in range(nodes):
+        alpha = jnp.max(jnp.where(group[:1] == k, alphas[2], 0.0))
+
+        def depth(r, carry, k=k, alpha=alpha):
+            places = [pl.ds(pl.multiple_of((c * windows.rows + r) * ny, ny), ny) for c in every]
+            ((p, m),) = splits([win_ref[k, at, :] for at in places], [None, None, alpha], (2,))
+            for c in every:
+                deep[k, places[c], :] = rolled(p[c], m[c])
+            return carry
+
+        lax.fori_loop(0, windows.rows, depth, 0)
+
+    def join(c, carry):
+        for r in range(windows.rows):
+            at = pl.ds(pl.multiple_of((c * windows.rows + r) * ny, ny), ny)
+            values = [deep[k, at, :] for k in range(nodes)]
+            for s in range(windows.slots):
+                rate[c, s * windows.rows + r] = windows.joined(values, s)
+        return carry
+
+    lax.fori_loop(0, comps, join, 0)
+    along_grid(lambda c, i: nat_ref[c, i], alphas, lo_ref, hi_ref, side_ref, rate, scratch, False)
+
+    weights = node_weights(me, nodes)
+    lanes = windows.group((ny, nz))
+
+    def finish(c, carry):
+        for q in range(nx // nodes):
+            at = pl.ds(pl.multiple_of((c * (nx // nodes) + q) * ny, ny), ny)
+            start = merged(
+                [turned(init_ref[c, q * nodes + i], windows.width * (i - me)) for i in range(nodes)], lanes
+            )
+            rows = [rate[c, q * nodes + i] for i in range(nodes)]
+            rates = [
+                merged([turned(rows[i], windows.width * (i - k)) for i in range(nodes)], lanes) for k in range(nodes)
+            ]
+            for k in range(nodes):
+                value = start
+                for j in range(nodes):
+                    value = value + weights[k][j] * rates[j]
+                outs[k][at, :] = value
+        return carry
+
+    lax.fori_loop(0, comps, finish, 0)
+
+
+def close_kernel(*refs):
+    parts, out_ref = refs[:-1], refs[-1]
+    nodes = len(parts)
+    comps, nx, ny, nz = out_ref.shape[1:]
+    width = nz // nodes
+    me = lax.axis_index("node")
+    lanes = lane_index((ny, nz)) // width
+
+    def step(c, carry):
+        for q in range(nx // nodes):
+            at = pl.ds(pl.multiple_of((c * (nx // nodes) + q) * ny, ny), ny)
+            values = [part[at, :] for part in parts]
+            for i in range(nodes):
+                out = turned(values[0], width * (me - i))
+                for k in range(1, nodes):
+                    out = jnp.where(lanes == (me ^ k), turned(values[k], width * ((me ^ k) - i)), out)
+                out_ref[0, c, q * nodes + i] = out
+        return carry
+
+    lax.fori_loop(0, comps, step, 0)
+
+
+def call(kernel, outs, operands, scratch=(), flops=1_000_000):
     vmem = pl.BlockSpec(memory_space=pltpu.VMEM)
+    moved = sum(4 * x.size for x in operands)
     return pl.pallas_call(
-        rhs_kernel,
-        out_shape=jax.ShapeDtypeStruct(fields.shape, jnp.float32),
-        in_specs=[vmem] * 5,
-        out_specs=vmem,
-        scratch_shapes=[
-            pltpu.VMEM((nx + 2 * HALO, comps * ny, nz), jnp.float32),
-            pltpu.VMEM((nx + 2 * HALO, comps * ny, nz), jnp.float32),
-            pltpu.VMEM(((ny + 2 * HALO) * rows, nz), jnp.float32),
-            pltpu.VMEM(((ny + 2 * HALO) * rows, nz), jnp.float32),
-            pltpu.VMEM((ny * rows, nz), jnp.float32),
-        ],
-        compiler_params=pltpu.CompilerParams(vmem_limit_bytes=24 * 1024 * 1024),
-        cost_estimate=pl.CostEstimate(flops=30_000_000, bytes_accessed=1_500_000, transcendentals=0),
-        name="right_hand_side",
-    )(fields, lower, upper, sides, alphas)
+        kernel,
+        out_shape=[jax.ShapeDtypeStruct(shape, jnp.float32) for shape in outs],
+        in_specs=[vmem] * len(operands),
+        out_specs=[vmem] * len(outs),
+        scratch_shapes=[pltpu.VMEM(shape, jnp.float32) for shape in scratch],
+        compiler_params=pltpu.CompilerParams(vmem_limit_bytes=32 * 1024 * 1024),
+        cost_estimate=pl.CostEstimate(flops=flops, bytes_accessed=2 * moved, transcendentals=0),
+        name=kernel.__name__,
+    )(*operands)
 
 
 def shifted(value, axis, by):
@@ -244,33 +489,69 @@
     return lax.ppermute(value, axis, [(i, (i + by) % count) for i in range(count)])
 
 
-def local_speeds(fields):
-    return jnp.stack([jnp.max(s) for s in signal_speeds([fields[c] for c in range(COMPONENTS)])])
-
-
-def evaluate(fields):
-    comps, nx, ny, nz = fields.shape
-    speeds = lax.pmax(local_speeds(fields), ("gx", "gy"))
-    alphas = jnp.broadcast_to(jnp.pad(speeds, (0, 5))[:, None], (8, nz))
-    lower = shifted(fields[:, -HALO:], "gx", 1)
-    upper = shifted(fields[:, :HALO], "gx", -1)
-    leading = jnp.moveaxis(fields, 2, 0).reshape(ny, comps * nx, nz)
-    pad = -(comps * nx) % 8
-    leading = jnp.pad(leading, ((0, 0), (0, pad), (0, 0)))
-    sides = jnp.concatenate([shifted(leading[-HALO:], "gy", 1), shifted(leading[:HALO], "gy", -1)])
-    return right_hand_side(fields, lower, upper, sides, alphas)
+def swapped(value, by):
+    return lax.ppermute(value, "node", [(i, i ^ by) for i in range(lax.axis_size("node"))])
+
+
+def neighbours(lo, hi, side, tile):
+    across, beside = lax.axis_size("gx"), lax.axis_size("gy")
+    lower, upper = shifted(hi, "gx", 1), shifted(lo, "gx", -1)
+    if across <= 4:
+        tiles = [tile, lower[0, -TILE:], upper[0, -TILE:]]
+        if across == 4:
+            tiles.append(shifted(tile, "gx", 2))
+        tile = functools.reduce(jnp.maximum, tiles)
+    else:
+        tile = lax.pmax(tile, "gx")
+    if beside == 2:
+        return lower, upper, shifted(side, "gy", 1), tile, shifted(tile, "gy", 1)
+    half = side.shape[1] // 2
+    side = jnp.concatenate([shifted(side[:, :half], "gy", 1), shifted(side[:, half:], "gy", -1)], axis=1)
+    tile = lax.pmax(tile, "gy")
+    return lower, upper, side, tile, tile
 
 
 def local(initial, guesses):
-    weights_table = jnp.array(radau_weights, jnp.float32) * (step_size / 12.0)
-    node_index = lax.axis_index("node")
-    current = guesses[0]
-    for sweep_index in range(SWEEPS):
-        rate = evaluate(current)
-        own_row = lax.dynamic_index_in_dim(weights_table, node_index, 0, keepdims=False)
-        gathered = lax.all_gather(rate[None], "node", axis=0, tiled=True)
-        current = initial + jnp.sum(own_row[:, None, None, None, None] * gathered, axis=0)
-    return current[None]
+    comps, nx, ny, nz = initial.shape
+    nodes = lax.axis_size("node")
+    rows = -(-comps * nx // TILE) * TILE
+    windows = Windows(nx, nz, nodes)
+    edge = (1, comps * HALO * ny + TILE, nz)
+    edges = [edge, edge, (1, 2 * HALO * rows, nz), (TILE, nz)]
+    part = (comps * windows.rows * ny, nz)
+    streams = [
+        (nx + 2 * HALO, comps * ny, nz),
+        (nx + 2 * HALO, comps * ny, nz),
+        ((ny + 2 * HALO) * rows, nz),
+        ((ny + 2 * HALO) * rows, nz),
+        (ny * rows, nz),
+    ]
+    lo, hi, side, tile = call(open_kernel, edges, [guesses])
+    lower, upper, side, tile, other = neighbours(lo, hi, side, tile)
+    parts = call(
+        first_kernel,
+        [part] * nodes,
+        [guesses, lower, upper, side, tile, other],
+        [initial.shape] + streams,
+        30_000_000,
+    )
+    parts = [parts[0]] + [swapped(parts[k], k) for k in range(1, nodes)]
+    win, nat, lo, hi, side, tile = call(
+        blend_kernel, [(nodes,) + part, initial.shape] + edges, [initial] + parts
+    )
+    lower, upper, side, tile, other = neighbours(lo, hi, side, tile)
+    tile = jnp.maximum(tile, other)
+    tiles = [tile] + [swapped(tile, k) for k in range(1, nodes)]
+    outs = call(
+        second_kernel,
+        [(comps * nx // nodes * ny, nz)] * nodes,
+        [initial, nat, win, lower, upper, side] + tiles,
+        [initial.shape, (nodes,) + part] + streams,
+        30_000_000,
+    )
+    outs = [outs[0]] + [swapped(outs[k], k) for k in range(1, nodes)]
+    (states,) = call(close_kernel, [(1,) + initial.shape], outs)
+    return states
 
 
 def solution(mesh):

time: 153 us -> 76.1 us (0.50)
  waiting for transfers between devices: 63.5 us -> 27 us
  blocking collectives: 34.1 us -> 0 us
  between operations: 13.5 us -> 0.06 us
  starting transfers between devices: 9.67 us -> 20.7 us
  other arithmetic: 10.1 us -> 0.01 us
  Pallas kernels: 18.7 us -> 27.2 us
  local copies, waits for them, and re-layouts: 3.29 us -> 1.03 us
    all_gather x2 -> x0, waiting for transfers between devices: 63.5 us -> none  [local(): gathered = lax.all_gather(rate[None], 'node', axis=0, tiled=True)]
    pmax x2 -> x0, blocking collectives: 34.1 us -> none  [evaluate(): speeds = lax.pmax(local_speeds(fields), ('gx', 'gy'))]
    ppermute x0 -> x9, waiting for transfers between devices: none -> 14.9 us  [swapped(): lax.ppermute(value, 'node', [(i, i ^ by) for i in range(lax.axis_size('no...]
    ppermute x8 -> x10, waiting for transfers between devices: 0.02 us -> 12.1 us  [shifted(): lax.ppermute(value, axis, [(i, (i + by) % count) for i in range(count)])]
    ppermute x0 -> x9, starting transfers between devices: none -> 10.6 us  [swapped(): lax.ppermute(value, 'node', [(i, i ^ by) for i in range(lax.axis_size('no...]
    pallas_call x2 -> x5, Pallas kernels: 18.7 us -> 27.2 us  [call(): pl.pallas_call(kernel, out_shape=[jax.ShapeDtypeStruct(shape, jnp.float32...]
    another operation x2 -> x0, other arithmetic: 3.93 us -> none  [local_speeds(): jnp.stack([jnp.max(s) for s in signal_speeds([fields[c] for c in range(CO...]
    reduce_sum x2 -> x0, other arithmetic: 3.66 us -> none  [local(): jnp.sum(own_row[:, None, None, None, None] * gathered, axis=0)]
  transfers between devices with their start and end apart: 10 -> 19, of which waited for: 2 -> 12; matrix products, arithmetic and copies ran while one was open for 4% -> 0% of each run, Pallas kernels for 0% -> 0%
where the time goes in v2:
time: 76.1 us; the launch traced here: 75.9 us
  Pallas kernels  27.2 us (36%)
  waiting for transfers between devices  27 us (35%)
  starting transfers between devices  20.7 us (27%)
  local copies, waits for them, and re-layouts  1.03 us (1%)
    pallas_call x5, Pallas kernels, call(): pl.pallas_call(kernel, out_shape=[jax.ShapeDtypeStruct(shape, jnp.float32...  27.2 us
    ppermute x9, waiting for transfers between devices, swapped(): lax.ppermute(value, 'node', [(i, i ^ by) for i in range(lax.axis_size('no...  14.9 us
    ppermute x10, waiting for transfers between devices, shifted(): lax.ppermute(value, axis, [(i, (i + by) % count) for i in range(count)])  12.1 us
    ppermute x9, starting transfers between devices, swapped(): lax.ppermute(value, 'node', [(i, i ^ by) for i in range(lax.axis_size('no...  10.6 us
    ppermute x10, starting transfers between devices, shifted(): lax.ppermute(value, axis, [(i, (i + by) % count) for i in range(count)])  10.1 us
  transfers between devices with their start and end apart: 19, of which 12 were waited for; matrix products, arithmetic and copies ran while one was open for 0% of the time, Pallas kernels for 0%

profile of v2, /device:TPU:0, one launch (start us, length us, event | category | flops | bytes accessed | tf_op | source)
XLA Modules:
  0.0 75.9 jit_solution(13980362433584147915)
XLA Ops:
  0.0 0.0 copy-start.1
  0.0 1.0 %copy-done.1 = f32[1,5,12,16,128]{4,3,2,1,0:T(8,128)S(1)} copy-done((f32[1,5,12,16,128]{4,3,2,1,0:T(8,128)S(1)}, f32[1,5,12,16,128]{4,3,2,1,0:T(8,128)}, u32[]{:S(2)}) %copy-start.1) | copy-done | bytes 491544
  1.0 1.0 %open_kernel.1 = (f32[1,248,128]{2,1,0:T(8,128)S(1)}, f32[1,248,128]{2,1,0:T(8,128)S(1)}, f32[1,384,128]{2,1,0:T(8,128)S(1)}, f32[8,128]{1,0:T(8,128)S(1)}) custom-call(f32[1,5,12,16,128]{4,3,2,1,0:T(8,128)S(1)} %copy-done.1), custom_call_target="tpu_custom_call" | custom-call | flops 1000000 | bytes 983040 | tf_op jit(solution)/shard_map/open_kernel/pallas_call | solution.py:475
  2.0 3.0 %collective-permute-start = (f32[1,248,128]{2,1,0:T(8,128)S(1)}, f32[1,248,128]{2,1,0:T(8,128)S(1)}, u32[]{:S(2)}, u32[]{:S(2)}) collective-permute-start(f32[1,248,128]{2,1,0:T(8,128)S(1)} %get-tuple-element.23), channel_id=1, source_target_pairs={{0,2},{2,4},{4,6},{6,0},{1,3},{3,5},{5,7},{7,1},{8,10},{10,12},{12... | collective-permute-start | bytes 380936 | tf_op jit(solution)/shard_map/ppermute | solution.py:489
  5.0 0.0 copy-start
  5.0 2.0 %collective-permute-start.1 = (f32[1,248,128]{2,1,0:T(8,128)S(1)}, f32[1,248,128]{2,1,0:T(8,128)S(1)}, u32[]{:S(2)}, u32[]{:S(2)}) collective-permute-start(f32[1,248,128]{2,1,0:T(8,128)S(1)} %get-tuple-element.24), channel_id=1, source_target_pairs={{0,6},{2,0},{4,2},{6,4},{1,7},{3,1},{5,3},{7,5},{8,14},{10,8},{12,... | collective-permute-start | bytes 380936 | tf_op jit(solution)/shard_map/ppermute | solution.py:489
  7.1 1.0 %collective-permute-start.3 = (f32[8,128]{1,0:T(8,128)S(1)}, f32[8,128]{1,0:T(8,128)S(1)}, u32[]{:S(2)}, u32[]{:S(2)}) collective-permute-start(f32[8,128]{1,0:T(8,128)S(1)} %get-tuple-element.26), channel_id=1, source_target_pairs={{0,4},{2,6},{4,0},{6,2},{1,5},{3,7},{5,1},{7,3},{8,12},{10,14},{12... | collective-permute-start | bytes 12296 | tf_op jit(solution)/shard_map/ppermute | solution.py:489
  8.1 0.0 collective-permute-start.2
  8.1 5.3 %collective-permute-done.3 = f32[8,128]{1,0:T(8,128)S(1)} collective-permute-done((f32[8,128]{1,0:T(8,128)S(1)}, f32[8,128]{1,0:T(8,128)S(1)}, u32[]{:S(2)}, u32[]{:S(2)}) %collective-permute-start.3) | collective-permute-done | bytes 4128 | tf_op jit(solution)/shard_map/ppermute | solution.py:489
  13.3 0.0 collective-permute-done.lo_ref
  13.3 0.0 collective-permute-done.1.hi_ref
  13.3 0.1 collective-permute-start.4
  13.4 1.2 %collective-permute-done.4.other_ref = f32[8,128]{1,0:T(8,128)S(1)} collective-permute-done((f32[8,128]{1,0:T(8,128)S(1)}, f32[8,128]{1,0:T(8,128)S(1)}, u32[]{:S(2)}, u32[]{:S(2)}) %collective-permute-start.4) | collective-permute-done | bytes 4128 | tf_op jit(solution)/shard_map/ppermute | solution.py:489
  14.6 0.0 collective-permute-done.2.side_ref
  14.6 9.4 %first_kernel.1 = (f32[320,128]{1,0:T(8,128)S(1)}, f32[320,128]{1,0:T(8,128)S(1)}, f32[320,128]{1,0:T(8,128)S(1)}, f32[320,128]{1,0:T(8,128)S(1)}) custom-call(f32[1,5,12,16,128]{4,3,2,1,0:T(8,128)S(1)} %copy-done.1, f32[1,248,128]{2,1,0:T(8,128)S(1)} %collective-permute-done.lo_ref, f32[1,248,128]{2,1,0:T(8,128)S(1)} %collective-permute-done.1.hi_ref, ...), custom_call_target="tpu_custom_call" | custom-call | flops 30000000 | bytes 1900544 | tf_op jit(solution)/shard_map/first_kernel/pallas_call | solution.py:475
  24.0 1.6 %collective-permute-start.5 = (f32[320,128]{1,0:T(8,128)S(1)}, f32[320,128]{1,0:T(8,128)S(1)}, u32[]{:S(2)}, u32[]{:S(2)}) collective-permute-start(f32[320,128]{1,0:T(8,128)S(1)} %get-tuple-element.28), channel_id=1, source_target_pairs={{0,8},{8,0},{16,24},{24,16},{1,9},{9,1},{17,25},{25,17},{2,10},{10... | collective-permute-start | bytes 491528 | tf_op jit(solution)/shard_map/ppermute | solution.py:493
  25.6 1.5 %collective-permute-start.6 = (f32[320,128]{1,0:T(8,128)S(1)}, f32[320,128]{1,0:T(8,128)S(1)}, u32[]{:S(2)}, u32[]{:S(2)}) collective-permute-start(f32[320,128]{1,0:T(8,128)S(1)} %get-tuple-element.29), channel_id=1, source_target_pairs={{0,16},{8,24},{16,0},{24,8},{1,17},{9,25},{17,1},{25,9},{2,18},{10... | collective-permute-start | bytes 491528 | tf_op jit(solution)/shard_map/ppermute | solution.py:493
  27.1 0.5 collective-permute-start.7
  27.6 3.6 %collective-permute-done.5.refs_1_ = f32[320,128]{1,0:T(8,128)S(1)} collective-permute-done((f32[320,128]{1,0:T(8,128)S(1)}, f32[320,128]{1,0:T(8,128)S(1)}, u32[]{:S(2)}, u32[]{:S(2)}) %collective-permute-start.5) | collective-permute-done | bytes 163872 | tf_op jit(solution)/shard_map/ppermute | solution.py:493
  31.1 3.9 %collective-permute-done.6.refs_2_ = f32[320,128]{1,0:T(8,128)S(1)} collective-permute-done((f32[320,128]{1,0:T(8,128)S(1)}, f32[320,128]{1,0:T(8,128)S(1)}, u32[]{:S(2)}, u32[]{:S(2)}) %collective-permute-start.6) | collective-permute-done | bytes 163872 | tf_op jit(solution)/shard_map/ppermute | solution.py:493
  35.1 0.0 collective-permute-done.7.refs_3_
  35.1 0.0 copy-done
  35.1 2.1 %blend_kernel.1 = (f32[4,320,128]{2,1,0:T(8,128)S(1)}, f32[5,12,16,128]{3,2,1,0:T(8,128)S(1)}, f32[1,248,128]{2,1,0:T(8,128)S(1)}, f32[1,248,128]{2,1,0:T(8,128)...) custom-call(f32[5,12,16,128]{3,2,1,0:T(8,128)S(1)} %copy-done, f32[320,128]{1,0:T(8,128)S(1)} %get-tuple-element.27.refs_0_, ...), custom_call_target="tpu_custom_call" | custom-call | flops 1000000 | bytes 2293760 | tf_op jit(solution)/shard_map/blend_kernel/pallas_call | solution.py:475
  37.2 0.6 collective-permute-start.8
  37.8 3.2 %collective-permute-start.9 = (f32[1,248,128]{2,1,0:T(8,128)S(1)}, f32[1,248,128]{2,1,0:T(8,128)S(1)}, u32[]{:S(2)}, u32[]{:S(2)}) collective-permute-start(f32[1,248,128]{2,1,0:T(8,128)S(1)} %get-tuple-element.34), channel_id=1, source_target_pairs={{0,6},{2,0},{4,2},{6,4},{1,7},{3,1},{5,3},{7,5},{8,14},{10,8},{12,... | collective-permute-start | bytes 380936 | tf_op jit(solution)/shard_map/ppermute | solution.py:489
  41.0 0.0 collective-permute-start.11
  41.1 0.0 collective-permute-start.10
  41.1 4.5 %collective-permute-done.11 = f32[8,128]{1,0:T(8,128)S(1)} collective-permute-done((f32[8,128]{1,0:T(8,128)S(1)}, f32[8,128]{1,0:T(8,128)S(1)}, u32[]{:S(2)}, u32[]{:S(2)}) %collective-permute-start.11) | collective-permute-done | bytes 4128 | tf_op jit(solution)/shard_map/ppermute | solution.py:489
  45.6 0.0 collective-permute-done.8.lo_ref
  45.6 0.0 collective-permute-done.9.hi_ref
  45.6 0.1 collective-permute-start.12
  45.6 1.2 %collective-permute-done.12 = f32[8,128]{1,0:T(8,128)S(1)} collective-permute-done((f32[8,128]{1,0:T(8,128)S(1)}, f32[8,128]{1,0:T(8,128)S(1)}, u32[]{:S(2)}, u32[]{:S(2)}) %collective-permute-start.12) | collective-permute-done | bytes 4128 | tf_op jit(solution)/shard_map/ppermute | solution.py:489
  46.8 1.5 %collective-permute-start.15 = (f32[8,128]{1,0:T(8,128)S(1)}, f32[8,128]{1,0:T(8,128)S(1)}, u32[]{:S(2)}, u32[]{:S(2)}) collective-permute-start(f32[8,128]{1,0:T(8,128)S(1)} %max.27.refs_0_), channel_id=1, source_target_pairs={{0,24},{8,16},{16,8},{24,0},{1,25},{9,17},{17,9},{25,1},{2,26},{10... | collective-permute-start | bytes 12296 | tf_op jit(solution)/shard_map/ppermute | solution.py:493
  48.3 1.2 %collective-permute-start.14 = (f32[8,128]{1,0:T(8,128)S(1)}, f32[8,128]{1,0:T(8,128)S(1)}, u32[]{:S(2)}, u32[]{:S(2)}) collective-permute-start(f32[8,128]{1,0:T(8,128)S(1)} %max.27.refs_0_), channel_id=1, source_target_pairs={{0,16},{8,24},{16,0},{24,8},{1,17},{9,25},{17,1},{25,9},{2,18},{10... | collective-permute-start | bytes 12296 | tf_op jit(solution)/shard_map/ppermute | solution.py:493
  49.5 0.8 %collective-permute-start.13 = (f32[8,128]{1,0:T(8,128)S(1)}, f32[8,128]{1,0:T(8,128)S(1)}, u32[]{:S(2)}, u32[]{:S(2)}) collective-permute-start(f32[8,128]{1,0:T(8,128)S(1)} %max.27.refs_0_), channel_id=1, source_target_pairs={{0,8},{8,0},{16,24},{24,16},{1,9},{9,1},{17,25},{25,17},{2,10},{10... | collective-permute-start | bytes 12296 | tf_op jit(solution)/shard_map/ppermute | solution.py:493
  50.3 1.0 %collective-permute-done.15.refs_3_ = f32[8,128]{1,0:T(8,128)S(1)} collective-permute-done((f32[8,128]{1,0:T(8,128)S(1)}, f32[8,128]{1,0:T(8,128)S(1)}, u32[]{:S(2)}, u32[]{:S(2)}) %collective-permute-start.15) | collective-permute-done | bytes 4128 | tf_op jit(solution)/shard_map/ppermute | solution.py:493
  51.3 0.6 collective-permute-done.14.refs_2_
  51.9 1.2 %collective-permute-done.13.refs_1_ = f32[8,128]{1,0:T(8,128)S(1)} collective-permute-done((f32[8,128]{1,0:T(8,128)S(1)}, f32[8,128]{1,0:T(8,128)S(1)}, u32[]{:S(2)}, u32[]{:S(2)}) %collective-permute-start.13) | collective-permute-done | bytes 4128 | tf_op jit(solution)/shard_map/ppermute | solution.py:493
  53.1 0.0 collective-permute-done.10.side_ref
  53.1 13.0 %second_kernel.1 = (f32[240,128]{1,0:T(8,128)S(1)}, f32[240,128]{1,0:T(8,128)S(1)}, f32[240,128]{1,0:T(8,128)S(1)}, f32[240,128]{1,0:T(8,128)S(1)}) custom-call(f32[5,12,16,128]{3,2,1,0:T(8,128)S(1)} %copy-done, f32[5,12,16,128]{3,2,1,0:T(8,128)S(1)} %get-tuple-element.31.nat_ref, f32[4,320,128]{2,1,0:T(8,128)S(1)} %get-tuple-element.32.win_ref, ...), custom_call_target="tpu_custom_call" | custom-call | flops 30000000 | bytes 4210688 | tf_op jit(solution)/shard_map/second_kernel/pallas_call | solution.py:475
  66.1 0.9 %collective-permute-start.16 = (f32[240,128]{1,0:T(8,128)S(1)}, f32[240,128]{1,0:T(8,128)S(1)}, u32[]{:S(2)}, u32[]{:S(2)}) collective-permute-start(f32[240,128]{1,0:T(8,128)S(1)} %get-tuple-element.38), channel_id=1, source_target_pairs={{0,8},{8,0},{16,24},{24,16},{1,9},{9,1},{17,25},{25,17},{2,10},{10... | collective-permute-start | bytes 368648 | tf_op jit(solution)/shard_map/ppermute | solution.py:493
  67.0 1.5 %collective-permute-start.17 = (f32[240,128]{1,0:T(8,128)S(1)}, f32[240,128]{1,0:T(8,128)S(1)}, u32[]{:S(2)}, u32[]{:S(2)}) collective-permute-start(f32[240,128]{1,0:T(8,128)S(1)} %get-tuple-element.39), channel_id=1, source_target_pairs={{0,16},{8,24},{16,0},{24,8},{1,17},{9,25},{17,1},{25,9},{2,18},{10... | collective-permute-start | bytes 368648 | tf_op jit(solution)/shard_map/ppermute | solution.py:493
  68.5 1.2 %collective-permute-start.18 = (f32[240,128]{1,0:T(8,128)S(1)}, f32[240,128]{1,0:T(8,128)S(1)}, u32[]{:S(2)}, u32[]{:S(2)}) collective-permute-start(f32[240,128]{1,0:T(8,128)S(1)} %get-tuple-element.40), channel_id=1, source_target_pairs={{0,24},{8,16},{16,8},{24,0},{1,25},{9,17},{17,9},{25,1},{2,26},{10... | collective-permute-start | bytes 368648 | tf_op jit(solution)/shard_map/ppermute | solution.py:493
  69.7 2.2 %collective-permute-done.16.refs_1_ = f32[240,128]{1,0:T(8,128)S(1)} collective-permute-done((f32[240,128]{1,0:T(8,128)S(1)}, f32[240,128]{1,0:T(8,128)S(1)}, u32[]{:S(2)}, u32[]{:S(2)}) %collective-permute-start.16) | collective-permute-done | bytes 122912 | tf_op jit(solution)/shard_map/ppermute | solution.py:493
  71.8 1.1 %collective-permute-done.17.refs_2_ = f32[240,128]{1,0:T(8,128)S(1)} collective-permute-done((f32[240,128]{1,0:T(8,128)S(1)}, f32[240,128]{1,0:T(8,128)S(1)}, u32[]{:S(2)}, u32[]{:S(2)}) %collective-permute-start.17) | collective-permute-done | bytes 122912 | tf_op jit(solution)/shard_map/ppermute | solution.py:493
  72.9 1.4 %collective-permute-done.18.refs_3_ = f32[240,128]{1,0:T(8,128)S(1)} collective-permute-done((f32[240,128]{1,0:T(8,128)S(1)}, f32[240,128]{1,0:T(8,128)S(1)}, u32[]{:S(2)}, u32[]{:S(2)}) %collective-permute-start.18) | collective-permute-done | bytes 122912 | tf_op jit(solution)/shard_map/ppermute | solution.py:493
  74.3 1.7 %close_kernel.1 = f32[1,5,12,16,128]{4,3,2,1,0:T(8,128)} custom-call(f32[240,128]{1,0:T(8,128)S(1)} %get-tuple-element.37.refs_0_, f32[240,128]{1,0:T(8,128)S(1)} %collective-permute-done.16.refs_1_, f32[240,128]{1,0:T(8,128)S(1)} %collective-permute-done.17.refs_2_, f32[240,128]{1,0:T(8,128)S(1)} %collective-permute-done.18.refs_3_), custom_call_target="tpu_custom_call" | custom-call | flops 1000000 | bytes 983040 | tf_op jit(solution)/shard_map/close_kernel/pallas_call | solution.py:475
  (3 shorter events, 0.0 us)
Async XLA Ops:
  0.0 1.0 %copy-start.1 = (f32[1,5,12,16,128]{4,3,2,1,0:T(8,128)S(1)}, f32[1,5,12,16,128]{4,3,2,1,0:T(8,128)}, u32[]{:S(2)}) copy-start(f32[1,5,12,16,128]{4,3,2,1,0:T(8,128)} %u_ref.3) | copy-start | bytes 1474564
  2.0 11.3 %collective-permute-start = (f32[1,248,128]{2,1,0:T(8,128)S(1)}, f32[1,248,128]{2,1,0:T(8,128)S(1)}, u32[]{:S(2)}, u32[]{:S(2)}) collective-permute-start(f32[1,248,128]{2,1,0:T(8,128)S(1)} %get-tuple-element.23), channel_id=1, source_target_pairs={{0,2},{2,4},{4,6},{6,0},{1,3},{3,5},{5,7},{7,1},{8,10},{10,12},{12... | collective-permute-start | bytes 380936 | tf_op jit(solution)/shard_map/ppermute | solution.py:489
  5.0 30.0 %copy-start = (f32[5,12,16,128]{3,2,1,0:T(8,128)S(1)}, f32[5,12,16,128]{3,2,1,0:T(8,128)}, u32[]{:S(2)}) copy-start(f32[5,12,16,128]{3,2,1,0:T(8,128)} %init_ref.3) | copy-start | bytes 1474564
  5.0 8.3 %collective-permute-start.1 = (f32[1,248,128]{2,1,0:T(8,128)S(1)}, f32[1,248,128]{2,1,0:T(8,128)S(1)}, u32[]{:S(2)}, u32[]{:S(2)}) collective-permute-start(f32[1,248,128]{2,1,0:T(8,128)S(1)} %get-tuple-element.24), channel_id=1, source_target_pairs={{0,6},{2,0},{4,2},{6,4},{1,7},{3,1},{5,3},{7,5},{8,14},{10,8},{12,... | collective-permute-start | bytes 380936 | tf_op jit(solution)/shard_map/ppermute | solution.py:489
  7.1 6.3 %collective-permute-start.3 = (f32[8,128]{1,0:T(8,128)S(1)}, f32[8,128]{1,0:T(8,128)S(1)}, u32[]{:S(2)}, u32[]{:S(2)}) collective-permute-start(f32[8,128]{1,0:T(8,128)S(1)} %get-tuple-element.26), channel_id=1, source_target_pairs={{0,4},{2,6},{4,0},{6,2},{1,5},{3,7},{5,1},{7,3},{8,12},{10,14},{12... | collective-permute-start | bytes 12296 | tf_op jit(solution)/shard_map/ppermute | solution.py:489
  8.1 6.5 %collective-permute-start.2 = (f32[1,384,128]{2,1,0:T(8,128)S(1)}, f32[1,384,128]{2,1,0:T(8,128)S(1)}, u32[]{:S(2)}, u32[]{:S(2)}) collective-permute-start(f32[1,384,128]{2,1,0:T(8,128)S(1)} %get-tuple-element.25), channel_id=1, source_target_pairs={{0,1},{1,0},{2,3},{3,2},{4,5},{5,4},{6,7},{7,6},{8,9},{9,8},{10,11... | collective-permute-start | bytes 589832 | tf_op jit(solution)/shard_map/ppermute | solution.py:489
  13.3 1.2 %collective-permute-start.4 = (f32[8,128]{1,0:T(8,128)S(1)}, f32[8,128]{1,0:T(8,128)S(1)}, u32[]{:S(2)}, u32[]{:S(2)}) collective-permute-start(f32[8,128]{1,0:T(8,128)S(1)} %fusion.4.al_ref), channel_id=1, source_target_pairs={{0,1},{1,0},{2,3},{3,2},{4,5},{5,4},{6,7},{7,6},{8,9},{9,8},{10,11... | collective-permute-start | bytes 12296 | tf_op jit(solution)/shard_map/ppermute | solution.py:489
  24.0 7.1 %collective-permute-start.5 = (f32[320,128]{1,0:T(8,128)S(1)}, f32[320,128]{1,0:T(8,128)S(1)}, u32[]{:S(2)}, u32[]{:S(2)}) collective-permute-start(f32[320,128]{1,0:T(8,128)S(1)} %get-tuple-element.28), channel_id=1, source_target_pairs={{0,8},{8,0},{16,24},{24,16},{1,9},{9,1},{17,25},{25,17},{2,10},{10... | collective-permute-start | bytes 491528 | tf_op jit(solution)/shard_map/ppermute | solution.py:493
  25.6 9.5 %collective-permute-start.6 = (f32[320,128]{1,0:T(8,128)S(1)}, f32[320,128]{1,0:T(8,128)S(1)}, u32[]{:S(2)}, u32[]{:S(2)}) collective-permute-start(f32[320,128]{1,0:T(8,128)S(1)} %get-tuple-element.29), channel_id=1, source_target_pairs={{0,16},{8,24},{16,0},{24,8},{1,17},{9,25},{17,1},{25,9},{2,18},{10... | collective-permute-start | bytes 491528 | tf_op jit(solution)/shard_map/ppermute | solution.py:493
  27.1 8.0 %collective-permute-start.7 = (f32[320,128]{1,0:T(8,128)S(1)}, f32[320,128]{1,0:T(8,128)S(1)}, u32[]{:S(2)}, u32[]{:S(2)}) collective-permute-start(f32[320,128]{1,0:T(8,128)S(1)} %get-tuple-element.30), channel_id=1, source_target_pairs={{0,24},{8,16},{16,8},{24,0},{1,25},{9,17},{17,9},{25,1},{2,26},{10... | collective-permute-start | bytes 491528 | tf_op jit(solution)/shard_map/ppermute | solution.py:493
  37.2 8.3 %collective-permute-start.8 = (f32[1,248,128]{2,1,0:T(8,128)S(1)}, f32[1,248,128]{2,1,0:T(8,128)S(1)}, u32[]{:S(2)}, u32[]{:S(2)}) collective-permute-start(f32[1,248,128]{2,1,0:T(8,128)S(1)} %get-tuple-element.33), channel_id=1, source_target_pairs={{0,2},{2,4},{4,6},{6,0},{1,3},{3,5},{5,7},{7,1},{8,10},{10,12},{12... | collective-permute-start | bytes 380936 | tf_op jit(solution)/shard_map/ppermute | solution.py:489
  37.8 7.7 %collective-permute-start.9 = (f32[1,248,128]{2,1,0:T(8,128)S(1)}, f32[1,248,128]{2,1,0:T(8,128)S(1)}, u32[]{:S(2)}, u32[]{:S(2)}) collective-permute-start(f32[1,248,128]{2,1,0:T(8,128)S(1)} %get-tuple-element.34), channel_id=1, source_target_pairs={{0,6},{2,0},{4,2},{6,4},{1,7},{3,1},{5,3},{7,5},{8,14},{10,8},{12,... | collective-permute-start | bytes 380936 | tf_op jit(solution)/shard_map/ppermute | solution.py:489
  41.0 4.5 %collective-permute-start.11 = (f32[8,128]{1,0:T(8,128)S(1)}, f32[8,128]{1,0:T(8,128)S(1)}, u32[]{:S(2)}, u32[]{:S(2)}) collective-permute-start(f32[8,128]{1,0:T(8,128)S(1)} %get-tuple-element.36), channel_id=1, source_target_pairs={{0,4},{2,6},{4,0},{6,2},{1,5},{3,7},{5,1},{7,3},{8,12},{10,14},{12... | collective-permute-start | bytes 12296 | tf_op jit(solution)/shard_map/ppermute | solution.py:489
  41.1 12.1 %collective-permute-start.10 = (f32[1,384,128]{2,1,0:T(8,128)S(1)}, f32[1,384,128]{2,1,0:T(8,128)S(1)}, u32[]{:S(2)}, u32[]{:S(2)}) collective-permute-start(f32[1,384,128]{2,1,0:T(8,128)S(1)} %get-tuple-element.35), channel_id=1, source_target_pairs={{0,1},{1,0},{2,3},{3,2},{4,5},{5,4},{6,7},{7,6},{8,9},{9,8},{10,11... | collective-permute-start | bytes 589832 | tf_op jit(solution)/shard_map/ppermute | solution.py:489
  45.6 1.2 %collective-permute-start.12 = (f32[8,128]{1,0:T(8,128)S(1)}, f32[8,128]{1,0:T(8,128)S(1)}, u32[]{:S(2)}, u32[]{:S(2)}) collective-permute-start(f32[8,128]{1,0:T(8,128)S(1)} %fusion.1), channel_id=1, source_target_pairs={{0,1},{1,0},{2,3},{3,2},{4,5},{5,4},{6,7},{7,6},{8,9},{9,8},{10,11... | collective-permute-start | bytes 12296 | tf_op jit(solution)/shard_map/ppermute | solution.py:489
  46.8 4.5 %collective-permute-start.15 = (f32[8,128]{1,0:T(8,128)S(1)}, f32[8,128]{1,0:T(8,128)S(1)}, u32[]{:S(2)}, u32[]{:S(2)}) collective-permute-start(f32[8,128]{1,0:T(8,128)S(1)} %max.27.refs_0_), channel_id=1, source_target_pairs={{0,24},{8,16},{16,8},{24,0},{1,25},{9,17},{17,9},{25,1},{2,26},{10... | collective-permute-start | bytes 12296 | tf_op jit(solution)/shard_map/ppermute | solution.py:493
  48.3 3.6 %collective-permute-start.14 = (f32[8,128]{1,0:T(8,128)S(1)}, f32[8,128]{1,0:T(8,128)S(1)}, u32[]{:S(2)}, u32[]{:S(2)}) collective-permute-start(f32[8,128]{1,0:T(8,128)S(1)} %max.27.refs_0_), channel_id=1, source_target_pairs={{0,16},{8,24},{16,0},{24,8},{1,17},{9,25},{17,1},{25,9},{2,18},{10... | collective-permute-start | bytes 12296 | tf_op jit(solution)/shard_map/ppermute | solution.py:493
  49.5 3.6 %collective-permute-start.13 = (f32[8,128]{1,0:T(8,128)S(1)}, f32[8,128]{1,0:T(8,128)S(1)}, u32[]{:S(2)}, u32[]{:S(2)}) collective-permute-start(f32[8,128]{1,0:T(8,128)S(1)} %max.27.refs_0_), channel_id=1, source_target_pairs={{0,8},{8,0},{16,24},{24,16},{1,9},{9,1},{17,25},{25,17},{2,10},{10... | collective-permute-start | bytes 12296 | tf_op jit(solution)/shard_map/ppermute | solution.py:493
  66.1 5.7 %collective-permute-start.16 = (f32[240,128]{1,0:T(8,128)S(1)}, f32[240,128]{1,0:T(8,128)S(1)}, u32[]{:S(2)}, u32[]{:S(2)}) collective-permute-start(f32[240,128]{1,0:T(8,128)S(1)} %get-tuple-element.38), channel_id=1, source_target_pairs={{0,8},{8,0},{16,24},{24,16},{1,9},{9,1},{17,25},{25,17},{2,10},{10... | collective-permute-start | bytes 368648 | tf_op jit(solution)/shard_map/ppermute | solution.py:493
  67.0 5.9 %collective-permute-start.17 = (f32[240,128]{1,0:T(8,128)S(1)}, f32[240,128]{1,0:T(8,128)S(1)}, u32[]{:S(2)}, u32[]{:S(2)}) collective-permute-start(f32[240,128]{1,0:T(8,128)S(1)} %get-tuple-element.39), channel_id=1, source_target_pairs={{0,16},{8,24},{16,0},{24,8},{1,17},{9,25},{17,1},{25,9},{2,18},{10... | collective-permute-start | bytes 368648 | tf_op jit(solution)/shard_map/ppermute | solution.py:493
  68.5 5.8 %collective-permute-start.18 = (f32[240,128]{1,0:T(8,128)S(1)}, f32[240,128]{1,0:T(8,128)S(1)}, u32[]{:S(2)}, u32[]{:S(2)}) collective-permute-start(f32[240,128]{1,0:T(8,128)S(1)} %get-tuple-element.40), channel_id=1, source_target_pairs={{0,24},{8,16},{16,8},{24,0},{1,25},{9,17},{17,9},{25,1},{2,26},{10... | collective-permute-start | bytes 368648 | tf_op jit(solution)/shard_map/ppermute | solution.py:493

commit v3 on v2

--- a/solution.py
+++ b/solution.py
@@ -120,26 +120,22 @@
             store(at - 3, (centre[at - 1] - centre[at + 1]) + (interface[at - 1] - interface[at]))
 
 
+def reconstructed(first, second, third, fourth, fifth):
+    one, two, three, four = second - first, third - second, fourth - third, fifth - fourth
+    bends = [two - one, three - two, four - three]
+    slopes = [two + 0.5 * bends[0], two + 0.5 * bends[1], three - 0.5 * bends[2]]
+    smooth = [((13.0 / 12.0) * (b * b) + epsilon) + v * v for b, v in zip(bends, slopes)]
+    return bends[1], bends[2], correction(*smooth, bends[1] - bends[0], bends[2] - bends[1])
+
+
 def rolled(plus, minus):
-    size = plus.shape[-1]
-
-    def nxt(value, by=1):
-        return pltpu.roll(value, size - by, value.ndim - 1)
-
-    def prev(value):
-        return pltpu.roll(value, 1, value.ndim - 1)
-
-    above = nxt(plus) - plus
-    second_plus, first_p, middle_p, last_p = cell_terms(prev(above), above)
-    above = nxt(minus) - minus
-    second_minus, first_m, middle_m, last_m = cell_terms(prev(above), above)
-    centre = 6.0 * (plus + minus) - (second_plus + second_minus)
-    third_plus = nxt(second_plus) - second_plus
-    third_minus = nxt(second_minus) - second_minus
-    right = correction(prev(first_p), middle_p, nxt(last_p), prev(third_plus), third_plus)
-    left = correction(nxt(last_m, 2), nxt(middle_m), first_m, nxt(third_minus), third_minus)
-    interface = (third_plus - third_minus) - 4.0 * (right - left)
-    return (prev(centre) - nxt(centre)) + (prev(interface) - interface)
+    p = {k: turned(plus, -k) for k in (-2, -1, 0, 1, 2)}
+    m = {k: turned(minus, -k) for k in (-1, 0, 1, 2, 3)}
+    plus_here, plus_next, right = reconstructed(p[-2], p[-1], p[0], p[1], p[2])
+    minus_next, minus_here, left = reconstructed(m[3], m[2], m[1], m[0], m[-1])
+    centre = 6.0 * ((p[0] + m[0]) + (p[1] + m[1])) - ((plus_here + minus_here) + (plus_next + minus_next))
+    interface = centre + ((plus_next - plus_here) - (minus_next - minus_here)) - 4.0 * (right + left)
+    return turned(interface, 1) - interface
 
 
 def lane_index(shape):
@@ -238,6 +234,11 @@
     return tile
 
 
+def reordered(tile, me, windows):
+    pieces = [turned(tile, windows.width * (g - (g ^ me))) for g in range(windows.nodes)]
+    return merged(pieces, windows.group(tile.shape))
+
+
 def open_kernel(u_ref, lo_ref, hi_ref, side_ref, al_ref):
     comps, nx, ny, nz = u_ref.shape[1:]
 
@@ -245,10 +246,7 @@
         return u_ref[0, c, i]
 
     write_edges(read, nx, ny, comps, lo_ref, hi_ref, side_ref)
-    tile = alpha_tile(speed_rows(read, nx, ny, nz, comps), nz)
-    al_ref[...] = tile
-    lo_ref[0, pl.ds(comps * HALO * ny, TILE), :] = tile
-    hi_ref[0, pl.ds(comps * HALO * ny, TILE), :] = tile
+    al_ref[...] = alpha_tile(speed_rows(read, nx, ny, nz, comps), nz)
 
 
 def blend_kernel(init_ref, *refs):
@@ -281,21 +279,24 @@
         return nat_ref[c, i]
 
     write_edges(read, nx, ny, comps, lo_ref, hi_ref, side_ref)
-    tile = alpha_tile(speed_rows(read, nx, ny, nz, comps), windows.width)
-    al_ref[...] = tile
-    lo_ref[0, pl.ds(comps * HALO * ny, TILE), :] = tile
-    hi_ref[0, pl.ds(comps * HALO * ny, TILE), :] = tile
-
-
-def along_grid(u, alphas, lo_ref, hi_ref, side_ref, out_ref, scratch, depth):
-    xp, xm, yp, ym, fy = scratch
-    comps, nx, ny, nz = out_ref.shape
+    tile = reordered(alpha_tile(speed_rows(read, nx, ny, nz, comps), windows.width), me, windows)
+
+    def spread(i, carry):
+        al_ref[i] = tile
+        return carry
+
+    lax.fori_loop(0, al_ref.shape[0], spread, 0)
+
+
+def along_grid(u, alphas, edges, rate, scratch, depth, extra, after):
+    xp, xm, yp, ym, zp, zm, fy = scratch
+    lo_ref, hi_ref, side_ref = edges
+    comps, nx, ny, nz = rate.shape
     rows = yp.shape[0] // (ny + 2 * HALO)
     every = range(comps)
 
     def own(i, carry):
-        split = splits([u(c, i) for c in every], alphas, (0, 1, 2) if depth else (0, 1))
-        along_x, along_y = split[:2]
+        along_x, along_y, *rest = splits([u(c, i) for c in every], alphas, (0, 1, 2) if depth else (0, 1))
         for c in every:
             xp[i + HALO, c * ny : (c + 1) * ny, :] = along_x[0][c]
             xm[i + HALO, c * ny : (c + 1) * ny, :] = along_x[1][c]
@@ -303,8 +304,8 @@
                 at = pl.ds((HALO + t) * rows + c * nx + i, TILE, stride=rows)
                 yp[at, :] = along_y[0][c][t : t + TILE]
                 ym[at, :] = along_y[1][c][t : t + TILE]
-            if depth:
-                out_ref[c, i] = rolled(split[2][0][c], split[2][1][c])
+        if depth:
+            depth(i, rest[0])
         return carry
 
     lax.fori_loop(0, nx, own, 0)
@@ -331,6 +332,11 @@
 
     lax.fori_loop(0, 2 * HALO, ghost_y, 0)
 
+    blocks = rows // TILE
+    share = zp.shape[0] // blocks
+    assert share * blocks == zp.shape[0]
+    piece = max(p for p in range(TILE, 41, TILE) if share % p == 0)
+
     def along_second(b, carry):
         first = pl.multiple_of(b * TILE, TILE)
 
@@ -342,98 +348,112 @@
             fy[pl.ds(i * rows + first, TILE), :] = value
 
         stream(load, store, ny)
-        return carry
-
-    lax.fori_loop(0, rows // TILE, along_second, 0)
-
-    for c in every:
-
-        def along_first(b, carry, c=c):
-            first = pl.multiple_of(b * TILE, TILE)
-
-            def load(j):
-                at = pl.ds(c * ny + first, TILE)
-                return xp[j, at, :], xm[j, at, :]
-
-            def store(i, value):
-                cross = fy[pl.ds(first * rows + c * nx + i, TILE, stride=rows), :]
-                here = pl.ds(first, TILE)
-                out_ref[c, i, here, :] = out_ref[c, i, here, :] + value + cross
-
-            stream(load, store, nx)
-            return carry
-
-        lax.fori_loop(0, ny // TILE, along_first, 0)
+        for n in range(0, share, piece):
+            at = pl.ds(pl.multiple_of(b * share + n, TILE), piece)
+            zp[at, :] = rolled(zp[at, :], zm[at, :])
+        return carry
+
+    lax.fori_loop(0, blocks, along_second, 0)
+
+    tiles = ny // TILE
+
+    def along_first(b, carry):
+        c, t = b // tiles, lax.rem(b, tiles) * TILE
+        first = pl.multiple_of(b * TILE, TILE)
+
+        def load(j):
+            return xp[j, pl.ds(first, TILE), :], xm[j, pl.ds(first, TILE), :]
+
+        def store(i, value):
+            cross = fy[pl.ds(t * rows + c * nx + i, TILE, stride=rows), :]
+            rate[c, i, pl.ds(pl.multiple_of(t, TILE), TILE), :] = value + (cross + extra(c, i, t))
+
+        stream(load, store, nx)
+        done = jnp.maximum(b - 1, 0)
+        after(done // tiles, pl.multiple_of(lax.rem(done, tiles) * TILE, TILE))
+        return carry
+
+    lax.fori_loop(0, comps * tiles, along_first, 0)
+    after(comps - 1, ny - TILE)
 
 
 def first_kernel(u_ref, lo_ref, hi_ref, side_ref, al_ref, other_ref, *refs):
-    nodes = len(refs) - 6
+    nodes = len(refs) - 8
     parts, rate, scratch = refs[:nodes], refs[nodes], refs[nodes + 1 :]
+    zp, zm = scratch[4:6]
     comps, nx, ny, nz = u_ref.shape[1:]
+    windows = Windows(nx, nz, nodes)
+    me = lax.axis_index("node")
     tile = jnp.maximum(al_ref[...], other_ref[...])
     alphas = [tile[k : k + 1, :] for k in range(3)]
-    along_grid(lambda c, i: u_ref[0, c, i], alphas, lo_ref, hi_ref, side_ref, rate, scratch, True)
-    windows = Windows(nx, nz, nodes)
-    me = lax.axis_index("node")
-
-    def cut(c, carry):
+
+    def depth(i, split):
+        for c in range(comps):
+            at = pl.ds(pl.multiple_of((c * nx + i) * ny, ny), ny)
+            zp[at, :] = split[0][c]
+            zm[at, :] = split[1][c]
+
+    def extra(c, i, t):
+        return zp[pl.ds(pl.multiple_of((c * nx + i) * ny + t, TILE), TILE), :]
+
+    def after(c, t):
         for r in range(windows.rows):
-            values = [rate[c, s * windows.rows + r] for s in range(windows.slots)]
-            at = pl.ds(pl.multiple_of((c * windows.rows + r) * ny, ny), ny)
+            values = [rate[c, s * windows.rows + r, pl.ds(t, TILE), :] for s in range(windows.slots)]
+            at = pl.ds(pl.multiple_of((c * windows.rows + r) * ny + t, TILE), TILE)
             for k in range(nodes):
                 parts[k][at, :] = windows.cut(values, me ^ k)
-        return carry
-
-    lax.fori_loop(0, comps, cut, 0)
-
-
-def second_kernel(init_ref, nat_ref, win_ref, lo_ref, hi_ref, side_ref, *refs):
+
+    along_grid(lambda c, i: u_ref[0, c, i], alphas, (lo_ref, hi_ref, side_ref), rate, scratch, depth, extra, after)
+
+
+def second_kernel(init_ref, nat_ref, win_ref, lo_ref, hi_ref, side_ref, al_ref, *refs):
     nodes = win_ref.shape[0]
-    tiles, outs, (rate, deep), scratch = refs[:nodes], refs[nodes : 2 * nodes], refs[2 * nodes : 2 * nodes + 2], refs[2 * nodes + 2 :]
+    outs, rate, scratch = refs[:nodes], refs[nodes], refs[nodes + 1 :]
+    zp, zm = scratch[4:6]
     comps, nx, ny, nz = nat_ref.shape
     every = range(comps)
     windows = Windows(nx, nz, nodes)
+    part = comps * windows.rows * ny
     me = lax.axis_index("node")
-    group = windows.group((TILE, nz))
-    tile = tiles[0][...]
-    for k in range(1, nodes):
-        value = tiles[k][...]
-        tile = jnp.maximum(tile, merged([turned(value, windows.width * (g - (g ^ k))) for g in range(nodes)], group))
+    tile = lax.fori_loop(
+        1, al_ref.shape[0], lambda i, best: jnp.maximum(best, al_ref[i]), al_ref[0], unroll=True if al_ref.shape[0] <= 32 else 1
+    )
+    tile = reordered(tile, me, windows)
     alphas = [tile[k : k + 1, :] for k in range(3)]
+    group = windows.group((1, nz))
 
     for k in range(nodes):
-        alpha = jnp.max(jnp.where(group[:1] == k, alphas[2], 0.0))
-
-        def depth(r, carry, k=k, alpha=alpha):
-            places = [pl.ds(pl.multiple_of((c * windows.rows + r) * ny, ny), ny) for c in every]
-            ((p, m),) = splits([win_ref[k, at, :] for at in places], [None, None, alpha], (2,))
+        alpha = jnp.max(jnp.where(group == k, alphas[2], 0.0))
+
+        def split_depth(r, carry, k=k, alpha=alpha):
+            places = [pl.multiple_of((c * windows.rows + r) * ny, ny) for c in every]
+            fields = [win_ref[k, pl.ds(place, ny), :] for place in places]
+            ((p, m),) = splits(fields, [None, None, alpha], (2,))
             for c in every:
-                deep[k, places[c], :] = rolled(p[c], m[c])
+                at = pl.ds(pl.multiple_of(k * part + places[c], TILE), ny)
+                zp[at, :] = p[c]
+                zm[at, :] = m[c]
             return carry
 
-        lax.fori_loop(0, windows.rows, depth, 0)
-
-    def join(c, carry):
-        for r in range(windows.rows):
-            at = pl.ds(pl.multiple_of((c * windows.rows + r) * ny, ny), ny)
-            values = [deep[k, at, :] for k in range(nodes)]
-            for s in range(windows.slots):
-                rate[c, s * windows.rows + r] = windows.joined(values, s)
-        return carry
-
-    lax.fori_loop(0, comps, join, 0)
-    along_grid(lambda c, i: nat_ref[c, i], alphas, lo_ref, hi_ref, side_ref, rate, scratch, False)
+        lax.fori_loop(0, windows.rows, split_depth, 0)
+
+    def extra(c, i, t):
+        s, r = i // windows.rows, i % windows.rows
+        place = (c * windows.rows + r) * ny + t
+        values = [zp[pl.ds(pl.multiple_of(k * part + place, TILE), TILE), :] for k in range(nodes)]
+        return windows.joined(values, s)
 
     weights = node_weights(me, nodes)
-    lanes = windows.group((ny, nz))
-
-    def finish(c, carry):
+    lanes = windows.group((TILE, nz))
+
+    def after(c, t):
+        here = pl.ds(t, TILE)
         for q in range(nx // nodes):
-            at = pl.ds(pl.multiple_of((c * (nx // nodes) + q) * ny, ny), ny)
+            at = pl.ds(pl.multiple_of((c * (nx // nodes) + q) * ny + t, TILE), TILE)
             start = merged(
-                [turned(init_ref[c, q * nodes + i], windows.width * (i - me)) for i in range(nodes)], lanes
+                [turned(init_ref[c, q * nodes + i, here, :], windows.width * (i - me)) for i in range(nodes)], lanes
             )
-            rows = [rate[c, q * nodes + i] for i in range(nodes)]
+            rows = [rate[c, q * nodes + i, here, :] for i in range(nodes)]
             rates = [
                 merged([turned(rows[i], windows.width * (i - k)) for i in range(nodes)], lanes) for k in range(nodes)
             ]
@@ -442,31 +462,25 @@
                 for j in range(nodes):
                     value = value + weights[k][j] * rates[j]
                 outs[k][at, :] = value
-        return carry
-
-    lax.fori_loop(0, comps, finish, 0)
+
+    along_grid(lambda c, i: nat_ref[c, i], alphas, (lo_ref, hi_ref, side_ref), rate, scratch, None, extra, after)
 
 
 def close_kernel(*refs):
     parts, out_ref = refs[:-1], refs[-1]
     nodes = len(parts)
-    comps, nx, ny, nz = out_ref.shape[1:]
+    nx, ny, nz = out_ref.shape[2:]
     width = nz // nodes
     me = lax.axis_index("node")
     lanes = lane_index((ny, nz)) // width
-
-    def step(c, carry):
-        for q in range(nx // nodes):
-            at = pl.ds(pl.multiple_of((c * (nx // nodes) + q) * ny, ny), ny)
-            values = [part[at, :] for part in parts]
-            for i in range(nodes):
-                out = turned(values[0], width * (me - i))
-                for k in range(1, nodes):
-                    out = jnp.where(lanes == (me ^ k), turned(values[k], width * ((me ^ k) - i)), out)
-                out_ref[0, c, q * nodes + i] = out
-        return carry
-
-    lax.fori_loop(0, comps, step, 0)
+    for q in range(nx // nodes):
+        values = [part[q * ny : (q + 1) * ny, :] for part in parts]
+        for i in range(nodes):
+            pieces = [turned(values[k], width * ((me ^ k) - i)) for k in range(nodes)]
+            out = pieces[0]
+            for k in range(1, nodes):
+                out = jnp.where(lanes == (me ^ k), pieces[k], out)
+            out_ref[0, 0, q * nodes + i] = out
 
 
 def call(kernel, outs, operands, scratch=(), flops=1_000_000):
@@ -493,65 +507,70 @@
     return lax.ppermute(value, "node", [(i, i ^ by) for i in range(lax.axis_size("node"))])
 
 
-def neighbours(lo, hi, side, tile):
-    across, beside = lax.axis_size("gx"), lax.axis_size("gy")
+def neighbours(lo, hi, side):
     lower, upper = shifted(hi, "gx", 1), shifted(lo, "gx", -1)
-    if across <= 4:
-        tiles = [tile, lower[0, -TILE:], upper[0, -TILE:]]
-        if across == 4:
-            tiles.append(shifted(tile, "gx", 2))
-        tile = functools.reduce(jnp.maximum, tiles)
-    else:
-        tile = lax.pmax(tile, "gx")
-    if beside == 2:
-        return lower, upper, shifted(side, "gy", 1), tile, shifted(tile, "gy", 1)
+    if lax.axis_size("gy") == 2:
+        return lower, upper, shifted(side, "gy", 1)
     half = side.shape[1] // 2
     side = jnp.concatenate([shifted(side[:, :half], "gy", 1), shifted(side[:, half:], "gy", -1)], axis=1)
-    tile = lax.pmax(tile, "gy")
-    return lower, upper, side, tile, tile
+    return lower, upper, side
+
+
+def largest(tile):
+    if lax.axis_size("gx") > 4 or lax.axis_size("gy") > 2:
+        tile = lax.pmax(tile, ("gx", "gy"))
+        return tile, tile
+    others = [shifted(tile, "gx", by) for by in range(1, lax.axis_size("gx"))]
+    tile = functools.reduce(jnp.maximum, others, tile)
+    return tile, shifted(tile, "gy", 1)
 
 
 def local(initial, guesses):
     comps, nx, ny, nz = initial.shape
     nodes = lax.axis_size("node")
+    devices = nodes * lax.axis_size("gx") * lax.axis_size("gy")
     rows = -(-comps * nx // TILE) * TILE
     windows = Windows(nx, nz, nodes)
-    edge = (1, comps * HALO * ny + TILE, nz)
-    edges = [edge, edge, (1, 2 * HALO * rows, nz), (TILE, nz)]
+    edge = (1, comps * HALO * ny, nz)
+    edges = [edge, edge, (1, 2 * HALO * rows, nz)]
     part = (comps * windows.rows * ny, nz)
-    streams = [
-        (nx + 2 * HALO, comps * ny, nz),
-        (nx + 2 * HALO, comps * ny, nz),
-        ((ny + 2 * HALO) * rows, nz),
-        ((ny + 2 * HALO) * rows, nz),
-        (ny * rows, nz),
-    ]
-    lo, hi, side, tile = call(open_kernel, edges, [guesses])
-    lower, upper, side, tile, other = neighbours(lo, hi, side, tile)
+    streams = [(nx + 2 * HALO, comps * ny, nz)] * 2 + [((ny + 2 * HALO) * rows, nz)] * 2
+    across = [(ny * rows, nz)]
+    lo, hi, side, tile = call(open_kernel, edges + [(TILE, nz)], [guesses])
+    lower, upper, side = neighbours(lo, hi, side)
+    tile, other = largest(tile)
     parts = call(
         first_kernel,
         [part] * nodes,
         [guesses, lower, upper, side, tile, other],
-        [initial.shape] + streams,
+        [initial.shape] + streams + [(comps * nx * ny, nz)] * 2 + across,
         30_000_000,
     )
     parts = [parts[0]] + [swapped(parts[k], k) for k in range(1, nodes)]
     win, nat, lo, hi, side, tile = call(
-        blend_kernel, [(nodes,) + part, initial.shape] + edges, [initial] + parts
+        blend_kernel,
+        [(nodes,) + part, initial.shape] + edges + [(devices, TILE, nz)],
+        [initial] + parts,
     )
-    lower, upper, side, tile, other = neighbours(lo, hi, side, tile)
-    tile = jnp.maximum(tile, other)
-    tiles = [tile] + [swapped(tile, k) for k in range(1, nodes)]
+    lower, upper, side = neighbours(lo, hi, side)
+    tiles = lax.all_to_all(tile, ("node", "gx", "gy"), 0, 0)
     outs = call(
         second_kernel,
         [(comps * nx // nodes * ny, nz)] * nodes,
-        [initial, nat, win, lower, upper, side] + tiles,
-        [initial.shape, (nodes,) + part] + streams,
+        [initial, nat, win, lower, upper, side, tiles],
+        [initial.shape] + streams + [(nodes * part[0], nz)] * 2 + across,
         30_000_000,
     )
     outs = [outs[0]] + [swapped(outs[k], k) for k in range(1, nodes)]
-    (states,) = call(close_kernel, [(1,) + initial.shape], outs)
-    return states
+    slab = nx // nodes * ny
+    return pl.pallas_call(
+        close_kernel,
+        grid=(comps,),
+        out_shape=jax.ShapeDtypeStruct((1,) + initial.shape, jnp.float32),
+        in_specs=[pl.BlockSpec((slab, nz), lambda c: (c, 0))] * nodes,
+        out_specs=pl.BlockSpec((1, 1, nx, ny, nz), lambda c: (0, c, 0, 0, 0)),
+        name="close_kernel",
+    )(*outs)
 
 
 def solution(mesh):

time: 76.1 us -> 75.9 us (level)
  waiting for transfers between devices: 27 us -> 24.1 us
  starting transfers between devices: 20.7 us -> 23.5 us
  Pallas kernels: 27.2 us -> 25.3 us
  local copies, waits for them, and re-layouts: 1.03 us -> 2.35 us
    pallas_call x5 -> x4, Pallas kernels: 27.2 us -> 21.7 us  [call(): pl.pallas_call(kernel, out_shape=[jax.ShapeDtypeStruct(shape, jnp.float32...]
    ppermute x10, starting transfers between devices: 10.1 us -> 13.9 us  [shifted(): lax.ppermute(value, axis, [(i, (i + by) % count) for i in range(count)])]
    pallas_call x0 -> x1, Pallas kernels: none -> 3.65 us  [local(): pl.pallas_call(close_kernel, grid=(comps,), out_shape=jax.ShapeDtypeStruc...]
    ppermute x9 -> x6, starting transfers between devices: 10.6 us -> 7.04 us  [swapped(): lax.ppermute(value, 'node', [(i, i ^ by) for i in range(lax.axis_size('no...]
    ppermute x9 -> x6, waiting for transfers between devices: 14.9 us -> 12.3 us  [swapped(): lax.ppermute(value, 'node', [(i, i ^ by) for i in range(lax.axis_size('no...]
    all_to_all x0 -> x1, starting transfers between devices: none -> 2.58 us  [local(): tiles = lax.all_to_all(tile, ('node', 'gx', 'gy'), 0, 0)]
    unnamed x4 -> x12, local copies, waits for them, and re-layouts: 1.03 us -> 2.35 us
  transfers between devices with their start and end apart: 19 -> 17, of which waited for: 12 -> 11; matrix products, arithmetic and copies ran while one was open for 0% -> 0% of each run, Pallas kernels for 0% -> 0%
where the time goes in v3:
time: 75.9 us; the launch traced here: 75.4 us
  Pallas kernels  25.3 us (33%)
  waiting for transfers between devices  24.1 us (32%)
  starting transfers between devices  23.5 us (31%)
  local copies, waits for them, and re-layouts  2.35 us (3%)
    pallas_call x4, Pallas kernels, call(): pl.pallas_call(kernel, out_shape=[jax.ShapeDtypeStruct(shape, jnp.float32...  21.7 us
    ppermute x10, starting transfers between devices, shifted(): lax.ppermute(value, axis, [(i, (i + by) % count) for i in range(count)])  13.9 us
    ppermute x6, waiting for transfers between devices, swapped(): lax.ppermute(value, 'node', [(i, i ^ by) for i in range(lax.axis_size('no...  12.3 us
    ppermute x10, waiting for transfers between devices, shifted(): lax.ppermute(value, axis, [(i, (i + by) % count) for i in range(count)])  11.8 us
    ppermute x6, starting transfers between devices, swapped(): lax.ppermute(value, 'node', [(i, i ^ by) for i in range(lax.axis_size('no...  7.04 us
    pallas_call x1, Pallas kernels, local(): pl.pallas_call(close_kernel, grid=(comps,), out_shape=jax.ShapeDtypeStruc...  3.65 us
    all_to_all x1, starting transfers between devices, local(): tiles = lax.all_to_all(tile, ('node', 'gx', 'gy'), 0, 0)  2.58 us
    unnamed x12, local copies, waits for them, and re-layouts  2.35 us
  transfers between devices with their start and end apart: 17, of which 11 were waited for; matrix products, arithmetic and copies ran while one was open for 0% of the time, Pallas kernels for 0%

profile of v3, /device:TPU:0, one launch (start us, length us, event | category | flops | bytes accessed | tf_op | source)
XLA Modules:
  0.0 75.4 jit_solution(10340795416197663346)
XLA Ops:
  0.0 0.0 copy-start
  0.0 1.0 %copy-done = f32[1,5,12,16,128]{4,3,2,1,0:T(8,128)S(1)} copy-done((f32[1,5,12,16,128]{4,3,2,1,0:T(8,128)S(1)}, f32[1,5,12,16,128]{4,3,2,1,0:T(8,128)}, u32[]{:S(2)}) %copy-start) | copy-done | bytes 491544
  1.0 1.0 %open_kernel.1 = (f32[1,240,128]{2,1,0:T(8,128)S(1)}, f32[1,240,128]{2,1,0:T(8,128)S(1)}, f32[1,384,128]{2,1,0:T(8,128)S(1)}, f32[8,128]{1,0:T(8,128)S(1)}) custom-call(f32[1,5,12,16,128]{4,3,2,1,0:T(8,128)S(1)} %copy-done), custom_call_target="tpu_custom_call" | custom-call | flops 1000000 | bytes 983040 | tf_op jit(solution)/shard_map/open_kernel/pallas_call | solution.py:489
  2.0 0.0 copy-start.1
  2.0 5.1 %collective-permute-start.5 = (f32[8,128]{1,0:T(8,128)S(1)}, f32[8,128]{1,0:T(8,128)S(1)}, u32[]{:S(2)}, u32[]{:S(2)}) collective-permute-start(f32[8,128]{1,0:T(8,128)S(1)} %get-tuple-element.26), channel_id=1, source_target_pairs={{0,6},{2,0},{4,2},{6,4},{1,7},{3,1},{5,3},{7,5},{8,14},{10,8},{12,... | collective-permute-start | bytes 12296 | tf_op jit(solution)/shard_map/ppermute | solution.py:503
  7.1 0.0 collective-permute-start.4
  7.1 1.0 %collective-permute-start.3 = (f32[8,128]{1,0:T(8,128)S(1)}, f32[8,128]{1,0:T(8,128)S(1)}, u32[]{:S(2)}, u32[]{:S(2)}) collective-permute-start(f32[8,128]{1,0:T(8,128)S(1)} %get-tuple-element.26), channel_id=1, source_target_pairs={{0,2},{2,4},{4,6},{6,0},{1,3},{3,5},{5,7},{7,1},{8,10},{10,12},{12... | collective-permute-start | bytes 12296 | tf_op jit(solution)/shard_map/ppermute | solution.py:503
  8.1 2.5 %collective-permute-start = (f32[1,240,128]{2,1,0:T(8,128)S(1)}, f32[1,240,128]{2,1,0:T(8,128)S(1)}, u32[]{:S(2)}, u32[]{:S(2)}) collective-permute-start(f32[1,240,128]{2,1,0:T(8,128)S(1)} %get-tuple-element.23), channel_id=1, source_target_pairs={{0,2},{2,4},{4,6},{6,0},{1,3},{3,5},{5,7},{7,1},{8,10},{10,12},{12... | collective-permute-start | bytes 368648 | tf_op jit(solution)/shard_map/ppermute | solution.py:503
  10.6 1.3 %collective-permute-start.1 = (f32[1,240,128]{2,1,0:T(8,128)S(1)}, f32[1,240,128]{2,1,0:T(8,128)S(1)}, u32[]{:S(2)}, u32[]{:S(2)}) collective-permute-start(f32[1,240,128]{2,1,0:T(8,128)S(1)} %get-tuple-element.24), channel_id=1, source_target_pairs={{0,6},{2,0},{4,2},{6,4},{1,7},{3,1},{5,3},{7,5},{8,14},{10,8},{12,... | collective-permute-start | bytes 368648 | tf_op jit(solution)/shard_map/ppermute | solution.py:503
  11.9 0.0 collective-permute-done.5
  11.9 0.0 collective-permute-start.2
  11.9 0.5 collective-permute-done.4
  12.4 0.2 collective-permute-done.3
  12.7 0.0 collective-permute-start.6
  12.7 1.2 %collective-permute-done.6.other_ref = f32[8,128]{1,0:T(8,128)S(1)} collective-permute-done((f32[8,128]{1,0:T(8,128)S(1)}, f32[8,128]{1,0:T(8,128)S(1)}, u32[]{:S(2)}, u32[]{:S(2)}) %collective-permute-start.6) | collective-permute-done | bytes 4128 | tf_op jit(solution)/shard_map/ppermute | solution.py:503
  13.8 1.8 %collective-permute-done.lo_ref = f32[1,240,128]{2,1,0:T(8,128)S(1)} collective-permute-done((f32[1,240,128]{2,1,0:T(8,128)S(1)}, f32[1,240,128]{2,1,0:T(8,128)S(1)}, u32[]{:S(2)}, u32[]{:S(2)}) %collective-permute-start) | collective-permute-done | bytes 122912 | tf_op jit(solution)/shard_map/ppermute | solution.py:503
  15.6 1.2 %collective-permute-done.1.hi_ref = f32[1,240,128]{2,1,0:T(8,128)S(1)} collective-permute-done((f32[1,240,128]{2,1,0:T(8,128)S(1)}, f32[1,240,128]{2,1,0:T(8,128)S(1)}, u32[]{:S(2)}, u32[]{:S(2)}) %collective-permute-start.1) | collective-permute-done | bytes 122912 | tf_op jit(solution)/shard_map/ppermute | solution.py:503
  16.8 0.0 collective-permute-done.2.side_ref
  16.8 7.9 %first_kernel.1 = (f32[320,128]{1,0:T(8,128)S(1)}, f32[320,128]{1,0:T(8,128)S(1)}, f32[320,128]{1,0:T(8,128)S(1)}, f32[320,128]{1,0:T(8,128)S(1)}) custom-call(f32[1,5,12,16,128]{4,3,2,1,0:T(8,128)S(1)} %copy-done, f32[1,240,128]{2,1,0:T(8,128)S(1)} %collective-permute-done.lo_ref, f32[1,240,128]{2,1,0:T(8,128)S(1)} %collective-permute-done.1.hi_ref, ...), custom_call_target="tpu_custom_call" | custom-call | flops 30000000 | bytes 1884160 | tf_op jit(solution)/shard_map/first_kernel/pallas_call | solution.py:489
  24.7 1.6 %collective-permute-start.7 = (f32[320,128]{1,0:T(8,128)S(1)}, f32[320,128]{1,0:T(8,128)S(1)}, u32[]{:S(2)}, u32[]{:S(2)}) collective-permute-start(f32[320,128]{1,0:T(8,128)S(1)} %get-tuple-element.28), channel_id=1, source_target_pairs={{0,8},{8,0},{16,24},{24,16},{1,9},{9,1},{17,25},{25,17},{2,10},{10... | collective-permute-start | bytes 491528 | tf_op jit(solution)/shard_map/ppermute | solution.py:507
  26.3 1.5 %collective-permute-start.8 = (f32[320,128]{1,0:T(8,128)S(1)}, f32[320,128]{1,0:T(8,128)S(1)}, u32[]{:S(2)}, u32[]{:S(2)}) collective-permute-start(f32[320,128]{1,0:T(8,128)S(1)} %get-tuple-element.29), channel_id=1, source_target_pairs={{0,16},{8,24},{16,0},{24,8},{1,17},{9,25},{17,1},{25,9},{2,18},{10... | collective-permute-start | bytes 491528 | tf_op jit(solution)/shard_map/ppermute | solution.py:507
  27.8 0.5 collective-permute-start.9
  28.3 3.1 %collective-permute-done.7.refs_1_ = f32[320,128]{1,0:T(8,128)S(1)} collective-permute-done((f32[320,128]{1,0:T(8,128)S(1)}, f32[320,128]{1,0:T(8,128)S(1)}, u32[]{:S(2)}, u32[]{:S(2)}) %collective-permute-start.7) | collective-permute-done | bytes 163872 | tf_op jit(solution)/shard_map/ppermute | solution.py:507
  31.4 3.7 %collective-permute-done.8.refs_2_ = f32[320,128]{1,0:T(8,128)S(1)} collective-permute-done((f32[320,128]{1,0:T(8,128)S(1)}, f32[320,128]{1,0:T(8,128)S(1)}, u32[]{:S(2)}, u32[]{:S(2)}) %collective-permute-start.8) | collective-permute-done | bytes 163872 | tf_op jit(solution)/shard_map/ppermute | solution.py:507
  35.1 0.0 collective-permute-done.9.refs_3_
  35.1 0.0 copy-done.1
  35.1 3.0 %blend_kernel.1 = (f32[4,320,128]{2,1,0:T(8,128)S(1)}, f32[5,12,16,128]{3,2,1,0:T(8,128)S(1)}, f32[1,240,128]{2,1,0:T(8,128)S(1)}, f32[1,240,128]{2,1,0:T(8,128)...) custom-call(f32[5,12,16,128]{3,2,1,0:T(8,128)S(1)} %copy-done.1, f32[320,128]{1,0:T(8,128)S(1)} %get-tuple-element.27.refs_0_, ...), custom_call_target="tpu_custom_call" | custom-call | flops 1000000 | bytes 2293760 | tf_op jit(solution)/shard_map/blend_kernel/pallas_call | solution.py:489
  38.1 2.6 %all-to-all-start = ((f32[32,8,128]{2,1,0:T(8,128)}), f32[32,8,128]{2,1,0:T(8,128)S(1)}, u32[]{:S(2)}, u32[]{:S(2)}) async-start(f32[32,8,128]{2,1,0:T(8,128)} %get-tuple-element.36), calls=%async_computation | async-start | bytes 262144 | tf_op jit(solution)/shard_map/all_to_all | solution.py:556
  40.7 0.2 collective-permute-start.12
  40.9 1.7 %collective-permute-start.10 = (f32[1,240,128]{2,1,0:T(8,128)S(1)}, f32[1,240,128]{2,1,0:T(8,128)S(1)}, u32[]{:S(2)}, u32[]{:S(2)}) collective-permute-start(f32[1,240,128]{2,1,0:T(8,128)S(1)} %get-tuple-element.33), channel_id=1, source_target_pairs={{0,2},{2,4},{4,6},{6,0},{1,3},{3,5},{5,7},{7,1},{8,10},{10,12},{12... | collective-permute-start | bytes 368648 | tf_op jit(solution)/shard_map/ppermute | solution.py:503
  42.6 2.1 %collective-permute-start.11 = (f32[1,240,128]{2,1,0:T(8,128)S(1)}, f32[1,240,128]{2,1,0:T(8,128)S(1)}, u32[]{:S(2)}, u32[]{:S(2)}) collective-permute-start(f32[1,240,128]{2,1,0:T(8,128)S(1)} %get-tuple-element.34), channel_id=1, source_target_pairs={{0,6},{2,0},{4,2},{6,4},{1,7},{3,1},{5,3},{7,5},{8,14},{10,8},{12,... | collective-permute-start | bytes 368648 | tf_op jit(solution)/shard_map/ppermute | solution.py:503
  44.7 5.9 %collective-permute-done.10.lo_ref = f32[1,240,128]{2,1,0:T(8,128)S(1)} collective-permute-done((f32[1,240,128]{2,1,0:T(8,128)S(1)}, f32[1,240,128]{2,1,0:T(8,128)S(1)}, u32[]{:S(2)}, u32[]{:S(2)}) %collective-permute-start.10) | collective-permute-done | bytes 122912 | tf_op jit(solution)/shard_map/ppermute | solution.py:503
  50.7 1.0 %collective-permute-done.11.hi_ref = f32[1,240,128]{2,1,0:T(8,128)S(1)} collective-permute-done((f32[1,240,128]{2,1,0:T(8,128)S(1)}, f32[1,240,128]{2,1,0:T(8,128)S(1)}, u32[]{:S(2)}, u32[]{:S(2)}) %collective-permute-start.11) | collective-permute-done | bytes 122912 | tf_op jit(solution)/shard_map/ppermute | solution.py:503
  51.6 0.0 collective-permute-done.12.side_ref
  51.6 0.0 all-to-all-done.al_ref
  51.6 9.8 %second_kernel.1 = (f32[240,128]{1,0:T(8,128)S(1)}, f32[240,128]{1,0:T(8,128)S(1)}, f32[240,128]{1,0:T(8,128)S(1)}, f32[240,128]{1,0:T(8,128)S(1)}) custom-call(f32[5,12,16,128]{3,2,1,0:T(8,128)S(1)} %copy-done.1, f32[5,12,16,128]{3,2,1,0:T(8,128)S(1)} %get-tuple-element.31.nat_ref, f32[4,320,128]{2,1,0:T(8,128)S(1)} %get-tuple-element.32.win_ref, ...), custom_call_target="tpu_custom_call" | custom-call | flops 30000000 | bytes 4423680 | tf_op jit(solution)/shard_map/second_kernel/pallas_call | solution.py:489
  61.5 0.0 copy-start.2
  61.5 0.6 copy-done.2
  62.1 1.5 %collective-permute-start.13 = (f32[240,128]{1,0:T(8,128)S(1)}, f32[240,128]{1,0:T(8,128)S(1)}, u32[]{:S(2)}, u32[]{:S(2)}) collective-permute-start(f32[240,128]{1,0:T(8,128)S(1)} %get-tuple-element.38), channel_id=1, source_target_pairs={{0,8},{8,0},{16,24},{24,16},{1,9},{9,1},{17,25},{25,17},{2,10},{10... | collective-permute-start | bytes 368648 | tf_op jit(solution)/shard_map/ppermute | solution.py:507
  63.6 1.5 %collective-permute-start.14 = (f32[240,128]{1,0:T(8,128)S(1)}, f32[240,128]{1,0:T(8,128)S(1)}, u32[]{:S(2)}, u32[]{:S(2)}) collective-permute-start(f32[240,128]{1,0:T(8,128)S(1)} %get-tuple-element.39), channel_id=1, source_target_pairs={{0,16},{8,24},{16,0},{24,8},{1,17},{9,25},{17,1},{25,9},{2,18},{10... | collective-permute-start | bytes 368648 | tf_op jit(solution)/shard_map/ppermute | solution.py:507
  65.1 0.5 collective-permute-start.15
  65.6 1.7 %collective-permute-done.13.refs_1_ = f32[240,128]{1,0:T(8,128)S(1)} collective-permute-done((f32[240,128]{1,0:T(8,128)S(1)}, f32[240,128]{1,0:T(8,128)S(1)}, u32[]{:S(2)}, u32[]{:S(2)}) %collective-permute-start.13) | collective-permute-done | bytes 122912 | tf_op jit(solution)/shard_map/ppermute | solution.py:507
  67.2 0.0 copy-start.3
  67.3 3.8 %collective-permute-done.14.refs_2_ = f32[240,128]{1,0:T(8,128)S(1)} collective-permute-done((f32[240,128]{1,0:T(8,128)S(1)}, f32[240,128]{1,0:T(8,128)S(1)}, u32[]{:S(2)}, u32[]{:S(2)}) %collective-permute-start.14) | collective-permute-done | bytes 122912 | tf_op jit(solution)/shard_map/ppermute | solution.py:507
  71.1 0.0 copy-start.4
  71.1 0.0 collective-permute-done.15.refs_3_
  71.1 0.0 copy-start.5
  71.1 0.0 copy-done.3
  71.1 0.6 copy-done.4
  71.7 0.0 copy-done.5
  71.8 3.6 %close_kernel.1 = f32[1,5,12,16,128]{4,3,2,1,0:T(8,128)} custom-call(f32[240,128]{1,0:T(8,128)} %copy-done.2, f32[240,128]{1,0:T(8,128)} %copy-done.3, f32[240,128]{1,0:T(8,128)} %copy-done.4, f32[240,128]{1,0:T(8,128)} %copy-done.5), custom_call_target="tpu_custom_call" | custom-call | tf_op jit(solution)/shard_map/close_kernel/pallas_call | solution.py:566
  (1 shorter events, 0.0 us)
Async XLA Ops:
  0.0 1.0 %copy-start = (f32[1,5,12,16,128]{4,3,2,1,0:T(8,128)S(1)}, f32[1,5,12,16,128]{4,3,2,1,0:T(8,128)}, u32[]{:S(2)}) copy-start(f32[1,5,12,16,128]{4,3,2,1,0:T(8,128)} %u_ref.3) | copy-start | bytes 1474564
  2.0 33.1 %copy-start.1 = (f32[5,12,16,128]{3,2,1,0:T(8,128)S(1)}, f32[5,12,16,128]{3,2,1,0:T(8,128)}, u32[]{:S(2)}) copy-start(f32[5,12,16,128]{3,2,1,0:T(8,128)} %init_ref.3) | copy-start | bytes 1474564
  2.0 9.9 %collective-permute-start.5 = (f32[8,128]{1,0:T(8,128)S(1)}, f32[8,128]{1,0:T(8,128)S(1)}, u32[]{:S(2)}, u32[]{:S(2)}) collective-permute-start(f32[8,128]{1,0:T(8,128)S(1)} %get-tuple-element.26), channel_id=1, source_target_pairs={{0,6},{2,0},{4,2},{6,4},{1,7},{3,1},{5,3},{7,5},{8,14},{10,8},{12,... | collective-permute-start | bytes 12296 | tf_op jit(solution)/shard_map/ppermute | solution.py:503
  7.1 5.4 %collective-permute-start.4 = (f32[8,128]{1,0:T(8,128)S(1)}, f32[8,128]{1,0:T(8,128)S(1)}, u32[]{:S(2)}, u32[]{:S(2)}) collective-permute-start(f32[8,128]{1,0:T(8,128)S(1)} %get-tuple-element.26), channel_id=1, source_target_pairs={{0,4},{2,6},{4,0},{6,2},{1,5},{3,7},{5,1},{7,3},{8,12},{10,14},{12... | collective-permute-start | bytes 12296 | tf_op jit(solution)/shard_map/ppermute | solution.py:503
  7.1 5.6 %collective-permute-start.3 = (f32[8,128]{1,0:T(8,128)S(1)}, f32[8,128]{1,0:T(8,128)S(1)}, u32[]{:S(2)}, u32[]{:S(2)}) collective-permute-start(f32[8,128]{1,0:T(8,128)S(1)} %get-tuple-element.26), channel_id=1, source_target_pairs={{0,2},{2,4},{4,6},{6,0},{1,3},{3,5},{5,7},{7,1},{8,10},{10,12},{12... | collective-permute-start | bytes 12296 | tf_op jit(solution)/shard_map/ppermute | solution.py:503
  8.1 7.5 %collective-permute-start = (f32[1,240,128]{2,1,0:T(8,128)S(1)}, f32[1,240,128]{2,1,0:T(8,128)S(1)}, u32[]{:S(2)}, u32[]{:S(2)}) collective-permute-start(f32[1,240,128]{2,1,0:T(8,128)S(1)} %get-tuple-element.23), channel_id=1, source_target_pairs={{0,2},{2,4},{4,6},{6,0},{1,3},{3,5},{5,7},{7,1},{8,10},{10,12},{12... | collective-permute-start | bytes 368648 | tf_op jit(solution)/shard_map/ppermute | solution.py:503
  10.6 6.3 %collective-permute-start.1 = (f32[1,240,128]{2,1,0:T(8,128)S(1)}, f32[1,240,128]{2,1,0:T(8,128)S(1)}, u32[]{:S(2)}, u32[]{:S(2)}) collective-permute-start(f32[1,240,128]{2,1,0:T(8,128)S(1)} %get-tuple-element.24), channel_id=1, source_target_pairs={{0,6},{2,0},{4,2},{6,4},{1,7},{3,1},{5,3},{7,5},{8,14},{10,8},{12,... | collective-permute-start | bytes 368648 | tf_op jit(solution)/shard_map/ppermute | solution.py:503
  11.9 4.9 %collective-permute-start.2 = (f32[1,384,128]{2,1,0:T(8,128)S(1)}, f32[1,384,128]{2,1,0:T(8,128)S(1)}, u32[]{:S(2)}, u32[]{:S(2)}) collective-permute-start(f32[1,384,128]{2,1,0:T(8,128)S(1)} %get-tuple-element.25), channel_id=1, source_target_pairs={{0,1},{1,0},{2,3},{3,2},{4,5},{5,4},{6,7},{7,6},{8,9},{9,8},{10,11... | collective-permute-start | bytes 589832 | tf_op jit(solution)/shard_map/ppermute | solution.py:503
  12.7 1.2 %collective-permute-start.6 = (f32[8,128]{1,0:T(8,128)S(1)}, f32[8,128]{1,0:T(8,128)S(1)}, u32[]{:S(2)}, u32[]{:S(2)}) collective-permute-start(f32[8,128]{1,0:T(8,128)S(1)} %maximum_maximum_fusion.al_ref), channel_id=1, source_target_pairs={{0,1},{1,0},{2,3},{3,2},{4,5},{5,4},{6,7},{7,6},{8,9},{9,8},{10,11... | collective-permute-start | bytes 12296 | tf_op jit(solution)/shard_map/ppermute | solution.py:503
  24.7 6.7 %collective-permute-start.7 = (f32[320,128]{1,0:T(8,128)S(1)}, f32[320,128]{1,0:T(8,128)S(1)}, u32[]{:S(2)}, u32[]{:S(2)}) collective-permute-start(f32[320,128]{1,0:T(8,128)S(1)} %get-tuple-element.28), channel_id=1, source_target_pairs={{0,8},{8,0},{16,24},{24,16},{1,9},{9,1},{17,25},{25,17},{2,10},{10... | collective-permute-start | bytes 491528 | tf_op jit(solution)/shard_map/ppermute | solution.py:507
  26.3 8.8 %collective-permute-start.8 = (f32[320,128]{1,0:T(8,128)S(1)}, f32[320,128]{1,0:T(8,128)S(1)}, u32[]{:S(2)}, u32[]{:S(2)}) collective-permute-start(f32[320,128]{1,0:T(8,128)S(1)} %get-tuple-element.29), channel_id=1, source_target_pairs={{0,16},{8,24},{16,0},{24,8},{1,17},{9,25},{17,1},{25,9},{2,18},{10... | collective-permute-start | bytes 491528 | tf_op jit(solution)/shard_map/ppermute | solution.py:507
  27.8 7.3 %collective-permute-start.9 = (f32[320,128]{1,0:T(8,128)S(1)}, f32[320,128]{1,0:T(8,128)S(1)}, u32[]{:S(2)}, u32[]{:S(2)}) collective-permute-start(f32[320,128]{1,0:T(8,128)S(1)} %get-tuple-element.30), channel_id=1, source_target_pairs={{0,24},{8,16},{16,8},{24,0},{1,25},{9,17},{17,9},{25,1},{2,26},{10... | collective-permute-start | bytes 491528 | tf_op jit(solution)/shard_map/ppermute | solution.py:507
  38.1 13.5 %all-to-all-start = ((f32[32,8,128]{2,1,0:T(8,128)}), f32[32,8,128]{2,1,0:T(8,128)S(1)}, u32[]{:S(2)}, u32[]{:S(2)}) async-start(f32[32,8,128]{2,1,0:T(8,128)} %get-tuple-element.36), calls=%async_computation | async-start | bytes 262144 | tf_op jit(solution)/shard_map/all_to_all | solution.py:556
  40.7 10.9 %collective-permute-start.12 = (f32[1,384,128]{2,1,0:T(8,128)S(1)}, f32[1,384,128]{2,1,0:T(8,128)S(1)}, u32[]{:S(2)}, u32[]{:S(2)}) collective-permute-start(f32[1,384,128]{2,1,0:T(8,128)S(1)} %get-tuple-element.35), channel_id=1, source_target_pairs={{0,1},{1,0},{2,3},{3,2},{4,5},{5,4},{6,7},{7,6},{8,9},{9,8},{10,11... | collective-permute-start | bytes 589832 | tf_op jit(solution)/shard_map/ppermute | solution.py:503
  40.9 9.8 %collective-permute-start.10 = (f32[1,240,128]{2,1,0:T(8,128)S(1)}, f32[1,240,128]{2,1,0:T(8,128)S(1)}, u32[]{:S(2)}, u32[]{:S(2)}) collective-permute-start(f32[1,240,128]{2,1,0:T(8,128)S(1)} %get-tuple-element.33), channel_id=1, source_target_pairs={{0,2},{2,4},{4,6},{6,0},{1,3},{3,5},{5,7},{7,1},{8,10},{10,12},{12... | collective-permute-start | bytes 368648 | tf_op jit(solution)/shard_map/ppermute | solution.py:503
  42.6 9.0 %collective-permute-start.11 = (f32[1,240,128]{2,1,0:T(8,128)S(1)}, f32[1,240,128]{2,1,0:T(8,128)S(1)}, u32[]{:S(2)}, u32[]{:S(2)}) collective-permute-start(f32[1,240,128]{2,1,0:T(8,128)S(1)} %get-tuple-element.34), channel_id=1, source_target_pairs={{0,6},{2,0},{4,2},{6,4},{1,7},{3,1},{5,3},{7,5},{8,14},{10,8},{12,... | collective-permute-start | bytes 368648 | tf_op jit(solution)/shard_map/ppermute | solution.py:503
  61.5 0.6 copy-start.2
  62.1 5.1 %collective-permute-start.13 = (f32[240,128]{1,0:T(8,128)S(1)}, f32[240,128]{1,0:T(8,128)S(1)}, u32[]{:S(2)}, u32[]{:S(2)}) collective-permute-start(f32[240,128]{1,0:T(8,128)S(1)} %get-tuple-element.38), channel_id=1, source_target_pairs={{0,8},{8,0},{16,24},{24,16},{1,9},{9,1},{17,25},{25,17},{2,10},{10... | collective-permute-start | bytes 368648 | tf_op jit(solution)/shard_map/ppermute | solution.py:507
  63.6 7.5 %collective-permute-start.14 = (f32[240,128]{1,0:T(8,128)S(1)}, f32[240,128]{1,0:T(8,128)S(1)}, u32[]{:S(2)}, u32[]{:S(2)}) collective-permute-start(f32[240,128]{1,0:T(8,128)S(1)} %get-tuple-element.39), channel_id=1, source_target_pairs={{0,16},{8,24},{16,0},{24,8},{1,17},{9,25},{17,1},{25,9},{2,18},{10... | collective-permute-start | bytes 368648 | tf_op jit(solution)/shard_map/ppermute | solution.py:507
  65.1 6.0 %collective-permute-start.15 = (f32[240,128]{1,0:T(8,128)S(1)}, f32[240,128]{1,0:T(8,128)S(1)}, u32[]{:S(2)}, u32[]{:S(2)}) collective-permute-start(f32[240,128]{1,0:T(8,128)S(1)} %get-tuple-element.40), channel_id=1, source_target_pairs={{0,24},{8,16},{16,8},{24,0},{1,25},{9,17},{17,9},{25,1},{2,26},{10... | collective-permute-start | bytes 368648 | tf_op jit(solution)/shard_map/ppermute | solution.py:507
  67.2 3.9 %copy-start.3 = (f32[240,128]{1,0:T(8,128)}, f32[240,128]{1,0:T(8,128)S(1)}, u32[]{:S(2)}) copy-start(f32[240,128]{1,0:T(8,128)S(1)} %collective-permute-done.13.refs_1_) | copy-start | bytes 368644
  71.1 0.6 copy-start.4
  71.1 0.7 copy-start.5

commit v4 on v3

v4 whole, which is shorter than its diff:
```python
import functools

import jax
import jax.numpy as jnp
from jax import lax
from jax.experimental import pallas as pl
from jax.experimental.pallas import tpu as pltpu
from jax.sharding import PartitionSpec as P

SWEEPS = 2
HALO = 3
COMPONENTS = 5
TILE = 8

heat_ratio = 1.4
step_size = 0.025
density_floor = 0.5
pressure_floor = 0.25
epsilon = 1e-06
radau_weights = [
    [0.112999479323156, -0.040309220723522, 0.025802377420336, -0.009904676507266],
    [0.2343839957474, 0.206892573935359, -0.047857128048541, 0.016047422806516],
    [0.21668178462325, 0.406123263867373, 0.189036518170056, -0.024182104899833],
    [0.220462211176768, 0.388193468843172, 0.32884431998006, 0.0625],
]


def reciprocal(value):
    return pl.reciprocal(value, approx=True)


def primitives(fields):
    inverse = 1.0 / jnp.maximum(fields[0], density_floor)
    velocity = [fields[k] * inverse for k in (1, 2, 3)]
    energy = fields[1] * velocity[0] + fields[2] * velocity[1] + fields[3] * velocity[2]
    pressure = jnp.maximum(0.4 * (fields[4] - 0.5 * energy), pressure_floor)
    return inverse, velocity, pressure


def signal_speeds(fields):
    inverse, velocity, pressure = primitives(fields)
    sound = jnp.sqrt(heat_ratio * pressure * inverse)
    return [jnp.abs(v) + sound for v in velocity]


def half_fluxes(half, speed, half_pressure, direction):
    flux = [half[direction + 1]] + [half[k] * speed for k in (1, 2, 3)]
    flux.append((half[4] + half_pressure) * speed)
    flux[direction + 1] = flux[direction + 1] + half_pressure
    return flux


def splits(fields, alphas, directions=(0, 1, 2)):
    _, velocity, pressure = primitives(fields)
    half = [0.5 * field for field in fields]
    half_pressure = 0.5 * pressure
    out = []
    for direction in directions:
        flux = half_fluxes(half, velocity[direction], half_pressure, direction)
        signal = [alphas[direction] * value for value in half]
        out.append(
            ([f + s for f, s in zip(flux, signal)], [f - s for f, s in zip(flux, signal)])
        )
    return out


def cell_terms(below, above):
    second = above - below
    both = below + above
    square = second * second
    middle = 0.25 * (both * both) + ((13.0 / 12.0) * square + epsilon)
    outer = middle + square
    cross = both * second
    return second, outer + cross, middle, outer - cross


def correction(first, middle, last, third_first, third_last):
    ratio_first = middle * reciprocal(first)
    ratio_last = middle * reciprocal(last)
    weight_first = ratio_first * ratio_first
    weight_last = 1.5 * (ratio_last * ratio_last)
    total = (6.0 + weight_first) + (weight_last + weight_last)
    return (weight_first * third_first + weight_last * third_last) * reciprocal(total)


def stream(load, store, count):
    plus, minus, centre = {}, {}, {}
    terms_plus, terms_minus, third_plus, third_minus, interface = {}, {}, {}, {}, {}
    differences_plus, differences_minus = {}, {}
    plus[0], minus[0] = load(0)
    for j in range(1, count + 2 * HALO):
        plus[j], minus[j] = load(j)
        differences_plus[j] = plus[j] - plus[j - 1]
        differences_minus[j] = minus[j] - minus[j - 1]
        cell = j - 1
        if cell < 1:
            continue
        terms_plus[cell] = cell_terms(differences_plus[cell], differences_plus[j])
        terms_minus[cell] = cell_terms(differences_minus[cell], differences_minus[j])
        if 2 <= cell <= count + 3:
            centre[cell] = 6.0 * (plus[cell] + minus[cell]) - (
                terms_plus[cell][0] + terms_minus[cell][0]
            )
        if cell < 2:
            continue
        third_plus[cell] = terms_plus[cell][0] - terms_plus[cell - 1][0]
        third_minus[cell] = terms_minus[cell][0] - terms_minus[cell - 1][0]
        if cell < 4:
            continue
        at = cell - 2
        right = correction(
            terms_plus[at - 1][1], terms_plus[at][2], terms_plus[at + 1][3], third_plus[at], third_plus[at + 1]
        )
        left = correction(
            terms_minus[at + 2][3], terms_minus[at + 1][2], terms_minus[at][1],
            third_minus[at + 2], third_minus[at + 1],
        )
        interface[at] = (third_plus[at + 1] - third_minus[at + 1]) - 4.0 * (right - left)
        if at >= 3:
            store(at - 3, (centre[at - 1] - centre[at + 1]) + (interface[at - 1] - interface[at]))


def reconstructed(first, second, third, fourth, fifth):
    one, two, three, four = second - first, third - second, fourth - third, fifth - fourth
    bends = [two - one, three - two, four - three]
    slopes = [two + 0.5 * bends[0], two + 0.5 * bends[1], three - 0.5 * bends[2]]
    smooth = [((13.0 / 12.0) * (b * b) + epsilon) + v * v for b, v in zip(bends, slopes)]
    return bends[1], bends[2], correction(*smooth, bends[1] - bends[0], bends[2] - bends[1])


def rolled(plus, minus):
    p = {k: turned(plus, -k) for k in (-2, -1, 0, 1, 2)}
    m = {k: turned(minus, -k) for k in (-1, 0, 1, 2, 3)}
    plus_here, plus_next, right = reconstructed(p[-2], p[-1], p[0], p[1], p[2])
    minus_next, minus_here, left = reconstructed(m[3], m[2], m[1], m[0], m[-1])
    centre = 6.0 * ((p[0] + m[0]) + (p[1] + m[1])) - ((plus_here + minus_here) + (plus_next + minus_next))
    interface = centre + ((plus_next - plus_here) - (minus_next - minus_here)) - 4.0 * (right + left)
    return turned(interface, 1) - interface


def lane_index(shape):
    return lax.broadcasted_iota(jnp.int32, shape, len(shape) - 1)


def turned(value, by):
    size = value.shape[-1]
    if isinstance(by, int):
        by = by % size
        return value if by == 0 else pltpu.roll(value, by, value.ndim - 1)
    return pltpu.roll(value, lax.rem(by + 4 * size, size), value.ndim - 1)


def merged(pieces, slot):
    out = pieces[0]
    for number, piece in enumerate(pieces[1:], 1):
        out = jnp.where(slot == number, piece, out)
    return out


def rows_at(start, size):
    return pl.ds(start if isinstance(start, int) else pl.multiple_of(start, TILE), size)


def by_node(me, values):
    out = jnp.float32(values[0])
    for n, value in enumerate(values[1:], 1):
        out = jnp.where(me == n, jnp.float32(value), out)
    return out


def scaled_weight(row, column):
    return radau_weights[row][column] * (step_size / 12.0)


class Windows:
    def __init__(self, nx, nz, nodes):
        self.nodes = nodes
        self.size = nz
        self.width = nz // nodes
        self.pitch = self.width + 8
        self.slots = nz // self.pitch
        assert nx % self.slots == 0 and nx % nodes == 0 and nz % nodes == 0
        self.rows = nx // self.slots

    def cut(self, values, quarter):
        pieces = [
            turned(value, self.pitch * s + HALO - self.width * quarter) for s, value in enumerate(values)
        ]
        return merged(pieces, lane_index(values[0].shape) // self.pitch)

    def joined(self, values, s):
        start = self.pitch * s + HALO
        lane = lane_index(values[0].shape)
        region = jnp.where(lane < start, lane + (self.size - start), lane - start) // self.width
        return turned(merged(values, region), -start)


def write_edges(read, nx, ny, comps, lo_ref, hi_ref, side_ref):
    rows = side_ref.shape[1] // (2 * HALO)
    for c in range(comps):
        for i in range(HALO):
            lo_ref[0, pl.ds((c * HALO + i) * ny, ny), :] = read(c, i)
            hi_ref[0, pl.ds((c * HALO + i) * ny, ny), :] = read(c, nx - HALO + i)

    def side(i, carry):
        for c in range(comps):
            value = read(c, i)
            side_ref[0, pl.ds(c * nx + i, HALO, stride=rows), :] = value[ny - HALO :]
            side_ref[0, pl.ds(HALO * rows + c * nx + i, HALO, stride=rows), :] = value[:HALO]
        return carry

    lax.fori_loop(0, nx, side, 0)


def faster(best, read, first, count, comps):
    def step(i, best):
        speeds = signal_speeds([read(c, i) for c in range(comps)])
        return tuple(jnp.maximum(b, s) for b, s in zip(best, speeds))

    return lax.fori_loop(first, first + count, step, best)


def alpha_tile(best, group):
    nz = best[0].shape[-1]
    rows = [jnp.max(b, axis=0, keepdims=True) for b in best]
    tile = jnp.concatenate(rows + [jnp.zeros((TILE - 3, nz), jnp.float32)], axis=0)
    lane = lane_index(tile.shape)
    by = 1
    while by < group:
        other = jnp.where((lane & by) != 0, turned(tile, by), turned(tile, -by))
        tile = jnp.maximum(tile, other)
        by *= 2
    return tile


def open_kernel(u_hbm, lo_ref, hi_ref, side_ref, al_ref, u_ref, sems):
    comps, nx, ny, nz = u_ref.shape
    chunks = sems.shape[0]
    size = nx // chunks
    copies = []
    for n in range(chunks):
        at = pl.ds(n * size, size)
        copies.append(pltpu.make_async_copy(u_hbm.at[0, :, at], u_ref.at[:, at], sems.at[n]))
        copies[-1].start()

    def read(c, i):
        return u_ref[c, i]

    best = tuple(jnp.zeros((ny, nz), jnp.float32) for _ in range(3))
    for n in range(chunks):
        copies[n].wait()
        best = faster(best, read, n * size, size, comps)
    al_ref[...] = alpha_tile(best, nz)
    write_edges(read, nx, ny, comps, lo_ref, hi_ref, side_ref)


def start_kernel(init_ref, win_ref, pack_ref, *, nodes):
    comps, nx, ny, nz = init_ref.shape
    windows = Windows(nx, nz, nodes)
    me = lax.axis_index("node")
    lanes = lane_index((ny, nz)) // windows.width

    def step(c, carry):
        for r in range(windows.rows):
            values = [init_ref[c, s * windows.rows + r] for s in range(windows.slots)]
            win_ref[rows_at((c * windows.rows + r) * ny, ny), :] = windows.cut(values, me)
        for q in range(nx // nodes):
            pieces = [turned(init_ref[c, q * nodes + i], windows.width * (i - me)) for i in range(nodes)]
            pack_ref[rows_at((c * (nx // nodes) + q) * ny, ny), :] = merged(pieces, lanes)
        return carry

    lax.fori_loop(0, comps, step, 0)


def blend_kernel(start_ref, *refs):
    nodes = len(refs) - 6
    parts, (win_ref, nat_ref, lo_ref, hi_ref, side_ref, al_ref) = refs[:nodes], refs[nodes:]
    comps, nx, ny, nz = nat_ref.shape
    windows = Windows(nx, nz, nodes)
    me = lax.axis_index("node")
    weights = [
        [by_node(me, [scaled_weight(m, n ^ k) for n in range(nodes)]) for k in range(nodes)] for m in range(nodes)
    ]

    def step(c, carry):
        for r in range(windows.rows):
            at = rows_at((c * windows.rows + r) * ny, ny)
            start = start_ref[at, :]
            rates = [part[at, :] for part in parts]
            states = []
            for m in range(nodes):
                value = start
                for k in range(nodes):
                    value = value + weights[m][k] * rates[k]
                value = turned(value, windows.width * m)
                win_ref[m, at, :] = value
                states.append(value)
            for s in range(windows.slots):
                nat_ref[c, s * windows.rows + r] = windows.joined(states, s)
        return carry

    lax.fori_loop(0, comps, step, 0)

    def read(c, i):
        return nat_ref[c, i]

    best = tuple(jnp.zeros((ny, nz), jnp.float32) for _ in range(3))
    tile = alpha_tile(faster(best, read, 0, nx, comps), windows.width)

    def spread(i, carry):
        al_ref[i] = tile
        return carry

    lax.fori_loop(0, al_ref.shape[0], spread, 0)
    write_edges(read, nx, ny, comps, lo_ref, hi_ref, side_ref)


def across_lanes(u, alphas, side_ref, dims, zp, zm, fy, yp, ym, depth):
    comps, nx, ny, nz = dims
    rows = yp.shape[0] // (ny + 2 * HALO)
    every = range(comps)

    def own(i, carry):
        along_y, *rest = splits([u(c, i) for c in every], alphas, (1, 2) if depth else (1,))
        for c in every:
            for t in range(0, ny, TILE):
                at = pl.ds((HALO + t) * rows + c * nx + i, TILE, stride=rows)
                yp[at, :] = along_y[0][c][t : t + TILE]
                ym[at, :] = along_y[1][c][t : t + TILE]
        if depth:
            depth(i, rest[0])
        return carry

    lax.fori_loop(0, nx, own, 0)

    def ghost(i, carry):
        row = jnp.where(i < HALO, i, i + ny) * rows
        ((p, m),) = splits([side_ref[0, pl.ds(i * rows + c * nx, nx), :] for c in every], alphas, (1,))
        for c in every:
            yp[pl.ds(row + c * nx, nx), :] = p[c]
            ym[pl.ds(row + c * nx, nx), :] = m[c]
        return carry

    lax.fori_loop(0, 2 * HALO, ghost, 0)

    blocks = rows // TILE
    share = zp.shape[0] // blocks
    assert share * blocks == zp.shape[0]
    piece = max(p for p in range(TILE, 41, TILE) if share % p == 0)

    def along(b, carry):
        first = pl.multiple_of(b * TILE, TILE)

        def load(j):
            at = pl.ds(j * rows + first, TILE)
            return yp[at, :], ym[at, :]

        def store(i, value):
            fy[pl.ds(i * rows + first, TILE), :] = value

        stream(load, store, ny)
        for n in range(0, share, piece):
            at = rows_at(b * share + n, piece)
            zp[at, :] = rolled(zp[at, :], zm[at, :])
        return carry

    lax.fori_loop(0, blocks, along, 0)


def along_first(u, alphas, lo_ref, hi_ref, fy, rate, xp, xm, extra, after):
    comps, nx, ny, nz = rate.shape
    rows = fy.shape[0] // ny
    every = range(comps)

    def split(fields, at):
        ((p, m),) = splits(fields, alphas, (0,))
        for c in every:
            xp[at, c * ny : (c + 1) * ny, :] = p[c]
            xm[at, c * ny : (c + 1) * ny, :] = m[c]

    def own(i, carry):
        split([u(c, i) for c in every], i + HALO)
        return carry

    lax.fori_loop(0, nx, own, 0)
    for ref, start in ((lo_ref, 0), (hi_ref, nx + HALO)):

        def ghost(i, carry, ref=ref, start=start):
            split([ref[0, rows_at((c * HALO + i) * ny, ny), :] for c in every], start + i)
            return carry

        lax.fori_loop(0, HALO, ghost, 0)

    tiles = ny // TILE

    def along(b, carry):
        c, t = b // tiles, lax.rem(b, tiles) * TILE
        first = pl.multiple_of(b * TILE, TILE)

        def load(j):
            return xp[j, pl.ds(first, TILE), :], xm[j, pl.ds(first, TILE), :]

        def store(i, value):
            cross = fy[pl.ds(t * rows + c * nx + i, TILE, stride=rows), :]
            rate[c, i, rows_at(t, TILE), :] = value + (cross + extra(c, i, t))

        stream(load, store, nx)
        done = jnp.maximum(b - 1, 0)
        after(done // tiles, pl.multiple_of(lax.rem(done, tiles) * TILE, TILE))
        return carry

    lax.fori_loop(0, comps * tiles, along, 0)
    after(comps - 1, ny - TILE)


def tile_rows(tile):
    return [tile[k : k + 1, :] for k in range(3)]


def first_lanes_kernel(u_ref, side_ref, al_ref, other_ref, zp, fy, al_out, zm, yp, ym):
    comps, nx, ny, nz = u_ref.shape[1:]
    tile = jnp.maximum(al_ref[...], other_ref[...])
    al_out[...] = tile

    def depth(i, split):
        for c in range(comps):
            at = rows_at((c * nx + i) * ny, ny)
            zp[at, :] = split[0][c]
            zm[at, :] = split[1][c]

    across_lanes(lambda c, i: u_ref[0, c, i], tile_rows(tile), side_ref, u_ref.shape[1:], zp, zm, fy, yp, ym, depth)


def first_rows_kernel(u_ref, lo_ref, hi_ref, al_ref, zp, fy, *refs):
    parts, (rate, xp, xm) = refs[:-3], refs[-3:]
    nodes = len(parts)
    comps, nx, ny, nz = u_ref.shape[1:]
    windows = Windows(nx, nz, nodes)
    me = lax.axis_index("node")

    def extra(c, i, t):
        return zp[rows_at((c * nx + i) * ny + t, TILE), :]

    def after(c, t):
        for r in range(windows.rows):
            values = [rate[c, s * windows.rows + r, pl.ds(t, TILE), :] for s in range(windows.slots)]
            at = rows_at((c * windows.rows + r) * ny + t, TILE)
            for k in range(nodes):
                parts[k][at, :] = windows.cut(values, me ^ k)

    along_first(lambda c, i: u_ref[0, c, i], tile_rows(al_ref), lo_ref, hi_ref, fy, rate, xp, xm, extra, after)


def second_lanes_kernel(nat_ref, win_ref, side_ref, al_ref, zp, fy, al_out, zm, yp, ym):
    nodes = win_ref.shape[0]
    comps, nx, ny, nz = nat_ref.shape
    windows = Windows(nx, nz, nodes)
    part = comps * windows.rows * ny
    tiles = al_ref.shape[0]
    tile = lax.fori_loop(
        1, tiles, lambda i, best: jnp.maximum(best, al_ref[i]), al_ref[0], unroll=True if tiles <= 32 else 1
    )
    al_out[...] = tile
    alphas = tile_rows(tile)
    group = lane_index((1, nz)) // windows.width

    for m in range(nodes):
        alpha = jnp.max(jnp.where(group == m, alphas[2], 0.0))

        def depth(r, carry, m=m, alpha=alpha):
            places = [(c * windows.rows + r) * ny for c in range(comps)]
            fields = [win_ref[m, rows_at(place, ny), :] for place in places]
            ((plus, minus),) = splits(fields, [None, None, alpha], (2,))
            for c in range(comps):
                at = rows_at(m * part + places[c], ny)
                zp[at, :] = plus[c]
                zm[at, :] = minus[c]
            return carry

        lax.fori_loop(0, windows.rows, depth, 0)

    across_lanes(lambda c, i: nat_ref[c, i], alphas, side_ref, nat_ref.shape, zp, zm, fy, yp, ym, None)


def second_rows_kernel(nat_ref, lo_ref, hi_ref, al_ref, zp, fy, pack_ref, *refs):
    outs, (rate, xp, xm) = refs[:-3], refs[-3:]
    nodes = len(outs)
    comps, nx, ny, nz = nat_ref.shape
    windows = Windows(nx, nz, nodes)
    part = comps * windows.rows * ny
    me = lax.axis_index("node")
    weights = [
        [by_node(me, [scaled_weight(n ^ k, j) for n in range(nodes)]) for j in range(nodes)] for k in range(nodes)
    ]
    lanes = lane_index((TILE, nz)) // windows.width

    def extra(c, i, t):
        s, r = i // windows.rows, i % windows.rows
        place = (c * windows.rows + r) * ny + t
        return windows.joined([zp[rows_at(m * part + place, TILE), :] for m in range(nodes)], s)

    def after(c, t):
        for q in range(nx // nodes):
            at = rows_at((c * (nx // nodes) + q) * ny + t, TILE)
            start = pack_ref[at, :]
            rows = [rate[c, q * nodes + i, pl.ds(t, TILE), :] for i in range(nodes)]
            rates = [
                merged([turned(rows[i], windows.width * (i - j)) for i in range(nodes)], lanes) for j in range(nodes)
            ]
            for k in range(nodes):
                value = start
                for j in range(nodes):
                    value = value + weights[k][j] * rates[j]
                outs[k][at, :] = turned(value, windows.width * me)

    along_first(lambda c, i: nat_ref[c, i], tile_rows(al_ref), lo_ref, hi_ref, fy, rate, xp, xm, extra, after)


def close_kernel(*refs):
    parts, (out_hbm, out_ref, sems) = refs[:-3], refs[-3:]
    nodes = len(parts)
    comps, nx, ny, nz = out_ref.shape
    width = nz // nodes
    me = lax.axis_index("node")
    lanes = lane_index((ny, nz)) // width
    copies = []
    for c in range(comps):
        for q in range(nx // nodes):
            at = pl.ds((c * (nx // nodes) + q) * ny, ny)
            values = [part[at, :] for part in parts]
            for i in range(nodes):
                out = values[0]
                for k in range(1, nodes):
                    out = jnp.where(lanes == lax.rem((me ^ k) + i, nodes), values[k], out)
                out_ref[c, q * nodes + i] = turned(out, -width * i)
        copies.append(pltpu.make_async_copy(out_ref.at[c], out_hbm.at[0, c], sems.at[c]))
        copies[-1].start()
    for copy in copies:
        copy.wait()


def call(kernel, name, outs, operands, scratch=(), flops=1_000_000, anywhere=False, outside=False):
    vmem, hbm = pl.BlockSpec(memory_space=pltpu.VMEM), pl.BlockSpec(memory_space=pl.ANY)
    moved = sum(4 * x.size for x in operands)
    scratch = [pltpu.VMEM(x, jnp.float32) if isinstance(x, tuple) else x for x in scratch]
    return pl.pallas_call(
        kernel,
        out_shape=[jax.ShapeDtypeStruct(shape, jnp.float32) for shape in outs],
        in_specs=[hbm if anywhere else vmem] * len(operands),
        out_specs=[hbm if outside else vmem] * len(outs),
        scratch_shapes=scratch,
        compiler_params=pltpu.CompilerParams(vmem_limit_bytes=32 * 1024 * 1024),
        cost_estimate=pl.CostEstimate(flops=flops, bytes_accessed=2 * moved, transcendentals=0),
        name=name,
    )(*operands)


def shifted(value, axis, by):
    count = lax.axis_size(axis)
    return lax.ppermute(value, axis, [(i, (i + by) % count) for i in range(count)])


def swapped(value, by):
    return lax.ppermute(value, "node", [(i, i ^ by) for i in range(lax.axis_size("node"))])


def neighbours(lo, hi, side):
    lower, upper = shifted(hi, "gx", 1), shifted(lo, "gx", -1)
    if lax.axis_size("gy") == 2:
        return lower, upper, shifted(side, "gy", 1)
    half = side.shape[1] // 2
    side = jnp.concatenate([shifted(side[:, :half], "gy", 1), shifted(side[:, half:], "gy", -1)], axis=1)
    return lower, upper, side


def largest(tile):
    if lax.axis_size("gx") > 4 or lax.axis_size("gy") > 2:
        tile = lax.pmax(tile, ("gx", "gy"))
        return tile, tile
    others = [shifted(tile, "gx", by) for by in range(1, lax.axis_size("gx"))]
    tile = functools.reduce(jnp.maximum, others, tile)
    return tile, shifted(tile, "gy", 1)


def exchanged(parts):
    moved = {k: swapped(parts[k], k) for k in sorted(range(1, len(parts)), reverse=True)}
    return [parts[0]] + [moved[k] for k in range(1, len(parts))]


def local(initial, guesses):
    comps, nx, ny, nz = initial.shape
    nodes = lax.axis_size("node")
    devices = nodes * lax.axis_size("gx") * lax.axis_size("gy")
    rows = -(-comps * nx // TILE) * TILE
    windows = Windows(nx, nz, nodes)
    edge = (1, comps * HALO * ny, nz)
    edges = [edge, edge, (1, 2 * HALO * rows, nz)]
    tile_shape = (TILE, nz)
    part = (comps * windows.rows * ny, nz)
    pack = (comps * nx // nodes * ny, nz)
    second = (ny * rows, nz)
    padded = [((ny + 2 * HALO) * rows, nz)] * 2
    slabs = [initial.shape] + [(nx + 2 * HALO, comps * ny, nz)] * 2
    chunks = 4 if nx % 4 == 0 else 1

    lo, hi, side, tile = call(
        open_kernel,
        "open_kernel",
        edges + [tile_shape],
        [guesses],
        [initial.shape, pltpu.SemaphoreType.DMA((chunks,))],
        anywhere=True,
    )
    lower, upper, side = neighbours(lo, hi, side)
    tile, other = largest(tile)
    start, start_pack = call(
        functools.partial(start_kernel, nodes=nodes), "start_kernel", [part, pack], [initial]
    )
    whole = (comps * nx * ny, nz)
    depth, across, tile = call(
        first_lanes_kernel,
        "first_lanes_kernel",
        [whole, second, tile_shape],
        [guesses, side, tile, other],
        [whole] + padded,
        20_000_000,
    )
    parts = call(
        first_rows_kernel, "first_rows_kernel", [part] * nodes, [guesses, lower, upper, tile, depth, across], slabs, 10_000_000
    )
    win, nat, lo, hi, side, tile = call(
        blend_kernel,
        "blend_kernel",
        [(nodes,) + part, initial.shape] + edges + [(devices,) + tile_shape],
        [start] + exchanged(parts),
    )
    lower, upper, side = neighbours(lo, hi, side)
    tiles = lax.all_to_all(tile, ("node", "gx", "gy"), 0, 0)
    whole = (nodes * part[0], nz)
    depth, across, tile = call(
        second_lanes_kernel,
        "second_lanes_kernel",
        [whole, second, tile_shape],
        [nat, win, side, tiles],
        [whole] + padded,
        20_000_000,
    )
    outs = call(
        second_rows_kernel,
        "second_rows_kernel",
        [pack] * nodes,
        [nat, lower, upper, tile, depth, across, start_pack],
        slabs,
        10_000_000,
    )
    (states,) = call(
        close_kernel,
        "close_kernel",
        [(1,) + initial.shape],
        exchanged(outs),
        [initial.shape, pltpu.SemaphoreType.DMA((comps,))],
        outside=True,
    )
    return states


def solution(mesh):
    return jax.shard_map(
        local,
        mesh=mesh,
        in_specs=(P(None, "gx", "gy", None), P("node", None, "gx", "gy", None)),
        out_specs=P("node", None, "gx", "gy", None),
        check_vma=False,
    )
```

time: 75.9 us -> 67.3 us (0.89)
  waiting for transfers between devices: 24.1 us -> 18.3 us
  local copies, waits for them, and re-layouts: 2.35 us -> 1.04 us
  Pallas kernels: 25.3 us -> 24.1 us
    ppermute x10, waiting for transfers between devices: 11.8 us -> 1.94 us  [shifted(): lax.ppermute(value, axis, [(i, (i + by) % count) for i in range(count)])]
    all_to_all x1, waiting for transfers between devices: 0.01 us -> 4.18 us  [local(): tiles = lax.all_to_all(tile, ('node', 'gx', 'gy'), 0, 0)]
    pallas_call x1 -> x0, Pallas kernels: 3.65 us -> none  [local(): pl.pallas_call(close_kernel, grid=(comps,), out_shape=jax.ShapeDtypeStruc...]
    pallas_call x4 -> x8, Pallas kernels: 21.7 us -> 24.1 us  [call(): pl.pallas_call(kernel, out_shape=[jax.ShapeDtypeStruct(shape, jnp.float32...]
    unnamed x12 -> x4, local copies, waits for them, and re-layouts: 2.35 us -> 1.04 us
  transfers between devices with their start and end apart: 17 -> 17, of which waited for: 11 -> 8; matrix products, arithmetic and copies ran while one was open for 0% -> 0% of each run, Pallas kernels for 0% -> 18%
where the time goes in v4:
time: 67.3 us; the launch traced here: 67.1 us
  Pallas kernels  24.1 us (36%)
  starting transfers between devices  23.6 us (35%)
  waiting for transfers between devices  18.3 us (27%)
  local copies, waits for them, and re-layouts  1.04 us (2%)
    pallas_call x8, Pallas kernels, call(): pl.pallas_call(kernel, out_shape=[jax.ShapeDtypeStruct(shape, jnp.float32...  24.1 us
    ppermute x10, starting transfers between devices, shifted(): lax.ppermute(value, axis, [(i, (i + by) % count) for i in range(count)])  13.9 us
    ppermute x6, waiting for transfers between devices, swapped(): lax.ppermute(value, 'node', [(i, i ^ by) for i in range(lax.axis_size('no...  12.2 us
    ppermute x6, starting transfers between devices, swapped(): lax.ppermute(value, 'node', [(i, i ^ by) for i in range(lax.axis_size('no...  7.05 us
    all_to_all x1, waiting for transfers between devices, local(): tiles = lax.all_to_all(tile, ('node', 'gx', 'gy'), 0, 0)  4.18 us
    all_to_all x1, starting transfers between devices, local(): tiles = lax.all_to_all(tile, ('node', 'gx', 'gy'), 0, 0)  2.58 us
    ppermute x10, waiting for transfers between devices, shifted(): lax.ppermute(value, axis, [(i, (i + by) % count) for i in range(count)])  1.94 us
  transfers between devices with their start and end apart: 17, of which 8 were waited for; matrix products, arithmetic and copies ran while one was open for 0% of the time, Pallas kernels for 18%

profile of v4, /device:TPU:0, one launch (start us, length us, event | category | flops | bytes accessed | tf_op | source)
XLA Modules:
  0.0 67.1 jit_solution(14596648896737309473)
XLA Ops:
  0.0 0.0 copy-start
  0.0 1.0 %copy-done = f32[1,5,12,16,128]{4,3,2,1,0:T(8,128)S(1)} copy-done((f32[1,5,12,16,128]{4,3,2,1,0:T(8,128)S(1)}, f32[1,5,12,16,128]{4,3,2,1,0:T(8,128)}, u32[]{:S(2)}) %copy-start) | copy-done | bytes 491544
  1.0 1.1 %open_kernel.1 = (f32[1,240,128]{2,1,0:T(8,128)S(1)}, f32[1,240,128]{2,1,0:T(8,128)S(1)}, f32[1,384,128]{2,1,0:T(8,128)S(1)}, f32[8,128]{1,0:T(8,128)S(1)}) custom-call(f32[1,5,12,16,128]{4,3,2,1,0:T(8,128)S(1)} %copy-done), custom_call_target="tpu_custom_call" | custom-call | flops 1000000 | bytes 983040 | tf_op jit(solution)/shard_map/open_kernel/pallas_call | solution.py:546
  2.2 5.1 %collective-permute-start.5 = (f32[8,128]{1,0:T(8,128)S(1)}, f32[8,128]{1,0:T(8,128)S(1)}, u32[]{:S(2)}, u32[]{:S(2)}) collective-permute-start(f32[8,128]{1,0:T(8,128)S(1)} %get-tuple-element.35), channel_id=1, source_target_pairs={{0,6},{2,0},{4,2},{6,4},{1,7},{3,1},{5,3},{7,5},{8,14},{10,8},{12,... | collective-permute-start | bytes 12296 | tf_op jit(solution)/shard_map/ppermute | solution.py:560
  7.3 0.0 collective-permute-start.4
  7.3 1.0 %collective-permute-start.3 = (f32[8,128]{1,0:T(8,128)S(1)}, f32[8,128]{1,0:T(8,128)S(1)}, u32[]{:S(2)}, u32[]{:S(2)}) collective-permute-start(f32[8,128]{1,0:T(8,128)S(1)} %get-tuple-element.35), channel_id=1, source_target_pairs={{0,2},{2,4},{4,6},{6,0},{1,3},{3,5},{5,7},{7,1},{8,10},{10,12},{12... | collective-permute-start | bytes 12296 | tf_op jit(solution)/shard_map/ppermute | solution.py:560
  8.3 2.5 %collective-permute-start = (f32[1,240,128]{2,1,0:T(8,128)S(1)}, f32[1,240,128]{2,1,0:T(8,128)S(1)}, u32[]{:S(2)}, u32[]{:S(2)}) collective-permute-start(f32[1,240,128]{2,1,0:T(8,128)S(1)} %get-tuple-element.32), channel_id=1, source_target_pairs={{0,2},{2,4},{4,6},{6,0},{1,3},{3,5},{5,7},{7,1},{8,10},{10,12},{12... | collective-permute-start | bytes 368648 | tf_op jit(solution)/shard_map/ppermute | solution.py:560
  10.8 1.3 %collective-permute-start.1 = (f32[1,240,128]{2,1,0:T(8,128)S(1)}, f32[1,240,128]{2,1,0:T(8,128)S(1)}, u32[]{:S(2)}, u32[]{:S(2)}) collective-permute-start(f32[1,240,128]{2,1,0:T(8,128)S(1)} %get-tuple-element.33), channel_id=1, source_target_pairs={{0,6},{2,0},{4,2},{6,4},{1,7},{3,1},{5,3},{7,5},{8,14},{10,8},{12,... | collective-permute-start | bytes 368648 | tf_op jit(solution)/shard_map/ppermute | solution.py:560
  12.1 0.0 collective-permute-done.5
  12.1 0.0 collective-permute-start.2
  12.1 0.5 collective-permute-done.4
  12.6 0.2 collective-permute-done.3
  12.9 0.0 collective-permute-start.6
  12.9 1.2 %collective-permute-done.6.other_ref = f32[8,128]{1,0:T(8,128)S(1)} collective-permute-done((f32[8,128]{1,0:T(8,128)S(1)}, f32[8,128]{1,0:T(8,128)S(1)}, u32[]{:S(2)}, u32[]{:S(2)}) %collective-permute-start.6) | collective-permute-done | bytes 4128 | tf_op jit(solution)/shard_map/ppermute | solution.py:560
  14.0 0.0 collective-permute-done.2.side_ref
  14.0 4.9 %first_lanes_kernel.1 = (f32[960,128]{1,0:T(8,128)S(1)}, f32[1024,128]{1,0:T(8,128)S(1)}, f32[8,128]{1,0:T(8,128)S(1)}) custom-call(f32[1,5,12,16,128]{4,3,2,1,0:T(8,128)S(1)} %copy-done, f32[1,384,128]{2,1,0:T(8,128)S(1)} %collective-permute-done.2.side_ref, f32[8,128]{1,0:T(8,128)S(1)} %maximum_maximum_fusion.al_ref, ...), custom_call_target="tpu_custom_call" | custom-call | flops 20000000 | bytes 1392640 | tf_op jit(solution)/shard_map/first_lanes_kernel/pallas_call | solution.py:546
  18.9 0.0 collective-permute-done.lo_ref
  18.9 0.0 collective-permute-done.1.hi_ref
  18.9 0.0 copy-start.1
  18.9 3.2 %first_rows_kernel.1 = (f32[320,128]{1,0:T(8,128)S(1)}, f32[320,128]{1,0:T(8,128)S(1)}, f32[320,128]{1,0:T(8,128)S(1)}, f32[320,128]{1,0:T(8,128)S(1)}) custom-call(f32[1,5,12,16,128]{4,3,2,1,0:T(8,128)S(1)} %copy-done, f32[1,240,128]{2,1,0:T(8,128)S(1)} %collective-permute-done.lo_ref, f32[1,240,128]{2,1,0:T(8,128)S(1)} %collective-permute-done.1.hi_ref, ...), custom_call_target="tpu_custom_call" | custom-call | flops 10000000 | bytes 3514368 | tf_op jit(solution)/shard_map/first_rows_kernel/pallas_call | solution.py:546
  22.2 1.6 %collective-permute-start.7 = (f32[320,128]{1,0:T(8,128)S(1)}, f32[320,128]{1,0:T(8,128)S(1)}, u32[]{:S(2)}, u32[]{:S(2)}) collective-permute-start(f32[320,128]{1,0:T(8,128)S(1)} %get-tuple-element.40), channel_id=1, source_target_pairs={{0,8},{8,0},{16,24},{24,16},{1,9},{9,1},{17,25},{25,17},{2,10},{10... | collective-permute-start | bytes 491528 | tf_op jit(solution)/shard_map/ppermute | solution.py:564
  23.7 1.5 %collective-permute-start.8 = (f32[320,128]{1,0:T(8,128)S(1)}, f32[320,128]{1,0:T(8,128)S(1)}, u32[]{:S(2)}, u32[]{:S(2)}) collective-permute-start(f32[320,128]{1,0:T(8,128)S(1)} %get-tuple-element.41), channel_id=1, source_target_pairs={{0,16},{8,24},{16,0},{24,8},{1,17},{9,25},{17,1},{25,9},{2,18},{10... | collective-permute-start | bytes 491528 | tf_op jit(solution)/shard_map/ppermute | solution.py:564
  25.3 0.5 collective-permute-start.9
  25.7 0.0 copy-done.1
  25.7 0.6 start_kernel.1
  26.4 2.9 %collective-permute-done.7.refs_1_ = f32[320,128]{1,0:T(8,128)S(1)} collective-permute-done((f32[320,128]{1,0:T(8,128)S(1)}, f32[320,128]{1,0:T(8,128)S(1)}, u32[]{:S(2)}, u32[]{:S(2)}) %collective-permute-start.7) | collective-permute-done | bytes 163872 | tf_op jit(solution)/shard_map/ppermute | solution.py:564
  29.3 3.9 %collective-permute-done.8.refs_2_ = f32[320,128]{1,0:T(8,128)S(1)} collective-permute-done((f32[320,128]{1,0:T(8,128)S(1)}, f32[320,128]{1,0:T(8,128)S(1)}, u32[]{:S(2)}, u32[]{:S(2)}) %collective-permute-start.8) | collective-permute-done | bytes 163872 | tf_op jit(solution)/shard_map/ppermute | solution.py:564
  33.2 0.0 collective-permute-done.9.refs_3_
  33.2 2.6 %blend_kernel.1 = (f32[4,320,128]{2,1,0:T(8,128)S(1)}, f32[5,12,16,128]{3,2,1,0:T(8,128)S(1)}, f32[1,240,128]{2,1,0:T(8,128)S(1)}, f32[1,240,128]{2,1,0:T(8,128)...) custom-call(f32[320,128]{1,0:T(8,128)S(1)} %get-tuple-element.31.start_ref, ...), custom_call_target="tpu_custom_call" | custom-call | flops 1000000 | bytes 1638400 | tf_op jit(solution)/shard_map/blend_kernel/pallas_call | solution.py:546
  35.8 2.6 %all-to-all-start = ((f32[32,8,128]{2,1,0:T(8,128)}), f32[32,8,128]{2,1,0:T(8,128)S(1)}, u32[]{:S(2)}, u32[]{:S(2)}) async-start(f32[32,8,128]{2,1,0:T(8,128)} %get-tuple-element.48), calls=%async_computation | async-start | bytes 262144 | tf_op jit(solution)/shard_map/all_to_all | solution.py:638
  38.4 0.2 collective-permute-start.12
  38.6 1.7 %collective-permute-start.10 = (f32[1,240,128]{2,1,0:T(8,128)S(1)}, f32[1,240,128]{2,1,0:T(8,128)S(1)}, u32[]{:S(2)}, u32[]{:S(2)}) collective-permute-start(f32[1,240,128]{2,1,0:T(8,128)S(1)} %get-tuple-element.44), channel_id=1, source_target_pairs={{0,2},{2,4},{4,6},{6,0},{1,3},{3,5},{5,7},{7,1},{8,10},{10,12},{12... | collective-permute-start | bytes 368648 | tf_op jit(solution)/shard_map/ppermute | solution.py:560
  40.3 2.1 %collective-permute-start.11 = (f32[1,240,128]{2,1,0:T(8,128)S(1)}, f32[1,240,128]{2,1,0:T(8,128)S(1)}, u32[]{:S(2)}, u32[]{:S(2)}) collective-permute-start(f32[1,240,128]{2,1,0:T(8,128)S(1)} %get-tuple-element.45), channel_id=1, source_target_pairs={{0,6},{2,0},{4,2},{6,4},{1,7},{3,1},{5,3},{7,5},{8,14},{10,8},{12,... | collective-permute-start | bytes 368648 | tf_op jit(solution)/shard_map/ppermute | solution.py:560
  42.4 0.0 collective-permute-done.12.side_ref
  42.4 4.2 %all-to-all-done.al_ref = f32[32,8,128]{2,1,0:T(8,128)S(1)} async-done(((f32[32,8,128]{2,1,0:T(8,128)}), f32[32,8,128]{2,1,0:T(8,128)S(1)}, u32[]{:S(2)}, u32[]{:S(2)}) %all-to-all-start) | async-done | bytes 131104 | tf_op jit(solution)/shard_map/all_to_all | solution.py:638
  46.6 6.6 %second_lanes_kernel.1 = (f32[1280,128]{1,0:T(8,128)S(1)}, f32[1024,128]{1,0:T(8,128)S(1)}, f32[8,128]{1,0:T(8,128)S(1)}) custom-call(f32[5,12,16,128]{3,2,1,0:T(8,128)S(1)} %get-tuple-element.43.nat_ref, f32[4,320,128]{2,1,0:T(8,128)S(1)} %get-tuple-element.46.win_ref, f32[1,384,128]{2,1,0:T(8,128)S(1)} %collective-permute-done.12.side_ref, ...), custom_call_target="tpu_custom_call" | custom-call | flops 20000000 | bytes 2949120 | tf_op jit(solution)/shard_map/second_lanes_kernel/pallas_call | solution.py:546
  53.2 0.0 collective-permute-done.10.lo_ref
  53.2 0.0 collective-permute-done.11.hi_ref
  53.2 4.1 %second_rows_kernel.1 = (f32[240,128]{1,0:T(8,128)S(1)}, f32[240,128]{1,0:T(8,128)S(1)}, f32[240,128]{1,0:T(8,128)S(1)}, f32[240,128]{1,0:T(8,128)S(1)}) custom-call(f32[5,12,16,128]{3,2,1,0:T(8,128)S(1)} %get-tuple-element.43.nat_ref, f32[1,240,128]{2,1,0:T(8,128)S(1)} %collective-permute-done.10.lo_ref, f32[1,240,128]{2,1,0:T(8,128)S(1)} %collective-permute-done.11.hi_ref, ...), custom_call_target="tpu_custom_call" | custom-call | flops 10000000 | bytes 4087808 | tf_op jit(solution)/shard_map/second_rows_kernel/pallas_call | solution.py:546
  57.4 1.1 %collective-permute-start.13 = (f32[240,128]{1,0:T(8,128)S(1)}, f32[240,128]{1,0:T(8,128)S(1)}, u32[]{:S(2)}, u32[]{:S(2)}) collective-permute-start(f32[240,128]{1,0:T(8,128)S(1)} %get-tuple-element.54), channel_id=1, source_target_pairs={{0,8},{8,0},{16,24},{24,16},{1,9},{9,1},{17,25},{25,17},{2,10},{10... | collective-permute-start | bytes 368648 | tf_op jit(solution)/shard_map/ppermute | solution.py:564
  58.5 0.8 %collective-permute-start.14 = (f32[240,128]{1,0:T(8,128)S(1)}, f32[240,128]{1,0:T(8,128)S(1)}, u32[]{:S(2)}, u32[]{:S(2)}) collective-permute-start(f32[240,128]{1,0:T(8,128)S(1)} %get-tuple-element.55), channel_id=1, source_target_pairs={{0,16},{8,24},{16,0},{24,8},{1,17},{9,25},{17,1},{25,9},{2,18},{10... | collective-permute-start | bytes 368648 | tf_op jit(solution)/shard_map/ppermute | solution.py:564
  59.3 1.6 %collective-permute-start.15 = (f32[240,128]{1,0:T(8,128)S(1)}, f32[240,128]{1,0:T(8,128)S(1)}, u32[]{:S(2)}, u32[]{:S(2)}) collective-permute-start(f32[240,128]{1,0:T(8,128)S(1)} %get-tuple-element.56), channel_id=1, source_target_pairs={{0,24},{8,16},{16,8},{24,0},{1,25},{9,17},{17,9},{25,1},{2,26},{10... | collective-permute-start | bytes 368648 | tf_op jit(solution)/shard_map/ppermute | solution.py:564
  60.9 2.7 %collective-permute-done.13.refs_1_ = f32[240,128]{1,0:T(8,128)S(1)} collective-permute-done((f32[240,128]{1,0:T(8,128)S(1)}, f32[240,128]{1,0:T(8,128)S(1)}, u32[]{:S(2)}, u32[]{:S(2)}) %collective-permute-start.13) | collective-permute-done | bytes 122912 | tf_op jit(solution)/shard_map/ppermute | solution.py:564
  63.6 2.6 %collective-permute-done.14.refs_2_ = f32[240,128]{1,0:T(8,128)S(1)} collective-permute-done((f32[240,128]{1,0:T(8,128)S(1)}, f32[240,128]{1,0:T(8,128)S(1)}, u32[]{:S(2)}, u32[]{:S(2)}) %collective-permute-start.14) | collective-permute-done | bytes 122912 | tf_op jit(solution)/shard_map/ppermute | solution.py:564
  66.1 0.0 collective-permute-done.15.refs_3_
  66.1 0.9 %close_kernel.1 = f32[1,5,12,16,128]{4,3,2,1,0:T(8,128)} custom-call(f32[240,128]{1,0:T(8,128)S(1)} %get-tuple-element.53.refs_0_, f32[240,128]{1,0:T(8,128)S(1)} %collective-permute-done.13.refs_1_, f32[240,128]{1,0:T(8,128)S(1)} %collective-permute-done.14.refs_2_, f32[240,128]{1,0:T(8,128)S(1)} %collective-permute-done.15.refs_3_), custom_call_target="tpu_custom_call" | custom-call | flops 1000000 | bytes 983040 | tf_op jit(solution)/shard_map/close_kernel/pallas_call | solution.py:546
  (1 shorter events, 0.0 us)
Async XLA Ops:
  0.0 1.0 %copy-start = (f32[1,5,12,16,128]{4,3,2,1,0:T(8,128)S(1)}, f32[1,5,12,16,128]{4,3,2,1,0:T(8,128)}, u32[]{:S(2)}) copy-start(f32[1,5,12,16,128]{4,3,2,1,0:T(8,128)} %u_ref.3) | copy-start | bytes 1474564
  2.2 9.9 %collective-permute-start.5 = (f32[8,128]{1,0:T(8,128)S(1)}, f32[8,128]{1,0:T(8,128)S(1)}, u32[]{:S(2)}, u32[]{:S(2)}) collective-permute-start(f32[8,128]{1,0:T(8,128)S(1)} %get-tuple-element.35), channel_id=1, source_target_pairs={{0,6},{2,0},{4,2},{6,4},{1,7},{3,1},{5,3},{7,5},{8,14},{10,8},{12,... | collective-permute-start | bytes 12296 | tf_op jit(solution)/shard_map/ppermute | solution.py:560
  7.3 5.4 %collective-permute-start.4 = (f32[8,128]{1,0:T(8,128)S(1)}, f32[8,128]{1,0:T(8,128)S(1)}, u32[]{:S(2)}, u32[]{:S(2)}) collective-permute-start(f32[8,128]{1,0:T(8,128)S(1)} %get-tuple-element.35), channel_id=1, source_target_pairs={{0,4},{2,6},{4,0},{6,2},{1,5},{3,7},{5,1},{7,3},{8,12},{10,14},{12... | collective-permute-start | bytes 12296 | tf_op jit(solution)/shard_map/ppermute | solution.py:560
  7.3 5.6 %collective-permute-start.3 = (f32[8,128]{1,0:T(8,128)S(1)}, f32[8,128]{1,0:T(8,128)S(1)}, u32[]{:S(2)}, u32[]{:S(2)}) collective-permute-start(f32[8,128]{1,0:T(8,128)S(1)} %get-tuple-element.35), channel_id=1, source_target_pairs={{0,2},{2,4},{4,6},{6,0},{1,3},{3,5},{5,7},{7,1},{8,10},{10,12},{12... | collective-permute-start | bytes 12296 | tf_op jit(solution)/shard_map/ppermute | solution.py:560
  8.3 10.6 %collective-permute-start = (f32[1,240,128]{2,1,0:T(8,128)S(1)}, f32[1,240,128]{2,1,0:T(8,128)S(1)}, u32[]{:S(2)}, u32[]{:S(2)}) collective-permute-start(f32[1,240,128]{2,1,0:T(8,128)S(1)} %get-tuple-element.32), channel_id=1, source_target_pairs={{0,2},{2,4},{4,6},{6,0},{1,3},{3,5},{5,7},{7,1},{8,10},{10,12},{12... | collective-permute-start | bytes 368648 | tf_op jit(solution)/shard_map/ppermute | solution.py:560
  10.8 8.2 %collective-permute-start.1 = (f32[1,240,128]{2,1,0:T(8,128)S(1)}, f32[1,240,128]{2,1,0:T(8,128)S(1)}, u32[]{:S(2)}, u32[]{:S(2)}) collective-permute-start(f32[1,240,128]{2,1,0:T(8,128)S(1)} %get-tuple-element.33), channel_id=1, source_target_pairs={{0,6},{2,0},{4,2},{6,4},{1,7},{3,1},{5,3},{7,5},{8,14},{10,8},{12,... | collective-permute-start | bytes 368648 | tf_op jit(solution)/shard_map/ppermute | solution.py:560
  12.1 1.9 %collective-permute-start.2 = (f32[1,384,128]{2,1,0:T(8,128)S(1)}, f32[1,384,128]{2,1,0:T(8,128)S(1)}, u32[]{:S(2)}, u32[]{:S(2)}) collective-permute-start(f32[1,384,128]{2,1,0:T(8,128)S(1)} %get-tuple-element.34), channel_id=1, source_target_pairs={{0,1},{1,0},{2,3},{3,2},{4,5},{5,4},{6,7},{7,6},{8,9},{9,8},{10,11... | collective-permute-start | bytes 589832 | tf_op jit(solution)/shard_map/ppermute | solution.py:560
  12.9 1.2 %collective-permute-start.6 = (f32[8,128]{1,0:T(8,128)S(1)}, f32[8,128]{1,0:T(8,128)S(1)}, u32[]{:S(2)}, u32[]{:S(2)}) collective-permute-start(f32[8,128]{1,0:T(8,128)S(1)} %maximum_maximum_fusion.al_ref), channel_id=1, source_target_pairs={{0,1},{1,0},{2,3},{3,2},{4,5},{5,4},{6,7},{7,6},{8,9},{9,8},{10,11... | collective-permute-start | bytes 12296 | tf_op jit(solution)/shard_map/ppermute | solution.py:560
  18.9 6.8 %copy-start.1 = (f32[5,12,16,128]{3,2,1,0:T(8,128)S(1)}, f32[5,12,16,128]{3,2,1,0:T(8,128)}, u32[]{:S(2)}) copy-start(f32[5,12,16,128]{3,2,1,0:T(8,128)} %init_ref.1) | copy-start | bytes 1474564
  22.2 7.1 %collective-permute-start.7 = (f32[320,128]{1,0:T(8,128)S(1)}, f32[320,128]{1,0:T(8,128)S(1)}, u32[]{:S(2)}, u32[]{:S(2)}) collective-permute-start(f32[320,128]{1,0:T(8,128)S(1)} %get-tuple-element.40), channel_id=1, source_target_pairs={{0,8},{8,0},{16,24},{24,16},{1,9},{9,1},{17,25},{25,17},{2,10},{10... | collective-permute-start | bytes 491528 | tf_op jit(solution)/shard_map/ppermute | solution.py:564
  23.7 9.5 %collective-permute-start.8 = (f32[320,128]{1,0:T(8,128)S(1)}, f32[320,128]{1,0:T(8,128)S(1)}, u32[]{:S(2)}, u32[]{:S(2)}) collective-permute-start(f32[320,128]{1,0:T(8,128)S(1)} %get-tuple-element.41), channel_id=1, source_target_pairs={{0,16},{8,24},{16,0},{24,8},{1,17},{9,25},{17,1},{25,9},{2,18},{10... | collective-permute-start | bytes 491528 | tf_op jit(solution)/shard_map/ppermute | solution.py:564
  25.3 8.0 %collective-permute-start.9 = (f32[320,128]{1,0:T(8,128)S(1)}, f32[320,128]{1,0:T(8,128)S(1)}, u32[]{:S(2)}, u32[]{:S(2)}) collective-permute-start(f32[320,128]{1,0:T(8,128)S(1)} %get-tuple-element.42), channel_id=1, source_target_pairs={{0,24},{8,16},{16,8},{24,0},{1,25},{9,17},{17,9},{25,1},{2,26},{10... | collective-permute-start | bytes 491528 | tf_op jit(solution)/shard_map/ppermute | solution.py:564
  35.8 10.8 %all-to-all-start = ((f32[32,8,128]{2,1,0:T(8,128)}), f32[32,8,128]{2,1,0:T(8,128)S(1)}, u32[]{:S(2)}, u32[]{:S(2)}) async-start(f32[32,8,128]{2,1,0:T(8,128)} %get-tuple-element.48), calls=%async_computation | async-start | bytes 262144 | tf_op jit(solution)/shard_map/all_to_all | solution.py:638
  38.4 4.0 %collective-permute-start.12 = (f32[1,384,128]{2,1,0:T(8,128)S(1)}, f32[1,384,128]{2,1,0:T(8,128)S(1)}, u32[]{:S(2)}, u32[]{:S(2)}) collective-permute-start(f32[1,384,128]{2,1,0:T(8,128)S(1)} %get-tuple-element.47), channel_id=1, source_target_pairs={{0,1},{1,0},{2,3},{3,2},{4,5},{5,4},{6,7},{7,6},{8,9},{9,8},{10,11... | collective-permute-start | bytes 589832 | tf_op jit(solution)/shard_map/ppermute | solution.py:560
  38.6 14.6 %collective-permute-start.10 = (f32[1,240,128]{2,1,0:T(8,128)S(1)}, f32[1,240,128]{2,1,0:T(8,128)S(1)}, u32[]{:S(2)}, u32[]{:S(2)}) collective-permute-start(f32[1,240,128]{2,1,0:T(8,128)S(1)} %get-tuple-element.44), channel_id=1, source_target_pairs={{0,2},{2,4},{4,6},{6,0},{1,3},{3,5},{5,7},{7,1},{8,10},{10,12},{12... | collective-permute-start | bytes 368648 | tf_op jit(solution)/shard_map/ppermute | solution.py:560
  40.3 12.9 %collective-permute-start.11 = (f32[1,240,128]{2,1,0:T(8,128)S(1)}, f32[1,240,128]{2,1,0:T(8,128)S(1)}, u32[]{:S(2)}, u32[]{:S(2)}) collective-permute-start(f32[1,240,128]{2,1,0:T(8,128)S(1)} %get-tuple-element.45), channel_id=1, source_target_pairs={{0,6},{2,0},{4,2},{6,4},{1,7},{3,1},{5,3},{7,5},{8,14},{10,8},{12,... | collective-permute-start | bytes 368648 | tf_op jit(solution)/shard_map/ppermute | solution.py:560
  57.4 6.2 %collective-permute-start.13 = (f32[240,128]{1,0:T(8,128)S(1)}, f32[240,128]{1,0:T(8,128)S(1)}, u32[]{:S(2)}, u32[]{:S(2)}) collective-permute-start(f32[240,128]{1,0:T(8,128)S(1)} %get-tuple-element.54), channel_id=1, source_target_pairs={{0,8},{8,0},{16,24},{24,16},{1,9},{9,1},{17,25},{25,17},{2,10},{10... | collective-permute-start | bytes 368648 | tf_op jit(solution)/shard_map/ppermute | solution.py:564
  58.5 7.7 %collective-permute-start.14 = (f32[240,128]{1,0:T(8,128)S(1)}, f32[240,128]{1,0:T(8,128)S(1)}, u32[]{:S(2)}, u32[]{:S(2)}) collective-permute-start(f32[240,128]{1,0:T(8,128)S(1)} %get-tuple-element.55), channel_id=1, source_target_pairs={{0,16},{8,24},{16,0},{24,8},{1,17},{9,25},{17,1},{25,9},{2,18},{10... | collective-permute-start | bytes 368648 | tf_op jit(solution)/shard_map/ppermute | solution.py:564
  59.3 6.8 %collective-permute-start.15 = (f32[240,128]{1,0:T(8,128)S(1)}, f32[240,128]{1,0:T(8,128)S(1)}, u32[]{:S(2)}, u32[]{:S(2)}) collective-permute-start(f32[240,128]{1,0:T(8,128)S(1)} %get-tuple-element.56), channel_id=1, source_target_pairs={{0,24},{8,16},{16,8},{24,0},{1,25},{9,17},{17,9},{25,1},{2,26},{10... | collective-permute-start | bytes 368648 | tf_op jit(solution)/shard_map/ppermute | solution.py:564

commit v5 on v4

--- a/solution.py
+++ b/solution.py
@@ -11,6 +11,7 @@
 HALO = 3
 COMPONENTS = 5
 TILE = 8
+CHUNK = 16
 
 heat_ratio = 1.4
 step_size = 0.025
@@ -120,24 +121,6 @@
             store(at - 3, (centre[at - 1] - centre[at + 1]) + (interface[at - 1] - interface[at]))
 
 
-def reconstructed(first, second, third, fourth, fifth):
-    one, two, three, four = second - first, third - second, fourth - third, fifth - fourth
-    bends = [two - one, three - two, four - three]
-    slopes = [two + 0.5 * bends[0], two + 0.5 * bends[1], three - 0.5 * bends[2]]
-    smooth = [((13.0 / 12.0) * (b * b) + epsilon) + v * v for b, v in zip(bends, slopes)]
-    return bends[1], bends[2], correction(*smooth, bends[1] - bends[0], bends[2] - bends[1])
-
-
-def rolled(plus, minus):
-    p = {k: turned(plus, -k) for k in (-2, -1, 0, 1, 2)}
-    m = {k: turned(minus, -k) for k in (-1, 0, 1, 2, 3)}
-    plus_here, plus_next, right = reconstructed(p[-2], p[-1], p[0], p[1], p[2])
-    minus_next, minus_here, left = reconstructed(m[3], m[2], m[1], m[0], m[-1])
-    centre = 6.0 * ((p[0] + m[0]) + (p[1] + m[1])) - ((plus_here + minus_here) + (plus_next + minus_next))
-    interface = centre + ((plus_next - plus_here) - (minus_next - minus_here)) - 4.0 * (right + left)
-    return turned(interface, 1) - interface
-
-
 def lane_index(shape):
     return lax.broadcasted_iota(jnp.int32, shape, len(shape) - 1)
 
@@ -172,27 +155,60 @@
     return radau_weights[row][column] * (step_size / 12.0)
 
 
-class Windows:
-    def __init__(self, nx, nz, nodes):
-        self.nodes = nodes
-        self.size = nz
-        self.width = nz // nodes
-        self.pitch = self.width + 8
-        self.slots = nz // self.pitch
-        assert nx % self.slots == 0 and nx % nodes == 0 and nz % nodes == 0
-        self.rows = nx // self.slots
-
-    def cut(self, values, quarter):
-        pieces = [
-            turned(value, self.pitch * s + HALO - self.width * quarter) for s, value in enumerate(values)
-        ]
-        return merged(pieces, lane_index(values[0].shape) // self.pitch)
-
-    def joined(self, values, s):
-        start = self.pitch * s + HALO
-        lane = lane_index(values[0].shape)
-        region = jnp.where(lane < start, lane + (self.size - start), lane - start) // self.width
-        return turned(merged(values, region), -start)
+class Blocks:
+    def __init__(self, comps, nx, ny, nz):
+        self.comps, self.nx, self.ny, self.nz = comps, nx, ny, nz
+        self.per = nz // ny
+        self.left = nx - self.per
+        assert nz % ny == 0 and ny % TILE == 0 and 2 * self.left == self.per
+        self.half = nz // 2
+        self.count = comps + (comps + 1) // 2
+        self.step = CHUNK + 8
+
+    def pair(self, b):
+        first = 2 * (b - self.comps)
+        return first, min(first + 1, self.comps - 1) if isinstance(b, int) else jnp.minimum(first + 1, self.comps - 1)
+
+    def whole(self, ref, c):
+        return ref[c, pl.ds(0, self.per)].reshape(self.nz, self.nz)
+
+    def leftovers(self, ref, first, second):
+        at = pl.ds(self.per, self.left)
+        shape = (self.half, self.nz)
+        return jnp.concatenate([ref[first, at].reshape(shape), ref[second, at].reshape(shape)], axis=0)
+
+    def natural(self, ref, b):
+        return self.whole(ref, b) if b < self.comps else self.leftovers(ref, *self.pair(b))
+
+    def put_natural(self, ref, b, value):
+        if b < self.comps:
+            ref[b, pl.ds(0, self.per)] = value.reshape(self.per, self.ny, self.nz)
+            return
+        at = pl.ds(self.per, self.left)
+        shape = (self.left, self.ny, self.nz)
+        first, second = self.pair(b)
+        ref[first, at] = value[: self.half].reshape(shape)
+        if second != first:
+            ref[second, at] = value[self.half :].reshape(shape)
+
+    def row(self, c, i, t):
+        if i < self.per:
+            return c * self.nz + (i * self.ny + t)
+        return (self.comps + c // 2) * self.nz + lax.rem(c, 2) * self.half + ((i - self.per) * self.ny + t)
+
+
+def split_depth(blocks, read, alpha, write):
+    comps = blocks.comps
+    ((plus, minus),) = splits([read(c) for c in range(comps)], [None, None, alpha], (2,))
+    for c in range(comps):
+        write(c, plus[c], minus[c])
+    shared = [read(b) for b in range(comps, blocks.count)]
+    fields = [shared[c // 2] if c % 2 == 0 else turned(shared[c // 2], blocks.half) for c in range(comps)]
+    ((plus, minus),) = splits(fields, [None, None, alpha], (2,))
+    lower = lane_index(fields[0].shape) < blocks.half
+    for b in range(comps, blocks.count):
+        first, second = blocks.pair(b)
+        write(b, *[jnp.where(lower, v[first], turned(v[second], blocks.half)) for v in (plus, minus)])
 
 
 def write_edges(read, nx, ny, comps, lo_ref, hi_ref, side_ref):
@@ -233,7 +249,7 @@
     return tile
 
 
-def open_kernel(u_hbm, lo_ref, hi_ref, side_ref, al_ref, u_ref, sems):
+def open_kernel(u_hbm, u_ref, lo_ref, hi_ref, side_ref, al_ref, sems):
     comps, nx, ny, nz = u_ref.shape
     chunks = sems.shape[0]
     size = nx // chunks
@@ -254,58 +270,74 @@
     write_edges(read, nx, ny, comps, lo_ref, hi_ref, side_ref)
 
 
-def start_kernel(init_ref, win_ref, pack_ref, *, nodes):
+def turn_kernel(u_ref, rows_ref):
+    blocks = Blocks(*u_ref.shape)
+    nz = blocks.nz
+    for b in range(blocks.count):
+        value = blocks.natural(u_ref, b).T
+        rows_ref[b, pl.ds(HALO, nz), :] = value
+        rows_ref[b, pl.ds(0, HALO), :] = value[nz - HALO :]
+        rows_ref[b, pl.ds(HALO + nz, HALO), :] = value[:HALO]
+
+
+def start_kernel(init_ref, rows_ref, pack_ref, turned_ref, *, nodes):
     comps, nx, ny, nz = init_ref.shape
-    windows = Windows(nx, nz, nodes)
+    blocks = Blocks(comps, nx, ny, nz)
+    width = nz // nodes
     me = lax.axis_index("node")
-    lanes = lane_index((ny, nz)) // windows.width
+    lanes = lane_index((ny, nz)) // width
+    for b in range(blocks.count):
+        send_quarter(blocks.natural(init_ref, b).T, turned_ref, b, [rows_ref], [me], width)
 
     def step(c, carry):
-        for r in range(windows.rows):
-            values = [init_ref[c, s * windows.rows + r] for s in range(windows.slots)]
-            win_ref[rows_at((c * windows.rows + r) * ny, ny), :] = windows.cut(values, me)
         for q in range(nx // nodes):
-            pieces = [turned(init_ref[c, q * nodes + i], windows.width * (i - me)) for i in range(nodes)]
+            pieces = [turned(init_ref[c, q * nodes + i], width * (i - me)) for i in range(nodes)]
             pack_ref[rows_at((c * (nx // nodes) + q) * ny, ny), :] = merged(pieces, lanes)
         return carry
 
     lax.fori_loop(0, comps, step, 0)
+
+
+def send_quarter(value, ring_ref, b, parts, quarters, width):
+    nz = value.shape[0]
+    base = b * (nz + 2 * TILE)
+    ring_ref[rows_at(base + TILE, nz), :] = value
+    ring_ref[rows_at(base, TILE), :] = value[nz - TILE :]
+    ring_ref[rows_at(base + TILE + nz, TILE), :] = value[:TILE]
+    size = width + 8
+    for part, quarter in zip(parts, quarters):
+        part[rows_at(b * size, size), :] = ring_ref[pl.ds(base + (TILE - HALO) + quarter * width, size), :]
 
 
 def blend_kernel(start_ref, *refs):
     nodes = len(refs) - 6
-    parts, (win_ref, nat_ref, lo_ref, hi_ref, side_ref, al_ref) = refs[:nodes], refs[nodes:]
+    parts, (rows_ref, nat_ref, lo_ref, hi_ref, side_ref, al_ref) = refs[:nodes], refs[nodes:]
     comps, nx, ny, nz = nat_ref.shape
-    windows = Windows(nx, nz, nodes)
+    blocks = Blocks(comps, nx, ny, nz)
+    width = nz // nodes
+    size = width + 8
     me = lax.axis_index("node")
     weights = [
         [by_node(me, [scaled_weight(m, n ^ k) for n in range(nodes)]) for k in range(nodes)] for m in range(nodes)
     ]
-
-    def step(c, carry):
-        for r in range(windows.rows):
-            at = rows_at((c * windows.rows + r) * ny, ny)
-            start = start_ref[at, :]
-            rates = [part[at, :] for part in parts]
-            states = []
-            for m in range(nodes):
-                value = start
-                for k in range(nodes):
-                    value = value + weights[m][k] * rates[k]
-                value = turned(value, windows.width * m)
-                win_ref[m, at, :] = value
-                states.append(value)
-            for s in range(windows.slots):
-                nat_ref[c, s * windows.rows + r] = windows.joined(states, s)
-        return carry
-
-    lax.fori_loop(0, comps, step, 0)
+    for b in range(blocks.count):
+        at = pl.ds(b * size, size)
+        start = start_ref[at, :]
+        rates = [part[at, :] for part in parts]
+        for m in range(nodes):
+            value = start
+            for k in range(nodes):
+                value = value + weights[m][k] * rates[k]
+            rows_ref[m, at, :] = value
+        own = pl.ds(b * size + HALO, width)
+        state = jnp.concatenate([rows_ref[m, own, :] for m in range(nodes)], axis=0)
+        blocks.put_natural(nat_ref, b, state.T)
 
     def read(c, i):
         return nat_ref[c, i]
 
     best = tuple(jnp.zeros((ny, nz), jnp.float32) for _ in range(3))
-    tile = alpha_tile(faster(best, read, 0, nx, comps), windows.width)
+    tile = alpha_tile(faster(best, read, 0, nx, comps), width)
 
     def spread(i, carry):
         al_ref[i] = tile
@@ -315,20 +347,18 @@
     write_edges(read, nx, ny, comps, lo_ref, hi_ref, side_ref)
 
 
-def across_lanes(u, alphas, side_ref, dims, zp, zm, fy, yp, ym, depth):
+def along_second(u, alphas, side_ref, dims, fy, yp, ym):
     comps, nx, ny, nz = dims
     rows = yp.shape[0] // (ny + 2 * HALO)
     every = range(comps)
 
     def own(i, carry):
-        along_y, *rest = splits([u(c, i) for c in every], alphas, (1, 2) if depth else (1,))
+        ((p, m),) = splits([u(c, i) for c in every], alphas, (1,))
         for c in every:
             for t in range(0, ny, TILE):
                 at = pl.ds((HALO + t) * rows + c * nx + i, TILE, stride=rows)
-                yp[at, :] = along_y[0][c][t : t + TILE]
-                ym[at, :] = along_y[1][c][t : t + TILE]
-        if depth:
-            depth(i, rest[0])
+                yp[at, :] = p[c][t : t + TILE]
+                ym[at, :] = m[c][t : t + TILE]
         return carry
 
     lax.fori_loop(0, nx, own, 0)
@@ -343,11 +373,6 @@
 
     lax.fori_loop(0, 2 * HALO, ghost, 0)
 
-    blocks = rows // TILE
-    share = zp.shape[0] // blocks
-    assert share * blocks == zp.shape[0]
-    piece = max(p for p in range(TILE, 41, TILE) if share % p == 0)
-
     def along(b, carry):
         first = pl.multiple_of(b * TILE, TILE)
 
@@ -359,12 +384,28 @@
             fy[pl.ds(i * rows + first, TILE), :] = value
 
         stream(load, store, ny)
-        for n in range(0, share, piece):
-            at = rows_at(b * share + n, piece)
-            zp[at, :] = rolled(zp[at, :], zm[at, :])
-        return carry
-
-    lax.fori_loop(0, blocks, along, 0)
+        return carry
+
+    lax.fori_loop(0, rows // TILE, along, 0)
+
+
+def along_last(blocks, zp, zm, fz, after):
+    size = blocks.step * TILE
+
+    def along(b, carry):
+        def load(j):
+            at = pl.ds(b * size + j, TILE, stride=blocks.step)
+            return zp[at, :], zm[at, :]
+
+        def store(i, value):
+            fz[pl.ds(b * blocks.nz + i, TILE, stride=CHUNK), :] = value
+
+        stream(load, store, CHUNK)
+        after(jnp.maximum(b - 1, 0))
+        return carry
+
+    lax.fori_loop(0, blocks.count, along, 0)
+    after(blocks.count - 1)
 
 
 def along_first(u, alphas, lo_ref, hi_ref, fy, rate, xp, xm, extra, after):
@@ -391,127 +432,140 @@
 
         lax.fori_loop(0, HALO, ghost, 0)
 
-    tiles = ny // TILE
-
-    def along(b, carry):
-        c, t = b // tiles, lax.rem(b, tiles) * TILE
-        first = pl.multiple_of(b * TILE, TILE)
-
-        def load(j):
-            return xp[j, pl.ds(first, TILE), :], xm[j, pl.ds(first, TILE), :]
-
-        def store(i, value):
-            cross = fy[pl.ds(t * rows + c * nx + i, TILE, stride=rows), :]
-            rate[c, i, rows_at(t, TILE), :] = value + (cross + extra(c, i, t))
-
-        stream(load, store, nx)
-        done = jnp.maximum(b - 1, 0)
-        after(done // tiles, pl.multiple_of(lax.rem(done, tiles) * TILE, TILE))
-        return carry
-
-    lax.fori_loop(0, comps * tiles, along, 0)
-    after(comps - 1, ny - TILE)
+    def along(c, carry):
+        for t in range(0, ny, TILE):
+
+            def load(j, t=t):
+                at = rows_at(c * ny + t, TILE)
+                return xp[j, at, :], xm[j, at, :]
+
+            def store(i, value, t=t):
+                value = value + fy[pl.ds(t * rows + c * nx + i, TILE, stride=rows), :]
+                rate[c, i, pl.ds(t, TILE), :] = value if extra is None else value + extra(c, i, t)
+
+            stream(load, store, nx)
+        after(jnp.maximum(c - 1, 0))
+        return carry
+
+    lax.fori_loop(0, comps, along, 0)
+    after(jnp.int32(comps - 1))
 
 
 def tile_rows(tile):
     return [tile[k : k + 1, :] for k in range(3)]
 
 
-def first_lanes_kernel(u_ref, side_ref, al_ref, other_ref, zp, fy, al_out, zm, yp, ym):
-    comps, nx, ny, nz = u_ref.shape[1:]
+def first_lanes_kernel(u_ref, rows_ref, side_ref, al_ref, other_ref, fz, fy, al_out, zp, zm, yp, ym):
+    dims = u_ref.shape
+    blocks = Blocks(*dims)
     tile = jnp.maximum(al_ref[...], other_ref[...])
     al_out[...] = tile
-
-    def depth(i, split):
-        for c in range(comps):
-            at = rows_at((c * nx + i) * ny, ny)
-            zp[at, :] = split[0][c]
-            zm[at, :] = split[1][c]
-
-    across_lanes(lambda c, i: u_ref[0, c, i], tile_rows(tile), side_ref, u_ref.shape[1:], zp, zm, fy, yp, ym, depth)
-
-
-def first_rows_kernel(u_ref, lo_ref, hi_ref, al_ref, zp, fy, *refs):
-    parts, (rate, xp, xm) = refs[:-3], refs[-3:]
+    alphas = tile_rows(tile)
+    along_second(lambda c, i: u_ref[c, i], alphas, side_ref, dims, fy, yp, ym)
+
+    def depth(n, carry):
+        at = rows_at(n * CHUNK, blocks.step)
+
+        def write(b, plus, minus):
+            to = rows_at((b * TILE + n) * blocks.step, blocks.step)
+            zp[to, :] = plus
+            zm[to, :] = minus
+
+        split_depth(blocks, lambda b: rows_ref[b, at, :], alphas[2], write)
+        return carry
+
+    lax.fori_loop(0, TILE, depth, 0)
+    along_last(blocks, zp, zm, fz, lambda b: None)
+
+
+def first_rows_kernel(u_ref, lo_ref, hi_ref, al_ref, fz, fy, *refs):
+    parts, (rate, xp, xm, ring) = refs[:-4], refs[-4:]
     nodes = len(parts)
-    comps, nx, ny, nz = u_ref.shape[1:]
-    windows = Windows(nx, nz, nodes)
+    blocks = Blocks(*u_ref.shape)
+    nz = blocks.nz
     me = lax.axis_index("node")
-
-    def extra(c, i, t):
-        return zp[rows_at((c * nx + i) * ny + t, TILE), :]
-
-    def after(c, t):
-        for r in range(windows.rows):
-            values = [rate[c, s * windows.rows + r, pl.ds(t, TILE), :] for s in range(windows.slots)]
-            at = rows_at((c * windows.rows + r) * ny + t, TILE)
-            for k in range(nodes):
-                parts[k][at, :] = windows.cut(values, me ^ k)
-
-    along_first(lambda c, i: u_ref[0, c, i], tile_rows(al_ref), lo_ref, hi_ref, fy, rate, xp, xm, extra, after)
-
-
-def second_lanes_kernel(nat_ref, win_ref, side_ref, al_ref, zp, fy, al_out, zm, yp, ym):
-    nodes = win_ref.shape[0]
-    comps, nx, ny, nz = nat_ref.shape
-    windows = Windows(nx, nz, nodes)
-    part = comps * windows.rows * ny
+    quarters = [me ^ k for k in range(nodes)]
+
+    def send(value, b):
+        value = value.T + fz[rows_at(b * nz, nz), :]
+        send_quarter(value, ring, b, parts, quarters, nz // nodes)
+
+    def after(c):
+        send(blocks.whole(rate, c), c)
+        b = blocks.comps + c // 2
+        send(blocks.leftovers(rate, *blocks.pair(b)), b)
+
+    along_first(lambda c, i: u_ref[c, i], tile_rows(al_ref), lo_ref, hi_ref, fy, rate, xp, xm, None, after)
+
+
+def second_lanes_kernel(nat_ref, rows_ref, side_ref, al_ref, fz, fy, al_out, zp, zm, yp, ym, back):
+    nodes = rows_ref.shape[0]
+    dims = nat_ref.shape
+    blocks = Blocks(*dims)
+    nz = blocks.nz
+    width = nz // nodes
     tiles = al_ref.shape[0]
     tile = lax.fori_loop(
         1, tiles, lambda i, best: jnp.maximum(best, al_ref[i]), al_ref[0], unroll=True if tiles <= 32 else 1
     )
     al_out[...] = tile
     alphas = tile_rows(tile)
-    group = lane_index((1, nz)) // windows.width
-
+    along_second(lambda c, i: nat_ref[c, i], alphas, side_ref, dims, fy, yp, ym)
+    group = lane_index((1, nz)) // width
+    each = width // CHUNK
     for m in range(nodes):
         alpha = jnp.max(jnp.where(group == m, alphas[2], 0.0))
 
-        def depth(r, carry, m=m, alpha=alpha):
-            places = [(c * windows.rows + r) * ny for c in range(comps)]
-            fields = [win_ref[m, rows_at(place, ny), :] for place in places]
-            ((plus, minus),) = splits(fields, [None, None, alpha], (2,))
-            for c in range(comps):
-                at = rows_at(m * part + places[c], ny)
-                zp[at, :] = plus[c]
-                zm[at, :] = minus[c]
+        def depth(n, carry, m=m, alpha=alpha):
+            def read(b):
+                return rows_ref[m, rows_at(b * (width + 8) + n * CHUNK, blocks.step), :]
+
+            def write(b, plus, minus):
+                to = rows_at((b * TILE + m * each + n) * blocks.step, blocks.step)
+                zp[to, :] = plus
+                zm[to, :] = minus
+
+            split_depth(blocks, read, alpha, write)
             return carry
 
-        lax.fori_loop(0, windows.rows, depth, 0)
-
-    across_lanes(lambda c, i: nat_ref[c, i], alphas, side_ref, nat_ref.shape, zp, zm, fy, yp, ym, None)
-
-
-def second_rows_kernel(nat_ref, lo_ref, hi_ref, al_ref, zp, fy, pack_ref, *refs):
+        lax.fori_loop(0, each, depth, 0)
+
+    def after(b):
+        at = rows_at(b * nz, nz)
+        fz[at, :] = back[at, :].T
+
+    along_last(blocks, zp, zm, back, after)
+
+
+def second_rows_kernel(nat_ref, lo_ref, hi_ref, al_ref, fz, fy, pack_ref, *refs):
     outs, (rate, xp, xm) = refs[:-3], refs[-3:]
     nodes = len(outs)
     comps, nx, ny, nz = nat_ref.shape
-    windows = Windows(nx, nz, nodes)
-    part = comps * windows.rows * ny
+    blocks = Blocks(comps, nx, ny, nz)
+    width = nz // nodes
     me = lax.axis_index("node")
     weights = [
         [by_node(me, [scaled_weight(n ^ k, j) for n in range(nodes)]) for j in range(nodes)] for k in range(nodes)
     ]
-    lanes = lane_index((TILE, nz)) // windows.width
+    lanes = lane_index((TILE, nz)) // width
 
     def extra(c, i, t):
-        s, r = i // windows.rows, i % windows.rows
-        place = (c * windows.rows + r) * ny + t
-        return windows.joined([zp[rows_at(m * part + place, TILE), :] for m in range(nodes)], s)
-
-    def after(c, t):
-        for q in range(nx // nodes):
-            at = rows_at((c * (nx // nodes) + q) * ny + t, TILE)
-            start = pack_ref[at, :]
-            rows = [rate[c, q * nodes + i, pl.ds(t, TILE), :] for i in range(nodes)]
-            rates = [
-                merged([turned(rows[i], windows.width * (i - j)) for i in range(nodes)], lanes) for j in range(nodes)
-            ]
-            for k in range(nodes):
-                value = start
-                for j in range(nodes):
-                    value = value + weights[k][j] * rates[j]
-                outs[k][at, :] = turned(value, windows.width * me)
+        return fz[rows_at(blocks.row(c, i, t), TILE), :]
+
+    def after(c):
+        for t in range(0, ny, TILE):
+            for q in range(nx // nodes):
+                at = rows_at((c * (nx // nodes) + q) * ny + t, TILE)
+                start = pack_ref[at, :]
+                rows = [rate[c, q * nodes + i, pl.ds(t, TILE), :] for i in range(nodes)]
+                rates = [
+                    merged([turned(rows[i], width * (i - j)) for i in range(nodes)], lanes) for j in range(nodes)
+                ]
+                for k in range(nodes):
+                    value = start
+                    for j in range(nodes):
+                        value = value + weights[k][j] * rates[j]
+                    outs[k][at, :] = turned(value, width * me)
 
     along_first(lambda c, i: nat_ref[c, i], tile_rows(al_ref), lo_ref, hi_ref, fy, rate, xp, xm, extra, after)
 
@@ -592,43 +646,52 @@
     nodes = lax.axis_size("node")
     devices = nodes * lax.axis_size("gx") * lax.axis_size("gy")
     rows = -(-comps * nx // TILE) * TILE
-    windows = Windows(nx, nz, nodes)
+    blocks = Blocks(comps, nx, ny, nz)
+    width = nz // nodes
+    assert nz == CHUNK * TILE and width % CHUNK == 0 and nx % nodes == 0
     edge = (1, comps * HALO * ny, nz)
     edges = [edge, edge, (1, 2 * HALO * rows, nz)]
     tile_shape = (TILE, nz)
-    part = (comps * windows.rows * ny, nz)
+    part = (blocks.count * (width + 8), nz)
     pack = (comps * nx // nodes * ny, nz)
-    second = (ny * rows, nz)
-    padded = [((ny + 2 * HALO) * rows, nz)] * 2
+    across_shape = (ny * rows, nz)
+    depth_shape = (blocks.count * nz, nz)
+    padded = [(blocks.count * TILE * blocks.step, nz)] * 2 + [((ny + 2 * HALO) * rows, nz)] * 2
     slabs = [initial.shape] + [(nx + 2 * HALO, comps * ny, nz)] * 2
+    ring = (blocks.count * (nz + 2 * TILE), nz)
     chunks = 4 if nx % 4 == 0 else 1
 
-    lo, hi, side, tile = call(
+    field, lo, hi, side, tile = call(
         open_kernel,
         "open_kernel",
-        edges + [tile_shape],
+        [initial.shape] + edges + [tile_shape],
         [guesses],
-        [initial.shape, pltpu.SemaphoreType.DMA((chunks,))],
+        [pltpu.SemaphoreType.DMA((chunks,))],
         anywhere=True,
     )
     lower, upper, side = neighbours(lo, hi, side)
     tile, other = largest(tile)
+    (turned_field,) = call(turn_kernel, "turn_kernel", [(blocks.count, nz + 8, nz)], [field])
     start, start_pack = call(
-        functools.partial(start_kernel, nodes=nodes), "start_kernel", [part, pack], [initial]
-    )
-    whole = (comps * nx * ny, nz)
+        functools.partial(start_kernel, nodes=nodes), "start_kernel", [part, pack], [initial], [ring]
+    )
     depth, across, tile = call(
         first_lanes_kernel,
         "first_lanes_kernel",
-        [whole, second, tile_shape],
-        [guesses, side, tile, other],
-        [whole] + padded,
+        [depth_shape, across_shape, tile_shape],
+        [field, turned_field, side, tile, other],
+        padded,
         20_000_000,
     )
     parts = call(
-        first_rows_kernel, "first_rows_kernel", [part] * nodes, [guesses, lower, upper, tile, depth, across], slabs, 10_000_000
-    )
-    win, nat, lo, hi, side, tile = call(
+        first_rows_kernel,
+        "first_rows_kernel",
+        [part] * nodes,
+        [field, lower, upper, tile, depth, across],
+        slabs + [ring],
+        10_000_000,
+    )
+    turned_field, field, lo, hi, side, tile = call(
         blend_kernel,
         "blend_kernel",
         [(nodes,) + part, initial.shape] + edges + [(devices,) + tile_shape],
@@ -636,20 +699,19 @@
     )
     lower, upper, side = neighbours(lo, hi, side)
     tiles = lax.all_to_all(tile, ("node", "gx", "gy"), 0, 0)
-    whole = (nodes * part[0], nz)
     depth, across, tile = call(
         second_lanes_kernel,
         "second_lanes_kernel",
-        [whole, second, tile_shape],
-        [nat, win, side, tiles],
-        [whole] + padded,
+        [depth_shape, across_shape, tile_shape],
+        [field, turned_field, side, tiles],
+        padded + [depth_shape],
         20_000_000,
     )
     outs = call(
         second_rows_kernel,
         "second_rows_kernel",
         [pack] * nodes,
-        [nat, lower, upper, tile, depth, across, start_pack],
+        [field, lower, upper, tile, depth, across, start_pack],
         slabs,
         10_000_000,
     )

time: 67.3 us -> 65.9 us (0.979)
  Pallas kernels: 24.1 us -> 22.9 us
    pallas_call x8 -> x9, Pallas kernels: 24.1 us -> 22.9 us  [call(): pl.pallas_call(kernel, out_shape=[jax.ShapeDtypeStruct(shape, jnp.float32...]
  transfers between devices with their start and end apart: 17 -> 17, of which waited for: 8 -> 8; matrix products, arithmetic and copies ran while one was open for 0% -> 0% of each run, Pallas kernels for 18% -> 20%
where the time goes in v5:
time: 65.9 us; the launch traced here: 65.7 us
  starting transfers between devices  23.6 us (36%)
  Pallas kernels  22.9 us (35%)
  waiting for transfers between devices  18 us (27%)
  local copies, waits for them, and re-layouts  1.04 us (2%)
    pallas_call x9, Pallas kernels, call(): pl.pallas_call(kernel, out_shape=[jax.ShapeDtypeStruct(shape, jnp.float32...  22.9 us
    ppermute x10, starting transfers between devices, shifted(): lax.ppermute(value, axis, [(i, (i + by) % count) for i in range(count)])  13.9 us
    ppermute x6, waiting for transfers between devices, swapped(): lax.ppermute(value, 'node', [(i, i ^ by) for i in range(lax.axis_size('no...  12.1 us
    ppermute x6, starting transfers between devices, swapped(): lax.ppermute(value, 'node', [(i, i ^ by) for i in range(lax.axis_size('no...  7.1 us
    all_to_all x1, waiting for transfers between devices, local(): tiles = lax.all_to_all(tile, ('node', 'gx', 'gy'), 0, 0)  4.18 us
    all_to_all x1, starting transfers between devices, local(): tiles = lax.all_to_all(tile, ('node', 'gx', 'gy'), 0, 0)  2.58 us
    ppermute x10, waiting for transfers between devices, shifted(): lax.ppermute(value, axis, [(i, (i + by) % count) for i in range(count)])  1.73 us
  transfers between devices with their start and end apart: 17, of which 8 were waited for; matrix products, arithmetic and copies ran while one was open for 0% of the time, Pallas kernels for 20%

profile of v5, /device:TPU:0, one launch (start us, length us, event | category | flops | bytes accessed | tf_op | source)
XLA Modules:
  0.0 65.7 jit_solution(6596341798935670333)
XLA Ops:
  0.0 0.0 copy-start
  0.0 1.0 %copy-done = f32[1,5,12,16,128]{4,3,2,1,0:T(8,128)S(1)} copy-done((f32[1,5,12,16,128]{4,3,2,1,0:T(8,128)S(1)}, f32[1,5,12,16,128]{4,3,2,1,0:T(8,128)}, u32[]{:S(2)}) %copy-start) | copy-done | bytes 491544
  1.0 1.1 %open_kernel.1 = (f32[5,12,16,128]{3,2,1,0:T(8,128)S(1)}, f32[1,240,128]{2,1,0:T(8,128)S(1)}, f32[1,240,128]{2,1,0:T(8,128)S(1)}, f32[1,384,128]{2,1,0:T(8,128)S(1)}, f32[8,128]{1,0:T(8,128)S(1)}) custom-call(f32[1,5,12,16,128]{4,3,2,1,0:T(8,128)S(1)} %copy-done), custom_call_target="tpu_custom_call" | custom-call | flops 1000000 | bytes 983040 | tf_op jit(solution)/shard_map/open_kernel/pallas_call | solution.py:600
  2.2 5.1 %collective-permute-start.5 = (f32[8,128]{1,0:T(8,128)S(1)}, f32[8,128]{1,0:T(8,128)S(1)}, u32[]{:S(2)}, u32[]{:S(2)}) collective-permute-start(f32[8,128]{1,0:T(8,128)S(1)} %get-tuple-element.37), channel_id=1, source_target_pairs={{0,6},{2,0},{4,2},{6,4},{1,7},{3,1},{5,3},{7,5},{8,14},{10,8},{12,... | collective-permute-start | bytes 12296 | tf_op jit(solution)/shard_map/ppermute | solution.py:614
  7.3 0.0 collective-permute-start.4
  7.3 1.0 %collective-permute-start.3 = (f32[8,128]{1,0:T(8,128)S(1)}, f32[8,128]{1,0:T(8,128)S(1)}, u32[]{:S(2)}, u32[]{:S(2)}) collective-permute-start(f32[8,128]{1,0:T(8,128)S(1)} %get-tuple-element.37), channel_id=1, source_target_pairs={{0,2},{2,4},{4,6},{6,0},{1,3},{3,5},{5,7},{7,1},{8,10},{10,12},{12... | collective-permute-start | bytes 12296 | tf_op jit(solution)/shard_map/ppermute | solution.py:614
  8.3 2.5 %collective-permute-start = (f32[1,240,128]{2,1,0:T(8,128)S(1)}, f32[1,240,128]{2,1,0:T(8,128)S(1)}, u32[]{:S(2)}, u32[]{:S(2)}) collective-permute-start(f32[1,240,128]{2,1,0:T(8,128)S(1)} %get-tuple-element.34), channel_id=1, source_target_pairs={{0,2},{2,4},{4,6},{6,0},{1,3},{3,5},{5,7},{7,1},{8,10},{10,12},{12... | collective-permute-start | bytes 368648 | tf_op jit(solution)/shard_map/ppermute | solution.py:614
  10.8 1.3 %collective-permute-start.1 = (f32[1,240,128]{2,1,0:T(8,128)S(1)}, f32[1,240,128]{2,1,0:T(8,128)S(1)}, u32[]{:S(2)}, u32[]{:S(2)}) collective-permute-start(f32[1,240,128]{2,1,0:T(8,128)S(1)} %get-tuple-element.35), channel_id=1, source_target_pairs={{0,6},{2,0},{4,2},{6,4},{1,7},{3,1},{5,3},{7,5},{8,14},{10,8},{12,... | collective-permute-start | bytes 368648 | tf_op jit(solution)/shard_map/ppermute | solution.py:614
  12.1 0.0 collective-permute-done.5
  12.1 0.0 collective-permute-start.2
  12.1 0.5 collective-permute-done.4
  12.6 0.2 collective-permute-done.3
  12.9 0.0 collective-permute-start.6
  12.9 0.2 turn_kernel.1.rows_ref
  13.1 1.0 %collective-permute-done.6.other_ref = f32[8,128]{1,0:T(8,128)S(1)} collective-permute-done((f32[8,128]{1,0:T(8,128)S(1)}, f32[8,128]{1,0:T(8,128)S(1)}, u32[]{:S(2)}, u32[]{:S(2)}) %collective-permute-start.6) | collective-permute-done | bytes 4128 | tf_op jit(solution)/shard_map/ppermute | solution.py:614
  14.0 0.0 collective-permute-done.2.side_ref
  14.0 5.4 %first_lanes_kernel.1 = (f32[1024,128]{1,0:T(8,128)S(1)}, f32[1024,128]{1,0:T(8,128)S(1)}, f32[8,128]{1,0:T(8,128)S(1)}) custom-call(f32[5,12,16,128]{3,2,1,0:T(8,128)S(1)} %get-tuple-element.33.u_ref, f32[8,136,128]{2,1,0:T(8,128)S(1)} %turn_kernel.1.rows_ref, f32[1,384,128]{2,1,0:T(8,128)S(1)} %collective-permute-done.2.side_ref, ...), custom_call_target="tpu_custom_call" | custom-call | flops 20000000 | bytes 2506752 | tf_op jit(solution)/shard_map/first_lanes_kernel/pallas_call | solution.py:600
  19.5 0.0 collective-permute-done.lo_ref
  19.5 0.0 collective-permute-done.1.hi_ref
  19.5 0.0 copy-start.1
  19.5 2.6 %first_rows_kernel.1 = (f32[320,128]{1,0:T(8,128)S(1)}, f32[320,128]{1,0:T(8,128)S(1)}, f32[320,128]{1,0:T(8,128)S(1)}, f32[320,128]{1,0:T(8,128)S(1)}) custom-call(f32[5,12,16,128]{3,2,1,0:T(8,128)S(1)} %get-tuple-element.33.u_ref, f32[1,240,128]{2,1,0:T(8,128)S(1)} %collective-permute-done.lo_ref, f32[1,240,128]{2,1,0:T(8,128)S(1)} %collective-permute-done.1.hi_ref, ...), custom_call_target="tpu_custom_call" | custom-call | flops 10000000 | bytes 3579904 | tf_op jit(solution)/shard_map/first_rows_kernel/pallas_call | solution.py:600
  22.1 1.5 %collective-permute-start.7 = (f32[320,128]{1,0:T(8,128)S(1)}, f32[320,128]{1,0:T(8,128)S(1)}, u32[]{:S(2)}, u32[]{:S(2)}) collective-permute-start(f32[320,128]{1,0:T(8,128)S(1)} %get-tuple-element.42), channel_id=1, source_target_pairs={{0,8},{8,0},{16,24},{24,16},{1,9},{9,1},{17,25},{25,17},{2,10},{10... | collective-permute-start | bytes 491528 | tf_op jit(solution)/shard_map/ppermute | solution.py:618
  23.6 1.5 %collective-permute-start.8 = (f32[320,128]{1,0:T(8,128)S(1)}, f32[320,128]{1,0:T(8,128)S(1)}, u32[]{:S(2)}, u32[]{:S(2)}) collective-permute-start(f32[320,128]{1,0:T(8,128)S(1)} %get-tuple-element.43), channel_id=1, source_target_pairs={{0,16},{8,24},{16,0},{24,8},{1,17},{9,25},{17,1},{25,9},{2,18},{10... | collective-permute-start | bytes 491528 | tf_op jit(solution)/shard_map/ppermute | solution.py:618
  25.2 0.5 collective-permute-start.9
  25.7 0.0 copy-done.1
  25.7 0.7 %start_kernel.1 = (f32[320,128]{1,0:T(8,128)S(1)}, f32[240,128]{1,0:T(8,128)S(1)}) custom-call(f32[5,12,16,128]{3,2,1,0:T(8,128)S(1)} %copy-done.1), custom_call_target="tpu_custom_call" | custom-call | flops 1000000 | bytes 983040 | tf_op jit(solution)/shard_map/start_kernel/pallas_call | solution.py:600
  26.4 2.9 %collective-permute-done.7.refs_1_ = f32[320,128]{1,0:T(8,128)S(1)} collective-permute-done((f32[320,128]{1,0:T(8,128)S(1)}, f32[320,128]{1,0:T(8,128)S(1)}, u32[]{:S(2)}, u32[]{:S(2)}) %collective-permute-start.7) | collective-permute-done | bytes 163872 | tf_op jit(solution)/shard_map/ppermute | solution.py:618
  29.2 3.9 %collective-permute-done.8.refs_2_ = f32[320,128]{1,0:T(8,128)S(1)} collective-permute-done((f32[320,128]{1,0:T(8,128)S(1)}, f32[320,128]{1,0:T(8,128)S(1)}, u32[]{:S(2)}, u32[]{:S(2)}) %collective-permute-start.8) | collective-permute-done | bytes 163872 | tf_op jit(solution)/shard_map/ppermute | solution.py:618
  33.2 0.0 collective-permute-done.9.refs_3_
  33.2 1.9 %blend_kernel.1 = (f32[4,320,128]{2,1,0:T(8,128)S(1)}, f32[5,12,16,128]{3,2,1,0:T(8,128)S(1)}, f32[1,240,128]{2,1,0:T(8,128)S(1)}, f32[1,240,128]{2,1,0:T(8,128)...) custom-call(f32[320,128]{1,0:T(8,128)S(1)} %get-tuple-element.32.start_ref, ...), custom_call_target="tpu_custom_call" | custom-call | flops 1000000 | bytes 1638400 | tf_op jit(solution)/shard_map/blend_kernel/pallas_call | solution.py:600
  35.1 2.6 %all-to-all-start = ((f32[32,8,128]{2,1,0:T(8,128)}), f32[32,8,128]{2,1,0:T(8,128)S(1)}, u32[]{:S(2)}, u32[]{:S(2)}) async-start(f32[32,8,128]{2,1,0:T(8,128)} %get-tuple-element.50), calls=%async_computation | async-start | bytes 262144 | tf_op jit(solution)/shard_map/all_to_all | solution.py:701
  37.7 0.2 collective-permute-start.12
  37.8 1.7 %collective-permute-start.10 = (f32[1,240,128]{2,1,0:T(8,128)S(1)}, f32[1,240,128]{2,1,0:T(8,128)S(1)}, u32[]{:S(2)}, u32[]{:S(2)}) collective-permute-start(f32[1,240,128]{2,1,0:T(8,128)S(1)} %get-tuple-element.46), channel_id=1, source_target_pairs={{0,2},{2,4},{4,6},{6,0},{1,3},{3,5},{5,7},{7,1},{8,10},{10,12},{12... | collective-permute-start | bytes 368648 | tf_op jit(solution)/shard_map/ppermute | solution.py:614
  39.6 2.1 %collective-permute-start.11 = (f32[1,240,128]{2,1,0:T(8,128)S(1)}, f32[1,240,128]{2,1,0:T(8,128)S(1)}, u32[]{:S(2)}, u32[]{:S(2)}) collective-permute-start(f32[1,240,128]{2,1,0:T(8,128)S(1)} %get-tuple-element.47), channel_id=1, source_target_pairs={{0,6},{2,0},{4,2},{6,4},{1,7},{3,1},{5,3},{7,5},{8,14},{10,8},{12,... | collective-permute-start | bytes 368648 | tf_op jit(solution)/shard_map/ppermute | solution.py:614
  41.7 0.0 collective-permute-done.12.side_ref
  41.7 4.2 %all-to-all-done.al_ref = f32[32,8,128]{2,1,0:T(8,128)S(1)} async-done(((f32[32,8,128]{2,1,0:T(8,128)}), f32[32,8,128]{2,1,0:T(8,128)S(1)}, u32[]{:S(2)}, u32[]{:S(2)}) %all-to-all-start) | async-done | bytes 131104 | tf_op jit(solution)/shard_map/all_to_all | solution.py:701
  45.9 6.7 %second_lanes_kernel.1 = (f32[1024,128]{1,0:T(8,128)S(1)}, f32[1024,128]{1,0:T(8,128)S(1)}, f32[8,128]{1,0:T(8,128)S(1)}) custom-call(f32[5,12,16,128]{3,2,1,0:T(8,128)S(1)} %get-tuple-element.45.nat_ref, f32[4,320,128]{2,1,0:T(8,128)S(1)} %get-tuple-element.48.rows_ref, f32[1,384,128]{2,1,0:T(8,128)S(1)} %collective-permute-done.12.side_ref, ...), custom_call_target="tpu_custom_call" | custom-call | flops 20000000 | bytes 2949120 | tf_op jit(solution)/shard_map/second_lanes_kernel/pallas_call | solution.py:600
  52.6 0.0 collective-permute-done.10.lo_ref
  52.6 0.0 collective-permute-done.11.hi_ref
  52.6 3.3 %second_rows_kernel.1 = (f32[240,128]{1,0:T(8,128)S(1)}, f32[240,128]{1,0:T(8,128)S(1)}, f32[240,128]{1,0:T(8,128)S(1)}, f32[240,128]{1,0:T(8,128)S(1)}) custom-call(f32[5,12,16,128]{3,2,1,0:T(8,128)S(1)} %get-tuple-element.45.nat_ref, f32[1,240,128]{2,1,0:T(8,128)S(1)} %collective-permute-done.10.lo_ref, f32[1,240,128]{2,1,0:T(8,128)S(1)} %collective-permute-done.11.hi_ref, ...), custom_call_target="tpu_custom_call" | custom-call | flops 10000000 | bytes 3825664 | tf_op jit(solution)/shard_map/second_rows_kernel/pallas_call | solution.py:600
  55.9 1.1 %collective-permute-start.13 = (f32[240,128]{1,0:T(8,128)S(1)}, f32[240,128]{1,0:T(8,128)S(1)}, u32[]{:S(2)}, u32[]{:S(2)}) collective-permute-start(f32[240,128]{1,0:T(8,128)S(1)} %get-tuple-element.56), channel_id=1, source_target_pairs={{0,8},{8,0},{16,24},{24,16},{1,9},{9,1},{17,25},{25,17},{2,10},{10... | collective-permute-start | bytes 368648 | tf_op jit(solution)/shard_map/ppermute | solution.py:618
  57.0 0.8 %collective-permute-start.14 = (f32[240,128]{1,0:T(8,128)S(1)}, f32[240,128]{1,0:T(8,128)S(1)}, u32[]{:S(2)}, u32[]{:S(2)}) collective-permute-start(f32[240,128]{1,0:T(8,128)S(1)} %get-tuple-element.57), channel_id=1, source_target_pairs={{0,16},{8,24},{16,0},{24,8},{1,17},{9,25},{17,1},{25,9},{2,18},{10... | collective-permute-start | bytes 368648 | tf_op jit(solution)/shard_map/ppermute | solution.py:618
  57.9 1.6 %collective-permute-start.15 = (f32[240,128]{1,0:T(8,128)S(1)}, f32[240,128]{1,0:T(8,128)S(1)}, u32[]{:S(2)}, u32[]{:S(2)}) collective-permute-start(f32[240,128]{1,0:T(8,128)S(1)} %get-tuple-element.58), channel_id=1, source_target_pairs={{0,24},{8,16},{16,8},{24,0},{1,25},{9,17},{17,9},{25,1},{2,26},{10... | collective-permute-start | bytes 368648 | tf_op jit(solution)/shard_map/ppermute | solution.py:618
  59.5 2.7 %collective-permute-done.13.refs_1_ = f32[240,128]{1,0:T(8,128)S(1)} collective-permute-done((f32[240,128]{1,0:T(8,128)S(1)}, f32[240,128]{1,0:T(8,128)S(1)}, u32[]{:S(2)}, u32[]{:S(2)}) %collective-permute-start.13) | collective-permute-done | bytes 122912 | tf_op jit(solution)/shard_map/ppermute | solution.py:618
  62.2 2.6 %collective-permute-done.14.refs_2_ = f32[240,128]{1,0:T(8,128)S(1)} collective-permute-done((f32[240,128]{1,0:T(8,128)S(1)}, f32[240,128]{1,0:T(8,128)S(1)}, u32[]{:S(2)}, u32[]{:S(2)}) %collective-permute-start.14) | collective-permute-done | bytes 122912 | tf_op jit(solution)/shard_map/ppermute | solution.py:618
  64.7 0.0 collective-permute-done.15.refs_3_
  64.7 0.9 %close_kernel.1 = f32[1,5,12,16,128]{4,3,2,1,0:T(8,128)} custom-call(f32[240,128]{1,0:T(8,128)S(1)} %get-tuple-element.55.refs_0_, f32[240,128]{1,0:T(8,128)S(1)} %collective-permute-done.13.refs_1_, f32[240,128]{1,0:T(8,128)S(1)} %collective-permute-done.14.refs_2_, f32[240,128]{1,0:T(8,128)S(1)} %collective-permute-done.15.refs_3_), custom_call_target="tpu_custom_call" | custom-call | flops 1000000 | bytes 983040 | tf_op jit(solution)/shard_map/close_kernel/pallas_call | solution.py:600
  (1 shorter events, 0.0 us)
Async XLA Ops:
  0.0 1.0 %copy-start = (f32[1,5,12,16,128]{4,3,2,1,0:T(8,128)S(1)}, f32[1,5,12,16,128]{4,3,2,1,0:T(8,128)}, u32[]{:S(2)}) copy-start(f32[1,5,12,16,128]{4,3,2,1,0:T(8,128)} %u_hbm.1) | copy-start | bytes 1474564
  2.2 9.9 %collective-permute-start.5 = (f32[8,128]{1,0:T(8,128)S(1)}, f32[8,128]{1,0:T(8,128)S(1)}, u32[]{:S(2)}, u32[]{:S(2)}) collective-permute-start(f32[8,128]{1,0:T(8,128)S(1)} %get-tuple-element.37), channel_id=1, source_target_pairs={{0,6},{2,0},{4,2},{6,4},{1,7},{3,1},{5,3},{7,5},{8,14},{10,8},{12,... | collective-permute-start | bytes 12296 | tf_op jit(solution)/shard_map/ppermute | solution.py:614
  7.3 5.4 %collective-permute-start.4 = (f32[8,128]{1,0:T(8,128)S(1)}, f32[8,128]{1,0:T(8,128)S(1)}, u32[]{:S(2)}, u32[]{:S(2)}) collective-permute-start(f32[8,128]{1,0:T(8,128)S(1)} %get-tuple-element.37), channel_id=1, source_target_pairs={{0,4},{2,6},{4,0},{6,2},{1,5},{3,7},{5,1},{7,3},{8,12},{10,14},{12... | collective-permute-start | bytes 12296 | tf_op jit(solution)/shard_map/ppermute | solution.py:614
  7.3 5.6 %collective-permute-start.3 = (f32[8,128]{1,0:T(8,128)S(1)}, f32[8,128]{1,0:T(8,128)S(1)}, u32[]{:S(2)}, u32[]{:S(2)}) collective-permute-start(f32[8,128]{1,0:T(8,128)S(1)} %get-tuple-element.37), channel_id=1, source_target_pairs={{0,2},{2,4},{4,6},{6,0},{1,3},{3,5},{5,7},{7,1},{8,10},{10,12},{12... | collective-permute-start | bytes 12296 | tf_op jit(solution)/shard_map/ppermute | solution.py:614
  8.3 11.2 %collective-permute-start = (f32[1,240,128]{2,1,0:T(8,128)S(1)}, f32[1,240,128]{2,1,0:T(8,128)S(1)}, u32[]{:S(2)}, u32[]{:S(2)}) collective-permute-start(f32[1,240,128]{2,1,0:T(8,128)S(1)} %get-tuple-element.34), channel_id=1, source_target_pairs={{0,2},{2,4},{4,6},{6,0},{1,3},{3,5},{5,7},{7,1},{8,10},{10,12},{12... | collective-permute-start | bytes 368648 | tf_op jit(solution)/shard_map/ppermute | solution.py:614
  10.8 8.7 %collective-permute-start.1 = (f32[1,240,128]{2,1,0:T(8,128)S(1)}, f32[1,240,128]{2,1,0:T(8,128)S(1)}, u32[]{:S(2)}, u32[]{:S(2)}) collective-permute-start(f32[1,240,128]{2,1,0:T(8,128)S(1)} %get-tuple-element.35), channel_id=1, source_target_pairs={{0,6},{2,0},{4,2},{6,4},{1,7},{3,1},{5,3},{7,5},{8,14},{10,8},{12,... | collective-permute-start | bytes 368648 | tf_op jit(solution)/shard_map/ppermute | solution.py:614
  12.1 1.9 %collective-permute-start.2 = (f32[1,384,128]{2,1,0:T(8,128)S(1)}, f32[1,384,128]{2,1,0:T(8,128)S(1)}, u32[]{:S(2)}, u32[]{:S(2)}) collective-permute-start(f32[1,384,128]{2,1,0:T(8,128)S(1)} %get-tuple-element.36), channel_id=1, source_target_pairs={{0,1},{1,0},{2,3},{3,2},{4,5},{5,4},{6,7},{7,6},{8,9},{9,8},{10,11... | collective-permute-start | bytes 589832 | tf_op jit(solution)/shard_map/ppermute | solution.py:614
  12.9 1.2 %collective-permute-start.6 = (f32[8,128]{1,0:T(8,128)S(1)}, f32[8,128]{1,0:T(8,128)S(1)}, u32[]{:S(2)}, u32[]{:S(2)}) collective-permute-start(f32[8,128]{1,0:T(8,128)S(1)} %maximum_maximum_fusion.al_ref), channel_id=1, source_target_pairs={{0,1},{1,0},{2,3},{3,2},{4,5},{5,4},{6,7},{7,6},{8,9},{9,8},{10,11... | collective-permute-start | bytes 12296 | tf_op jit(solution)/shard_map/ppermute | solution.py:614
  19.5 6.2 %copy-start.1 = (f32[5,12,16,128]{3,2,1,0:T(8,128)S(1)}, f32[5,12,16,128]{3,2,1,0:T(8,128)}, u32[]{:S(2)}) copy-start(f32[5,12,16,128]{3,2,1,0:T(8,128)} %init_ref.1) | copy-start | bytes 1474564
  22.1 7.1 %collective-permute-start.7 = (f32[320,128]{1,0:T(8,128)S(1)}, f32[320,128]{1,0:T(8,128)S(1)}, u32[]{:S(2)}, u32[]{:S(2)}) collective-permute-start(f32[320,128]{1,0:T(8,128)S(1)} %get-tuple-element.42), channel_id=1, source_target_pairs={{0,8},{8,0},{16,24},{24,16},{1,9},{9,1},{17,25},{25,17},{2,10},{10... | collective-permute-start | bytes 491528 | tf_op jit(solution)/shard_map/ppermute | solution.py:618
  23.6 9.5 %collective-permute-start.8 = (f32[320,128]{1,0:T(8,128)S(1)}, f32[320,128]{1,0:T(8,128)S(1)}, u32[]{:S(2)}, u32[]{:S(2)}) collective-permute-start(f32[320,128]{1,0:T(8,128)S(1)} %get-tuple-element.43), channel_id=1, source_target_pairs={{0,16},{8,24},{16,0},{24,8},{1,17},{9,25},{17,1},{25,9},{2,18},{10... | collective-permute-start | bytes 491528 | tf_op jit(solution)/shard_map/ppermute | solution.py:618
  25.2 8.0 %collective-permute-start.9 = (f32[320,128]{1,0:T(8,128)S(1)}, f32[320,128]{1,0:T(8,128)S(1)}, u32[]{:S(2)}, u32[]{:S(2)}) collective-permute-start(f32[320,128]{1,0:T(8,128)S(1)} %get-tuple-element.44), channel_id=1, source_target_pairs={{0,24},{8,16},{16,8},{24,0},{1,25},{9,17},{17,9},{25,1},{2,26},{10... | collective-permute-start | bytes 491528 | tf_op jit(solution)/shard_map/ppermute | solution.py:618
  35.1 10.8 %all-to-all-start = ((f32[32,8,128]{2,1,0:T(8,128)}), f32[32,8,128]{2,1,0:T(8,128)S(1)}, u32[]{:S(2)}, u32[]{:S(2)}) async-start(f32[32,8,128]{2,1,0:T(8,128)} %get-tuple-element.50), calls=%async_computation | async-start | bytes 262144 | tf_op jit(solution)/shard_map/all_to_all | solution.py:701
  37.7 4.0 %collective-permute-start.12 = (f32[1,384,128]{2,1,0:T(8,128)S(1)}, f32[1,384,128]{2,1,0:T(8,128)S(1)}, u32[]{:S(2)}, u32[]{:S(2)}) collective-permute-start(f32[1,384,128]{2,1,0:T(8,128)S(1)} %get-tuple-element.49), channel_id=1, source_target_pairs={{0,1},{1,0},{2,3},{3,2},{4,5},{5,4},{6,7},{7,6},{8,9},{9,8},{10,11... | collective-permute-start | bytes 589832 | tf_op jit(solution)/shard_map/ppermute | solution.py:614
  37.8 14.8 %collective-permute-start.10 = (f32[1,240,128]{2,1,0:T(8,128)S(1)}, f32[1,240,128]{2,1,0:T(8,128)S(1)}, u32[]{:S(2)}, u32[]{:S(2)}) collective-permute-start(f32[1,240,128]{2,1,0:T(8,128)S(1)} %get-tuple-element.46), channel_id=1, source_target_pairs={{0,2},{2,4},{4,6},{6,0},{1,3},{3,5},{5,7},{7,1},{8,10},{10,12},{12... | collective-permute-start | bytes 368648 | tf_op jit(solution)/shard_map/ppermute | solution.py:614
  39.6 13.0 %collective-permute-start.11 = (f32[1,240,128]{2,1,0:T(8,128)S(1)}, f32[1,240,128]{2,1,0:T(8,128)S(1)}, u32[]{:S(2)}, u32[]{:S(2)}) collective-permute-start(f32[1,240,128]{2,1,0:T(8,128)S(1)} %get-tuple-element.47), channel_id=1, source_target_pairs={{0,6},{2,0},{4,2},{6,4},{1,7},{3,1},{5,3},{7,5},{8,14},{10,8},{12,... | collective-permute-start | bytes 368648 | tf_op jit(solution)/shard_map/ppermute | solution.py:614
  55.9 6.3 %collective-permute-start.13 = (f32[240,128]{1,0:T(8,128)S(1)}, f32[240,128]{1,0:T(8,128)S(1)}, u32[]{:S(2)}, u32[]{:S(2)}) collective-permute-start(f32[240,128]{1,0:T(8,128)S(1)} %get-tuple-element.56), channel_id=1, source_target_pairs={{0,8},{8,0},{16,24},{24,16},{1,9},{9,1},{17,25},{25,17},{2,10},{10... | collective-permute-start | bytes 368648 | tf_op jit(solution)/shard_map/ppermute | solution.py:618
  57.0 7.7 %collective-permute-start.14 = (f32[240,128]{1,0:T(8,128)S(1)}, f32[240,128]{1,0:T(8,128)S(1)}, u32[]{:S(2)}, u32[]{:S(2)}) collective-permute-start(f32[240,128]{1,0:T(8,128)S(1)} %get-tuple-element.57), channel_id=1, source_target_pairs={{0,16},{8,24},{16,0},{24,8},{1,17},{9,25},{17,1},{25,9},{2,18},{10... | collective-permute-start | bytes 368648 | tf_op jit(solution)/shard_map/ppermute | solution.py:618
  57.9 6.8 %collective-permute-start.15 = (f32[240,128]{1,0:T(8,128)S(1)}, f32[240,128]{1,0:T(8,128)S(1)}, u32[]{:S(2)}, u32[]{:S(2)}) collective-permute-start(f32[240,128]{1,0:T(8,128)S(1)} %get-tuple-element.58), channel_id=1, source_target_pairs={{0,24},{8,16},{16,8},{24,0},{1,25},{9,17},{17,9},{25,1},{2,26},{10... | collective-permute-start | bytes 368648 | tf_op jit(solution)/shard_map/ppermute | solution.py:618

commit v6 on v5

--- a/solution.py
+++ b/solution.py
@@ -347,38 +347,39 @@
     write_edges(read, nx, ny, comps, lo_ref, hi_ref, side_ref)
 
 
-def along_second(u, alphas, side_ref, dims, fy, yp, ym):
+def along_second(u, alphas, side_ref, dims, fy, yp, ym, gp, gm):
     comps, nx, ny, nz = dims
-    rows = yp.shape[0] // (ny + 2 * HALO)
+    rows = gp.shape[0] // (2 * HALO)
     every = range(comps)
 
     def own(i, carry):
         ((p, m),) = splits([u(c, i) for c in every], alphas, (1,))
         for c in every:
-            for t in range(0, ny, TILE):
-                at = pl.ds((HALO + t) * rows + c * nx + i, TILE, stride=rows)
-                yp[at, :] = p[c][t : t + TILE]
-                ym[at, :] = m[c][t : t + TILE]
-        return carry
-
-    lax.fori_loop(0, nx, own, 0)
+            at = rows_at((c * nx + i) * ny, ny)
+            yp[at, :] = p[c]
+            ym[at, :] = m[c]
+        return carry
+
+    lax.fori_loop(0, nx, own, 0, unroll=4)
 
     def ghost(i, carry):
-        row = jnp.where(i < HALO, i, i + ny) * rows
         ((p, m),) = splits([side_ref[0, pl.ds(i * rows + c * nx, nx), :] for c in every], alphas, (1,))
         for c in every:
-            yp[pl.ds(row + c * nx, nx), :] = p[c]
-            ym[pl.ds(row + c * nx, nx), :] = m[c]
-        return carry
-
-    lax.fori_loop(0, 2 * HALO, ghost, 0)
+            gp[pl.ds(i * rows + c * nx, nx), :] = p[c]
+            gm[pl.ds(i * rows + c * nx, nx), :] = m[c]
+        return carry
+
+    lax.fori_loop(0, 2 * HALO, ghost, 0, unroll=HALO)
 
     def along(b, carry):
         first = pl.multiple_of(b * TILE, TILE)
 
         def load(j):
-            at = pl.ds(j * rows + first, TILE)
-            return yp[at, :], ym[at, :]
+            if HALO <= j < HALO + ny:
+                at = pl.ds(first * ny + (j - HALO), TILE, stride=ny)
+                return yp[at, :], ym[at, :]
+            at = pl.ds((j if j < HALO else j - ny) * rows + first, TILE)
+            return gp[at, :], gm[at, :]
 
         def store(i, value):
             fy[pl.ds(i * rows + first, TILE), :] = value
@@ -400,8 +401,8 @@
         def store(i, value):
             fz[pl.ds(b * blocks.nz + i, TILE, stride=CHUNK), :] = value
 
+        after(jnp.maximum(b - 1, 0))
         stream(load, store, CHUNK)
-        after(jnp.maximum(b - 1, 0))
         return carry
 
     lax.fori_loop(0, blocks.count, along, 0)
@@ -423,16 +424,17 @@
         split([u(c, i) for c in every], i + HALO)
         return carry
 
-    lax.fori_loop(0, nx, own, 0)
+    lax.fori_loop(0, nx, own, 0, unroll=4)
     for ref, start in ((lo_ref, 0), (hi_ref, nx + HALO)):
 
         def ghost(i, carry, ref=ref, start=start):
             split([ref[0, rows_at((c * HALO + i) * ny, ny), :] for c in every], start + i)
             return carry
 
-        lax.fori_loop(0, HALO, ghost, 0)
+        lax.fori_loop(0, HALO, ghost, 0, unroll=HALO)
 
     def along(c, carry):
+        after(jnp.maximum(c - 1, 0))
         for t in range(0, ny, TILE):
 
             def load(j, t=t):
@@ -444,7 +446,6 @@
                 rate[c, i, pl.ds(t, TILE), :] = value if extra is None else value + extra(c, i, t)
 
             stream(load, store, nx)
-        after(jnp.maximum(c - 1, 0))
         return carry
 
     lax.fori_loop(0, comps, along, 0)
@@ -455,13 +456,13 @@
     return [tile[k : k + 1, :] for k in range(3)]
 
 
-def first_lanes_kernel(u_ref, rows_ref, side_ref, al_ref, other_ref, fz, fy, al_out, zp, zm, yp, ym):
+def first_lanes_kernel(u_ref, rows_ref, side_ref, al_ref, other_ref, fz, fy, al_out, zp, zm, yp, ym, gp, gm):
     dims = u_ref.shape
     blocks = Blocks(*dims)
     tile = jnp.maximum(al_ref[...], other_ref[...])
     al_out[...] = tile
     alphas = tile_rows(tile)
-    along_second(lambda c, i: u_ref[c, i], alphas, side_ref, dims, fy, yp, ym)
+    along_second(lambda c, i: u_ref[c, i], alphas, side_ref, dims, fy, yp, ym, gp, gm)
 
     def depth(n, carry):
         at = rows_at(n * CHUNK, blocks.step)
@@ -474,7 +475,7 @@
         split_depth(blocks, lambda b: rows_ref[b, at, :], alphas[2], write)
         return carry
 
-    lax.fori_loop(0, TILE, depth, 0)
+    lax.fori_loop(0, TILE, depth, 0, unroll=4)
     along_last(blocks, zp, zm, fz, lambda b: None)
 
 
@@ -498,7 +499,7 @@
     along_first(lambda c, i: u_ref[c, i], tile_rows(al_ref), lo_ref, hi_ref, fy, rate, xp, xm, None, after)
 
 
-def second_lanes_kernel(nat_ref, rows_ref, side_ref, al_ref, fz, fy, al_out, zp, zm, yp, ym, back):
+def second_lanes_kernel(nat_ref, rows_ref, side_ref, al_ref, fz, fy, al_out, zp, zm, yp, ym, gp, gm, back):
     nodes = rows_ref.shape[0]
     dims = nat_ref.shape
     blocks = Blocks(*dims)
@@ -510,7 +511,7 @@
     )
     al_out[...] = tile
     alphas = tile_rows(tile)
-    along_second(lambda c, i: nat_ref[c, i], alphas, side_ref, dims, fy, yp, ym)
+    along_second(lambda c, i: nat_ref[c, i], alphas, side_ref, dims, fy, yp, ym, gp, gm)
     group = lane_index((1, nz)) // width
     each = width // CHUNK
     for m in range(nodes):
@@ -528,7 +529,7 @@
             split_depth(blocks, read, alpha, write)
             return carry
 
-        lax.fori_loop(0, each, depth, 0)
+        lax.fori_loop(0, each, depth, 0, unroll=True)
 
     def after(b):
         at = rows_at(b * nz, nz)
@@ -594,7 +595,7 @@
 
 
 def call(kernel, name, outs, operands, scratch=(), flops=1_000_000, anywhere=False, outside=False):
-    vmem, hbm = pl.BlockSpec(memory_space=pltpu.VMEM), pl.BlockSpec(memory_space=pl.ANY)
+    vmem, hbm = pl.BlockSpec(memory_space=pltpu.VMEM), pl.BlockSpec(memory_space=pltpu.HBM)
     moved = sum(4 * x.size for x in operands)
     scratch = [pltpu.VMEM(x, jnp.float32) if isinstance(x, tuple) else x for x in scratch]
     return pl.pallas_call(
@@ -656,7 +657,7 @@
     pack = (comps * nx // nodes * ny, nz)
     across_shape = (ny * rows, nz)
     depth_shape = (blocks.count * nz, nz)
-    padded = [(blocks.count * TILE * blocks.step, nz)] * 2 + [((ny + 2 * HALO) * rows, nz)] * 2
+    padded = [(blocks.count * TILE * blocks.step, nz)] * 2 + [(ny * rows, nz)] * 2 + [(2 * HALO * rows, nz)] * 2
     slabs = [initial.shape] + [(nx + 2 * HALO, comps * ny, nz)] * 2
     ring = (blocks.count * (nz + 2 * TILE), nz)
     chunks = 4 if nx % 4 == 0 else 1

time: 65.9 us -> 60 us (0.910)
  Pallas kernels: 22.9 us -> 17.1 us
    pallas_call x9, Pallas kernels: 22.9 us -> 17.1 us  [call(): pl.pallas_call(kernel, out_shape=[jax.ShapeDtypeStruct(shape, jnp.float32...]
  transfers between devices with their start and end apart: 17 -> 17, of which waited for: 8 -> 8; matrix products, arithmetic and copies ran while one was open for 0% -> 0% of each run, Pallas kernels for 20% -> 15%
where the time goes in v6:
time: 60 us; the launch traced here: 59.8 us
  starting transfers between devices  23.6 us (39%)
  waiting for transfers between devices  18 us (30%)
  Pallas kernels  17.1 us (29%)
  local copies, waits for them, and re-layouts  1.04 us (2%)
    pallas_call x9, Pallas kernels, call(): pl.pallas_call(kernel, out_shape=[jax.ShapeDtypeStruct(shape, jnp.float32...  17.1 us
    ppermute x10, starting transfers between devices, shifted(): lax.ppermute(value, axis, [(i, (i + by) % count) for i in range(count)])  13.9 us
    ppermute x6, waiting for transfers between devices, swapped(): lax.ppermute(value, 'node', [(i, i ^ by) for i in range(lax.axis_size('no...  12.1 us
    ppermute x6, starting transfers between devices, swapped(): lax.ppermute(value, 'node', [(i, i ^ by) for i in range(lax.axis_size('no...  7.1 us
    all_to_all x1, waiting for transfers between devices, local(): tiles = lax.all_to_all(tile, ('node', 'gx', 'gy'), 0, 0)  4.18 us
    all_to_all x1, starting transfers between devices, local(): tiles = lax.all_to_all(tile, ('node', 'gx', 'gy'), 0, 0)  2.58 us
    ppermute x10, waiting for transfers between devices, shifted(): lax.ppermute(value, axis, [(i, (i + by) % count) for i in range(count)])  1.73 us
  transfers between devices with their start and end apart: 17, of which 8 were waited for; matrix products, arithmetic and copies ran while one was open for 0% of the time, Pallas kernels for 15%

profile of v6, /device:TPU:0, one launch (start us, length us, event | category | flops | bytes accessed | tf_op | source)
XLA Modules:
  0.0 59.8 jit_solution(12225157452403296865)
XLA Ops:
  0.0 0.0 copy-start
  0.0 1.0 %copy-done = f32[1,5,12,16,128]{4,3,2,1,0:T(8,128)S(1)} copy-done((f32[1,5,12,16,128]{4,3,2,1,0:T(8,128)S(1)}, f32[1,5,12,16,128]{4,3,2,1,0:T(8,128)}, u32[]{:S(2)}) %copy-start) | copy-done | bytes 491544
  1.0 1.1 %open_kernel.1 = (f32[5,12,16,128]{3,2,1,0:T(8,128)S(1)}, f32[1,240,128]{2,1,0:T(8,128)S(1)}, f32[1,240,128]{2,1,0:T(8,128)S(1)}, f32[1,384,128]{2,1,0:T(8,128)S(1)}, f32[8,128]{1,0:T(8,128)S(1)}) custom-call(f32[1,5,12,16,128]{4,3,2,1,0:T(8,128)S(1)} %copy-done), custom_call_target="tpu_custom_call" | custom-call | flops 1000000 | bytes 983040 | tf_op jit(solution)/shard_map/open_kernel/pallas_call | solution.py:601
  2.2 5.1 %collective-permute-start.5 = (f32[8,128]{1,0:T(8,128)S(1)}, f32[8,128]{1,0:T(8,128)S(1)}, u32[]{:S(2)}, u32[]{:S(2)}) collective-permute-start(f32[8,128]{1,0:T(8,128)S(1)} %get-tuple-element.37), channel_id=1, source_target_pairs={{0,6},{2,0},{4,2},{6,4},{1,7},{3,1},{5,3},{7,5},{8,14},{10,8},{12,... | collective-permute-start | bytes 12296 | tf_op jit(solution)/shard_map/ppermute | solution.py:615
  7.3 0.0 collective-permute-start.4
  7.3 1.0 %collective-permute-start.3 = (f32[8,128]{1,0:T(8,128)S(1)}, f32[8,128]{1,0:T(8,128)S(1)}, u32[]{:S(2)}, u32[]{:S(2)}) collective-permute-start(f32[8,128]{1,0:T(8,128)S(1)} %get-tuple-element.37), channel_id=1, source_target_pairs={{0,2},{2,4},{4,6},{6,0},{1,3},{3,5},{5,7},{7,1},{8,10},{10,12},{12... | collective-permute-start | bytes 12296 | tf_op jit(solution)/shard_map/ppermute | solution.py:615
  8.3 2.5 %collective-permute-start = (f32[1,240,128]{2,1,0:T(8,128)S(1)}, f32[1,240,128]{2,1,0:T(8,128)S(1)}, u32[]{:S(2)}, u32[]{:S(2)}) collective-permute-start(f32[1,240,128]{2,1,0:T(8,128)S(1)} %get-tuple-element.34), channel_id=1, source_target_pairs={{0,2},{2,4},{4,6},{6,0},{1,3},{3,5},{5,7},{7,1},{8,10},{10,12},{12... | collective-permute-start | bytes 368648 | tf_op jit(solution)/shard_map/ppermute | solution.py:615
  10.8 1.3 %collective-permute-start.1 = (f32[1,240,128]{2,1,0:T(8,128)S(1)}, f32[1,240,128]{2,1,0:T(8,128)S(1)}, u32[]{:S(2)}, u32[]{:S(2)}) collective-permute-start(f32[1,240,128]{2,1,0:T(8,128)S(1)} %get-tuple-element.35), channel_id=1, source_target_pairs={{0,6},{2,0},{4,2},{6,4},{1,7},{3,1},{5,3},{7,5},{8,14},{10,8},{12,... | collective-permute-start | bytes 368648 | tf_op jit(solution)/shard_map/ppermute | solution.py:615
  12.1 0.0 collective-permute-done.5
  12.1 0.0 collective-permute-start.2
  12.1 0.5 collective-permute-done.4
  12.6 0.2 collective-permute-done.3
  12.9 0.0 collective-permute-start.6
  12.9 0.2 turn_kernel.1.rows_ref
  13.1 1.0 %collective-permute-done.6.other_ref = f32[8,128]{1,0:T(8,128)S(1)} collective-permute-done((f32[8,128]{1,0:T(8,128)S(1)}, f32[8,128]{1,0:T(8,128)S(1)}, u32[]{:S(2)}, u32[]{:S(2)}) %collective-permute-start.6) | collective-permute-done | bytes 4128 | tf_op jit(solution)/shard_map/ppermute | solution.py:615
  14.0 0.0 collective-permute-done.2.side_ref
  14.0 3.8 %first_lanes_kernel.1 = (f32[1024,128]{1,0:T(8,128)S(1)}, f32[1024,128]{1,0:T(8,128)S(1)}, f32[8,128]{1,0:T(8,128)S(1)}) custom-call(f32[5,12,16,128]{3,2,1,0:T(8,128)S(1)} %get-tuple-element.33.u_ref, f32[8,136,128]{2,1,0:T(8,128)S(1)} %turn_kernel.1.rows_ref, f32[1,384,128]{2,1,0:T(8,128)S(1)} %collective-permute-done.2.side_ref, ...), custom_call_target="tpu_custom_call" | custom-call | flops 20000000 | bytes 2506752 | tf_op jit(solution)/shard_map/first_lanes_kernel/pallas_call | solution.py:601
  17.8 0.0 collective-permute-done.lo_ref
  17.8 0.0 collective-permute-done.1.hi_ref
  17.9 0.0 copy-start.1
  17.9 1.9 %first_rows_kernel.1 = (f32[320,128]{1,0:T(8,128)S(1)}, f32[320,128]{1,0:T(8,128)S(1)}, f32[320,128]{1,0:T(8,128)S(1)}, f32[320,128]{1,0:T(8,128)S(1)}) custom-call(f32[5,12,16,128]{3,2,1,0:T(8,128)S(1)} %get-tuple-element.33.u_ref, f32[1,240,128]{2,1,0:T(8,128)S(1)} %collective-permute-done.lo_ref, f32[1,240,128]{2,1,0:T(8,128)S(1)} %collective-permute-done.1.hi_ref, ...), custom_call_target="tpu_custom_call" | custom-call | flops 10000000 | bytes 3579904 | tf_op jit(solution)/shard_map/first_rows_kernel/pallas_call | solution.py:601
  19.8 1.5 %collective-permute-start.7 = (f32[320,128]{1,0:T(8,128)S(1)}, f32[320,128]{1,0:T(8,128)S(1)}, u32[]{:S(2)}, u32[]{:S(2)}) collective-permute-start(f32[320,128]{1,0:T(8,128)S(1)} %get-tuple-element.42), channel_id=1, source_target_pairs={{0,8},{8,0},{16,24},{24,16},{1,9},{9,1},{17,25},{25,17},{2,10},{10... | collective-permute-start | bytes 491528 | tf_op jit(solution)/shard_map/ppermute | solution.py:619
  21.3 1.5 %collective-permute-start.8 = (f32[320,128]{1,0:T(8,128)S(1)}, f32[320,128]{1,0:T(8,128)S(1)}, u32[]{:S(2)}, u32[]{:S(2)}) collective-permute-start(f32[320,128]{1,0:T(8,128)S(1)} %get-tuple-element.43), channel_id=1, source_target_pairs={{0,16},{8,24},{16,0},{24,8},{1,17},{9,25},{17,1},{25,9},{2,18},{10... | collective-permute-start | bytes 491528 | tf_op jit(solution)/shard_map/ppermute | solution.py:619
  22.8 0.5 collective-permute-start.9
  23.3 0.0 copy-done.1
  23.3 0.7 %start_kernel.1 = (f32[320,128]{1,0:T(8,128)S(1)}, f32[240,128]{1,0:T(8,128)S(1)}) custom-call(f32[5,12,16,128]{3,2,1,0:T(8,128)S(1)} %copy-done.1), custom_call_target="tpu_custom_call" | custom-call | flops 1000000 | bytes 983040 | tf_op jit(solution)/shard_map/start_kernel/pallas_call | solution.py:601
  24.0 2.9 %collective-permute-done.7.refs_1_ = f32[320,128]{1,0:T(8,128)S(1)} collective-permute-done((f32[320,128]{1,0:T(8,128)S(1)}, f32[320,128]{1,0:T(8,128)S(1)}, u32[]{:S(2)}, u32[]{:S(2)}) %collective-permute-start.7) | collective-permute-done | bytes 163872 | tf_op jit(solution)/shard_map/ppermute | solution.py:619
  26.9 3.9 %collective-permute-done.8.refs_2_ = f32[320,128]{1,0:T(8,128)S(1)} collective-permute-done((f32[320,128]{1,0:T(8,128)S(1)}, f32[320,128]{1,0:T(8,128)S(1)}, u32[]{:S(2)}, u32[]{:S(2)}) %collective-permute-start.8) | collective-permute-done | bytes 163872 | tf_op jit(solution)/shard_map/ppermute | solution.py:619
  30.8 0.0 collective-permute-done.9.refs_3_
  30.8 1.9 %blend_kernel.1 = (f32[4,320,128]{2,1,0:T(8,128)S(1)}, f32[5,12,16,128]{3,2,1,0:T(8,128)S(1)}, f32[1,240,128]{2,1,0:T(8,128)S(1)}, f32[1,240,128]{2,1,0:T(8,128)...) custom-call(f32[320,128]{1,0:T(8,128)S(1)} %get-tuple-element.32.start_ref, ...), custom_call_target="tpu_custom_call" | custom-call | flops 1000000 | bytes 1638400 | tf_op jit(solution)/shard_map/blend_kernel/pallas_call | solution.py:601
  32.7 2.6 %all-to-all-start = ((f32[32,8,128]{2,1,0:T(8,128)}), f32[32,8,128]{2,1,0:T(8,128)S(1)}, u32[]{:S(2)}, u32[]{:S(2)}) async-start(f32[32,8,128]{2,1,0:T(8,128)} %get-tuple-element.50), calls=%async_computation | async-start | bytes 262144 | tf_op jit(solution)/shard_map/all_to_all | solution.py:702
  35.3 0.2 collective-permute-start.12
  35.5 1.7 %collective-permute-start.10 = (f32[1,240,128]{2,1,0:T(8,128)S(1)}, f32[1,240,128]{2,1,0:T(8,128)S(1)}, u32[]{:S(2)}, u32[]{:S(2)}) collective-permute-start(f32[1,240,128]{2,1,0:T(8,128)S(1)} %get-tuple-element.46), channel_id=1, source_target_pairs={{0,2},{2,4},{4,6},{6,0},{1,3},{3,5},{5,7},{7,1},{8,10},{10,12},{12... | collective-permute-start | bytes 368648 | tf_op jit(solution)/shard_map/ppermute | solution.py:615
  37.2 2.1 %collective-permute-start.11 = (f32[1,240,128]{2,1,0:T(8,128)S(1)}, f32[1,240,128]{2,1,0:T(8,128)S(1)}, u32[]{:S(2)}, u32[]{:S(2)}) collective-permute-start(f32[1,240,128]{2,1,0:T(8,128)S(1)} %get-tuple-element.47), channel_id=1, source_target_pairs={{0,6},{2,0},{4,2},{6,4},{1,7},{3,1},{5,3},{7,5},{8,14},{10,8},{12,... | collective-permute-start | bytes 368648 | tf_op jit(solution)/shard_map/ppermute | solution.py:615
  39.3 0.0 collective-permute-done.12.side_ref
  39.3 4.2 %all-to-all-done.al_ref = f32[32,8,128]{2,1,0:T(8,128)S(1)} async-done(((f32[32,8,128]{2,1,0:T(8,128)}), f32[32,8,128]{2,1,0:T(8,128)S(1)}, u32[]{:S(2)}, u32[]{:S(2)}) %all-to-all-start) | async-done | bytes 131104 | tf_op jit(solution)/shard_map/all_to_all | solution.py:702
  43.5 4.1 %second_lanes_kernel.1 = (f32[1024,128]{1,0:T(8,128)S(1)}, f32[1024,128]{1,0:T(8,128)S(1)}, f32[8,128]{1,0:T(8,128)S(1)}) custom-call(f32[5,12,16,128]{3,2,1,0:T(8,128)S(1)} %get-tuple-element.45.nat_ref, f32[4,320,128]{2,1,0:T(8,128)S(1)} %get-tuple-element.48.rows_ref, f32[1,384,128]{2,1,0:T(8,128)S(1)} %collective-permute-done.12.side_ref, ...), custom_call_target="tpu_custom_call" | custom-call | flops 20000000 | bytes 2949120 | tf_op jit(solution)/shard_map/second_lanes_kernel/pallas_call | solution.py:601
  47.6 0.0 collective-permute-done.10.lo_ref
  47.6 0.0 collective-permute-done.11.hi_ref
  47.6 2.5 %second_rows_kernel.1 = (f32[240,128]{1,0:T(8,128)S(1)}, f32[240,128]{1,0:T(8,128)S(1)}, f32[240,128]{1,0:T(8,128)S(1)}, f32[240,128]{1,0:T(8,128)S(1)}) custom-call(f32[5,12,16,128]{3,2,1,0:T(8,128)S(1)} %get-tuple-element.45.nat_ref, f32[1,240,128]{2,1,0:T(8,128)S(1)} %collective-permute-done.10.lo_ref, f32[1,240,128]{2,1,0:T(8,128)S(1)} %collective-permute-done.11.hi_ref, ...), custom_call_target="tpu_custom_call" | custom-call | flops 10000000 | bytes 3825664 | tf_op jit(solution)/shard_map/second_rows_kernel/pallas_call | solution.py:601
  50.1 1.1 %collective-permute-start.13 = (f32[240,128]{1,0:T(8,128)S(1)}, f32[240,128]{1,0:T(8,128)S(1)}, u32[]{:S(2)}, u32[]{:S(2)}) collective-permute-start(f32[240,128]{1,0:T(8,128)S(1)} %get-tuple-element.56), channel_id=1, source_target_pairs={{0,8},{8,0},{16,24},{24,16},{1,9},{9,1},{17,25},{25,17},{2,10},{10... | collective-permute-start | bytes 368648 | tf_op jit(solution)/shard_map/ppermute | solution.py:619
  51.2 0.8 %collective-permute-start.14 = (f32[240,128]{1,0:T(8,128)S(1)}, f32[240,128]{1,0:T(8,128)S(1)}, u32[]{:S(2)}, u32[]{:S(2)}) collective-permute-start(f32[240,128]{1,0:T(8,128)S(1)} %get-tuple-element.57), channel_id=1, source_target_pairs={{0,16},{8,24},{16,0},{24,8},{1,17},{9,25},{17,1},{25,9},{2,18},{10... | collective-permute-start | bytes 368648 | tf_op jit(solution)/shard_map/ppermute | solution.py:619
  52.1 1.6 %collective-permute-start.15 = (f32[240,128]{1,0:T(8,128)S(1)}, f32[240,128]{1,0:T(8,128)S(1)}, u32[]{:S(2)}, u32[]{:S(2)}) collective-permute-start(f32[240,128]{1,0:T(8,128)S(1)} %get-tuple-element.58), channel_id=1, source_target_pairs={{0,24},{8,16},{16,8},{24,0},{1,25},{9,17},{17,9},{25,1},{2,26},{10... | collective-permute-start | bytes 368648 | tf_op jit(solution)/shard_map/ppermute | solution.py:619
  53.6 2.7 %collective-permute-done.13.refs_1_ = f32[240,128]{1,0:T(8,128)S(1)} collective-permute-done((f32[240,128]{1,0:T(8,128)S(1)}, f32[240,128]{1,0:T(8,128)S(1)}, u32[]{:S(2)}, u32[]{:S(2)}) %collective-permute-start.13) | collective-permute-done | bytes 122912 | tf_op jit(solution)/shard_map/ppermute | solution.py:619
  56.3 2.6 %collective-permute-done.14.refs_2_ = f32[240,128]{1,0:T(8,128)S(1)} collective-permute-done((f32[240,128]{1,0:T(8,128)S(1)}, f32[240,128]{1,0:T(8,128)S(1)}, u32[]{:S(2)}, u32[]{:S(2)}) %collective-permute-start.14) | collective-permute-done | bytes 122912 | tf_op jit(solution)/shard_map/ppermute | solution.py:619
  58.9 0.0 collective-permute-done.15.refs_3_
  58.9 0.9 %close_kernel.1 = f32[1,5,12,16,128]{4,3,2,1,0:T(8,128)} custom-call(f32[240,128]{1,0:T(8,128)S(1)} %get-tuple-element.55.refs_0_, f32[240,128]{1,0:T(8,128)S(1)} %collective-permute-done.13.refs_1_, f32[240,128]{1,0:T(8,128)S(1)} %collective-permute-done.14.refs_2_, f32[240,128]{1,0:T(8,128)S(1)} %collective-permute-done.15.refs_3_), custom_call_target="tpu_custom_call" | custom-call | flops 1000000 | bytes 983040 | tf_op jit(solution)/shard_map/close_kernel/pallas_call | solution.py:601
  (1 shorter events, 0.0 us)
Async XLA Ops:
  0.0 1.0 %copy-start = (f32[1,5,12,16,128]{4,3,2,1,0:T(8,128)S(1)}, f32[1,5,12,16,128]{4,3,2,1,0:T(8,128)}, u32[]{:S(2)}) copy-start(f32[1,5,12,16,128]{4,3,2,1,0:T(8,128)} %u_hbm.1) | copy-start | bytes 1474564
  2.2 9.9 %collective-permute-start.5 = (f32[8,128]{1,0:T(8,128)S(1)}, f32[8,128]{1,0:T(8,128)S(1)}, u32[]{:S(2)}, u32[]{:S(2)}) collective-permute-start(f32[8,128]{1,0:T(8,128)S(1)} %get-tuple-element.37), channel_id=1, source_target_pairs={{0,6},{2,0},{4,2},{6,4},{1,7},{3,1},{5,3},{7,5},{8,14},{10,8},{12,... | collective-permute-start | bytes 12296 | tf_op jit(solution)/shard_map/ppermute | solution.py:615
  7.3 5.4 %collective-permute-start.4 = (f32[8,128]{1,0:T(8,128)S(1)}, f32[8,128]{1,0:T(8,128)S(1)}, u32[]{:S(2)}, u32[]{:S(2)}) collective-permute-start(f32[8,128]{1,0:T(8,128)S(1)} %get-tuple-element.37), channel_id=1, source_target_pairs={{0,4},{2,6},{4,0},{6,2},{1,5},{3,7},{5,1},{7,3},{8,12},{10,14},{12... | collective-permute-start | bytes 12296 | tf_op jit(solution)/shard_map/ppermute | solution.py:615
  7.3 5.6 %collective-permute-start.3 = (f32[8,128]{1,0:T(8,128)S(1)}, f32[8,128]{1,0:T(8,128)S(1)}, u32[]{:S(2)}, u32[]{:S(2)}) collective-permute-start(f32[8,128]{1,0:T(8,128)S(1)} %get-tuple-element.37), channel_id=1, source_target_pairs={{0,2},{2,4},{4,6},{6,0},{1,3},{3,5},{5,7},{7,1},{8,10},{10,12},{12... | collective-permute-start | bytes 12296 | tf_op jit(solution)/shard_map/ppermute | solution.py:615
  8.3 9.6 %collective-permute-start = (f32[1,240,128]{2,1,0:T(8,128)S(1)}, f32[1,240,128]{2,1,0:T(8,128)S(1)}, u32[]{:S(2)}, u32[]{:S(2)}) collective-permute-start(f32[1,240,128]{2,1,0:T(8,128)S(1)} %get-tuple-element.34), channel_id=1, source_target_pairs={{0,2},{2,4},{4,6},{6,0},{1,3},{3,5},{5,7},{7,1},{8,10},{10,12},{12... | collective-permute-start | bytes 368648 | tf_op jit(solution)/shard_map/ppermute | solution.py:615
  10.8 7.1 %collective-permute-start.1 = (f32[1,240,128]{2,1,0:T(8,128)S(1)}, f32[1,240,128]{2,1,0:T(8,128)S(1)}, u32[]{:S(2)}, u32[]{:S(2)}) collective-permute-start(f32[1,240,128]{2,1,0:T(8,128)S(1)} %get-tuple-element.35), channel_id=1, source_target_pairs={{0,6},{2,0},{4,2},{6,4},{1,7},{3,1},{5,3},{7,5},{8,14},{10,8},{12,... | collective-permute-start | bytes 368648 | tf_op jit(solution)/shard_map/ppermute | solution.py:615
  12.1 1.9 %collective-permute-start.2 = (f32[1,384,128]{2,1,0:T(8,128)S(1)}, f32[1,384,128]{2,1,0:T(8,128)S(1)}, u32[]{:S(2)}, u32[]{:S(2)}) collective-permute-start(f32[1,384,128]{2,1,0:T(8,128)S(1)} %get-tuple-element.36), channel_id=1, source_target_pairs={{0,1},{1,0},{2,3},{3,2},{4,5},{5,4},{6,7},{7,6},{8,9},{9,8},{10,11... | collective-permute-start | bytes 589832 | tf_op jit(solution)/shard_map/ppermute | solution.py:615
  12.9 1.2 %collective-permute-start.6 = (f32[8,128]{1,0:T(8,128)S(1)}, f32[8,128]{1,0:T(8,128)S(1)}, u32[]{:S(2)}, u32[]{:S(2)}) collective-permute-start(f32[8,128]{1,0:T(8,128)S(1)} %maximum_maximum_fusion.al_ref), channel_id=1, source_target_pairs={{0,1},{1,0},{2,3},{3,2},{4,5},{5,4},{6,7},{7,6},{8,9},{9,8},{10,11... | collective-permute-start | bytes 12296 | tf_op jit(solution)/shard_map/ppermute | solution.py:615
  17.9 5.5 %copy-start.1 = (f32[5,12,16,128]{3,2,1,0:T(8,128)S(1)}, f32[5,12,16,128]{3,2,1,0:T(8,128)}, u32[]{:S(2)}) copy-start(f32[5,12,16,128]{3,2,1,0:T(8,128)} %init_ref.1) | copy-start | bytes 1474564
  19.8 7.1 %collective-permute-start.7 = (f32[320,128]{1,0:T(8,128)S(1)}, f32[320,128]{1,0:T(8,128)S(1)}, u32[]{:S(2)}, u32[]{:S(2)}) collective-permute-start(f32[320,128]{1,0:T(8,128)S(1)} %get-tuple-element.42), channel_id=1, source_target_pairs={{0,8},{8,0},{16,24},{24,16},{1,9},{9,1},{17,25},{25,17},{2,10},{10... | collective-permute-start | bytes 491528 | tf_op jit(solution)/shard_map/ppermute | solution.py:619
  21.3 9.5 %collective-permute-start.8 = (f32[320,128]{1,0:T(8,128)S(1)}, f32[320,128]{1,0:T(8,128)S(1)}, u32[]{:S(2)}, u32[]{:S(2)}) collective-permute-start(f32[320,128]{1,0:T(8,128)S(1)} %get-tuple-element.43), channel_id=1, source_target_pairs={{0,16},{8,24},{16,0},{24,8},{1,17},{9,25},{17,1},{25,9},{2,18},{10... | collective-permute-start | bytes 491528 | tf_op jit(solution)/shard_map/ppermute | solution.py:619
  22.8 8.0 %collective-permute-start.9 = (f32[320,128]{1,0:T(8,128)S(1)}, f32[320,128]{1,0:T(8,128)S(1)}, u32[]{:S(2)}, u32[]{:S(2)}) collective-permute-start(f32[320,128]{1,0:T(8,128)S(1)} %get-tuple-element.44), channel_id=1, source_target_pairs={{0,24},{8,16},{16,8},{24,0},{1,25},{9,17},{17,9},{25,1},{2,26},{10... | collective-permute-start | bytes 491528 | tf_op jit(solution)/shard_map/ppermute | solution.py:619
  32.7 10.8 %all-to-all-start = ((f32[32,8,128]{2,1,0:T(8,128)}), f32[32,8,128]{2,1,0:T(8,128)S(1)}, u32[]{:S(2)}, u32[]{:S(2)}) async-start(f32[32,8,128]{2,1,0:T(8,128)} %get-tuple-element.50), calls=%async_computation | async-start | bytes 262144 | tf_op jit(solution)/shard_map/all_to_all | solution.py:702
  35.3 4.0 %collective-permute-start.12 = (f32[1,384,128]{2,1,0:T(8,128)S(1)}, f32[1,384,128]{2,1,0:T(8,128)S(1)}, u32[]{:S(2)}, u32[]{:S(2)}) collective-permute-start(f32[1,384,128]{2,1,0:T(8,128)S(1)} %get-tuple-element.49), channel_id=1, source_target_pairs={{0,1},{1,0},{2,3},{3,2},{4,5},{5,4},{6,7},{7,6},{8,9},{9,8},{10,11... | collective-permute-start | bytes 589832 | tf_op jit(solution)/shard_map/ppermute | solution.py:615
  35.5 12.1 %collective-permute-start.10 = (f32[1,240,128]{2,1,0:T(8,128)S(1)}, f32[1,240,128]{2,1,0:T(8,128)S(1)}, u32[]{:S(2)}, u32[]{:S(2)}) collective-permute-start(f32[1,240,128]{2,1,0:T(8,128)S(1)} %get-tuple-element.46), channel_id=1, source_target_pairs={{0,2},{2,4},{4,6},{6,0},{1,3},{3,5},{5,7},{7,1},{8,10},{10,12},{12... | collective-permute-start | bytes 368648 | tf_op jit(solution)/shard_map/ppermute | solution.py:615
  37.2 10.4 %collective-permute-start.11 = (f32[1,240,128]{2,1,0:T(8,128)S(1)}, f32[1,240,128]{2,1,0:T(8,128)S(1)}, u32[]{:S(2)}, u32[]{:S(2)}) collective-permute-start(f32[1,240,128]{2,1,0:T(8,128)S(1)} %get-tuple-element.47), channel_id=1, source_target_pairs={{0,6},{2,0},{4,2},{6,4},{1,7},{3,1},{5,3},{7,5},{8,14},{10,8},{12,... | collective-permute-start | bytes 368648 | tf_op jit(solution)/shard_map/ppermute | solution.py:615
  50.1 6.3 %collective-permute-start.13 = (f32[240,128]{1,0:T(8,128)S(1)}, f32[240,128]{1,0:T(8,128)S(1)}, u32[]{:S(2)}, u32[]{:S(2)}) collective-permute-start(f32[240,128]{1,0:T(8,128)S(1)} %get-tuple-element.56), channel_id=1, source_target_pairs={{0,8},{8,0},{16,24},{24,16},{1,9},{9,1},{17,25},{25,17},{2,10},{10... | collective-permute-start | bytes 368648 | tf_op jit(solution)/shard_map/ppermute | solution.py:619
  51.2 7.7 %collective-permute-start.14 = (f32[240,128]{1,0:T(8,128)S(1)}, f32[240,128]{1,0:T(8,128)S(1)}, u32[]{:S(2)}, u32[]{:S(2)}) collective-permute-start(f32[240,128]{1,0:T(8,128)S(1)} %get-tuple-element.57), channel_id=1, source_target_pairs={{0,16},{8,24},{16,0},{24,8},{1,17},{9,25},{17,1},{25,9},{2,18},{10... | collective-permute-start | bytes 368648 | tf_op jit(solution)/shard_map/ppermute | solution.py:619
  52.1 6.8 %collective-permute-start.15 = (f32[240,128]{1,0:T(8,128)S(1)}, f32[240,128]{1,0:T(8,128)S(1)}, u32[]{:S(2)}, u32[]{:S(2)}) collective-permute-start(f32[240,128]{1,0:T(8,128)S(1)} %get-tuple-element.58), channel_id=1, source_target_pairs={{0,24},{8,16},{16,8},{24,0},{1,25},{9,17},{17,9},{25,1},{2,26},{10... | collective-permute-start | bytes 368648 | tf_op jit(solution)/shard_map/ppermute | solution.py:619

commit v7 on v6

--- a/solution.py
+++ b/solution.py
@@ -180,16 +180,21 @@
     def natural(self, ref, b):
         return self.whole(ref, b) if b < self.comps else self.leftovers(ref, *self.pair(b))
 
-    def put_natural(self, ref, b, value):
-        if b < self.comps:
-            ref[b, pl.ds(0, self.per)] = value.reshape(self.per, self.ny, self.nz)
-            return
+    def put_whole(self, ref, c, value):
+        ref[c, pl.ds(0, self.per)] = value.reshape(self.per, self.ny, self.nz)
+
+    def put_leftovers(self, ref, b, value):
         at = pl.ds(self.per, self.left)
         shape = (self.left, self.ny, self.nz)
         first, second = self.pair(b)
+        ref[second, at] = value[self.half :].reshape(shape)
         ref[first, at] = value[: self.half].reshape(shape)
-        if second != first:
-            ref[second, at] = value[self.half :].reshape(shape)
+
+    def put_natural(self, ref, b, value):
+        if b < self.comps:
+            self.put_whole(ref, b, value)
+        else:
+            self.put_leftovers(ref, b, value)
 
     def row(self, c, i, t):
         if i < self.per:
@@ -249,8 +254,21 @@
     return tile
 
 
-def open_kernel(u_hbm, u_ref, lo_ref, hi_ref, side_ref, al_ref, sems):
+def spread(tile, al_ref):
+    def step(i, carry):
+        al_ref[i] = tile
+        return carry
+
+    lax.fori_loop(0, al_ref.shape[0], step, 0)
+
+
+def open_kernel(u_hbm, *refs):
+    parts, (al_ref, u_ref, ring, sems) = refs[:-4], refs[-4:]
+    nodes = len(parts)
     comps, nx, ny, nz = u_ref.shape
+    blocks = Blocks(comps, nx, ny, nz)
+    width = nz // nodes
+    me = lax.axis_index("node")
     chunks = sems.shape[0]
     size = nx // chunks
     copies = []
@@ -266,36 +284,11 @@
     for n in range(chunks):
         copies[n].wait()
         best = faster(best, read, n * size, size, comps)
-    al_ref[...] = alpha_tile(best, nz)
-    write_edges(read, nx, ny, comps, lo_ref, hi_ref, side_ref)
-
-
-def turn_kernel(u_ref, rows_ref):
-    blocks = Blocks(*u_ref.shape)
-    nz = blocks.nz
+    tile = alpha_tile(best, nz)
+    spread(jnp.where(lane_index(tile.shape) // width == me, tile, 0.0), al_ref)
+    quarters = [me ^ k for k in range(nodes)]
     for b in range(blocks.count):
-        value = blocks.natural(u_ref, b).T
-        rows_ref[b, pl.ds(HALO, nz), :] = value
-        rows_ref[b, pl.ds(0, HALO), :] = value[nz - HALO :]
-        rows_ref[b, pl.ds(HALO + nz, HALO), :] = value[:HALO]
-
-
-def start_kernel(init_ref, rows_ref, pack_ref, turned_ref, *, nodes):
-    comps, nx, ny, nz = init_ref.shape
-    blocks = Blocks(comps, nx, ny, nz)
-    width = nz // nodes
-    me = lax.axis_index("node")
-    lanes = lane_index((ny, nz)) // width
-    for b in range(blocks.count):
-        send_quarter(blocks.natural(init_ref, b).T, turned_ref, b, [rows_ref], [me], width)
-
-    def step(c, carry):
-        for q in range(nx // nodes):
-            pieces = [turned(init_ref[c, q * nodes + i], width * (i - me)) for i in range(nodes)]
-            pack_ref[rows_at((c * (nx // nodes) + q) * ny, ny), :] = merged(pieces, lanes)
-        return carry
-
-    lax.fori_loop(0, comps, step, 0)
+        send_quarter(blocks.natural(u_ref, b).T, ring, b, parts, quarters, width)
 
 
 def send_quarter(value, ring_ref, b, parts, quarters, width):
@@ -309,42 +302,40 @@
         part[rows_at(b * size, size), :] = ring_ref[pl.ds(base + (TILE - HALO) + quarter * width, size), :]
 
 
-def blend_kernel(start_ref, *refs):
-    nodes = len(refs) - 6
-    parts, (rows_ref, nat_ref, lo_ref, hi_ref, side_ref, al_ref) = refs[:nodes], refs[nodes:]
+def start_kernel(init_ref, rows_ref, pack_ref, turned_ref, *, nodes):
+    comps, nx, ny, nz = init_ref.shape
+    blocks = Blocks(comps, nx, ny, nz)
+    width = nz // nodes
+    me = lax.axis_index("node")
+    lanes = lane_index((ny, nz)) // width
+    for b in range(blocks.count):
+        turned_ref[rows_at(b * nz, nz), :] = blocks.natural(init_ref, b).T
+        rows_ref[rows_at(b * width, width), :] = turned_ref[rows_at(b * nz + me * width, width), :]
+
+    def step(c, carry):
+        for q in range(nx // nodes):
+            pieces = [turned(init_ref[c, q * nodes + i], width * (i - me)) for i in range(nodes)]
+            pack_ref[rows_at((c * (nx // nodes) + q) * ny, ny), :] = merged(pieces, lanes)
+        return carry
+
+    lax.fori_loop(0, comps, step, 0)
+
+
+def gather_kernel(*refs):
+    parts, (rows_ref, nat_ref, lo_ref, hi_ref, side_ref) = refs[:-5], refs[-5:]
+    nodes = len(parts)
     comps, nx, ny, nz = nat_ref.shape
     blocks = Blocks(comps, nx, ny, nz)
     width = nz // nodes
     size = width + 8
     me = lax.axis_index("node")
-    weights = [
-        [by_node(me, [scaled_weight(m, n ^ k) for n in range(nodes)]) for k in range(nodes)] for m in range(nodes)
-    ]
+    for k in range(nodes):
+        rows_ref[me ^ k] = parts[k][...]
     for b in range(blocks.count):
-        at = pl.ds(b * size, size)
-        start = start_ref[at, :]
-        rates = [part[at, :] for part in parts]
-        for m in range(nodes):
-            value = start
-            for k in range(nodes):
-                value = value + weights[m][k] * rates[k]
-            rows_ref[m, at, :] = value
         own = pl.ds(b * size + HALO, width)
         state = jnp.concatenate([rows_ref[m, own, :] for m in range(nodes)], axis=0)
         blocks.put_natural(nat_ref, b, state.T)
-
-    def read(c, i):
-        return nat_ref[c, i]
-
-    best = tuple(jnp.zeros((ny, nz), jnp.float32) for _ in range(3))
-    tile = alpha_tile(faster(best, read, 0, nx, comps), width)
-
-    def spread(i, carry):
-        al_ref[i] = tile
-        return carry
-
-    lax.fori_loop(0, al_ref.shape[0], spread, 0)
-    write_edges(read, nx, ny, comps, lo_ref, hi_ref, side_ref)
+    write_edges(lambda c, i: nat_ref[c, i], nx, ny, comps, lo_ref, hi_ref, side_ref)
 
 
 def along_second(u, alphas, side_ref, dims, fy, yp, ym, gp, gm):
@@ -456,50 +447,8 @@
     return [tile[k : k + 1, :] for k in range(3)]
 
 
-def first_lanes_kernel(u_ref, rows_ref, side_ref, al_ref, other_ref, fz, fy, al_out, zp, zm, yp, ym, gp, gm):
-    dims = u_ref.shape
-    blocks = Blocks(*dims)
-    tile = jnp.maximum(al_ref[...], other_ref[...])
-    al_out[...] = tile
-    alphas = tile_rows(tile)
-    along_second(lambda c, i: u_ref[c, i], alphas, side_ref, dims, fy, yp, ym, gp, gm)
-
-    def depth(n, carry):
-        at = rows_at(n * CHUNK, blocks.step)
-
-        def write(b, plus, minus):
-            to = rows_at((b * TILE + n) * blocks.step, blocks.step)
-            zp[to, :] = plus
-            zm[to, :] = minus
-
-        split_depth(blocks, lambda b: rows_ref[b, at, :], alphas[2], write)
-        return carry
-
-    lax.fori_loop(0, TILE, depth, 0, unroll=4)
-    along_last(blocks, zp, zm, fz, lambda b: None)
-
-
-def first_rows_kernel(u_ref, lo_ref, hi_ref, al_ref, fz, fy, *refs):
-    parts, (rate, xp, xm, ring) = refs[:-4], refs[-4:]
-    nodes = len(parts)
-    blocks = Blocks(*u_ref.shape)
-    nz = blocks.nz
-    me = lax.axis_index("node")
-    quarters = [me ^ k for k in range(nodes)]
-
-    def send(value, b):
-        value = value.T + fz[rows_at(b * nz, nz), :]
-        send_quarter(value, ring, b, parts, quarters, nz // nodes)
-
-    def after(c):
-        send(blocks.whole(rate, c), c)
-        b = blocks.comps + c // 2
-        send(blocks.leftovers(rate, *blocks.pair(b)), b)
-
-    along_first(lambda c, i: u_ref[c, i], tile_rows(al_ref), lo_ref, hi_ref, fy, rate, xp, xm, None, after)
-
-
-def second_lanes_kernel(nat_ref, rows_ref, side_ref, al_ref, fz, fy, al_out, zp, zm, yp, ym, gp, gm, back):
+def along_lanes(nat_ref, rows_ref, side_ref, al_ref, fz, fy, al_out, scratch, after):
+    zp, zm, yp, ym, gp, gm = scratch
     nodes = rows_ref.shape[0]
     dims = nat_ref.shape
     blocks = Blocks(*dims)
@@ -530,12 +479,71 @@
             return carry
 
         lax.fori_loop(0, each, depth, 0, unroll=True)
+    along_last(blocks, zp, zm, fz, after)
+
+
+def first_lanes_kernel(nat_ref, rows_ref, side_ref, al_ref, fz, fy, al_out, *scratch):
+    along_lanes(nat_ref, rows_ref, side_ref, al_ref, fz, fy, al_out, scratch, lambda b: None)
+
+
+def second_lanes_kernel(
+    nat_ref, own_ref, before_ref, behind_ref, side_ref, al_ref, fz, fy, al_out, back, rows_ref, *scratch
+):
+    nodes = own_ref.shape[0]
+    blocks = Blocks(*nat_ref.shape)
+    nz = blocks.nz
+    width = nz // nodes
+    size = width + 8
+    for m in range(nodes):
+        rows_ref[m] = own_ref[m]
+        for b in range(blocks.count):
+            ghost = pl.ds((m * blocks.count + b) * 4, HALO)
+            rows_ref[m, pl.ds(b * size, HALO), :] = before_ref[ghost, :]
+            rows_ref[m, pl.ds(b * size + HALO + width, HALO), :] = behind_ref[ghost, :]
 
     def after(b):
         at = rows_at(b * nz, nz)
         fz[at, :] = back[at, :].T
 
-    along_last(blocks, zp, zm, back, after)
+    along_lanes(nat_ref, rows_ref, side_ref, al_ref, back, fy, al_out, scratch, after)
+
+
+def first_rows_kernel(nat_in, lo_in, hi_in, al_in, fz, fy, start_ref, *refs):
+    rows_ref, nat_ref, lo_ref, hi_ref, side_ref, first_ref, last_ref, al_ref, rate, xp, xm = refs
+    nodes = rows_ref.shape[0]
+    comps, nx, ny, nz = nat_ref.shape
+    blocks = Blocks(comps, nx, ny, nz)
+    width = nz // nodes
+    size = width + 8
+
+    def state(value, b):
+        rates = value.T + fz[rows_at(b * nz, nz), :]
+        start = start_ref[rows_at(b * width, width), :]
+        states = []
+        for m in range(nodes):
+            new = start
+            for n in range(nodes):
+                new = new + scaled_weight(m, n) * rates[n * width : (n + 1) * width]
+            rows_ref[m, pl.ds(b * size + HALO, width), :] = new
+            ghost = pl.ds((m * blocks.count + b) * 4, HALO)
+            first_ref[ghost, :] = new[:HALO]
+            last_ref[ghost, :] = new[width - HALO :]
+            states.append(new)
+        return jnp.concatenate(states, axis=0).T
+
+    def after(c):
+        blocks.put_whole(nat_ref, c, state(blocks.whole(rate, c), c))
+        b = blocks.comps + c // 2
+        blocks.put_leftovers(nat_ref, b, state(blocks.leftovers(rate, *blocks.pair(b)), b))
+
+    along_first(lambda c, i: nat_in[c, i], tile_rows(al_in), lo_in, hi_in, fy, rate, xp, xm, None, after)
+
+    def read(c, i):
+        return nat_ref[c, i]
+
+    best = tuple(jnp.zeros((ny, nz), jnp.float32) for _ in range(3))
+    spread(alpha_tile(faster(best, read, 0, nx, comps), width), al_ref)
+    write_edges(read, nx, ny, comps, lo_ref, hi_ref, side_ref)
 
 
 def second_rows_kernel(nat_ref, lo_ref, hi_ref, al_ref, fz, fy, pack_ref, *refs):
@@ -628,15 +636,6 @@
     return lower, upper, side
 
 
-def largest(tile):
-    if lax.axis_size("gx") > 4 or lax.axis_size("gy") > 2:
-        tile = lax.pmax(tile, ("gx", "gy"))
-        return tile, tile
-    others = [shifted(tile, "gx", by) for by in range(1, lax.axis_size("gx"))]
-    tile = functools.reduce(jnp.maximum, others, tile)
-    return tile, shifted(tile, "gy", 1)
-
-
 def exchanged(parts):
     moved = {k: swapped(parts[k], k) for k in sorted(range(1, len(parts)), reverse=True)}
     return [parts[0]] + [moved[k] for k in range(1, len(parts))]
@@ -645,6 +644,7 @@
 def local(initial, guesses):
     comps, nx, ny, nz = initial.shape
     nodes = lax.axis_size("node")
+    everyone = ("node", "gx", "gy")
     devices = nodes * lax.axis_size("gx") * lax.axis_size("gy")
     rows = -(-comps * nx // TILE) * TILE
     blocks = Blocks(comps, nx, ny, nz)
@@ -653,59 +653,62 @@
     edge = (1, comps * HALO * ny, nz)
     edges = [edge, edge, (1, 2 * HALO * rows, nz)]
     tile_shape = (TILE, nz)
+    tiles_shape = (devices,) + tile_shape
     part = (blocks.count * (width + 8), nz)
     pack = (comps * nx // nodes * ny, nz)
-    across_shape = (ny * rows, nz)
+    ghost = (nodes * blocks.count * 4, nz)
     depth_shape = (blocks.count * nz, nz)
-    padded = [(blocks.count * TILE * blocks.step, nz)] * 2 + [(ny * rows, nz)] * 2 + [(2 * HALO * rows, nz)] * 2
+    lanes_out = [depth_shape, (ny * rows, nz), tile_shape]
+    lanes_scratch = [(blocks.count * TILE * blocks.step, nz)] * 2 + [(ny * rows, nz)] * 2 + [(2 * HALO * rows, nz)] * 2
     slabs = [initial.shape] + [(nx + 2 * HALO, comps * ny, nz)] * 2
     ring = (blocks.count * (nz + 2 * TILE), nz)
     chunks = 4 if nx % 4 == 0 else 1
 
-    field, lo, hi, side, tile = call(
+    *parts, tile = call(
         open_kernel,
         "open_kernel",
-        [initial.shape] + edges + [tile_shape],
+        [part] * nodes + [tiles_shape],
         [guesses],
-        [pltpu.SemaphoreType.DMA((chunks,))],
+        [initial.shape, ring, pltpu.SemaphoreType.DMA((chunks,))],
         anywhere=True,
     )
+    tiles = lax.all_to_all(tile, everyone, 0, 0)
+    start, start_pack = call(
+        functools.partial(start_kernel, nodes=nodes),
+        "start_kernel",
+        [(blocks.count * width, nz), pack],
+        [initial],
+        [depth_shape],
+    )
+    turned_field, field, lo, hi, side = call(
+        gather_kernel, "gather_kernel", [(nodes,) + part, initial.shape] + edges, exchanged(parts)
+    )
     lower, upper, side = neighbours(lo, hi, side)
-    tile, other = largest(tile)
-    (turned_field,) = call(turn_kernel, "turn_kernel", [(blocks.count, nz + 8, nz)], [field])
-    start, start_pack = call(
-        functools.partial(start_kernel, nodes=nodes), "start_kernel", [part, pack], [initial], [ring]
-    )
     depth, across, tile = call(
         first_lanes_kernel,
         "first_lanes_kernel",
-        [depth_shape, across_shape, tile_shape],
-        [field, turned_field, side, tile, other],
-        padded,
+        lanes_out,
+        [field, turned_field, side, tiles],
+        lanes_scratch,
         20_000_000,
     )
-    parts = call(
+    turned_field, field, lo, hi, side, first, last, tile = call(
         first_rows_kernel,
         "first_rows_kernel",
-        [part] * nodes,
-        [field, lower, upper, tile, depth, across],
-        slabs + [ring],
+        [(nodes,) + part, initial.shape] + edges + [ghost, ghost, tiles_shape],
+        [field, lower, upper, tile, depth, across, start],
+        slabs,
         10_000_000,
     )
-    turned_field, field, lo, hi, side, tile = call(
-        blend_kernel,
-        "blend_kernel",
-        [(nodes,) + part, initial.shape] + edges + [(devices,) + tile_shape],
-        [start] + exchanged(parts),
-    )
+    tiles = lax.all_to_all(tile, everyone, 0, 0)
     lower, upper, side = neighbours(lo, hi, side)
-    tiles = lax.all_to_all(tile, ("node", "gx", "gy"), 0, 0)
+    before, behind = shifted(last, "node", 1), shifted(first, "node", -1)
     depth, across, tile = call(
         second_lanes_kernel,
         "second_lanes_kernel",
-        [depth_shape, across_shape, tile_shape],
-        [field, turned_field, side, tiles],
-        padded + [depth_shape],
+        lanes_out,
+        [field, turned_field, before, behind, side, tiles],
+        [depth_shape, (nodes,) + part] + lanes_scratch,
         20_000_000,
     )
     outs = call(

time: 60 us -> 60.1 us (level)
  waiting for transfers between devices: 18 us -> 12 us
  starting transfers between devices: 23.6 us -> 28.5 us
  Pallas kernels: 17.1 us -> 18.3 us
    all_to_all x1 -> x2, starting transfers between devices: 2.58 us -> 9.35 us  [local(): tiles = lax.all_to_all(tile, everyone, 0, 0)]
    ppermute x6, waiting for transfers between devices: 12.1 us -> 6.67 us  [swapped(): lax.ppermute(value, 'node', [(i, i ^ by) for i in range(lax.axis_size('no...]
    ppermute x10 -> x8, starting transfers between devices: 13.9 us -> 11 us  [shifted(): lax.ppermute(value, axis, [(i, (i + by) % count) for i in range(count)])]
    all_to_all x1 -> x2, waiting for transfers between devices: 4.18 us -> 1.83 us  [local(): tiles = lax.all_to_all(tile, everyone, 0, 0)]
    ppermute x10 -> x8, waiting for transfers between devices: 1.73 us -> 3.48 us  [shifted(): lax.ppermute(value, axis, [(i, (i + by) % count) for i in range(count)])]
    pallas_call x9 -> x8, Pallas kernels: 17.1 us -> 18.3 us  [call(): pl.pallas_call(kernel, out_shape=[jax.ShapeDtypeStruct(shape, jnp.float32...]
    ppermute x6, starting transfers between devices: 7.1 us -> 8.09 us  [swapped(): lax.ppermute(value, 'node', [(i, i ^ by) for i in range(lax.axis_size('no...]
  transfers between devices with their start and end apart: 17 -> 16, of which waited for: 8 -> 6; matrix products, arithmetic and copies ran while one was open for 0% -> 0% of each run, Pallas kernels for 15% -> 15%
where the time goes in v7:
time: 60.1 us; the launch traced here: 59.9 us
  starting transfers between devices  28.5 us (47%)
  Pallas kernels  18.3 us (30%)
  waiting for transfers between devices  12 us (20%)
  local copies, waits for them, and re-layouts  1.04 us (2%)
    pallas_call x8, Pallas kernels, call(): pl.pallas_call(kernel, out_shape=[jax.ShapeDtypeStruct(shape, jnp.float32...  18.3 us
    ppermute x8, starting transfers between devices, shifted(): lax.ppermute(value, axis, [(i, (i + by) % count) for i in range(count)])  11 us
    all_to_all x2, starting transfers between devices, local(): tiles = lax.all_to_all(tile, everyone, 0, 0)  9.35 us
    ppermute x6, starting transfers between devices, swapped(): lax.ppermute(value, 'node', [(i, i ^ by) for i in range(lax.axis_size('no...  8.09 us
    ppermute x6, waiting for transfers between devices, swapped(): lax.ppermute(value, 'node', [(i, i ^ by) for i in range(lax.axis_size('no...  6.67 us
    ppermute x8, waiting for transfers between devices, shifted(): lax.ppermute(value, axis, [(i, (i + by) % count) for i in range(count)])  3.48 us
    all_to_all x2, waiting for transfers between devices, local(): tiles = lax.all_to_all(tile, everyone, 0, 0)  1.83 us
  transfers between devices with their start and end apart: 16, of which 6 were waited for; matrix products, arithmetic and copies ran while one was open for 0% of the time, Pallas kernels for 15%

profile of v7, /device:TPU:0, one launch (start us, length us, event | category | flops | bytes accessed | tf_op | source)
XLA Modules:
  0.0 59.9 jit_solution(9177040925946692581)
XLA Ops:
  0.0 0.0 copy-start
  0.0 1.0 %copy-done = f32[1,5,12,16,128]{4,3,2,1,0:T(8,128)S(1)} copy-done((f32[1,5,12,16,128]{4,3,2,1,0:T(8,128)S(1)}, f32[1,5,12,16,128]{4,3,2,1,0:T(8,128)}, u32[]{:S(2)}) %copy-start) | copy-done | bytes 491544
  1.0 1.8 %open_kernel.1 = (f32[320,128]{1,0:T(8,128)S(1)}, f32[320,128]{1,0:T(8,128)S(1)}, f32[320,128]{1,0:T(8,128)S(1)}, f32[320,128]{1,0:T(8,128)S(1)}, f32[32,8,128]{2,1,0:T(8,128)}) custom-call(f32[1,5,12,16,128]{4,3,2,1,0:T(8,128)S(1)} %copy-done), custom_call_target="tpu_custom_call" | custom-call | flops 1000000 | bytes 983040 | tf_op jit(solution)/shard_map/open_kernel/pallas_call | solution.py:609
  2.8 0.0 copy-start.1
  2.8 3.0 %collective-permute-start = (f32[320,128]{1,0:T(8,128)S(1)}, f32[320,128]{1,0:T(8,128)S(1)}, u32[]{:S(2)}, u32[]{:S(2)}) collective-permute-start(f32[320,128]{1,0:T(8,128)S(1)} %get-tuple-element.36), channel_id=1, source_target_pairs={{0,8},{8,0},{16,24},{24,16},{1,9},{9,1},{17,25},{25,17},{2,10},{10... | collective-permute-start | bytes 491528 | tf_op jit(solution)/shard_map/ppermute | solution.py:627
  5.8 1.5 %collective-permute-start.1 = (f32[320,128]{1,0:T(8,128)S(1)}, f32[320,128]{1,0:T(8,128)S(1)}, u32[]{:S(2)}, u32[]{:S(2)}) collective-permute-start(f32[320,128]{1,0:T(8,128)S(1)} %get-tuple-element.37), channel_id=1, source_target_pairs={{0,16},{8,24},{16,0},{24,8},{1,17},{9,25},{17,1},{25,9},{2,18},{10... | collective-permute-start | bytes 491528 | tf_op jit(solution)/shard_map/ppermute | solution.py:627
  7.3 0.0 collective-permute-start.2
  7.3 6.3 %all-to-all-start = ((f32[32,8,128]{2,1,0:T(8,128)}), f32[32,8,128]{2,1,0:T(8,128)S(1)}, u32[]{:S(2)}, u32[]{:S(2)}) async-start(f32[32,8,128]{2,1,0:T(8,128)} %get-tuple-element.44), calls=%async_computation | async-start | bytes 262144 | tf_op jit(solution)/shard_map/all_to_all | solution.py:675
  13.7 0.0 collective-permute-done.refs_1_
  13.7 1.3 %collective-permute-done.1.refs_2_ = f32[320,128]{1,0:T(8,128)S(1)} collective-permute-done((f32[320,128]{1,0:T(8,128)S(1)}, f32[320,128]{1,0:T(8,128)S(1)}, u32[]{:S(2)}, u32[]{:S(2)}) %collective-permute-start.1) | collective-permute-done | bytes 163872 | tf_op jit(solution)/shard_map/ppermute | solution.py:627
  15.0 0.0 collective-permute-done.2.refs_3_
  15.0 0.4 gather_kernel.1
  15.4 0.1 collective-permute-start.5
  15.5 1.6 %collective-permute-start.3 = (f32[1,240,128]{2,1,0:T(8,128)S(1)}, f32[1,240,128]{2,1,0:T(8,128)S(1)}, u32[]{:S(2)}, u32[]{:S(2)}) collective-permute-start(f32[1,240,128]{2,1,0:T(8,128)S(1)} %get-tuple-element.40), channel_id=1, source_target_pairs={{0,2},{2,4},{4,6},{6,0},{1,3},{3,5},{5,7},{7,1},{8,10},{10,12},{12... | collective-permute-start | bytes 368648 | tf_op jit(solution)/shard_map/ppermute | solution.py:623
  17.1 2.2 %collective-permute-start.4 = (f32[1,240,128]{2,1,0:T(8,128)S(1)}, f32[1,240,128]{2,1,0:T(8,128)S(1)}, u32[]{:S(2)}, u32[]{:S(2)}) collective-permute-start(f32[1,240,128]{2,1,0:T(8,128)S(1)} %get-tuple-element.41), channel_id=1, source_target_pairs={{0,6},{2,0},{4,2},{6,4},{1,7},{3,1},{5,3},{7,5},{8,14},{10,8},{12,... | collective-permute-start | bytes 368648 | tf_op jit(solution)/shard_map/ppermute | solution.py:623
  19.3 0.0 copy-done.1
  19.3 0.7 %start_kernel.1 = (f32[256,128]{1,0:T(8,128)S(1)}, f32[240,128]{1,0:T(8,128)S(1)}) custom-call(f32[5,12,16,128]{3,2,1,0:T(8,128)S(1)} %copy-done.1), custom_call_target="tpu_custom_call" | custom-call | flops 1000000 | bytes 983040 | tf_op jit(solution)/shard_map/start_kernel/pallas_call | solution.py:609
  20.0 1.8 %all-to-all-done.al_ref = f32[32,8,128]{2,1,0:T(8,128)S(1)} async-done(((f32[32,8,128]{2,1,0:T(8,128)}), f32[32,8,128]{2,1,0:T(8,128)S(1)}, u32[]{:S(2)}, u32[]{:S(2)}) %all-to-all-start) | async-done | bytes 131104 | tf_op jit(solution)/shard_map/all_to_all | solution.py:675
  21.8 0.0 collective-permute-done.5.side_ref
  21.8 4.0 %first_lanes_kernel.1 = (f32[1024,128]{1,0:T(8,128)S(1)}, f32[1024,128]{1,0:T(8,128)S(1)}, f32[8,128]{1,0:T(8,128)S(1)}) custom-call(f32[5,12,16,128]{3,2,1,0:T(8,128)S(1)} %get-tuple-element.39.nat_ref.nat_in, f32[4,320,128]{2,1,0:T(8,128)S(1)} %get-tuple-element.42.rows_ref, f32[1,384,128]{2,1,0:T(8,128)S(1)} %collective-permute-done.5.side_ref, ...), custom_call_target="tpu_custom_call" | custom-call | flops 20000000 | bytes 2949120 | tf_op jit(solution)/shard_map/first_lanes_kernel/pallas_call | solution.py:609
  25.8 0.0 collective-permute-done.3.lo_in
  25.8 0.0 collective-permute-done.4.hi_in
  25.8 4.0 %first_rows_kernel.1 = (f32[4,320,128]{2,1,0:T(8,128)S(1)}, f32[5,12,16,128]{3,2,1,0:T(8,128)S(1)}, f32[1,240,128]{2,1,0:T(8,128)S(1)}, f32[1,240,128]{2,1,0:T(8...) custom-call(f32[5,12,16,128]{3,2,1,0:T(8,128)S(1)} %get-tuple-elemen, ...), custom_call_target="tpu_custom_call" | custom-call | flops 10000000 | bytes 3842048 | tf_op jit(solution)/shard_map/first_rows_kernel/pallas_call | solution.py:609
  29.8 3.0 %all-to-all-start.1 = ((f32[32,8,128]{2,1,0:T(8,128)}), f32[32,8,128]{2,1,0:T(8,128)S(1)}, u32[]{:S(2)}, u32[]{:S(2)}) async-start(f32[32,8,128]{2,1,0:T(8,128)} %get-tuple-element.56), calls=%async_computation.1 | async-start | bytes 262144 | tf_op jit(solution)/shard_map/all_to_all | solution.py:703
  32.9 0.3 collective-permute-start.10
  33.2 1.7 %collective-permute-start.6 = (f32[1,240,128]{2,1,0:T(8,128)S(1)}, f32[1,240,128]{2,1,0:T(8,128)S(1)}, u32[]{:S(2)}, u32[]{:S(2)}) collective-permute-start(f32[1,240,128]{2,1,0:T(8,128)S(1)} %get-tuple-element.50), channel_id=1, source_target_pairs={{0,2},{2,4},{4,6},{6,0},{1,3},{3,5},{5,7},{7,1},{8,10},{10,12},{12... | collective-permute-start | bytes 368648 | tf_op jit(solution)/shard_map/ppermute | solution.py:623
  34.9 2.1 %collective-permute-start.7 = (f32[1,240,128]{2,1,0:T(8,128)S(1)}, f32[1,240,128]{2,1,0:T(8,128)S(1)}, u32[]{:S(2)}, u32[]{:S(2)}) collective-permute-start(f32[1,240,128]{2,1,0:T(8,128)S(1)} %get-tuple-element.51), channel_id=1, source_target_pairs={{0,6},{2,0},{4,2},{6,4},{1,7},{3,1},{5,3},{7,5},{8,14},{10,8},{12,... | collective-permute-start | bytes 368648 | tf_op jit(solution)/shard_map/ppermute | solution.py:623
  37.0 1.7 %collective-permute-start.8 = (f32[128,128]{1,0:T(8,128)S(1)}, f32[128,128]{1,0:T(8,128)S(1)}, u32[]{:S(2)}, u32[]{:S(2)}) collective-permute-start(f32[128,128]{1,0:T(8,128)S(1)} %get-tuple-element.53), channel_id=1, source_target_pairs={{0,8},{8,16},{16,24},{24,0},{1,9},{9,17},{17,25},{25,1},{2,10},{10... | collective-permute-start | bytes 196616 | tf_op jit(solution)/shard_map/ppermute | solution.py:623
  38.7 1.2 %collective-permute-start.9 = (f32[128,128]{1,0:T(8,128)S(1)}, f32[128,128]{1,0:T(8,128)S(1)}, u32[]{:S(2)}, u32[]{:S(2)}) collective-permute-start(f32[128,128]{1,0:T(8,128)S(1)} %get-tuple-element.54), channel_id=1, source_target_pairs={{0,24},{8,0},{16,8},{24,16},{1,25},{9,1},{17,9},{25,17},{2,26},{10... | collective-permute-start | bytes 196616 | tf_op jit(solution)/shard_map/ppermute | solution.py:623
  39.9 2.9 %collective-permute-done.8.before_ref = f32[128,128]{1,0:T(8,128)S(1)} collective-permute-done((f32[128,128]{1,0:T(8,128)S(1)}, f32[128,128]{1,0:T(8,128)S(1)}, u32[]{:S(2)}, u32[]{:S(2)}) %collective-permute-start.8) | collective-permute-done | bytes 65568 | tf_op jit(solution)/shard_map/ppermute | solution.py:623
  42.8 0.6 %collective-permute-done.9.behind_ref = f32[128,128]{1,0:T(8,128)S(1)} collective-permute-done((f32[128,128]{1,0:T(8,128)S(1)}, f32[128,128]{1,0:T(8,128)S(1)}, u32[]{:S(2)}, u32[]{:S(2)}) %collective-permute-start.9) | collective-permute-done | bytes 65568 | tf_op jit(solution)/shard_map/ppermute | solution.py:623
  43.4 0.0 collective-permute-done.10.side_ref
  43.4 0.0 all-to-all-done.1.al_ref
  43.4 4.1 %second_lanes_kernel.1 = (f32[1024,128]{1,0:T(8,128)S(1)}, f32[1024,128]{1,0:T(8,128)S(1)}, f32[8,128]{1,0:T(8,128)S(1)}) custom-call(f32[5,12,16,128]{3,2,1,0:T(8,128)S(1)} %get-tuple-element.49.nat_ref, f32[4,320,128]{2,1,0:T(8,128)S(1)} %get-tuple-element.52.own_ref, f32[128,128]{1,0:T(8,128)S(1)} %collective-permute-done.8.before_ref, ...), custom_call_target="tpu_custom_call" | custom-call | flops 20000000 | bytes 3211264 | tf_op jit(solution)/shard_map/second_lanes_kernel/pallas_call | solution.py:609
  47.5 0.0 collective-permute-done.6.lo_ref
  47.5 0.0 collective-permute-done.7.hi_ref
  47.6 2.5 %second_rows_kernel.1 = (f32[240,128]{1,0:T(8,128)S(1)}, f32[240,128]{1,0:T(8,128)S(1)}, f32[240,128]{1,0:T(8,128)S(1)}, f32[240,128]{1,0:T(8,128)S(1)}) custom-call(f32[5,12,16,128]{3,2,1,0:T(8,128)S(1)} %get-tuple-element.49.nat_ref, f32[1,240,128]{2,1,0:T(8,128)S(1)} %collective-permute-done.6.lo_ref, f32[1,240,128]{2,1,0:T(8,128)S(1)} %collective-permute-done.7.hi_ref, ...), custom_call_target="tpu_custom_call" | custom-call | flops 10000000 | bytes 3825664 | tf_op jit(solution)/shard_map/second_rows_kernel/pallas_call | solution.py:609
  50.0 2.0 %collective-permute-start.11 = (f32[240,128]{1,0:T(8,128)S(1)}, f32[240,128]{1,0:T(8,128)S(1)}, u32[]{:S(2)}, u32[]{:S(2)}) collective-permute-start(f32[240,128]{1,0:T(8,128)S(1)} %get-tuple-element.62), channel_id=1, source_target_pairs={{0,8},{8,0},{16,24},{24,16},{1,9},{9,1},{17,25},{25,17},{2,10},{10... | collective-permute-start | bytes 368648 | tf_op jit(solution)/shard_map/ppermute | solution.py:627
  52.0 0.3 collective-permute-start.12
  52.3 1.2 %collective-permute-start.13 = (f32[240,128]{1,0:T(8,128)S(1)}, f32[240,128]{1,0:T(8,128)S(1)}, u32[]{:S(2)}, u32[]{:S(2)}) collective-permute-start(f32[240,128]{1,0:T(8,128)S(1)} %get-tuple-element.64), channel_id=1, source_target_pairs={{0,24},{8,16},{16,8},{24,0},{1,25},{9,17},{17,9},{25,1},{2,26},{10... | collective-permute-start | bytes 368648 | tf_op jit(solution)/shard_map/ppermute | solution.py:627
  53.6 1.8 %collective-permute-done.11.refs_1_ = f32[240,128]{1,0:T(8,128)S(1)} collective-permute-done((f32[240,128]{1,0:T(8,128)S(1)}, f32[240,128]{1,0:T(8,128)S(1)}, u32[]{:S(2)}, u32[]{:S(2)}) %collective-permute-start.11) | collective-permute-done | bytes 122912 | tf_op jit(solution)/shard_map/ppermute | solution.py:627
  55.4 3.6 %collective-permute-done.12.refs_2_ = f32[240,128]{1,0:T(8,128)S(1)} collective-permute-done((f32[240,128]{1,0:T(8,128)S(1)}, f32[240,128]{1,0:T(8,128)S(1)}, u32[]{:S(2)}, u32[]{:S(2)}) %collective-permute-start.12) | collective-permute-done | bytes 122912 | tf_op jit(solution)/shard_map/ppermute | solution.py:627
  58.9 0.0 collective-permute-done.13.refs_3_
  58.9 0.9 %close_kernel.1 = f32[1,5,12,16,128]{4,3,2,1,0:T(8,128)} custom-call(f32[240,128]{1,0:T(8,128)S(1)} %get-tuple-element.61.refs_0_, f32[240,128]{1,0:T(8,128)S(1)} %collective-permute-done.11.refs_1_, f32[240,128]{1,0:T(8,128)S(1)} %collective-permute-done.12.refs_2_, f32[240,128]{1,0:T(8,128)S(1)} %collective-permute-done.13.refs_3_), custom_call_target="tpu_custom_call" | custom-call | flops 1000000 | bytes 983040 | tf_op jit(solution)/shard_map/close_kernel/pallas_call | solution.py:609
Async XLA Ops:
  0.0 1.0 %copy-start = (f32[1,5,12,16,128]{4,3,2,1,0:T(8,128)S(1)}, f32[1,5,12,16,128]{4,3,2,1,0:T(8,128)}, u32[]{:S(2)}) copy-start(f32[1,5,12,16,128]{4,3,2,1,0:T(8,128)} %u_hbm.1) | copy-start | bytes 1474564
  2.8 16.5 %copy-start.1 = (f32[5,12,16,128]{3,2,1,0:T(8,128)S(1)}, f32[5,12,16,128]{3,2,1,0:T(8,128)}, u32[]{:S(2)}) copy-start(f32[5,12,16,128]{3,2,1,0:T(8,128)} %init_ref.1) | copy-start | bytes 1474564
  2.8 10.9 %collective-permute-start = (f32[320,128]{1,0:T(8,128)S(1)}, f32[320,128]{1,0:T(8,128)S(1)}, u32[]{:S(2)}, u32[]{:S(2)}) collective-permute-start(f32[320,128]{1,0:T(8,128)S(1)} %get-tuple-element.36), channel_id=1, source_target_pairs={{0,8},{8,0},{16,24},{24,16},{1,9},{9,1},{17,25},{25,17},{2,10},{10... | collective-permute-start | bytes 491528 | tf_op jit(solution)/shard_map/ppermute | solution.py:627
  5.8 9.2 %collective-permute-start.1 = (f32[320,128]{1,0:T(8,128)S(1)}, f32[320,128]{1,0:T(8,128)S(1)}, u32[]{:S(2)}, u32[]{:S(2)}) collective-permute-start(f32[320,128]{1,0:T(8,128)S(1)} %get-tuple-element.37), channel_id=1, source_target_pairs={{0,16},{8,24},{16,0},{24,8},{1,17},{9,25},{17,1},{25,9},{2,18},{10... | collective-permute-start | bytes 491528 | tf_op jit(solution)/shard_map/ppermute | solution.py:627
  7.3 7.7 %collective-permute-start.2 = (f32[320,128]{1,0:T(8,128)S(1)}, f32[320,128]{1,0:T(8,128)S(1)}, u32[]{:S(2)}, u32[]{:S(2)}) collective-permute-start(f32[320,128]{1,0:T(8,128)S(1)} %get-tuple-element.38), channel_id=1, source_target_pairs={{0,24},{8,16},{16,8},{24,0},{1,25},{9,17},{17,9},{25,1},{2,26},{10... | collective-permute-start | bytes 491528 | tf_op jit(solution)/shard_map/ppermute | solution.py:627
  7.3 14.5 %all-to-all-start = ((f32[32,8,128]{2,1,0:T(8,128)}), f32[32,8,128]{2,1,0:T(8,128)S(1)}, u32[]{:S(2)}, u32[]{:S(2)}) async-start(f32[32,8,128]{2,1,0:T(8,128)} %get-tuple-element.44), calls=%async_computation | async-start | bytes 262144 | tf_op jit(solution)/shard_map/all_to_all | solution.py:675
  15.4 6.5 %collective-permute-start.5 = (f32[1,384,128]{2,1,0:T(8,128)S(1)}, f32[1,384,128]{2,1,0:T(8,128)S(1)}, u32[]{:S(2)}, u32[]{:S(2)}) collective-permute-start(f32[1,384,128]{2,1,0:T(8,128)S(1)} %get-tuple-element.43), channel_id=1, source_target_pairs={{0,1},{1,0},{2,3},{3,2},{4,5},{5,4},{6,7},{7,6},{8,9},{9,8},{10,11... | collective-permute-start | bytes 589832 | tf_op jit(solution)/shard_map/ppermute | solution.py:623
  15.5 10.4 %collective-permute-start.3 = (f32[1,240,128]{2,1,0:T(8,128)S(1)}, f32[1,240,128]{2,1,0:T(8,128)S(1)}, u32[]{:S(2)}, u32[]{:S(2)}) collective-permute-start(f32[1,240,128]{2,1,0:T(8,128)S(1)} %get-tuple-element.40), channel_id=1, source_target_pairs={{0,2},{2,4},{4,6},{6,0},{1,3},{3,5},{5,7},{7,1},{8,10},{10,12},{12... | collective-permute-start | bytes 368648 | tf_op jit(solution)/shard_map/ppermute | solution.py:623
  17.1 8.7 %collective-permute-start.4 = (f32[1,240,128]{2,1,0:T(8,128)S(1)}, f32[1,240,128]{2,1,0:T(8,128)S(1)}, u32[]{:S(2)}, u32[]{:S(2)}) collective-permute-start(f32[1,240,128]{2,1,0:T(8,128)S(1)} %get-tuple-element.41), channel_id=1, source_target_pairs={{0,6},{2,0},{4,2},{6,4},{1,7},{3,1},{5,3},{7,5},{8,14},{10,8},{12,... | collective-permute-start | bytes 368648 | tf_op jit(solution)/shard_map/ppermute | solution.py:623
  29.8 13.6 %all-to-all-start.1 = ((f32[32,8,128]{2,1,0:T(8,128)}), f32[32,8,128]{2,1,0:T(8,128)S(1)}, u32[]{:S(2)}, u32[]{:S(2)}) async-start(f32[32,8,128]{2,1,0:T(8,128)} %get-tuple-element.56), calls=%async_computation.1 | async-start | bytes 262144 | tf_op jit(solution)/shard_map/all_to_all | solution.py:703
  32.9 10.5 %collective-permute-start.10 = (f32[1,384,128]{2,1,0:T(8,128)S(1)}, f32[1,384,128]{2,1,0:T(8,128)S(1)}, u32[]{:S(2)}, u32[]{:S(2)}) collective-permute-start(f32[1,384,128]{2,1,0:T(8,128)S(1)} %get-tuple-element.55), channel_id=1, source_target_pairs={{0,1},{1,0},{2,3},{3,2},{4,5},{5,4},{6,7},{7,6},{8,9},{9,8},{10,11... | collective-permute-start | bytes 589832 | tf_op jit(solution)/shard_map/ppermute | solution.py:623
  33.2 14.4 %collective-permute-start.6 = (f32[1,240,128]{2,1,0:T(8,128)S(1)}, f32[1,240,128]{2,1,0:T(8,128)S(1)}, u32[]{:S(2)}, u32[]{:S(2)}) collective-permute-start(f32[1,240,128]{2,1,0:T(8,128)S(1)} %get-tuple-element.50), channel_id=1, source_target_pairs={{0,2},{2,4},{4,6},{6,0},{1,3},{3,5},{5,7},{7,1},{8,10},{10,12},{12... | collective-permute-start | bytes 368648 | tf_op jit(solution)/shard_map/ppermute | solution.py:623
  34.9 12.7 %collective-permute-start.7 = (f32[1,240,128]{2,1,0:T(8,128)S(1)}, f32[1,240,128]{2,1,0:T(8,128)S(1)}, u32[]{:S(2)}, u32[]{:S(2)}) collective-permute-start(f32[1,240,128]{2,1,0:T(8,128)S(1)} %get-tuple-element.51), channel_id=1, source_target_pairs={{0,6},{2,0},{4,2},{6,4},{1,7},{3,1},{5,3},{7,5},{8,14},{10,8},{12,... | collective-permute-start | bytes 368648 | tf_op jit(solution)/shard_map/ppermute | solution.py:623
  37.0 5.8 %collective-permute-start.8 = (f32[128,128]{1,0:T(8,128)S(1)}, f32[128,128]{1,0:T(8,128)S(1)}, u32[]{:S(2)}, u32[]{:S(2)}) collective-permute-start(f32[128,128]{1,0:T(8,128)S(1)} %get-tuple-element.53), channel_id=1, source_target_pairs={{0,8},{8,16},{16,24},{24,0},{1,9},{9,17},{17,25},{25,1},{2,10},{10... | collective-permute-start | bytes 196616 | tf_op jit(solution)/shard_map/ppermute | solution.py:623
  38.7 4.7 %collective-permute-start.9 = (f32[128,128]{1,0:T(8,128)S(1)}, f32[128,128]{1,0:T(8,128)S(1)}, u32[]{:S(2)}, u32[]{:S(2)}) collective-permute-start(f32[128,128]{1,0:T(8,128)S(1)} %get-tuple-element.54), channel_id=1, source_target_pairs={{0,24},{8,0},{16,8},{24,16},{1,25},{9,1},{17,9},{25,17},{2,26},{10... | collective-permute-start | bytes 196616 | tf_op jit(solution)/shard_map/ppermute | solution.py:623
  50.0 5.4 %collective-permute-start.11 = (f32[240,128]{1,0:T(8,128)S(1)}, f32[240,128]{1,0:T(8,128)S(1)}, u32[]{:S(2)}, u32[]{:S(2)}) collective-permute-start(f32[240,128]{1,0:T(8,128)S(1)} %get-tuple-element.62), channel_id=1, source_target_pairs={{0,8},{8,0},{16,24},{24,16},{1,9},{9,1},{17,25},{25,17},{2,10},{10... | collective-permute-start | bytes 368648 | tf_op jit(solution)/shard_map/ppermute | solution.py:627
  52.0 6.9 %collective-permute-start.12 = (f32[240,128]{1,0:T(8,128)S(1)}, f32[240,128]{1,0:T(8,128)S(1)}, u32[]{:S(2)}, u32[]{:S(2)}) collective-permute-start(f32[240,128]{1,0:T(8,128)S(1)} %get-tuple-element.63), channel_id=1, source_target_pairs={{0,16},{8,24},{16,0},{24,8},{1,17},{9,25},{17,1},{25,9},{2,18},{10... | collective-permute-start | bytes 368648 | tf_op jit(solution)/shard_map/ppermute | solution.py:627
  52.3 6.6 %collective-permute-start.13 = (f32[240,128]{1,0:T(8,128)S(1)}, f32[240,128]{1,0:T(8,128)S(1)}, u32[]{:S(2)}, u32[]{:S(2)}) collective-permute-start(f32[240,128]{1,0:T(8,128)S(1)} %get-tuple-element.64), channel_id=1, source_target_pairs={{0,24},{8,16},{16,8},{24,0},{1,25},{9,17},{17,9},{25,1},{2,26},{10... | collective-permute-start | bytes 368648 | tf_op jit(solution)/shard_map/ppermute | solution.py:627

commit v8 on v7

--- a/solution.py
+++ b/solution.py
@@ -230,7 +230,7 @@
             side_ref[0, pl.ds(HALO * rows + c * nx + i, HALO, stride=rows), :] = value[:HALO]
         return carry
 
-    lax.fori_loop(0, nx, side, 0)
+    lax.fori_loop(0, nx, side, 0, unroll=4)
 
 
 def faster(best, read, first, count, comps):
@@ -238,36 +238,34 @@
         speeds = signal_speeds([read(c, i) for c in range(comps)])
         return tuple(jnp.maximum(b, s) for b, s in zip(best, speeds))
 
-    return lax.fori_loop(first, first + count, step, best)
-
-
-def alpha_tile(best, group):
-    nz = best[0].shape[-1]
+    return lax.fori_loop(first, first + count, step, best, unroll=4 if count % 4 == 0 else count)
+
+
+def speed_row(best, width):
     rows = [jnp.max(b, axis=0, keepdims=True) for b in best]
-    tile = jnp.concatenate(rows + [jnp.zeros((TILE - 3, nz), jnp.float32)], axis=0)
-    lane = lane_index(tile.shape)
-    by = 1
-    while by < group:
-        other = jnp.where((lane & by) != 0, turned(tile, by), turned(tile, -by))
-        tile = jnp.maximum(tile, other)
-        by *= 2
-    return tile
-
-
-def spread(tile, al_ref):
-    def step(i, carry):
-        al_ref[i] = tile
-        return carry
-
-    lax.fori_loop(0, al_ref.shape[0], step, 0)
-
-
-def open_kernel(u_hbm, *refs):
-    parts, (al_ref, u_ref, ring, sems) = refs[:-4], refs[-4:]
-    nodes = len(parts)
+    size = width
+    while size > TILE:
+        size //= 2
+        rows = [jnp.maximum(r, turned(r, -size)) for r in rows]
+    rows = [turned(r, TILE * k) for k, r in enumerate(rows)]
+    return merged(rows, lane_index(rows[0].shape) % width // TILE)
+
+
+def speed_tile(row, nodes):
+    nz = row.shape[-1]
+    width = nz // nodes
+    shape = (3 * nodes, nz)
+    lane = lane_index(shape)
+    place = lax.broadcasted_iota(jnp.int32, shape, 0)
+    mine = (lane // width == place % nodes) & (lane % width // TILE == place // nodes)
+    spots = jnp.max(jnp.where(mine, row, 0.0), axis=1, keepdims=True)
+    group = lane_index((1, nz)) // width
+    rows = [merged([spots[k * nodes + m : k * nodes + m + 1] for m in range(nodes)], group) for k in range(3)]
+    return jnp.concatenate(rows + [jnp.zeros((TILE - 3, nz), jnp.float32)], axis=0)
+
+
+def open_kernel(u_hbm, u_ref, al_ref, sems, *, nodes):
     comps, nx, ny, nz = u_ref.shape
-    blocks = Blocks(comps, nx, ny, nz)
-    width = nz // nodes
     me = lax.axis_index("node")
     chunks = sems.shape[0]
     size = nx // chunks
@@ -284,11 +282,22 @@
     for n in range(chunks):
         copies[n].wait()
         best = faster(best, read, n * size, size, comps)
-    tile = alpha_tile(best, nz)
-    spread(jnp.where(lane_index(tile.shape) // width == me, tile, 0.0), al_ref)
+    width = nz // nodes
+    rows = [jnp.max(b, axis=0, keepdims=True) for b in best]
+    rows = [functools.reduce(jnp.maximum, [turned(r, width * k) for k in range(nodes)]) for r in rows]
+    row = speed_row(rows, width)
+    row = jnp.where(lane_index(row.shape) // width == me, row, 0.0)
+    al_ref[...] = jnp.broadcast_to(row[None], al_ref.shape)
+
+
+def quarters_kernel(u_ref, *refs):
+    parts, ring = refs[:-1], refs[-1]
+    nodes = len(parts)
+    blocks = Blocks(*u_ref.shape)
+    me = lax.axis_index("node")
     quarters = [me ^ k for k in range(nodes)]
     for b in range(blocks.count):
-        send_quarter(blocks.natural(u_ref, b).T, ring, b, parts, quarters, width)
+        send_quarter(blocks.natural(u_ref, b).T, ring, b, parts, quarters, blocks.nz // nodes)
 
 
 def send_quarter(value, ring_ref, b, parts, quarters, width):
@@ -454,10 +463,7 @@
     blocks = Blocks(*dims)
     nz = blocks.nz
     width = nz // nodes
-    tiles = al_ref.shape[0]
-    tile = lax.fori_loop(
-        1, tiles, lambda i, best: jnp.maximum(best, al_ref[i]), al_ref[0], unroll=True if tiles <= 32 else 1
-    )
+    tile = speed_tile(jnp.max(al_ref[...], axis=0)[:1], nodes)
     al_out[...] = tile
     alphas = tile_rows(tile)
     along_second(lambda c, i: nat_ref[c, i], alphas, side_ref, dims, fy, yp, ym, gp, gm)
@@ -542,7 +548,8 @@
         return nat_ref[c, i]
 
     best = tuple(jnp.zeros((ny, nz), jnp.float32) for _ in range(3))
-    spread(alpha_tile(faster(best, read, 0, nx, comps), width), al_ref)
+    row = speed_row(faster(best, read, 0, nx, comps), width)
+    al_ref[...] = jnp.broadcast_to(row[None], al_ref.shape)
     write_edges(read, nx, ny, comps, lo_ref, hi_ref, side_ref)
 
 
@@ -602,7 +609,7 @@
         copy.wait()
 
 
-def call(kernel, name, outs, operands, scratch=(), flops=1_000_000, anywhere=False, outside=False):
+def call(kernel, name, outs, operands, scratch=(), flops=500_000_000, anywhere=False, outside=False):
     vmem, hbm = pl.BlockSpec(memory_space=pltpu.VMEM), pl.BlockSpec(memory_space=pltpu.HBM)
     moved = sum(4 * x.size for x in operands)
     scratch = [pltpu.VMEM(x, jnp.float32) if isinstance(x, tuple) else x for x in scratch]
@@ -627,13 +634,15 @@
     return lax.ppermute(value, "node", [(i, i ^ by) for i in range(lax.axis_size("node"))])
 
 
-def neighbours(lo, hi, side):
-    lower, upper = shifted(hi, "gx", 1), shifted(lo, "gx", -1)
+def beside(side):
     if lax.axis_size("gy") == 2:
-        return lower, upper, shifted(side, "gy", 1)
+        return shifted(side, "gy", 1)
     half = side.shape[1] // 2
-    side = jnp.concatenate([shifted(side[:, :half], "gy", 1), shifted(side[:, half:], "gy", -1)], axis=1)
-    return lower, upper, side
+    return jnp.concatenate([shifted(side[:, :half], "gy", 1), shifted(side[:, half:], "gy", -1)], axis=1)
+
+
+def across(lo, hi):
+    return shifted(hi, "gx", 1), shifted(lo, "gx", -1)
 
 
 def exchanged(parts):
@@ -653,7 +662,7 @@
     edge = (1, comps * HALO * ny, nz)
     edges = [edge, edge, (1, 2 * HALO * rows, nz)]
     tile_shape = (TILE, nz)
-    tiles_shape = (devices,) + tile_shape
+    speeds_shape = (devices, TILE, nz)
     part = (blocks.count * (width + 8), nz)
     pack = (comps * nx // nodes * ny, nz)
     ghost = (nodes * blocks.count * 4, nz)
@@ -664,15 +673,16 @@
     ring = (blocks.count * (nz + 2 * TILE), nz)
     chunks = 4 if nx % 4 == 0 else 1
 
-    *parts, tile = call(
-        open_kernel,
+    field, speeds = call(
+        functools.partial(open_kernel, nodes=nodes),
         "open_kernel",
-        [part] * nodes + [tiles_shape],
+        [initial.shape, speeds_shape],
         [guesses],
-        [initial.shape, ring, pltpu.SemaphoreType.DMA((chunks,))],
+        [pltpu.SemaphoreType.DMA((chunks,))],
         anywhere=True,
     )
-    tiles = lax.all_to_all(tile, everyone, 0, 0)
+    speeds = lax.all_to_all(speeds, everyone, 0, 0)
+    parts = call(quarters_kernel, "quarters_kernel", [part] * nodes, [field], [ring])
     start, start_pack = call(
         functools.partial(start_kernel, nodes=nodes),
         "start_kernel",
@@ -680,44 +690,47 @@
         [initial],
         [depth_shape],
     )
+    start, start_pack, *parts = lax.optimization_barrier((start, start_pack, *exchanged(parts)))
     turned_field, field, lo, hi, side = call(
-        gather_kernel, "gather_kernel", [(nodes,) + part, initial.shape] + edges, exchanged(parts)
-    )
-    lower, upper, side = neighbours(lo, hi, side)
-    depth, across, tile = call(
+        gather_kernel, "gather_kernel", [(nodes,) + part, initial.shape] + edges, parts
+    )
+    side = beside(side)
+    lower, upper = across(lo, hi)
+    depth, rates, tile = call(
         first_lanes_kernel,
         "first_lanes_kernel",
         lanes_out,
-        [field, turned_field, side, tiles],
+        [field, turned_field, side, speeds],
         lanes_scratch,
-        20_000_000,
-    )
-    turned_field, field, lo, hi, side, first, last, tile = call(
+        4_000_000_000,
+    )
+    turned_field, field, lo, hi, side, first, last, speeds = call(
         first_rows_kernel,
         "first_rows_kernel",
-        [(nodes,) + part, initial.shape] + edges + [ghost, ghost, tiles_shape],
-        [field, lower, upper, tile, depth, across, start],
+        [(nodes,) + part, initial.shape] + edges + [ghost, ghost, speeds_shape],
+        [field, lower, upper, tile, depth, rates, start],
         slabs,
-        10_000_000,
-    )
-    tiles = lax.all_to_all(tile, everyone, 0, 0)
-    lower, upper, side = neighbours(lo, hi, side)
+        2_500_000_000,
+    )
+    speeds = lax.all_to_all(speeds, everyone, 0, 0)
     before, behind = shifted(last, "node", 1), shifted(first, "node", -1)
-    depth, across, tile = call(
+    side = beside(side)
+    lower, upper = across(lo, hi)
+    depth, rates, tile = call(
         second_lanes_kernel,
         "second_lanes_kernel",
         lanes_out,
-        [field, turned_field, before, behind, side, tiles],
+        [field, turned_field, before, behind, side, speeds],
         [depth_shape, (nodes,) + part] + lanes_scratch,
-        20_000_000,
+        4_000_000_000,
     )
     outs = call(
         second_rows_kernel,
         "second_rows_kernel",
         [pack] * nodes,
-        [field, lower, upper, tile, depth, across, start_pack],
+        [field, lower, upper, tile, depth, rates, start_pack],
         slabs,
-        10_000_000,
+        2_500_000_000,
     )
     (states,) = call(
         close_kernel,

time: 60.1 us -> 57.1 us (0.950)
  waiting for transfers between devices: 12 us -> 9.47 us
  Pallas kernels: 18.3 us -> 17.5 us
    ppermute x8, waiting for transfers between devices: 3.48 us -> 0.97 us  [shifted(): lax.ppermute(value, axis, [(i, (i + by) % count) for i in range(count)])]
    all_to_all x2, waiting for transfers between devices: 1.83 us -> 2.68 us  [local(): speeds = lax.all_to_all(speeds, everyone, 0, 0)]
    ppermute x6, waiting for transfers between devices: 6.67 us -> 5.82 us  [swapped(): lax.ppermute(value, 'node', [(i, i ^ by) for i in range(lax.axis_size('no...]
    pallas_call x8 -> x9, Pallas kernels: 18.3 us -> 17.5 us  [call(): pl.pallas_call(kernel, out_shape=[jax.ShapeDtypeStruct(shape, jnp.float32...]
  transfers between devices with their start and end apart: 16 -> 16, of which waited for: 6 -> 6; matrix products, arithmetic and copies ran while one was open for 0% -> 0% of each run, Pallas kernels for 15% -> 16%
where the time goes in v8:
time: 57.1 us; the launch traced here: 56.8 us
  starting transfers between devices  28.6 us (50%)
  Pallas kernels  17.5 us (31%)
  waiting for transfers between devices  9.47 us (17%)
  local copies, waits for them, and re-layouts  1.04 us (2%)
    pallas_call x9, Pallas kernels, call(): pl.pallas_call(kernel, out_shape=[jax.ShapeDtypeStruct(shape, jnp.float32...  17.5 us
    ppermute x8, starting transfers between devices, shifted(): lax.ppermute(value, axis, [(i, (i + by) % count) for i in range(count)])  11 us
    all_to_all x2, starting transfers between devices, local(): speeds = lax.all_to_all(speeds, everyone, 0, 0)  9.52 us
    ppermute x6, starting transfers between devices, swapped(): lax.ppermute(value, 'node', [(i, i ^ by) for i in range(lax.axis_size('no...  8.11 us
    ppermute x6, waiting for transfers between devices, swapped(): lax.ppermute(value, 'node', [(i, i ^ by) for i in range(lax.axis_size('no...  5.82 us
    all_to_all x2, waiting for transfers between devices, local(): speeds = lax.all_to_all(speeds, everyone, 0, 0)  2.68 us
  transfers between devices with their start and end apart: 16, of which 6 were waited for; matrix products, arithmetic and copies ran while one was open for 0% of the time, Pallas kernels for 16%

profile of v8, /device:TPU:0, one launch (start us, length us, event | category | flops | bytes accessed | tf_op | source)
XLA Modules:
  0.0 56.8 jit_solution(8702826841206771779)
XLA Ops:
  0.0 0.0 copy-start
  0.0 1.0 %copy-done = f32[1,5,12,16,128]{4,3,2,1,0:T(8,128)S(1)} copy-done((f32[1,5,12,16,128]{4,3,2,1,0:T(8,128)S(1)}, f32[1,5,12,16,128]{4,3,2,1,0:T(8,128)}, u32[]{:S(2)}) %copy-start) | copy-done | bytes 491544
  1.0 1.2 %open_kernel.1 = (f32[5,12,16,128]{3,2,1,0:T(8,128)S(1)}, f32[32,8,128]{2,1,0:T(8,128)}) custom-call(f32[1,5,12,16,128]{4,3,2,1,0:T(8,128)S(1)} %copy-done), custom_call_target="tpu_custom_call" | custom-call | flops 500000000 | bytes 983040 | tf_op jit(solution)/shard_map/open_kernel/pallas_call | solution.py:616
  2.3 0.0 copy-start.1
  2.3 0.3 quarters_kernel.1
  2.6 3.0 %collective-permute-start = (f32[320,128]{1,0:T(8,128)S(1)}, f32[320,128]{1,0:T(8,128)S(1)}, u32[]{:S(2)}, u32[]{:S(2)}) collective-permute-start(f32[320,128]{1,0:T(8,128)S(1)} %get-tuple-element.46), channel_id=1, source_target_pairs={{0,8},{8,0},{16,24},{24,16},{1,9},{9,1},{17,25},{25,17},{2,10},{10... | collective-permute-start | bytes 491528 | tf_op jit(solution)/shard_map/ppermute | solution.py:634
  5.5 1.5 %collective-permute-start.1 = (f32[320,128]{1,0:T(8,128)S(1)}, f32[320,128]{1,0:T(8,128)S(1)}, u32[]{:S(2)}, u32[]{:S(2)}) collective-permute-start(f32[320,128]{1,0:T(8,128)S(1)} %get-tuple-element.47), channel_id=1, source_target_pairs={{0,16},{8,24},{16,0},{24,8},{1,17},{9,25},{17,1},{25,9},{2,18},{10... | collective-permute-start | bytes 491528 | tf_op jit(solution)/shard_map/ppermute | solution.py:634
  7.1 0.0 collective-permute-start.2
  7.1 6.3 %all-to-all-start = ((f32[32,8,128]{2,1,0:T(8,128)}), f32[32,8,128]{2,1,0:T(8,128)S(1)}, u32[]{:S(2)}, u32[]{:S(2)}) async-start(f32[32,8,128]{2,1,0:T(8,128)} %get-tuple-element.58), calls=%async_computation | async-start | bytes 262144 | tf_op jit(solution)/shard_map/all_to_all | solution.py:684
  13.4 0.0 copy-done.1
  13.4 0.7 %start_kernel.1 = (f32[256,128]{1,0:T(8,128)S(1)}, f32[240,128]{1,0:T(8,128)S(1)}) custom-call(f32[5,12,16,128]{3,2,1,0:T(8,128)S(1)} %copy-done.1), custom_call_target="tpu_custom_call" | custom-call | flops 500000000 | bytes 983040 | tf_op jit(solution)/shard_map/start_kernel/pallas_call | solution.py:616
  14.1 0.0 collective-permute-done.refs_1_
  14.1 0.6 %collective-permute-done.1.refs_2_ = f32[320,128]{1,0:T(8,128)S(1)} collective-permute-done((f32[320,128]{1,0:T(8,128)S(1)}, f32[320,128]{1,0:T(8,128)S(1)}, u32[]{:S(2)}, u32[]{:S(2)}) %collective-permute-start.1) | collective-permute-done | bytes 163872 | tf_op jit(solution)/shard_map/ppermute | solution.py:634
  14.7 0.0 collective-permute-done.2.refs_3_
  14.7 0.4 gather_kernel.1
  15.1 0.1 collective-permute-start.5
  15.2 1.6 %collective-permute-start.3 = (f32[1,240,128]{2,1,0:T(8,128)S(1)}, f32[1,240,128]{2,1,0:T(8,128)S(1)}, u32[]{:S(2)}, u32[]{:S(2)}) collective-permute-start(f32[1,240,128]{2,1,0:T(8,128)S(1)} %get-tuple-element.54), channel_id=1, source_target_pairs={{0,2},{2,4},{4,6},{6,0},{1,3},{3,5},{5,7},{7,1},{8,10},{10,12},{12... | collective-permute-start | bytes 368648 | tf_op jit(solution)/shard_map/ppermute | solution.py:630
  16.8 2.2 %collective-permute-start.4 = (f32[1,240,128]{2,1,0:T(8,128)S(1)}, f32[1,240,128]{2,1,0:T(8,128)S(1)}, u32[]{:S(2)}, u32[]{:S(2)}) collective-permute-start(f32[1,240,128]{2,1,0:T(8,128)S(1)} %get-tuple-element.55), channel_id=1, source_target_pairs={{0,6},{2,0},{4,2},{6,4},{1,7},{3,1},{5,3},{7,5},{8,14},{10,8},{12,... | collective-permute-start | bytes 368648 | tf_op jit(solution)/shard_map/ppermute | solution.py:630
  19.1 2.5 %all-to-all-done.al_ref = f32[32,8,128]{2,1,0:T(8,128)S(1)} async-done(((f32[32,8,128]{2,1,0:T(8,128)}), f32[32,8,128]{2,1,0:T(8,128)S(1)}, u32[]{:S(2)}, u32[]{:S(2)}) %all-to-all-start) | async-done | bytes 131104 | tf_op jit(solution)/shard_map/all_to_all | solution.py:684
  21.6 0.0 collective-permute-done.5.side_ref
  21.6 4.0 %first_lanes_kernel.1 = (f32[1024,128]{1,0:T(8,128)S(1)}, f32[1024,128]{1,0:T(8,128)S(1)}, f32[8,128]{1,0:T(8,128)S(1)}) custom-call(f32[5,12,16,128]{3,2,1,0:T(8,128)S(1)} %get-tuple-element.53.nat_ref.nat_in, f32[4,320,128]{2,1,0:T(8,128)S(1)} %get-tuple-element.56.rows_ref, f32[1,384,128]{2,1,0:T(8,128)S(1)} %collective-permute-done.5.side_ref, ...), custom_call_target="tpu_custom_call" | custom-call | flops 4000000000 | bytes 2949120 | tf_op jit(solution)/shard_map/first_lanes_kernel/pallas_call | solution.py:616
  25.6 0.0 collective-permute-done.3.lo_in
  25.6 0.0 collective-permute-done.4.hi_in
  25.6 3.5 %first_rows_kernel.1 = (f32[4,320,128]{2,1,0:T(8,128)S(1)}, f32[5,12,16,128]{3,2,1,0:T(8,128)S(1)}, f32[1,240,128]{2,1,0:T(8,128)S(1)}, f32[1,240,128]{2,1,0:T(8...) custom-call(f32[5,12,16,128]{3,2,1,0:T(8,128)S(1)} %get-tuple-elemen, ...), custom_call_target="tpu_custom_call" | custom-call | flops 2500000000 | bytes 3842048 | tf_op jit(solution)/shard_map/first_rows_kernel/pallas_call | solution.py:616
  29.1 3.2 %all-to-all-start.1 = ((f32[32,8,128]{2,1,0:T(8,128)}), f32[32,8,128]{2,1,0:T(8,128)S(1)}, u32[]{:S(2)}, u32[]{:S(2)}) async-start(f32[32,8,128]{2,1,0:T(8,128)} %get-tuple-element.70), calls=%async_computation.1 | async-start | bytes 262144 | tf_op jit(solution)/shard_map/all_to_all | solution.py:715
  32.3 0.3 collective-permute-start.10
  32.6 1.7 %collective-permute-start.8 = (f32[128,128]{1,0:T(8,128)S(1)}, f32[128,128]{1,0:T(8,128)S(1)}, u32[]{:S(2)}, u32[]{:S(2)}) collective-permute-start(f32[128,128]{1,0:T(8,128)S(1)} %get-tuple-element.67), channel_id=1, source_target_pairs={{0,8},{8,16},{16,24},{24,0},{1,9},{9,17},{17,25},{25,1},{2,10},{10... | collective-permute-start | bytes 196616 | tf_op jit(solution)/shard_map/ppermute | solution.py:630
  34.3 1.2 %collective-permute-start.9 = (f32[128,128]{1,0:T(8,128)S(1)}, f32[128,128]{1,0:T(8,128)S(1)}, u32[]{:S(2)}, u32[]{:S(2)}) collective-permute-start(f32[128,128]{1,0:T(8,128)S(1)} %get-tuple-element.68), channel_id=1, source_target_pairs={{0,24},{8,0},{16,8},{24,16},{1,25},{9,1},{17,9},{25,17},{2,26},{10... | collective-permute-start | bytes 196616 | tf_op jit(solution)/shard_map/ppermute | solution.py:630
  35.6 1.7 %collective-permute-start.6 = (f32[1,240,128]{2,1,0:T(8,128)S(1)}, f32[1,240,128]{2,1,0:T(8,128)S(1)}, u32[]{:S(2)}, u32[]{:S(2)}) collective-permute-start(f32[1,240,128]{2,1,0:T(8,128)S(1)} %get-tuple-element.64), channel_id=1, source_target_pairs={{0,2},{2,4},{4,6},{6,0},{1,3},{3,5},{5,7},{7,1},{8,10},{10,12},{12... | collective-permute-start | bytes 368648 | tf_op jit(solution)/shard_map/ppermute | solution.py:630
  37.2 2.1 %collective-permute-start.7 = (f32[1,240,128]{2,1,0:T(8,128)S(1)}, f32[1,240,128]{2,1,0:T(8,128)S(1)}, u32[]{:S(2)}, u32[]{:S(2)}) collective-permute-start(f32[1,240,128]{2,1,0:T(8,128)S(1)} %get-tuple-element.65), channel_id=1, source_target_pairs={{0,6},{2,0},{4,2},{6,4},{1,7},{3,1},{5,3},{7,5},{8,14},{10,8},{12,... | collective-permute-start | bytes 368648 | tf_op jit(solution)/shard_map/ppermute | solution.py:630
  39.4 0.0 collective-permute-done.8.before_ref
  39.4 0.9 %collective-permute-done.9.behind_ref = f32[128,128]{1,0:T(8,128)S(1)} collective-permute-done((f32[128,128]{1,0:T(8,128)S(1)}, f32[128,128]{1,0:T(8,128)S(1)}, u32[]{:S(2)}, u32[]{:S(2)}) %collective-permute-start.9) | collective-permute-done | bytes 65568 | tf_op jit(solution)/shard_map/ppermute | solution.py:630
  40.3 0.0 collective-permute-done.10.side_ref
  40.3 0.2 all-to-all-done.1.al_ref
  40.5 4.1 %second_lanes_kernel.1 = (f32[1024,128]{1,0:T(8,128)S(1)}, f32[1024,128]{1,0:T(8,128)S(1)}, f32[8,128]{1,0:T(8,128)S(1)}) custom-call(f32[5,12,16,128]{3,2,1,0:T(8,128)S(1)} %get-tuple-element.63.nat_ref, f32[4,320,128]{2,1,0:T(8,128)S(1)} %get-tuple-element.66.own_ref, f32[128,128]{1,0:T(8,128)S(1)} %collective-permute-done.8.before_ref, ...), custom_call_target="tpu_custom_call" | custom-call | flops 4000000000 | bytes 3211264 | tf_op jit(solution)/shard_map/second_lanes_kernel/pallas_call | solution.py:616
  44.6 0.0 collective-permute-done.6.lo_ref
  44.6 0.0 collective-permute-done.7.hi_ref
  44.6 2.5 %second_rows_kernel.1 = (f32[240,128]{1,0:T(8,128)S(1)}, f32[240,128]{1,0:T(8,128)S(1)}, f32[240,128]{1,0:T(8,128)S(1)}, f32[240,128]{1,0:T(8,128)S(1)}) custom-call(f32[5,12,16,128]{3,2,1,0:T(8,128)S(1)} %get-tuple-element.63.nat_ref, f32[1,240,128]{2,1,0:T(8,128)S(1)} %collective-permute-done.6.lo_ref, f32[1,240,128]{2,1,0:T(8,128)S(1)} %collective-permute-done.7.hi_ref, ...), custom_call_target="tpu_custom_call" | custom-call | flops 2500000000 | bytes 3825664 | tf_op jit(solution)/shard_map/second_rows_kernel/pallas_call | solution.py:616
  47.1 1.4 %collective-permute-start.11 = (f32[240,128]{1,0:T(8,128)S(1)}, f32[240,128]{1,0:T(8,128)S(1)}, u32[]{:S(2)}, u32[]{:S(2)}) collective-permute-start(f32[240,128]{1,0:T(8,128)S(1)} %get-tuple-element.76), channel_id=1, source_target_pairs={{0,8},{8,0},{16,24},{24,16},{1,9},{9,1},{17,25},{25,17},{2,10},{10... | collective-permute-start | bytes 368648 | tf_op jit(solution)/shard_map/ppermute | solution.py:634
  48.5 0.9 %collective-permute-start.12 = (f32[240,128]{1,0:T(8,128)S(1)}, f32[240,128]{1,0:T(8,128)S(1)}, u32[]{:S(2)}, u32[]{:S(2)}) collective-permute-start(f32[240,128]{1,0:T(8,128)S(1)} %get-tuple-element.77), channel_id=1, source_target_pairs={{0,16},{8,24},{16,0},{24,8},{1,17},{9,25},{17,1},{25,9},{2,18},{10... | collective-permute-start | bytes 368648 | tf_op jit(solution)/shard_map/ppermute | solution.py:634
  49.4 1.3 %collective-permute-start.13 = (f32[240,128]{1,0:T(8,128)S(1)}, f32[240,128]{1,0:T(8,128)S(1)}, u32[]{:S(2)}, u32[]{:S(2)}) collective-permute-start(f32[240,128]{1,0:T(8,128)S(1)} %get-tuple-element.78), channel_id=1, source_target_pairs={{0,24},{8,16},{16,8},{24,0},{1,25},{9,17},{17,9},{25,1},{2,26},{10... | collective-permute-start | bytes 368648 | tf_op jit(solution)/shard_map/ppermute | solution.py:634
  50.7 2.6 %collective-permute-done.11.refs_1_ = f32[240,128]{1,0:T(8,128)S(1)} collective-permute-done((f32[240,128]{1,0:T(8,128)S(1)}, f32[240,128]{1,0:T(8,128)S(1)}, u32[]{:S(2)}, u32[]{:S(2)}) %collective-permute-start.11) | collective-permute-done | bytes 122912 | tf_op jit(solution)/shard_map/ppermute | solution.py:634
  53.3 2.6 %collective-permute-done.12.refs_2_ = f32[240,128]{1,0:T(8,128)S(1)} collective-permute-done((f32[240,128]{1,0:T(8,128)S(1)}, f32[240,128]{1,0:T(8,128)S(1)}, u32[]{:S(2)}, u32[]{:S(2)}) %collective-permute-start.12) | collective-permute-done | bytes 122912 | tf_op jit(solution)/shard_map/ppermute | solution.py:634
  55.9 0.0 collective-permute-done.13.refs_3_
  55.9 0.9 %close_kernel.1 = f32[1,5,12,16,128]{4,3,2,1,0:T(8,128)} custom-call(f32[240,128]{1,0:T(8,128)S(1)} %get-tuple-element.75.refs_0_, f32[240,128]{1,0:T(8,128)S(1)} %collective-permute-done.11.refs_1_, f32[240,128]{1,0:T(8,128)S(1)} %collective-permute-done.12.refs_2_, f32[240,128]{1,0:T(8,128)S(1)} %collective-permute-done.13.refs_3_), custom_call_target="tpu_custom_call" | custom-call | flops 500000000 | bytes 983040 | tf_op jit(solution)/shard_map/close_kernel/pallas_call | solution.py:616
Async XLA Ops:
  0.0 1.0 %copy-start = (f32[1,5,12,16,128]{4,3,2,1,0:T(8,128)S(1)}, f32[1,5,12,16,128]{4,3,2,1,0:T(8,128)}, u32[]{:S(2)}) copy-start(f32[1,5,12,16,128]{4,3,2,1,0:T(8,128)} %u_hbm.1) | copy-start | bytes 1474564
  2.3 11.1 %copy-start.1 = (f32[5,12,16,128]{3,2,1,0:T(8,128)S(1)}, f32[5,12,16,128]{3,2,1,0:T(8,128)}, u32[]{:S(2)}) copy-start(f32[5,12,16,128]{3,2,1,0:T(8,128)} %init_ref.1) | copy-start | bytes 1474564
  2.6 11.6 %collective-permute-start = (f32[320,128]{1,0:T(8,128)S(1)}, f32[320,128]{1,0:T(8,128)S(1)}, u32[]{:S(2)}, u32[]{:S(2)}) collective-permute-start(f32[320,128]{1,0:T(8,128)S(1)} %get-tuple-element.46), channel_id=1, source_target_pairs={{0,8},{8,0},{16,24},{24,16},{1,9},{9,1},{17,25},{25,17},{2,10},{10... | collective-permute-start | bytes 491528 | tf_op jit(solution)/shard_map/ppermute | solution.py:634
  5.5 9.2 %collective-permute-start.1 = (f32[320,128]{1,0:T(8,128)S(1)}, f32[320,128]{1,0:T(8,128)S(1)}, u32[]{:S(2)}, u32[]{:S(2)}) collective-permute-start(f32[320,128]{1,0:T(8,128)S(1)} %get-tuple-element.47), channel_id=1, source_target_pairs={{0,16},{8,24},{16,0},{24,8},{1,17},{9,25},{17,1},{25,9},{2,18},{10... | collective-permute-start | bytes 491528 | tf_op jit(solution)/shard_map/ppermute | solution.py:634
  7.1 7.7 %collective-permute-start.2 = (f32[320,128]{1,0:T(8,128)S(1)}, f32[320,128]{1,0:T(8,128)S(1)}, u32[]{:S(2)}, u32[]{:S(2)}) collective-permute-start(f32[320,128]{1,0:T(8,128)S(1)} %get-tuple-element.48), channel_id=1, source_target_pairs={{0,24},{8,16},{16,8},{24,0},{1,25},{9,17},{17,9},{25,1},{2,26},{10... | collective-permute-start | bytes 491528 | tf_op jit(solution)/shard_map/ppermute | solution.py:634
  7.1 14.5 %all-to-all-start = ((f32[32,8,128]{2,1,0:T(8,128)}), f32[32,8,128]{2,1,0:T(8,128)S(1)}, u32[]{:S(2)}, u32[]{:S(2)}) async-start(f32[32,8,128]{2,1,0:T(8,128)} %get-tuple-element.58), calls=%async_computation | async-start | bytes 262144 | tf_op jit(solution)/shard_map/all_to_all | solution.py:684
  15.1 6.5 %collective-permute-start.5 = (f32[1,384,128]{2,1,0:T(8,128)S(1)}, f32[1,384,128]{2,1,0:T(8,128)S(1)}, u32[]{:S(2)}, u32[]{:S(2)}) collective-permute-start(f32[1,384,128]{2,1,0:T(8,128)S(1)} %get-tuple-element.57), channel_id=1, source_target_pairs={{0,1},{1,0},{2,3},{3,2},{4,5},{5,4},{6,7},{7,6},{8,9},{9,8},{10,11... | collective-permute-start | bytes 589832 | tf_op jit(solution)/shard_map/ppermute | solution.py:630
  15.2 10.4 %collective-permute-start.3 = (f32[1,240,128]{2,1,0:T(8,128)S(1)}, f32[1,240,128]{2,1,0:T(8,128)S(1)}, u32[]{:S(2)}, u32[]{:S(2)}) collective-permute-start(f32[1,240,128]{2,1,0:T(8,128)S(1)} %get-tuple-element.54), channel_id=1, source_target_pairs={{0,2},{2,4},{4,6},{6,0},{1,3},{3,5},{5,7},{7,1},{8,10},{10,12},{12... | collective-permute-start | bytes 368648 | tf_op jit(solution)/shard_map/ppermute | solution.py:630
  16.8 8.8 %collective-permute-start.4 = (f32[1,240,128]{2,1,0:T(8,128)S(1)}, f32[1,240,128]{2,1,0:T(8,128)S(1)}, u32[]{:S(2)}, u32[]{:S(2)}) collective-permute-start(f32[1,240,128]{2,1,0:T(8,128)S(1)} %get-tuple-element.55), channel_id=1, source_target_pairs={{0,6},{2,0},{4,2},{6,4},{1,7},{3,1},{5,3},{7,5},{8,14},{10,8},{12,... | collective-permute-start | bytes 368648 | tf_op jit(solution)/shard_map/ppermute | solution.py:630
  29.1 11.4 %all-to-all-start.1 = ((f32[32,8,128]{2,1,0:T(8,128)}), f32[32,8,128]{2,1,0:T(8,128)S(1)}, u32[]{:S(2)}, u32[]{:S(2)}) async-start(f32[32,8,128]{2,1,0:T(8,128)} %get-tuple-element.70), calls=%async_computation.1 | async-start | bytes 262144 | tf_op jit(solution)/shard_map/all_to_all | solution.py:715
  32.3 8.0 %collective-permute-start.10 = (f32[1,384,128]{2,1,0:T(8,128)S(1)}, f32[1,384,128]{2,1,0:T(8,128)S(1)}, u32[]{:S(2)}, u32[]{:S(2)}) collective-permute-start(f32[1,384,128]{2,1,0:T(8,128)S(1)} %get-tuple-element.69), channel_id=1, source_target_pairs={{0,1},{1,0},{2,3},{3,2},{4,5},{5,4},{6,7},{7,6},{8,9},{9,8},{10,11... | collective-permute-start | bytes 589832 | tf_op jit(solution)/shard_map/ppermute | solution.py:630
  32.6 6.8 %collective-permute-start.8 = (f32[128,128]{1,0:T(8,128)S(1)}, f32[128,128]{1,0:T(8,128)S(1)}, u32[]{:S(2)}, u32[]{:S(2)}) collective-permute-start(f32[128,128]{1,0:T(8,128)S(1)} %get-tuple-element.67), channel_id=1, source_target_pairs={{0,8},{8,16},{16,24},{24,0},{1,9},{9,17},{17,25},{25,1},{2,10},{10... | collective-permute-start | bytes 196616 | tf_op jit(solution)/shard_map/ppermute | solution.py:630
  34.3 6.0 %collective-permute-start.9 = (f32[128,128]{1,0:T(8,128)S(1)}, f32[128,128]{1,0:T(8,128)S(1)}, u32[]{:S(2)}, u32[]{:S(2)}) collective-permute-start(f32[128,128]{1,0:T(8,128)S(1)} %get-tuple-element.68), channel_id=1, source_target_pairs={{0,24},{8,0},{16,8},{24,16},{1,25},{9,1},{17,9},{25,17},{2,26},{10... | collective-permute-start | bytes 196616 | tf_op jit(solution)/shard_map/ppermute | solution.py:630
  35.6 9.1 %collective-permute-start.6 = (f32[1,240,128]{2,1,0:T(8,128)S(1)}, f32[1,240,128]{2,1,0:T(8,128)S(1)}, u32[]{:S(2)}, u32[]{:S(2)}) collective-permute-start(f32[1,240,128]{2,1,0:T(8,128)S(1)} %get-tuple-element.64), channel_id=1, source_target_pairs={{0,2},{2,4},{4,6},{6,0},{1,3},{3,5},{5,7},{7,1},{8,10},{10,12},{12... | collective-permute-start | bytes 368648 | tf_op jit(solution)/shard_map/ppermute | solution.py:630
  37.2 7.4 %collective-permute-start.7 = (f32[1,240,128]{2,1,0:T(8,128)S(1)}, f32[1,240,128]{2,1,0:T(8,128)S(1)}, u32[]{:S(2)}, u32[]{:S(2)}) collective-permute-start(f32[1,240,128]{2,1,0:T(8,128)S(1)} %get-tuple-element.65), channel_id=1, source_target_pairs={{0,6},{2,0},{4,2},{6,4},{1,7},{3,1},{5,3},{7,5},{8,14},{10,8},{12,... | collective-permute-start | bytes 368648 | tf_op jit(solution)/shard_map/ppermute | solution.py:630
  47.1 6.2 %collective-permute-start.11 = (f32[240,128]{1,0:T(8,128)S(1)}, f32[240,128]{1,0:T(8,128)S(1)}, u32[]{:S(2)}, u32[]{:S(2)}) collective-permute-start(f32[240,128]{1,0:T(8,128)S(1)} %get-tuple-element.76), channel_id=1, source_target_pairs={{0,8},{8,0},{16,24},{24,16},{1,9},{9,1},{17,25},{25,17},{2,10},{10... | collective-permute-start | bytes 368648 | tf_op jit(solution)/shard_map/ppermute | solution.py:634
  48.5 7.4 %collective-permute-start.12 = (f32[240,128]{1,0:T(8,128)S(1)}, f32[240,128]{1,0:T(8,128)S(1)}, u32[]{:S(2)}, u32[]{:S(2)}) collective-permute-start(f32[240,128]{1,0:T(8,128)S(1)} %get-tuple-element.77), channel_id=1, source_target_pairs={{0,16},{8,24},{16,0},{24,8},{1,17},{9,25},{17,1},{25,9},{2,18},{10... | collective-permute-start | bytes 368648 | tf_op jit(solution)/shard_map/ppermute | solution.py:634
  49.4 6.5 %collective-permute-start.13 = (f32[240,128]{1,0:T(8,128)S(1)}, f32[240,128]{1,0:T(8,128)S(1)}, u32[]{:S(2)}, u32[]{:S(2)}) collective-permute-start(f32[240,128]{1,0:T(8,128)S(1)} %get-tuple-element.78), channel_id=1, source_target_pairs={{0,24},{8,16},{16,8},{24,0},{1,25},{9,17},{17,9},{25,1},{2,26},{10... | collective-permute-start | bytes 368648 | tf_op jit(solution)/shard_map/ppermute | solution.py:634

commit v9 on v8

--- a/solution.py
+++ b/solution.py
@@ -264,40 +264,31 @@
     return jnp.concatenate(rows + [jnp.zeros((TILE - 3, nz), jnp.float32)], axis=0)
 
 
-def open_kernel(u_hbm, u_ref, al_ref, sems, *, nodes):
-    comps, nx, ny, nz = u_ref.shape
+def send_speeds(row, tiles_ref, out_hbm, sem):
+    tiles_ref[...] = jnp.broadcast_to(row[None], tiles_ref.shape)
+    copy = pltpu.make_async_copy(tiles_ref, out_hbm, sem)
+    copy.start()
+    return copy
+
+
+def open_kernel(u_ref, *refs):
+    parts, (speeds_hbm, ring, tiles_ref, sem) = refs[:-4], refs[-4:]
+    nodes = len(parts)
+    comps, nx, ny, nz = u_ref.shape[1:]
+    blocks = Blocks(comps, nx, ny, nz)
     me = lax.axis_index("node")
-    chunks = sems.shape[0]
-    size = nx // chunks
-    copies = []
-    for n in range(chunks):
-        at = pl.ds(n * size, size)
-        copies.append(pltpu.make_async_copy(u_hbm.at[0, :, at], u_ref.at[:, at], sems.at[n]))
-        copies[-1].start()
-
-    def read(c, i):
-        return u_ref[c, i]
-
     best = tuple(jnp.zeros((ny, nz), jnp.float32) for _ in range(3))
-    for n in range(chunks):
-        copies[n].wait()
-        best = faster(best, read, n * size, size, comps)
+    best = faster(best, lambda c, i: u_ref[0, c, i], 0, nx, comps)
     width = nz // nodes
     rows = [jnp.max(b, axis=0, keepdims=True) for b in best]
     rows = [functools.reduce(jnp.maximum, [turned(r, width * k) for k in range(nodes)]) for r in rows]
     row = speed_row(rows, width)
     row = jnp.where(lane_index(row.shape) // width == me, row, 0.0)
-    al_ref[...] = jnp.broadcast_to(row[None], al_ref.shape)
-
-
-def quarters_kernel(u_ref, *refs):
-    parts, ring = refs[:-1], refs[-1]
-    nodes = len(parts)
-    blocks = Blocks(*u_ref.shape)
-    me = lax.axis_index("node")
+    copy = send_speeds(row, tiles_ref, speeds_hbm, sem)
     quarters = [me ^ k for k in range(nodes)]
     for b in range(blocks.count):
-        send_quarter(blocks.natural(u_ref, b).T, ring, b, parts, quarters, blocks.nz // nodes)
+        send_quarter(blocks.natural(u_ref.at[0], b).T, ring, b, parts, quarters, width)
+    copy.wait()
 
 
 def send_quarter(value, ring_ref, b, parts, quarters, width):
@@ -323,8 +314,11 @@
 
     def step(c, carry):
         for q in range(nx // nodes):
-            pieces = [turned(init_ref[c, q * nodes + i], width * (i - me)) for i in range(nodes)]
-            pack_ref[rows_at((c * (nx // nodes) + q) * ny, ny), :] = merged(pieces, lanes)
+            pieces = [turned(init_ref[c, q * nodes + i], width * i) for i in range(nodes)]
+            out = pieces[0]
+            for i in range(1, nodes):
+                out = jnp.where(lanes == lax.rem(me + i, nodes), pieces[i], out)
+            pack_ref[rows_at((c * (nx // nodes) + q) * ny, ny), :] = out
         return carry
 
     lax.fori_loop(0, comps, step, 0)
@@ -515,7 +509,7 @@
 
 
 def first_rows_kernel(nat_in, lo_in, hi_in, al_in, fz, fy, start_ref, *refs):
-    rows_ref, nat_ref, lo_ref, hi_ref, side_ref, first_ref, last_ref, al_ref, rate, xp, xm = refs
+    rows_ref, nat_ref, lo_ref, hi_ref, side_ref, first_ref, last_ref, speeds_hbm, rate, xp, xm, tiles_ref, sem = refs
     nodes = rows_ref.shape[0]
     comps, nx, ny, nz = nat_ref.shape
     blocks = Blocks(comps, nx, ny, nz)
@@ -549,8 +543,9 @@
 
     best = tuple(jnp.zeros((ny, nz), jnp.float32) for _ in range(3))
     row = speed_row(faster(best, read, 0, nx, comps), width)
-    al_ref[...] = jnp.broadcast_to(row[None], al_ref.shape)
+    copy = send_speeds(row, tiles_ref, speeds_hbm, sem)
     write_edges(read, nx, ny, comps, lo_ref, hi_ref, side_ref)
+    copy.wait()
 
 
 def second_rows_kernel(nat_ref, lo_ref, hi_ref, al_ref, fz, fy, pack_ref, *refs):
@@ -573,15 +568,16 @@
             for q in range(nx // nodes):
                 at = rows_at((c * (nx // nodes) + q) * ny + t, TILE)
                 start = pack_ref[at, :]
-                rows = [rate[c, q * nodes + i, pl.ds(t, TILE), :] for i in range(nodes)]
+                rows = [turned(rate[c, q * nodes + i, pl.ds(t, TILE), :], width * i) for i in range(nodes)]
                 rates = [
-                    merged([turned(rows[i], width * (i - j)) for i in range(nodes)], lanes) for j in range(nodes)
+                    turned(merged([rows[(g - j) % nodes] for g in range(nodes)], lanes), width * (me - j))
+                    for j in range(nodes)
                 ]
                 for k in range(nodes):
                     value = start
                     for j in range(nodes):
                         value = value + weights[k][j] * rates[j]
-                    outs[k][at, :] = turned(value, width * me)
+                    outs[k][at, :] = value
 
     along_first(lambda c, i: nat_ref[c, i], tile_rows(al_ref), lo_ref, hi_ref, fy, rate, xp, xm, extra, after)
 
@@ -609,7 +605,7 @@
         copy.wait()
 
 
-def call(kernel, name, outs, operands, scratch=(), flops=500_000_000, anywhere=False, outside=False):
+def call(kernel, name, outs, operands, scratch=(), flops=500_000_000, anywhere=False, outside=()):
     vmem, hbm = pl.BlockSpec(memory_space=pltpu.VMEM), pl.BlockSpec(memory_space=pltpu.HBM)
     moved = sum(4 * x.size for x in operands)
     scratch = [pltpu.VMEM(x, jnp.float32) if isinstance(x, tuple) else x for x in scratch]
@@ -617,7 +613,7 @@
         kernel,
         out_shape=[jax.ShapeDtypeStruct(shape, jnp.float32) for shape in outs],
         in_specs=[hbm if anywhere else vmem] * len(operands),
-        out_specs=[hbm if outside else vmem] * len(outs),
+        out_specs=[hbm if n in outside else vmem for n in range(len(outs))],
         scratch_shapes=scratch,
         compiler_params=pltpu.CompilerParams(vmem_limit_bytes=32 * 1024 * 1024),
         cost_estimate=pl.CostEstimate(flops=flops, bytes_accessed=2 * moved, transcendentals=0),
@@ -671,18 +667,16 @@
     lanes_scratch = [(blocks.count * TILE * blocks.step, nz)] * 2 + [(ny * rows, nz)] * 2 + [(2 * HALO * rows, nz)] * 2
     slabs = [initial.shape] + [(nx + 2 * HALO, comps * ny, nz)] * 2
     ring = (blocks.count * (nz + 2 * TILE), nz)
-    chunks = 4 if nx % 4 == 0 else 1
-
-    field, speeds = call(
-        functools.partial(open_kernel, nodes=nodes),
+
+    *parts, speeds = call(
+        open_kernel,
         "open_kernel",
-        [initial.shape, speeds_shape],
+        [part] * nodes + [speeds_shape],
         [guesses],
-        [pltpu.SemaphoreType.DMA((chunks,))],
-        anywhere=True,
+        [ring, speeds_shape, pltpu.SemaphoreType.DMA],
+        outside=(nodes,),
     )
     speeds = lax.all_to_all(speeds, everyone, 0, 0)
-    parts = call(quarters_kernel, "quarters_kernel", [part] * nodes, [field], [ring])
     start, start_pack = call(
         functools.partial(start_kernel, nodes=nodes),
         "start_kernel",
@@ -709,8 +703,9 @@
         "first_rows_kernel",
         [(nodes,) + part, initial.shape] + edges + [ghost, ghost, speeds_shape],
         [field, lower, upper, tile, depth, rates, start],
-        slabs,
+        slabs + [speeds_shape, pltpu.SemaphoreType.DMA],
         2_500_000_000,
+        outside=(7,),
     )
     speeds = lax.all_to_all(speeds, everyone, 0, 0)
     before, behind = shifted(last, "node", 1), shifted(first, "node", -1)
@@ -738,7 +733,7 @@
         [(1,) + initial.shape],
         exchanged(outs),
         [initial.shape, pltpu.SemaphoreType.DMA((comps,))],
-        outside=True,
+        outside=(0,),
     )
     return states
 

time: 57.1 us -> 56.5 us (0.989)
  Pallas kernels: 17.5 us -> 16.9 us
    pallas_call x9 -> x8, Pallas kernels: 17.5 us -> 16.9 us  [call(): pl.pallas_call(kernel, out_shape=[jax.ShapeDtypeStruct(shape, jnp.float32...]
where the time goes in v9:
time: 56.5 us; the launch traced here: 56.2 us
  starting transfers between devices  28.6 us (51%)
  Pallas kernels  16.9 us (30%)
  waiting for transfers between devices  9.51 us (17%)
  local copies, waits for them, and re-layouts  1.03 us (2%)
    pallas_call x8, Pallas kernels, call(): pl.pallas_call(kernel, out_shape=[jax.ShapeDtypeStruct(shape, jnp.float32...  16.9 us
    ppermute x8, starting transfers between devices, shifted(): lax.ppermute(value, axis, [(i, (i + by) % count) for i in range(count)])  11 us
    all_to_all x2, starting transfers between devices, local(): speeds = lax.all_to_all(speeds, everyone, 0, 0)  9.48 us
    ppermute x6, starting transfers between devices, swapped(): lax.ppermute(value, 'node', [(i, i ^ by) for i in range(lax.axis_size('no...  8.12 us
    ppermute x6, waiting for transfers between devices, swapped(): lax.ppermute(value, 'node', [(i, i ^ by) for i in range(lax.axis_size('no...  5.87 us
    all_to_all x2, waiting for transfers between devices, local(): speeds = lax.all_to_all(speeds, everyone, 0, 0)  2.68 us
  transfers between devices with their start and end apart: 16, of which 6 were waited for; matrix products, arithmetic and copies ran while one was open for 0% of the time, Pallas kernels for 16%

profile of v9, /device:TPU:0, one launch (start us, length us, event | category | flops | bytes accessed | tf_op | source)
XLA Modules:
  0.0 56.2 jit_solution(9563397202317637488)
XLA Ops:
  0.0 0.0 copy-start
  0.0 1.0 %copy-done = f32[1,5,12,16,128]{4,3,2,1,0:T(8,128)S(1)} copy-done((f32[1,5,12,16,128]{4,3,2,1,0:T(8,128)S(1)}, f32[1,5,12,16,128]{4,3,2,1,0:T(8,128)}, u32[]{:S(2)}) %copy-start) | copy-done | bytes 491544
  1.0 0.0 copy-start.1
  1.0 1.2 %open_kernel.1 = (f32[320,128]{1,0:T(8,128)S(1)}, f32[320,128]{1,0:T(8,128)S(1)}, f32[320,128]{1,0:T(8,128)S(1)}, f32[320,128]{1,0:T(8,128)S(1)}, f32[32,8,128]{2,1,0:T(8,128)}) custom-call(f32[1,5,12,16,128]{4,3,2,1,0:T(8,128)S(1)} %copy-done), custom_call_target="tpu_custom_call" | custom-call | flops 500000000 | bytes 983040 | tf_op jit(solution)/shard_map/open_kernel/pallas_call | solution.py:612
  2.2 3.0 %collective-permute-start = (f32[320,128]{1,0:T(8,128)S(1)}, f32[320,128]{1,0:T(8,128)S(1)}, u32[]{:S(2)}, u32[]{:S(2)}) collective-permute-start(f32[320,128]{1,0:T(8,128)S(1)} %get-tuple-element.44), channel_id=1, source_target_pairs={{0,8},{8,0},{16,24},{24,16},{1,9},{9,1},{17,25},{25,17},{2,10},{10... | collective-permute-start | bytes 491528 | tf_op jit(solution)/shard_map/ppermute | solution.py:630
  5.2 1.5 %collective-permute-start.1 = (f32[320,128]{1,0:T(8,128)S(1)}, f32[320,128]{1,0:T(8,128)S(1)}, u32[]{:S(2)}, u32[]{:S(2)}) collective-permute-start(f32[320,128]{1,0:T(8,128)S(1)} %get-tuple-element.45), channel_id=1, source_target_pairs={{0,16},{8,24},{16,0},{24,8},{1,17},{9,25},{17,1},{25,9},{2,18},{10... | collective-permute-start | bytes 491528 | tf_op jit(solution)/shard_map/ppermute | solution.py:630
  6.7 0.0 collective-permute-start.2
  6.8 6.3 %all-to-all-start = ((f32[32,8,128]{2,1,0:T(8,128)}), f32[32,8,128]{2,1,0:T(8,128)S(1)}, u32[]{:S(2)}, u32[]{:S(2)}) async-start(f32[32,8,128]{2,1,0:T(8,128)} %get-tuple-element.56), calls=%async_computation | async-start | bytes 262144 | tf_op jit(solution)/shard_map/all_to_all | solution.py:679
  13.1 0.0 copy-done.1
  13.1 0.6 %start_kernel.1 = (f32[256,128]{1,0:T(8,128)S(1)}, f32[240,128]{1,0:T(8,128)S(1)}) custom-call(f32[5,12,16,128]{3,2,1,0:T(8,128)S(1)} %copy-done.1), custom_call_target="tpu_custom_call" | custom-call | flops 500000000 | bytes 983040 | tf_op jit(solution)/shard_map/start_kernel/pallas_call | solution.py:612
  13.7 0.0 collective-permute-done.refs_1_
  13.7 0.6 %collective-permute-done.1.refs_2_ = f32[320,128]{1,0:T(8,128)S(1)} collective-permute-done((f32[320,128]{1,0:T(8,128)S(1)}, f32[320,128]{1,0:T(8,128)S(1)}, u32[]{:S(2)}, u32[]{:S(2)}) %collective-permute-start.1) | collective-permute-done | bytes 163872 | tf_op jit(solution)/shard_map/ppermute | solution.py:630
  14.4 0.0 collective-permute-done.2.refs_3_
  14.4 0.4 gather_kernel.1
  14.8 0.1 collective-permute-start.5
  14.8 1.6 %collective-permute-start.3 = (f32[1,240,128]{2,1,0:T(8,128)S(1)}, f32[1,240,128]{2,1,0:T(8,128)S(1)}, u32[]{:S(2)}, u32[]{:S(2)}) collective-permute-start(f32[1,240,128]{2,1,0:T(8,128)S(1)} %get-tuple-element.52), channel_id=1, source_target_pairs={{0,2},{2,4},{4,6},{6,0},{1,3},{3,5},{5,7},{7,1},{8,10},{10,12},{12... | collective-permute-start | bytes 368648 | tf_op jit(solution)/shard_map/ppermute | solution.py:626
  16.5 2.2 %collective-permute-start.4 = (f32[1,240,128]{2,1,0:T(8,128)S(1)}, f32[1,240,128]{2,1,0:T(8,128)S(1)}, u32[]{:S(2)}, u32[]{:S(2)}) collective-permute-start(f32[1,240,128]{2,1,0:T(8,128)S(1)} %get-tuple-element.53), channel_id=1, source_target_pairs={{0,6},{2,0},{4,2},{6,4},{1,7},{3,1},{5,3},{7,5},{8,14},{10,8},{12,... | collective-permute-start | bytes 368648 | tf_op jit(solution)/shard_map/ppermute | solution.py:626
  18.7 2.5 %all-to-all-done.al_ref = f32[32,8,128]{2,1,0:T(8,128)S(1)} async-done(((f32[32,8,128]{2,1,0:T(8,128)}), f32[32,8,128]{2,1,0:T(8,128)S(1)}, u32[]{:S(2)}, u32[]{:S(2)}) %all-to-all-start) | async-done | bytes 131104 | tf_op jit(solution)/shard_map/all_to_all | solution.py:679
  21.3 0.0 collective-permute-done.5.side_ref
  21.3 4.0 %first_lanes_kernel.1 = (f32[1024,128]{1,0:T(8,128)S(1)}, f32[1024,128]{1,0:T(8,128)S(1)}, f32[8,128]{1,0:T(8,128)S(1)}) custom-call(f32[5,12,16,128]{3,2,1,0:T(8,128)S(1)} %get-tuple-element.51.nat_ref.nat_in, f32[4,320,128]{2,1,0:T(8,128)S(1)} %get-tuple-element.54.rows_ref, f32[1,384,128]{2,1,0:T(8,128)S(1)} %collective-permute-done.5.side_ref, ...), custom_call_target="tpu_custom_call" | custom-call | flops 4000000000 | bytes 2949120 | tf_op jit(solution)/shard_map/first_lanes_kernel/pallas_call | solution.py:612
  25.3 0.0 collective-permute-done.3.lo_in
  25.3 0.0 collective-permute-done.4.hi_in
  25.3 3.4 %first_rows_kernel.1 = (f32[4,320,128]{2,1,0:T(8,128)S(1)}, f32[5,12,16,128]{3,2,1,0:T(8,128)S(1)}, f32[1,240,128]{2,1,0:T(8,128)S(1)}, f32[1,240,128]{2,1,0:T(8...) custom-call(f32[5,12,16,128]{3,2,1,0:T(8,128)S(1)} %get-tuple-elemen, ...), custom_call_target="tpu_custom_call" | custom-call | flops 2500000000 | bytes 3842048 | tf_op jit(solution)/shard_map/first_rows_kernel/pallas_call | solution.py:612
  28.7 3.2 %all-to-all-start.1 = ((f32[32,8,128]{2,1,0:T(8,128)}), f32[32,8,128]{2,1,0:T(8,128)S(1)}, u32[]{:S(2)}, u32[]{:S(2)}) async-start(f32[32,8,128]{2,1,0:T(8,128)} %get-tuple-element.68), calls=%async_computation.1 | async-start | bytes 262144 | tf_op jit(solution)/shard_map/all_to_all | solution.py:710
  31.9 0.3 collective-permute-start.10
  32.2 1.7 %collective-permute-start.8 = (f32[128,128]{1,0:T(8,128)S(1)}, f32[128,128]{1,0:T(8,128)S(1)}, u32[]{:S(2)}, u32[]{:S(2)}) collective-permute-start(f32[128,128]{1,0:T(8,128)S(1)} %get-tuple-element.65), channel_id=1, source_target_pairs={{0,8},{8,16},{16,24},{24,0},{1,9},{9,17},{17,25},{25,1},{2,10},{10... | collective-permute-start | bytes 196616 | tf_op jit(solution)/shard_map/ppermute | solution.py:626
  33.9 1.2 %collective-permute-start.9 = (f32[128,128]{1,0:T(8,128)S(1)}, f32[128,128]{1,0:T(8,128)S(1)}, u32[]{:S(2)}, u32[]{:S(2)}) collective-permute-start(f32[128,128]{1,0:T(8,128)S(1)} %get-tuple-element.66), channel_id=1, source_target_pairs={{0,24},{8,0},{16,8},{24,16},{1,25},{9,1},{17,9},{25,17},{2,26},{10... | collective-permute-start | bytes 196616 | tf_op jit(solution)/shard_map/ppermute | solution.py:626
  35.1 1.7 %collective-permute-start.6 = (f32[1,240,128]{2,1,0:T(8,128)S(1)}, f32[1,240,128]{2,1,0:T(8,128)S(1)}, u32[]{:S(2)}, u32[]{:S(2)}) collective-permute-start(f32[1,240,128]{2,1,0:T(8,128)S(1)} %get-tuple-element.62), channel_id=1, source_target_pairs={{0,2},{2,4},{4,6},{6,0},{1,3},{3,5},{5,7},{7,1},{8,10},{10,12},{12... | collective-permute-start | bytes 368648 | tf_op jit(solution)/shard_map/ppermute | solution.py:626
  36.8 2.1 %collective-permute-start.7 = (f32[1,240,128]{2,1,0:T(8,128)S(1)}, f32[1,240,128]{2,1,0:T(8,128)S(1)}, u32[]{:S(2)}, u32[]{:S(2)}) collective-permute-start(f32[1,240,128]{2,1,0:T(8,128)S(1)} %get-tuple-element.63), channel_id=1, source_target_pairs={{0,6},{2,0},{4,2},{6,4},{1,7},{3,1},{5,3},{7,5},{8,14},{10,8},{12,... | collective-permute-start | bytes 368648 | tf_op jit(solution)/shard_map/ppermute | solution.py:626
  38.9 0.0 collective-permute-done.8.before_ref
  38.9 0.9 %collective-permute-done.9.behind_ref = f32[128,128]{1,0:T(8,128)S(1)} collective-permute-done((f32[128,128]{1,0:T(8,128)S(1)}, f32[128,128]{1,0:T(8,128)S(1)}, u32[]{:S(2)}, u32[]{:S(2)}) %collective-permute-start.9) | collective-permute-done | bytes 65568 | tf_op jit(solution)/shard_map/ppermute | solution.py:626
  39.9 0.0 collective-permute-done.10.side_ref
  39.9 0.2 all-to-all-done.1.al_ref
  40.0 4.1 %second_lanes_kernel.1 = (f32[1024,128]{1,0:T(8,128)S(1)}, f32[1024,128]{1,0:T(8,128)S(1)}, f32[8,128]{1,0:T(8,128)S(1)}) custom-call(f32[5,12,16,128]{3,2,1,0:T(8,128)S(1)} %get-tuple-element.61.nat_ref, f32[4,320,128]{2,1,0:T(8,128)S(1)} %get-tuple-element.64.own_ref, f32[128,128]{1,0:T(8,128)S(1)} %collective-permute-done.8.before_ref, ...), custom_call_target="tpu_custom_call" | custom-call | flops 4000000000 | bytes 3211264 | tf_op jit(solution)/shard_map/second_lanes_kernel/pallas_call | solution.py:612
  44.2 0.0 collective-permute-done.6.lo_ref
  44.2 0.0 collective-permute-done.7.hi_ref
  44.2 2.3 %second_rows_kernel.1 = (f32[240,128]{1,0:T(8,128)S(1)}, f32[240,128]{1,0:T(8,128)S(1)}, f32[240,128]{1,0:T(8,128)S(1)}, f32[240,128]{1,0:T(8,128)S(1)}) custom-call(f32[5,12,16,128]{3,2,1,0:T(8,128)S(1)} %get-tuple-element.61.nat_ref, f32[1,240,128]{2,1,0:T(8,128)S(1)} %collective-permute-done.6.lo_ref, f32[1,240,128]{2,1,0:T(8,128)S(1)} %collective-permute-done.7.hi_ref, ...), custom_call_target="tpu_custom_call" | custom-call | flops 2500000000 | bytes 3825664 | tf_op jit(solution)/shard_map/second_rows_kernel/pallas_call | solution.py:612
  46.5 1.4 %collective-permute-start.11 = (f32[240,128]{1,0:T(8,128)S(1)}, f32[240,128]{1,0:T(8,128)S(1)}, u32[]{:S(2)}, u32[]{:S(2)}) collective-permute-start(f32[240,128]{1,0:T(8,128)S(1)} %get-tuple-element.74), channel_id=1, source_target_pairs={{0,8},{8,0},{16,24},{24,16},{1,9},{9,1},{17,25},{25,17},{2,10},{10... | collective-permute-start | bytes 368648 | tf_op jit(solution)/shard_map/ppermute | solution.py:630
  47.9 0.9 %collective-permute-start.12 = (f32[240,128]{1,0:T(8,128)S(1)}, f32[240,128]{1,0:T(8,128)S(1)}, u32[]{:S(2)}, u32[]{:S(2)}) collective-permute-start(f32[240,128]{1,0:T(8,128)S(1)} %get-tuple-element.75), channel_id=1, source_target_pairs={{0,16},{8,24},{16,0},{24,8},{1,17},{9,25},{17,1},{25,9},{2,18},{10... | collective-permute-start | bytes 368648 | tf_op jit(solution)/shard_map/ppermute | solution.py:630
  48.8 1.3 %collective-permute-start.13 = (f32[240,128]{1,0:T(8,128)S(1)}, f32[240,128]{1,0:T(8,128)S(1)}, u32[]{:S(2)}, u32[]{:S(2)}) collective-permute-start(f32[240,128]{1,0:T(8,128)S(1)} %get-tuple-element.76), channel_id=1, source_target_pairs={{0,24},{8,16},{16,8},{24,0},{1,25},{9,17},{17,9},{25,1},{2,26},{10... | collective-permute-start | bytes 368648 | tf_op jit(solution)/shard_map/ppermute | solution.py:630
  50.1 2.6 %collective-permute-done.11.refs_1_ = f32[240,128]{1,0:T(8,128)S(1)} collective-permute-done((f32[240,128]{1,0:T(8,128)S(1)}, f32[240,128]{1,0:T(8,128)S(1)}, u32[]{:S(2)}, u32[]{:S(2)}) %collective-permute-start.11) | collective-permute-done | bytes 122912 | tf_op jit(solution)/shard_map/ppermute | solution.py:630
  52.7 2.6 %collective-permute-done.12.refs_2_ = f32[240,128]{1,0:T(8,128)S(1)} collective-permute-done((f32[240,128]{1,0:T(8,128)S(1)}, f32[240,128]{1,0:T(8,128)S(1)}, u32[]{:S(2)}, u32[]{:S(2)}) %collective-permute-start.12) | collective-permute-done | bytes 122912 | tf_op jit(solution)/shard_map/ppermute | solution.py:630
  55.3 0.0 collective-permute-done.13.refs_3_
  55.3 0.9 %close_kernel.1 = f32[1,5,12,16,128]{4,3,2,1,0:T(8,128)} custom-call(f32[240,128]{1,0:T(8,128)S(1)} %get-tuple-element.73.refs_0_, f32[240,128]{1,0:T(8,128)S(1)} %collective-permute-done.11.refs_1_, f32[240,128]{1,0:T(8,128)S(1)} %collective-permute-done.12.refs_2_, f32[240,128]{1,0:T(8,128)S(1)} %collective-permute-done.13.refs_3_), custom_call_target="tpu_custom_call" | custom-call | flops 500000000 | bytes 983040 | tf_op jit(solution)/shard_map/close_kernel/pallas_call | solution.py:612
Async XLA Ops:
  0.0 1.0 %copy-start = (f32[1,5,12,16,128]{4,3,2,1,0:T(8,128)S(1)}, f32[1,5,12,16,128]{4,3,2,1,0:T(8,128)}, u32[]{:S(2)}) copy-start(f32[1,5,12,16,128]{4,3,2,1,0:T(8,128)} %u_ref.1) | copy-start | bytes 1474564
  1.0 12.0 %copy-start.1 = (f32[5,12,16,128]{3,2,1,0:T(8,128)S(1)}, f32[5,12,16,128]{3,2,1,0:T(8,128)}, u32[]{:S(2)}) copy-start(f32[5,12,16,128]{3,2,1,0:T(8,128)} %init_ref.1) | copy-start | bytes 1474564
  2.2 11.5 %collective-permute-start = (f32[320,128]{1,0:T(8,128)S(1)}, f32[320,128]{1,0:T(8,128)S(1)}, u32[]{:S(2)}, u32[]{:S(2)}) collective-permute-start(f32[320,128]{1,0:T(8,128)S(1)} %get-tuple-element.44), channel_id=1, source_target_pairs={{0,8},{8,0},{16,24},{24,16},{1,9},{9,1},{17,25},{25,17},{2,10},{10... | collective-permute-start | bytes 491528 | tf_op jit(solution)/shard_map/ppermute | solution.py:630
  5.2 9.2 %collective-permute-start.1 = (f32[320,128]{1,0:T(8,128)S(1)}, f32[320,128]{1,0:T(8,128)S(1)}, u32[]{:S(2)}, u32[]{:S(2)}) collective-permute-start(f32[320,128]{1,0:T(8,128)S(1)} %get-tuple-element.45), channel_id=1, source_target_pairs={{0,16},{8,24},{16,0},{24,8},{1,17},{9,25},{17,1},{25,9},{2,18},{10... | collective-permute-start | bytes 491528 | tf_op jit(solution)/shard_map/ppermute | solution.py:630
  6.7 7.7 %collective-permute-start.2 = (f32[320,128]{1,0:T(8,128)S(1)}, f32[320,128]{1,0:T(8,128)S(1)}, u32[]{:S(2)}, u32[]{:S(2)}) collective-permute-start(f32[320,128]{1,0:T(8,128)S(1)} %get-tuple-element.46), channel_id=1, source_target_pairs={{0,24},{8,16},{16,8},{24,0},{1,25},{9,17},{17,9},{25,1},{2,26},{10... | collective-permute-start | bytes 491528 | tf_op jit(solution)/shard_map/ppermute | solution.py:630
  6.8 14.5 %all-to-all-start = ((f32[32,8,128]{2,1,0:T(8,128)}), f32[32,8,128]{2,1,0:T(8,128)S(1)}, u32[]{:S(2)}, u32[]{:S(2)}) async-start(f32[32,8,128]{2,1,0:T(8,128)} %get-tuple-element.56), calls=%async_computation | async-start | bytes 262144 | tf_op jit(solution)/shard_map/all_to_all | solution.py:679
  14.8 6.5 %collective-permute-start.5 = (f32[1,384,128]{2,1,0:T(8,128)S(1)}, f32[1,384,128]{2,1,0:T(8,128)S(1)}, u32[]{:S(2)}, u32[]{:S(2)}) collective-permute-start(f32[1,384,128]{2,1,0:T(8,128)S(1)} %get-tuple-element.55), channel_id=1, source_target_pairs={{0,1},{1,0},{2,3},{3,2},{4,5},{5,4},{6,7},{7,6},{8,9},{9,8},{10,11... | collective-permute-start | bytes 589832 | tf_op jit(solution)/shard_map/ppermute | solution.py:626
  14.8 10.4 %collective-permute-start.3 = (f32[1,240,128]{2,1,0:T(8,128)S(1)}, f32[1,240,128]{2,1,0:T(8,128)S(1)}, u32[]{:S(2)}, u32[]{:S(2)}) collective-permute-start(f32[1,240,128]{2,1,0:T(8,128)S(1)} %get-tuple-element.52), channel_id=1, source_target_pairs={{0,2},{2,4},{4,6},{6,0},{1,3},{3,5},{5,7},{7,1},{8,10},{10,12},{12... | collective-permute-start | bytes 368648 | tf_op jit(solution)/shard_map/ppermute | solution.py:626
  16.5 8.8 %collective-permute-start.4 = (f32[1,240,128]{2,1,0:T(8,128)S(1)}, f32[1,240,128]{2,1,0:T(8,128)S(1)}, u32[]{:S(2)}, u32[]{:S(2)}) collective-permute-start(f32[1,240,128]{2,1,0:T(8,128)S(1)} %get-tuple-element.53), channel_id=1, source_target_pairs={{0,6},{2,0},{4,2},{6,4},{1,7},{3,1},{5,3},{7,5},{8,14},{10,8},{12,... | collective-permute-start | bytes 368648 | tf_op jit(solution)/shard_map/ppermute | solution.py:626
  28.7 11.4 %all-to-all-start.1 = ((f32[32,8,128]{2,1,0:T(8,128)}), f32[32,8,128]{2,1,0:T(8,128)S(1)}, u32[]{:S(2)}, u32[]{:S(2)}) async-start(f32[32,8,128]{2,1,0:T(8,128)} %get-tuple-element.68), calls=%async_computation.1 | async-start | bytes 262144 | tf_op jit(solution)/shard_map/all_to_all | solution.py:710
  31.9 8.0 %collective-permute-start.10 = (f32[1,384,128]{2,1,0:T(8,128)S(1)}, f32[1,384,128]{2,1,0:T(8,128)S(1)}, u32[]{:S(2)}, u32[]{:S(2)}) collective-permute-start(f32[1,384,128]{2,1,0:T(8,128)S(1)} %get-tuple-element.67), channel_id=1, source_target_pairs={{0,1},{1,0},{2,3},{3,2},{4,5},{5,4},{6,7},{7,6},{8,9},{9,8},{10,11... | collective-permute-start | bytes 589832 | tf_op jit(solution)/shard_map/ppermute | solution.py:626
  32.2 6.8 %collective-permute-start.8 = (f32[128,128]{1,0:T(8,128)S(1)}, f32[128,128]{1,0:T(8,128)S(1)}, u32[]{:S(2)}, u32[]{:S(2)}) collective-permute-start(f32[128,128]{1,0:T(8,128)S(1)} %get-tuple-element.65), channel_id=1, source_target_pairs={{0,8},{8,16},{16,24},{24,0},{1,9},{9,17},{17,25},{25,1},{2,10},{10... | collective-permute-start | bytes 196616 | tf_op jit(solution)/shard_map/ppermute | solution.py:626
  33.9 6.0 %collective-permute-start.9 = (f32[128,128]{1,0:T(8,128)S(1)}, f32[128,128]{1,0:T(8,128)S(1)}, u32[]{:S(2)}, u32[]{:S(2)}) collective-permute-start(f32[128,128]{1,0:T(8,128)S(1)} %get-tuple-element.66), channel_id=1, source_target_pairs={{0,24},{8,0},{16,8},{24,16},{1,25},{9,1},{17,9},{25,17},{2,26},{10... | collective-permute-start | bytes 196616 | tf_op jit(solution)/shard_map/ppermute | solution.py:626
  35.1 9.1 %collective-permute-start.6 = (f32[1,240,128]{2,1,0:T(8,128)S(1)}, f32[1,240,128]{2,1,0:T(8,128)S(1)}, u32[]{:S(2)}, u32[]{:S(2)}) collective-permute-start(f32[1,240,128]{2,1,0:T(8,128)S(1)} %get-tuple-element.62), channel_id=1, source_target_pairs={{0,2},{2,4},{4,6},{6,0},{1,3},{3,5},{5,7},{7,1},{8,10},{10,12},{12... | collective-permute-start | bytes 368648 | tf_op jit(solution)/shard_map/ppermute | solution.py:626
  36.8 7.4 %collective-permute-start.7 = (f32[1,240,128]{2,1,0:T(8,128)S(1)}, f32[1,240,128]{2,1,0:T(8,128)S(1)}, u32[]{:S(2)}, u32[]{:S(2)}) collective-permute-start(f32[1,240,128]{2,1,0:T(8,128)S(1)} %get-tuple-element.63), channel_id=1, source_target_pairs={{0,6},{2,0},{4,2},{6,4},{1,7},{3,1},{5,3},{7,5},{8,14},{10,8},{12,... | collective-permute-start | bytes 368648 | tf_op jit(solution)/shard_map/ppermute | solution.py:626
  46.5 6.2 %collective-permute-start.11 = (f32[240,128]{1,0:T(8,128)S(1)}, f32[240,128]{1,0:T(8,128)S(1)}, u32[]{:S(2)}, u32[]{:S(2)}) collective-permute-start(f32[240,128]{1,0:T(8,128)S(1)} %get-tuple-element.74), channel_id=1, source_target_pairs={{0,8},{8,0},{16,24},{24,16},{1,9},{9,1},{17,25},{25,17},{2,10},{10... | collective-permute-start | bytes 368648 | tf_op jit(solution)/shard_map/ppermute | solution.py:630
  47.9 7.4 %collective-permute-start.12 = (f32[240,128]{1,0:T(8,128)S(1)}, f32[240,128]{1,0:T(8,128)S(1)}, u32[]{:S(2)}, u32[]{:S(2)}) collective-permute-start(f32[240,128]{1,0:T(8,128)S(1)} %get-tuple-element.75), channel_id=1, source_target_pairs={{0,16},{8,24},{16,0},{24,8},{1,17},{9,25},{17,1},{25,9},{2,18},{10... | collective-permute-start | bytes 368648 | tf_op jit(solution)/shard_map/ppermute | solution.py:630
  48.8 6.5 %collective-permute-start.13 = (f32[240,128]{1,0:T(8,128)S(1)}, f32[240,128]{1,0:T(8,128)S(1)}, u32[]{:S(2)}, u32[]{:S(2)}) collective-permute-start(f32[240,128]{1,0:T(8,128)S(1)} %get-tuple-element.76), channel_id=1, source_target_pairs={{0,24},{8,16},{16,8},{24,0},{1,25},{9,17},{17,9},{25,1},{2,26},{10... | collective-permute-start | bytes 368648 | tf_op jit(solution)/shard_map/ppermute | solution.py:630

commit v10 on v9

--- a/solution.py
+++ b/solution.py
@@ -51,18 +51,16 @@
     return flux
 
 
-def splits(fields, alphas, directions=(0, 1, 2)):
+def halves(fields, directions):
     _, velocity, pressure = primitives(fields)
     half = [0.5 * field for field in fields]
     half_pressure = 0.5 * pressure
-    out = []
-    for direction in directions:
-        flux = half_fluxes(half, velocity[direction], half_pressure, direction)
-        signal = [alphas[direction] * value for value in half]
-        out.append(
-            ([f + s for f, s in zip(flux, signal)], [f - s for f, s in zip(flux, signal)])
-        )
-    return out
+    return [half_fluxes(half, velocity[d], half_pressure, d) for d in directions], half
+
+
+def split(flux, field, alpha):
+    signal = alpha * field
+    return flux + signal, flux - signal
 
 
 def cell_terms(below, above):
@@ -163,7 +161,14 @@
         assert nz % ny == 0 and ny % TILE == 0 and 2 * self.left == self.per
         self.half = nz // 2
         self.count = comps + (comps + 1) // 2
-        self.step = CHUNK + 8
+
+    def message(self, width):
+        span = width + 2 * HALO
+        rows = self.count * span - (span // 2 if self.comps % 2 else 0)
+        return -(-rows // TILE) * TILE
+
+    def lone(self, b):
+        return self.comps % 2 == 1 and b == self.count - 1
 
     def pair(self, b):
         first = 2 * (b - self.comps)
@@ -202,18 +207,34 @@
         return (self.comps + c // 2) * self.nz + lax.rem(c, 2) * self.half + ((i - self.per) * self.ny + t)
 
 
-def split_depth(blocks, read, alpha, write):
+def depth_fluxes(blocks, read, write):
     comps = blocks.comps
-    ((plus, minus),) = splits([read(c) for c in range(comps)], [None, None, alpha], (2,))
+    (flux,), _ = halves([read(c) for c in range(comps)], (2,))
     for c in range(comps):
-        write(c, plus[c], minus[c])
+        write(c, flux[c])
     shared = [read(b) for b in range(comps, blocks.count)]
     fields = [shared[c // 2] if c % 2 == 0 else turned(shared[c // 2], blocks.half) for c in range(comps)]
-    ((plus, minus),) = splits(fields, [None, None, alpha], (2,))
+    (flux,), _ = halves(fields, (2,))
     lower = lane_index(fields[0].shape) < blocks.half
     for b in range(comps, blocks.count):
         first, second = blocks.pair(b)
-        write(b, *[jnp.where(lower, v[first], turned(v[second], blocks.half)) for v in (plus, minus)])
+        write(b, jnp.where(lower, flux[first], turned(flux[second], blocks.half)))
+
+
+def write_halves(blocks, nodes, rows_ref, zf):
+    size = blocks.nz // nodes + 8
+
+    def node(m, carry):
+        def read(b):
+            return rows_ref[rows_at((m * blocks.count + b) * size, size), :]
+
+        def write(b, flux):
+            zf[rows_at((m * blocks.count + b) * size, size), :] = flux
+
+        depth_fluxes(blocks, read, write)
+        return carry
+
+    lax.fori_loop(0, nodes, node, 0, unroll=2)
 
 
 def write_edges(read, nx, ny, comps, lo_ref, hi_ref, side_ref):
@@ -261,7 +282,7 @@
     spots = jnp.max(jnp.where(mine, row, 0.0), axis=1, keepdims=True)
     group = lane_index((1, nz)) // width
     rows = [merged([spots[k * nodes + m : k * nodes + m + 1] for m in range(nodes)], group) for k in range(3)]
-    return jnp.concatenate(rows + [jnp.zeros((TILE - 3, nz), jnp.float32)], axis=0)
+    return jnp.concatenate(rows + [jnp.zeros((TILE - 3, nz), jnp.float32)], axis=0), spots
 
 
 def send_speeds(row, tiles_ref, out_hbm, sem):
@@ -287,19 +308,26 @@
     copy = send_speeds(row, tiles_ref, speeds_hbm, sem)
     quarters = [me ^ k for k in range(nodes)]
     for b in range(blocks.count):
-        send_quarter(blocks.natural(u_ref.at[0], b).T, ring, b, parts, quarters, width)
+        send_quarter(blocks, blocks.natural(u_ref.at[0], b).T, ring, b, parts, quarters, width)
     copy.wait()
 
 
-def send_quarter(value, ring_ref, b, parts, quarters, width):
+def send_quarter(blocks, value, ring_ref, b, parts, quarters, width):
     nz = value.shape[0]
     base = b * (nz + 2 * TILE)
-    ring_ref[rows_at(base + TILE, nz), :] = value
-    ring_ref[rows_at(base, TILE), :] = value[nz - TILE :]
-    ring_ref[rows_at(base + TILE + nz, TILE), :] = value[:TILE]
-    size = width + 8
+    ring_ref[pl.ds(base + TILE, nz), :] = value
+    ring_ref[pl.ds(base, TILE), :] = value[nz - TILE :]
+    ring_ref[pl.ds(base + TILE + nz, TILE), :] = value[:TILE]
+    span = width + 2 * HALO
+    half = span // 2
     for part, quarter in zip(parts, quarters):
-        part[rows_at(b * size, size), :] = ring_ref[pl.ds(base + (TILE - HALO) + quarter * width, size), :]
+        start = base + (TILE - HALO) + quarter * width
+        if blocks.lone(b):
+            low, high = ring_ref[pl.ds(start, half), :], ring_ref[pl.ds(start + half, half), :]
+            lower = lane_index(low.shape) < blocks.half
+            part[pl.ds(b * span, half), :] = jnp.where(lower, low, turned(high, blocks.half))
+        else:
+            part[pl.ds(b * span, span), :] = ring_ref[pl.ds(start, span), :]
 
 
 def start_kernel(init_ref, rows_ref, pack_ref, turned_ref, *, nodes):
@@ -332,35 +360,46 @@
     width = nz // nodes
     size = width + 8
     me = lax.axis_index("node")
+    whole = blocks.count * size
+    span = width + 2 * HALO
+    half = span // 2
     for k in range(nodes):
-        rows_ref[me ^ k] = parts[k][...]
+        for b in range(blocks.count):
+            start = (me ^ k) * whole + b * size
+            if blocks.lone(b):
+                both = parts[k][pl.ds(b * span, half), :]
+                rows_ref[rows_at(start, half), :] = both
+                rows_ref[pl.ds(start + half, half), :] = turned(both, blocks.half)
+            else:
+                rows_ref[rows_at(start, span), :] = parts[k][pl.ds(b * span, span), :]
     for b in range(blocks.count):
-        own = pl.ds(b * size + HALO, width)
-        state = jnp.concatenate([rows_ref[m, own, :] for m in range(nodes)], axis=0)
+        own = [pl.ds(m * whole + b * size + HALO, width) for m in range(nodes)]
+        state = jnp.concatenate([rows_ref[at, :] for at in own], axis=0)
         blocks.put_natural(nat_ref, b, state.T)
     write_edges(lambda c, i: nat_ref[c, i], nx, ny, comps, lo_ref, hi_ref, side_ref)
 
 
-def along_second(u, alphas, side_ref, dims, fy, yp, ym, gp, gm):
-    comps, nx, ny, nz = dims
+def along_second(nat_ref, side_ref, alpha, fy, yp, ym, gp, gm):
+    comps, nx, ny, nz = nat_ref.shape
     rows = gp.shape[0] // (2 * HALO)
-    every = range(comps)
+
+    def prepare(fields, place, plus, minus):
+        (flux,), half = halves(fields, (1,))
+        for c in range(comps):
+            at = place(c)
+            plus[at, :], minus[at, :] = split(flux[c], half[c], alpha)
 
     def own(i, carry):
-        ((p, m),) = splits([u(c, i) for c in every], alphas, (1,))
-        for c in every:
-            at = rows_at((c * nx + i) * ny, ny)
-            yp[at, :] = p[c]
-            ym[at, :] = m[c]
+        prepare([nat_ref[c, i] for c in range(comps)], lambda c: rows_at((c * nx + i) * ny, ny), yp, ym)
         return carry
 
     lax.fori_loop(0, nx, own, 0, unroll=4)
 
     def ghost(i, carry):
-        ((p, m),) = splits([side_ref[0, pl.ds(i * rows + c * nx, nx), :] for c in every], alphas, (1,))
-        for c in every:
-            gp[pl.ds(i * rows + c * nx, nx), :] = p[c]
-            gm[pl.ds(i * rows + c * nx, nx), :] = m[c]
+        def place(c):
+            return pl.ds(i * rows + c * nx, nx)
+
+        prepare([side_ref[0, place(c), :] for c in range(comps)], place, gp, gm)
         return carry
 
     lax.fori_loop(0, 2 * HALO, ghost, 0, unroll=HALO)
@@ -384,45 +423,56 @@
     lax.fori_loop(0, rows // TILE, along, 0)
 
 
-def along_last(blocks, zp, zm, fz, after):
-    size = blocks.step * TILE
-
-    def along(b, carry):
+def along_last(blocks, nodes, zf, zu, alphas):
+    width = blocks.nz // nodes
+    size = width + 8
+    each = width // CHUNK
+
+    def along(n, carry):
+        m = n // each
+        start = m * (blocks.count * size) + lax.rem(n, each) * CHUNK
+        alpha = alphas[pl.ds(m * TILE, TILE), :]
+
         def load(j):
-            at = pl.ds(b * size + j, TILE, stride=blocks.step)
-            return zp[at, :], zm[at, :]
+            at = pl.ds(start + j, TILE, stride=size)
+            return split(zf[at, :], zu[at, :], alpha)
 
         def store(i, value):
-            fz[pl.ds(b * blocks.nz + i, TILE, stride=CHUNK), :] = value
-
-        after(jnp.maximum(b - 1, 0))
+            zf[pl.ds(start + i, TILE, stride=size), :] = value
+
         stream(load, store, CHUNK)
         return carry
 
-    lax.fori_loop(0, blocks.count, along, 0)
-    after(blocks.count - 1)
+    lax.fori_loop(0, nodes * each, along, 0)
+
+
+def block_rates(blocks, nodes, zf, b):
+    width = blocks.nz // nodes
+    size = width + 8
+    return jnp.concatenate([zf[rows_at((m * blocks.count + b) * size, width), :] for m in range(nodes)], axis=0)
 
 
 def along_first(u, alphas, lo_ref, hi_ref, fy, rate, xp, xm, extra, after):
     comps, nx, ny, nz = rate.shape
-    rows = fy.shape[0] // ny
+    rows = -(-comps * nx // TILE) * TILE
     every = range(comps)
 
-    def split(fields, at):
-        ((p, m),) = splits(fields, alphas, (0,))
+    def prepare(fields, at):
+        (flux,), half = halves(fields, (0,))
         for c in every:
-            xp[at, c * ny : (c + 1) * ny, :] = p[c]
-            xm[at, c * ny : (c + 1) * ny, :] = m[c]
+            p, m = split(flux[c], half[c], alphas[0])
+            xp[at, c * ny : (c + 1) * ny, :] = p
+            xm[at, c * ny : (c + 1) * ny, :] = m
 
     def own(i, carry):
-        split([u(c, i) for c in every], i + HALO)
+        prepare([u(c, i) for c in every], i + HALO)
         return carry
 
     lax.fori_loop(0, nx, own, 0, unroll=4)
     for ref, start in ((lo_ref, 0), (hi_ref, nx + HALO)):
 
         def ghost(i, carry, ref=ref, start=start):
-            split([ref[0, rows_at((c * HALO + i) * ny, ny), :] for c in every], start + i)
+            prepare([ref[0, rows_at((c * HALO + i) * ny, ny), :] for c in every], start + i)
             return carry
 
         lax.fori_loop(0, HALO, ghost, 0, unroll=HALO)
@@ -450,81 +500,65 @@
     return [tile[k : k + 1, :] for k in range(3)]
 
 
-def along_lanes(nat_ref, rows_ref, side_ref, al_ref, fz, fy, al_out, scratch, after):
-    zp, zm, yp, ym, gp, gm = scratch
-    nodes = rows_ref.shape[0]
-    dims = nat_ref.shape
-    blocks = Blocks(*dims)
-    nz = blocks.nz
-    width = nz // nodes
-    tile = speed_tile(jnp.max(al_ref[...], axis=0)[:1], nodes)
+def speeds_of(al_ref, al_out, alphas, nodes):
+    tile, spots = speed_tile(jnp.max(al_ref[...], axis=0)[:1], nodes)
     al_out[...] = tile
-    alphas = tile_rows(tile)
-    along_second(lambda c, i: nat_ref[c, i], alphas, side_ref, dims, fy, yp, ym, gp, gm)
-    group = lane_index((1, nz)) // width
-    each = width // CHUNK
     for m in range(nodes):
-        alpha = jnp.max(jnp.where(group == m, alphas[2], 0.0))
-
-        def depth(n, carry, m=m, alpha=alpha):
-            def read(b):
-                return rows_ref[m, rows_at(b * (width + 8) + n * CHUNK, blocks.step), :]
-
-            def write(b, plus, minus):
-                to = rows_at((b * TILE + m * each + n) * blocks.step, blocks.step)
-                zp[to, :] = plus
-                zm[to, :] = minus
-
-            split_depth(blocks, read, alpha, write)
-            return carry
-
-        lax.fori_loop(0, each, depth, 0, unroll=True)
-    along_last(blocks, zp, zm, fz, after)
-
-
-def first_lanes_kernel(nat_ref, rows_ref, side_ref, al_ref, fz, fy, al_out, *scratch):
-    along_lanes(nat_ref, rows_ref, side_ref, al_ref, fz, fy, al_out, scratch, lambda b: None)
+        at = 2 * nodes + m
+        alphas[m * TILE : (m + 1) * TILE, :] = jnp.broadcast_to(spots[at : at + 1], (TILE, tile.shape[-1])) * 0.5
+    return tile
+
+
+def halves_kernel(rows_ref, zf, *, dims, nodes):
+    write_halves(Blocks(*dims), nodes, rows_ref, zf)
+
+
+def first_lanes_kernel(nat_ref, zu, zf_in, side_ref, al_ref, fy, zf, al_out, *scratch, nodes):
+    del zf_in
+    *scratch, alphas = scratch
+    tile = speeds_of(al_ref, al_out, alphas, nodes)
+    along_last(Blocks(*nat_ref.shape), nodes, zf, zu, alphas)
+    along_second(nat_ref, side_ref, tile[1:2], fy, *scratch)
 
 
 def second_lanes_kernel(
-    nat_ref, own_ref, before_ref, behind_ref, side_ref, al_ref, fz, fy, al_out, back, rows_ref, *scratch
+    nat_ref, before_ref, behind_ref, side_ref, al_ref, fz, fy, al_out, zu, zf, *scratch, nodes
 ):
-    nodes = own_ref.shape[0]
+    *scratch, alphas = scratch
     blocks = Blocks(*nat_ref.shape)
     nz = blocks.nz
-    width = nz // nodes
-    size = width + 8
-    for m in range(nodes):
-        rows_ref[m] = own_ref[m]
-        for b in range(blocks.count):
+    size = nz // nodes + 8
+    width = nz // nodes
+    for b in range(blocks.count):
+        value = blocks.natural(nat_ref, b).T
+        for m in range(nodes):
             ghost = pl.ds((m * blocks.count + b) * 4, HALO)
-            rows_ref[m, pl.ds(b * size, HALO), :] = before_ref[ghost, :]
-            rows_ref[m, pl.ds(b * size + HALO + width, HALO), :] = behind_ref[ghost, :]
-
-    def after(b):
-        at = rows_at(b * nz, nz)
-        fz[at, :] = back[at, :].T
-
-    along_lanes(nat_ref, rows_ref, side_ref, al_ref, back, fy, al_out, scratch, after)
-
-
-def first_rows_kernel(nat_in, lo_in, hi_in, al_in, fz, fy, start_ref, *refs):
-    rows_ref, nat_ref, lo_ref, hi_ref, side_ref, first_ref, last_ref, speeds_hbm, rate, xp, xm, tiles_ref, sem = refs
-    nodes = rows_ref.shape[0]
+            start = (m * blocks.count + b) * size
+            zu[pl.ds(start, HALO), :] = before_ref[ghost, :]
+            zu[pl.ds(start + HALO, width), :] = value[m * width : (m + 1) * width]
+            zu[pl.ds(start + HALO + width, HALO), :] = behind_ref[ghost, :]
+    write_halves(blocks, nodes, zu, zf)
+    tile = speeds_of(al_ref, al_out, alphas, nodes)
+    along_last(blocks, nodes, zf, zu, alphas)
+    for b in range(blocks.count):
+        fz[pl.ds(b * nz, nz), :] = block_rates(blocks, nodes, zf, b).T
+    along_second(nat_ref, side_ref, tile[1:2], fy, *scratch)
+
+
+def first_rows_kernel(nat_in, lo_in, hi_in, al_in, zf, fy, start_ref, *refs, nodes):
+    nat_ref, lo_ref, hi_ref, side_ref, first_ref, last_ref, speeds_hbm, rate, xp, xm, tiles_ref, sem = refs
     comps, nx, ny, nz = nat_ref.shape
     blocks = Blocks(comps, nx, ny, nz)
     width = nz // nodes
-    size = width + 8
 
     def state(value, b):
-        rates = value.T + fz[rows_at(b * nz, nz), :]
+        rates = value.T + block_rates(blocks, nodes, zf, b)
         start = start_ref[rows_at(b * width, width), :]
         states = []
         for m in range(nodes):
             new = start
             for n in range(nodes):
                 new = new + scaled_weight(m, n) * rates[n * width : (n + 1) * width]
-            rows_ref[m, pl.ds(b * size + HALO, width), :] = new
             ghost = pl.ds((m * blocks.count + b) * 4, HALO)
             first_ref[ghost, :] = new[:HALO]
             last_ref[ghost, :] = new[width - HALO :]
@@ -605,7 +639,7 @@
         copy.wait()
 
 
-def call(kernel, name, outs, operands, scratch=(), flops=500_000_000, anywhere=False, outside=()):
+def call(kernel, name, outs, operands, scratch=(), flops=500_000_000, anywhere=False, outside=(), aliases=None):
     vmem, hbm = pl.BlockSpec(memory_space=pltpu.VMEM), pl.BlockSpec(memory_space=pltpu.HBM)
     moved = sum(4 * x.size for x in operands)
     scratch = [pltpu.VMEM(x, jnp.float32) if isinstance(x, tuple) else x for x in scratch]
@@ -615,6 +649,7 @@
         in_specs=[hbm if anywhere else vmem] * len(operands),
         out_specs=[hbm if n in outside else vmem for n in range(len(outs))],
         scratch_shapes=scratch,
+        input_output_aliases=aliases or {},
         compiler_params=pltpu.CompilerParams(vmem_limit_bytes=32 * 1024 * 1024),
         cost_estimate=pl.CostEstimate(flops=flops, bytes_accessed=2 * moved, transcendentals=0),
         name=name,
@@ -654,7 +689,7 @@
     rows = -(-comps * nx // TILE) * TILE
     blocks = Blocks(comps, nx, ny, nz)
     width = nz // nodes
-    assert nz == CHUNK * TILE and width % CHUNK == 0 and nx % nodes == 0
+    assert blocks.count == TILE and width % CHUNK == 0 and nx % nodes == 0
     edge = (1, comps * HALO * ny, nz)
     edges = [edge, edge, (1, 2 * HALO * rows, nz)]
     tile_shape = (TILE, nz)
@@ -663,20 +698,27 @@
     pack = (comps * nx // nodes * ny, nz)
     ghost = (nodes * blocks.count * 4, nz)
     depth_shape = (blocks.count * nz, nz)
-    lanes_out = [depth_shape, (ny * rows, nz), tile_shape]
-    lanes_scratch = [(blocks.count * TILE * blocks.step, nz)] * 2 + [(ny * rows, nz)] * 2 + [(2 * HALO * rows, nz)] * 2
+    lanes_scratch = [(ny * rows, nz)] * 2 + [(2 * HALO * rows, nz)] * 2 + [(nodes * TILE, nz)]
+    whole = (nodes * part[0], nz)
     slabs = [initial.shape] + [(nx + 2 * HALO, comps * ny, nz)] * 2
     ring = (blocks.count * (nz + 2 * TILE), nz)
 
     *parts, speeds = call(
         open_kernel,
         "open_kernel",
-        [part] * nodes + [speeds_shape],
+        [(blocks.message(width), nz)] * nodes + [speeds_shape],
         [guesses],
         [ring, speeds_shape, pltpu.SemaphoreType.DMA],
         outside=(nodes,),
     )
     speeds = lax.all_to_all(speeds, everyone, 0, 0)
+    parts = exchanged(parts)
+    turned_field, field, lo, hi, side = call(
+        gather_kernel, "gather_kernel", [whole, initial.shape] + edges, parts
+    )
+    side = beside(side)
+    lower, upper = across(lo, hi)
+    initial, side = lax.optimization_barrier((initial, side))
     start, start_pack = call(
         functools.partial(start_kernel, nodes=nodes),
         "start_kernel",
@@ -684,39 +726,39 @@
         [initial],
         [depth_shape],
     )
-    start, start_pack, *parts = lax.optimization_barrier((start, start_pack, *exchanged(parts)))
-    turned_field, field, lo, hi, side = call(
-        gather_kernel, "gather_kernel", [(nodes,) + part, initial.shape] + edges, parts
-    )
-    side = beside(side)
-    lower, upper = across(lo, hi)
-    depth, rates, tile = call(
-        first_lanes_kernel,
+    (fluxes,) = call(
+        functools.partial(halves_kernel, dims=initial.shape, nodes=nodes), "halves_kernel", [whole], [turned_field]
+    )
+    fluxes, start, start_pack = lax.optimization_barrier((fluxes, start, start_pack))
+    rates, depth, tile = call(
+        functools.partial(first_lanes_kernel, nodes=nodes),
         "first_lanes_kernel",
-        lanes_out,
-        [field, turned_field, side, speeds],
+        [(ny * rows, nz), whole, tile_shape],
+        [field, turned_field, fluxes, side, speeds],
         lanes_scratch,
         4_000_000_000,
-    )
-    turned_field, field, lo, hi, side, first, last, speeds = call(
-        first_rows_kernel,
+        aliases={2: 1},
+    )
+    field, lo, hi, side, first, last, speeds = call(
+        functools.partial(first_rows_kernel, nodes=nodes),
         "first_rows_kernel",
-        [(nodes,) + part, initial.shape] + edges + [ghost, ghost, speeds_shape],
+        [initial.shape] + edges + [ghost, ghost, speeds_shape],
         [field, lower, upper, tile, depth, rates, start],
         slabs + [speeds_shape, pltpu.SemaphoreType.DMA],
         2_500_000_000,
-        outside=(7,),
+        outside=(6,),
+        aliases={0: 0, 1: 1, 2: 2},
     )
     speeds = lax.all_to_all(speeds, everyone, 0, 0)
     before, behind = shifted(last, "node", 1), shifted(first, "node", -1)
     side = beside(side)
     lower, upper = across(lo, hi)
     depth, rates, tile = call(
-        second_lanes_kernel,
+        functools.partial(second_lanes_kernel, nodes=nodes),
         "second_lanes_kernel",
-        lanes_out,
-        [field, turned_field, before, behind, side, speeds],
-        [depth_shape, (nodes,) + part] + lanes_scratch,
+        [depth_shape, (ny * rows, nz), tile_shape],
+        [field, before, behind, side, speeds],
+        [whole, whole] + lanes_scratch,
         4_000_000_000,
     )
     outs = call(

time: 56.5 us -> 56.3 us (level)
  waiting for transfers between devices: 9.51 us -> 8.37 us
  local copies, waits for them, and re-layouts: 1.03 us -> 1.67 us
    all_to_all x2, waiting for transfers between devices: 2.68 us -> 1.66 us  [local(): speeds = lax.all_to_all(speeds, everyone, 0, 0)]
    unnamed x4, local copies, waits for them, and re-layouts: 1.03 us -> 1.67 us
    pallas_call x8 -> x9, Pallas kernels: 16.9 us -> 17.1 us  [call(): pl.pallas_call(kernel, out_shape=[jax.ShapeDtypeStruct(shape, jnp.float32...]
where the time goes in v10:
time: 56.3 us; the launch traced here: 56 us
  starting transfers between devices  28.8 us (51%)
  Pallas kernels  17.1 us (30%)
  waiting for transfers between devices  8.37 us (15%)
  local copies, waits for them, and re-layouts  1.67 us (3%)
    pallas_call x9, Pallas kernels, call(): pl.pallas_call(kernel, out_shape=[jax.ShapeDtypeStruct(shape, jnp.float32...  17.1 us
    ppermute x8, starting transfers between devices, shifted(): lax.ppermute(value, axis, [(i, (i + by) % count) for i in range(count)])  11 us
    all_to_all x2, starting transfers between devices, local(): speeds = lax.all_to_all(speeds, everyone, 0, 0)  9.64 us
    ppermute x6, starting transfers between devices, swapped(): lax.ppermute(value, 'node', [(i, i ^ by) for i in range(lax.axis_size('no...  8.14 us
    ppermute x6, waiting for transfers between devices, swapped(): lax.ppermute(value, 'node', [(i, i ^ by) for i in range(lax.axis_size('no...  5.75 us
    unnamed x4, local copies, waits for them, and re-layouts  1.67 us
    all_to_all x2, waiting for transfers between devices, local(): speeds = lax.all_to_all(speeds, everyone, 0, 0)  1.66 us
  transfers between devices with their start and end apart: 16, of which 6 were waited for; matrix products, arithmetic and copies ran while one was open for 0% of the time, Pallas kernels for 16%

profile of v10, /device:TPU:0, one launch (start us, length us, event | category | flops | bytes accessed | tf_op | source)
XLA Modules:
  0.0 56.0 jit_solution(565939448838109766)
XLA Ops:
  0.0 0.0 copy-start
  0.0 1.0 %copy-done = f32[1,5,12,16,128]{4,3,2,1,0:T(8,128)S(1)} copy-done((f32[1,5,12,16,128]{4,3,2,1,0:T(8,128)S(1)}, f32[1,5,12,16,128]{4,3,2,1,0:T(8,128)}, u32[]{:S(2)}) %copy-start) | copy-done | bytes 491544
  1.0 1.2 %open_kernel.1 = (f32[288,128]{1,0:T(8,128)S(1)}, f32[288,128]{1,0:T(8,128)S(1)}, f32[288,128]{1,0:T(8,128)S(1)}, f32[288,128]{1,0:T(8,128)S(1)}, f32[32,8,128]{2,1,0:T(8,128)}) custom-call(f32[1,5,12,16,128]{4,3,2,1,0:T(8,128)S(1)} %copy-done), custom_call_target="tpu_custom_call" | custom-call | flops 500000000 | bytes 983040 | tf_op jit(solution)/shard_map/open_kernel/pallas_call | solution.py:646
  2.3 3.0 %collective-permute-start = (f32[288,128]{1,0:T(8,128)S(1)}, f32[288,128]{1,0:T(8,128)S(1)}, u32[]{:S(2)}, u32[]{:S(2)}) collective-permute-start(f32[288,128]{1,0:T(8,128)S(1)} %get-tuple-element.40), channel_id=1, source_target_pairs={{0,8},{8,0},{16,24},{24,16},{1,9},{9,1},{17,25},{25,17},{2,10},{10... | collective-permute-start | bytes 442376 | tf_op jit(solution)/shard_map/ppermute | solution.py:665
  5.3 1.5 %collective-permute-start.1 = (f32[288,128]{1,0:T(8,128)S(1)}, f32[288,128]{1,0:T(8,128)S(1)}, u32[]{:S(2)}, u32[]{:S(2)}) collective-permute-start(f32[288,128]{1,0:T(8,128)S(1)} %get-tuple-element.41), channel_id=1, source_target_pairs={{0,16},{8,24},{16,0},{24,8},{1,17},{9,25},{17,1},{25,9},{2,18},{10... | collective-permute-start | bytes 442376 | tf_op jit(solution)/shard_map/ppermute | solution.py:665
  6.8 0.0 collective-permute-start.2
  6.8 6.3 %all-to-all-start = ((f32[32,8,128]{2,1,0:T(8,128)}), f32[32,8,128]{2,1,0:T(8,128)S(1)}, u32[]{:S(2)}, u32[]{:S(2)}) async-start(f32[32,8,128]{2,1,0:T(8,128)} %get-tuple-element.53), calls=%async_computation | async-start | bytes 262144 | tf_op jit(solution)/shard_map/all_to_all | solution.py:714
  13.1 0.0 collective-permute-done.refs_1_
  13.2 0.6 %collective-permute-done.1.refs_2_ = f32[288,128]{1,0:T(8,128)S(1)} collective-permute-done((f32[288,128]{1,0:T(8,128)S(1)}, f32[288,128]{1,0:T(8,128)S(1)}, u32[]{:S(2)}, u32[]{:S(2)}) %collective-permute-start.1) | collective-permute-done | bytes 147488 | tf_op jit(solution)/shard_map/ppermute | solution.py:665
  13.8 0.0 collective-permute-done.2.refs_3_
  13.8 0.4 gather_kernel.1
  14.2 0.1 collective-permute-start.5
  14.3 1.6 %collective-permute-start.3 = (f32[1,240,128]{2,1,0:T(8,128)S(1)}, f32[1,240,128]{2,1,0:T(8,128)S(1)}, u32[]{:S(2)}, u32[]{:S(2)}) collective-permute-start(f32[1,240,128]{2,1,0:T(8,128)S(1)} %get-tuple-element.44), channel_id=1, source_target_pairs={{0,2},{2,4},{4,6},{6,0},{1,3},{3,5},{5,7},{7,1},{8,10},{10,12},{12... | collective-permute-start | bytes 368648 | tf_op jit(solution)/shard_map/ppermute | solution.py:661
  15.9 2.2 %collective-permute-start.4 = (f32[1,240,128]{2,1,0:T(8,128)S(1)}, f32[1,240,128]{2,1,0:T(8,128)S(1)}, u32[]{:S(2)}, u32[]{:S(2)}) collective-permute-start(f32[1,240,128]{2,1,0:T(8,128)S(1)} %get-tuple-element.45), channel_id=1, source_target_pairs={{0,6},{2,0},{4,2},{6,4},{1,7},{3,1},{5,3},{7,5},{8,14},{10,8},{12,... | collective-permute-start | bytes 368648 | tf_op jit(solution)/shard_map/ppermute | solution.py:661
  18.1 0.0 copy-start.1
  18.1 0.4 halves_kernel.1.zf_in
  18.5 0.0 collective-permute-done.5.side_ref
  18.5 0.6 %copy-done.1 = f32[5,12,16,128]{3,2,1,0:T(8,128)S(1)} copy-done((f32[5,12,16,128]{3,2,1,0:T(8,128)S(1)}, f32[5,12,16,128]{3,2,1,0:T(8,128)}, u32[]{:S(2)}) %copy-start.1) | copy-done | bytes 491544
  19.2 0.6 %start_kernel.1 = (f32[256,128]{1,0:T(8,128)S(1)}, f32[240,128]{1,0:T(8,128)S(1)}) custom-call(f32[5,12,16,128]{3,2,1,0:T(8,128)S(1)} %copy-done.1), custom_call_target="tpu_custom_call" | custom-call | flops 500000000 | bytes 983040 | tf_op jit(solution)/shard_map/start_kernel/pallas_call | solution.py:646
  19.8 1.5 %all-to-all-done.al_ref = f32[32,8,128]{2,1,0:T(8,128)S(1)} async-done(((f32[32,8,128]{2,1,0:T(8,128)}), f32[32,8,128]{2,1,0:T(8,128)S(1)}, u32[]{:S(2)}, u32[]{:S(2)}) %all-to-all-start) | async-done | bytes 131104 | tf_op jit(solution)/shard_map/all_to_all | solution.py:714
  21.3 3.5 %first_lanes_kernel.1 = (f32[1024,128]{1,0:T(8,128)S(1)}, f32[1280,128]{1,0:T(8,128)S(1)}, f32[8,128]{1,0:T(8,128)S(1)}) custom-call(f32[5,12,16,128]{3,2,1,0:T(8,128)S(1)} %get-tuple-element.43.nat_ref.nat_in, f32[1280,128]{1,0:T(8,128)S(1)} %get-tuple-element.46.rows_ref.zu, f32[1280,128]{1,0:T(8,128)S(1)} %halves_kernel.1.zf_in, ...), custom_call_target="tpu_custom_call", output_to_operand_aliasing={{1}: (2, {})} | custom-call | flops 4000000000 | bytes 4259840 | tf_op jit(solution)/shard_map/first_lanes_kernel/pallas_call | solution.py:646
  24.8 0.0 collective-permute-done.3.lo_in
  24.8 0.0 collective-permute-done.4.hi_in
  24.9 3.4 %first_rows_kernel.1 = (f32[5,12,16,128]{3,2,1,0:T(8,128)S(1)}, f32[1,240,128]{2,1,0:T(8,128)S(1)}, f32[1,240,128]{2,1,0:T(8,128)S(1)}, f32[1,384,128]{2,1,0:T(8...) custom-call(f32[5,12,16,128]{3,2,1,0:T(8,128)S(1)} %get-tuple-elemen, ...), custom_call_target="tpu_custom_call", output_to_operand_aliasing={{0}: (0, {}), {1}: (1, {}), {2}: (2, {})} | custom-call | flops 2500000000 | bytes 4104192 | tf_op jit(solution)/shard_map/first_rows_kernel/pallas_call | solution.py:646
  28.2 3.3 %all-to-all-start.1 = ((f32[32,8,128]{2,1,0:T(8,128)}), f32[32,8,128]{2,1,0:T(8,128)S(1)}, u32[]{:S(2)}, u32[]{:S(2)}) async-start(f32[32,8,128]{2,1,0:T(8,128)} %get-tuple-element.64), calls=%async_computation.1 | async-start | bytes 262144 | tf_op jit(solution)/shard_map/all_to_all | solution.py:752
  31.6 0.3 collective-permute-start.10
  31.9 1.7 %collective-permute-start.8 = (f32[128,128]{1,0:T(8,128)S(1)}, f32[128,128]{1,0:T(8,128)S(1)}, u32[]{:S(2)}, u32[]{:S(2)}) collective-permute-start(f32[128,128]{1,0:T(8,128)S(1)} %get-tuple-element.61), channel_id=1, source_target_pairs={{0,8},{8,16},{16,24},{24,0},{1,9},{9,17},{17,25},{25,1},{2,10},{10... | collective-permute-start | bytes 196616 | tf_op jit(solution)/shard_map/ppermute | solution.py:661
  33.6 1.2 %collective-permute-start.9 = (f32[128,128]{1,0:T(8,128)S(1)}, f32[128,128]{1,0:T(8,128)S(1)}, u32[]{:S(2)}, u32[]{:S(2)}) collective-permute-start(f32[128,128]{1,0:T(8,128)S(1)} %get-tuple-element.62), channel_id=1, source_target_pairs={{0,24},{8,0},{16,8},{24,16},{1,25},{9,1},{17,9},{25,17},{2,26},{10... | collective-permute-start | bytes 196616 | tf_op jit(solution)/shard_map/ppermute | solution.py:661
  34.8 1.7 %collective-permute-start.6 = (f32[1,240,128]{2,1,0:T(8,128)S(1)}, f32[1,240,128]{2,1,0:T(8,128)S(1)}, u32[]{:S(2)}, u32[]{:S(2)}) collective-permute-start(f32[1,240,128]{2,1,0:T(8,128)S(1)} %get-tuple-element.59), channel_id=1, source_target_pairs={{0,2},{2,4},{4,6},{6,0},{1,3},{3,5},{5,7},{7,1},{8,10},{10,12},{12... | collective-permute-start | bytes 368648 | tf_op jit(solution)/shard_map/ppermute | solution.py:661
  36.5 2.1 %collective-permute-start.7 = (f32[1,240,128]{2,1,0:T(8,128)S(1)}, f32[1,240,128]{2,1,0:T(8,128)S(1)}, u32[]{:S(2)}, u32[]{:S(2)}) collective-permute-start(f32[1,240,128]{2,1,0:T(8,128)S(1)} %get-tuple-element.60), channel_id=1, source_target_pairs={{0,6},{2,0},{4,2},{6,4},{1,7},{3,1},{5,3},{7,5},{8,14},{10,8},{12,... | collective-permute-start | bytes 368648 | tf_op jit(solution)/shard_map/ppermute | solution.py:661
  38.6 0.0 collective-permute-done.8.before_ref
  38.6 0.9 %collective-permute-done.9.behind_ref = f32[128,128]{1,0:T(8,128)S(1)} collective-permute-done((f32[128,128]{1,0:T(8,128)S(1)}, f32[128,128]{1,0:T(8,128)S(1)}, u32[]{:S(2)}, u32[]{:S(2)}) %collective-permute-start.9) | collective-permute-done | bytes 65568 | tf_op jit(solution)/shard_map/ppermute | solution.py:661
  39.6 0.0 collective-permute-done.10.side_ref
  39.6 0.2 all-to-all-done.1.al_ref
  39.8 4.3 %second_lanes_kernel.1 = (f32[1024,128]{1,0:T(8,128)S(1)}, f32[1024,128]{1,0:T(8,128)S(1)}, f32[8,128]{1,0:T(8,128)S(1)}) custom-call(f32[5,12,16,128]{3,2,1,0:T(8,128)S(1)} %get-tuple-element.58.nat_ref, f32[128,128]{1,0:T(8,128)S(1)} %collective-permute-done.8.before_ref, f32[128,128]{1,0:T(8,128)S(1)} %collective-permute-done.9.behind_ref, ...), custom_call_target="tpu_custom_call" | custom-call | flops 4000000000 | bytes 1900544 | tf_op jit(solution)/shard_map/second_lanes_kernel/pallas_call | solution.py:646
  44.0 0.0 collective-permute-done.6.lo_ref
  44.1 0.0 collective-permute-done.7.hi_ref
  44.1 2.3 %second_rows_kernel.1 = (f32[240,128]{1,0:T(8,128)S(1)}, f32[240,128]{1,0:T(8,128)S(1)}, f32[240,128]{1,0:T(8,128)S(1)}, f32[240,128]{1,0:T(8,128)S(1)}) custom-call(f32[5,12,16,128]{3,2,1,0:T(8,128)S(1)} %get-tuple-element.58.nat_ref, f32[1,240,128]{2,1,0:T(8,128)S(1)} %collective-permute-done.6.lo_ref, f32[1,240,128]{2,1,0:T(8,128)S(1)} %collective-permute-done.7.hi_ref, ...), custom_call_target="tpu_custom_call" | custom-call | flops 2500000000 | bytes 3825664 | tf_op jit(solution)/shard_map/second_rows_kernel/pallas_call | solution.py:646
  46.4 1.4 %collective-permute-start.11 = (f32[240,128]{1,0:T(8,128)S(1)}, f32[240,128]{1,0:T(8,128)S(1)}, u32[]{:S(2)}, u32[]{:S(2)}) collective-permute-start(f32[240,128]{1,0:T(8,128)S(1)} %get-tuple-element.70), channel_id=1, source_target_pairs={{0,8},{8,0},{16,24},{24,16},{1,9},{9,1},{17,25},{25,17},{2,10},{10... | collective-permute-start | bytes 368648 | tf_op jit(solution)/shard_map/ppermute | solution.py:665
  47.8 0.7 %collective-permute-start.12 = (f32[240,128]{1,0:T(8,128)S(1)}, f32[240,128]{1,0:T(8,128)S(1)}, u32[]{:S(2)}, u32[]{:S(2)}) collective-permute-start(f32[240,128]{1,0:T(8,128)S(1)} %get-tuple-element.71), channel_id=1, source_target_pairs={{0,16},{8,24},{16,0},{24,8},{1,17},{9,25},{17,1},{25,9},{2,18},{10... | collective-permute-start | bytes 368648 | tf_op jit(solution)/shard_map/ppermute | solution.py:665
  48.5 1.5 %collective-permute-start.13 = (f32[240,128]{1,0:T(8,128)S(1)}, f32[240,128]{1,0:T(8,128)S(1)}, u32[]{:S(2)}, u32[]{:S(2)}) collective-permute-start(f32[240,128]{1,0:T(8,128)S(1)} %get-tuple-element.72), channel_id=1, source_target_pairs={{0,24},{8,16},{16,8},{24,0},{1,25},{9,17},{17,9},{25,1},{2,26},{10... | collective-permute-start | bytes 368648 | tf_op jit(solution)/shard_map/ppermute | solution.py:665
  50.0 2.6 %collective-permute-done.11.refs_1_ = f32[240,128]{1,0:T(8,128)S(1)} collective-permute-done((f32[240,128]{1,0:T(8,128)S(1)}, f32[240,128]{1,0:T(8,128)S(1)}, u32[]{:S(2)}, u32[]{:S(2)}) %collective-permute-start.11) | collective-permute-done | bytes 122912 | tf_op jit(solution)/shard_map/ppermute | solution.py:665
  52.6 2.5 %collective-permute-done.12.refs_2_ = f32[240,128]{1,0:T(8,128)S(1)} collective-permute-done((f32[240,128]{1,0:T(8,128)S(1)}, f32[240,128]{1,0:T(8,128)S(1)}, u32[]{:S(2)}, u32[]{:S(2)}) %collective-permute-start.12) | collective-permute-done | bytes 122912 | tf_op jit(solution)/shard_map/ppermute | solution.py:665
  55.1 0.0 collective-permute-done.13.refs_3_
  55.1 0.9 %close_kernel.1 = f32[1,5,12,16,128]{4,3,2,1,0:T(8,128)} custom-call(f32[240,128]{1,0:T(8,128)S(1)} %get-tuple-element.69.refs_0_, f32[240,128]{1,0:T(8,128)S(1)} %collective-permute-done.11.refs_1_, f32[240,128]{1,0:T(8,128)S(1)} %collective-permute-done.12.refs_2_, f32[240,128]{1,0:T(8,128)S(1)} %collective-permute-done.13.refs_3_), custom_call_target="tpu_custom_call" | custom-call | flops 500000000 | bytes 983040 | tf_op jit(solution)/shard_map/close_kernel/pallas_call | solution.py:646
Async XLA Ops:
  0.0 1.0 %copy-start = (f32[1,5,12,16,128]{4,3,2,1,0:T(8,128)S(1)}, f32[1,5,12,16,128]{4,3,2,1,0:T(8,128)}, u32[]{:S(2)}) copy-start(f32[1,5,12,16,128]{4,3,2,1,0:T(8,128)} %u_ref.1) | copy-start | bytes 1474564
  2.3 10.9 %collective-permute-start = (f32[288,128]{1,0:T(8,128)S(1)}, f32[288,128]{1,0:T(8,128)S(1)}, u32[]{:S(2)}, u32[]{:S(2)}) collective-permute-start(f32[288,128]{1,0:T(8,128)S(1)} %get-tuple-element.40), channel_id=1, source_target_pairs={{0,8},{8,0},{16,24},{24,16},{1,9},{9,1},{17,25},{25,17},{2,10},{10... | collective-permute-start | bytes 442376 | tf_op jit(solution)/shard_map/ppermute | solution.py:665
  5.3 8.5 %collective-permute-start.1 = (f32[288,128]{1,0:T(8,128)S(1)}, f32[288,128]{1,0:T(8,128)S(1)}, u32[]{:S(2)}, u32[]{:S(2)}) collective-permute-start(f32[288,128]{1,0:T(8,128)S(1)} %get-tuple-element.41), channel_id=1, source_target_pairs={{0,16},{8,24},{16,0},{24,8},{1,17},{9,25},{17,1},{25,9},{2,18},{10... | collective-permute-start | bytes 442376 | tf_op jit(solution)/shard_map/ppermute | solution.py:665
  6.8 7.0 %collective-permute-start.2 = (f32[288,128]{1,0:T(8,128)S(1)}, f32[288,128]{1,0:T(8,128)S(1)}, u32[]{:S(2)}, u32[]{:S(2)}) collective-permute-start(f32[288,128]{1,0:T(8,128)S(1)} %get-tuple-element.42), channel_id=1, source_target_pairs={{0,24},{8,16},{16,8},{24,0},{1,25},{9,17},{17,9},{25,1},{2,26},{10... | collective-permute-start | bytes 442376 | tf_op jit(solution)/shard_map/ppermute | solution.py:665
  6.8 14.5 %all-to-all-start = ((f32[32,8,128]{2,1,0:T(8,128)}), f32[32,8,128]{2,1,0:T(8,128)S(1)}, u32[]{:S(2)}, u32[]{:S(2)}) async-start(f32[32,8,128]{2,1,0:T(8,128)} %get-tuple-element.53), calls=%async_computation | async-start | bytes 262144 | tf_op jit(solution)/shard_map/all_to_all | solution.py:714
  14.2 4.3 %collective-permute-start.5 = (f32[1,384,128]{2,1,0:T(8,128)S(1)}, f32[1,384,128]{2,1,0:T(8,128)S(1)}, u32[]{:S(2)}, u32[]{:S(2)}) collective-permute-start(f32[1,384,128]{2,1,0:T(8,128)S(1)} %get-tuple-element.47), channel_id=1, source_target_pairs={{0,1},{1,0},{2,3},{3,2},{4,5},{5,4},{6,7},{7,6},{8,9},{9,8},{10,11... | collective-permute-start | bytes 589832 | tf_op jit(solution)/shard_map/ppermute | solution.py:661
  14.3 10.6 %collective-permute-start.3 = (f32[1,240,128]{2,1,0:T(8,128)S(1)}, f32[1,240,128]{2,1,0:T(8,128)S(1)}, u32[]{:S(2)}, u32[]{:S(2)}) collective-permute-start(f32[1,240,128]{2,1,0:T(8,128)S(1)} %get-tuple-element.44), channel_id=1, source_target_pairs={{0,2},{2,4},{4,6},{6,0},{1,3},{3,5},{5,7},{7,1},{8,10},{10,12},{12... | collective-permute-start | bytes 368648 | tf_op jit(solution)/shard_map/ppermute | solution.py:661
  15.9 9.0 %collective-permute-start.4 = (f32[1,240,128]{2,1,0:T(8,128)S(1)}, f32[1,240,128]{2,1,0:T(8,128)S(1)}, u32[]{:S(2)}, u32[]{:S(2)}) collective-permute-start(f32[1,240,128]{2,1,0:T(8,128)S(1)} %get-tuple-element.45), channel_id=1, source_target_pairs={{0,6},{2,0},{4,2},{6,4},{1,7},{3,1},{5,3},{7,5},{8,14},{10,8},{12,... | collective-permute-start | bytes 368648 | tf_op jit(solution)/shard_map/ppermute | solution.py:661
  18.1 1.0 %copy-start.1 = (f32[5,12,16,128]{3,2,1,0:T(8,128)S(1)}, f32[5,12,16,128]{3,2,1,0:T(8,128)}, u32[]{:S(2)}) copy-start(f32[5,12,16,128]{3,2,1,0:T(8,128)} %init_ref) | copy-start | bytes 1474564
  28.2 11.5 %all-to-all-start.1 = ((f32[32,8,128]{2,1,0:T(8,128)}), f32[32,8,128]{2,1,0:T(8,128)S(1)}, u32[]{:S(2)}, u32[]{:S(2)}) async-start(f32[32,8,128]{2,1,0:T(8,128)} %get-tuple-element.64), calls=%async_computation.1 | async-start | bytes 262144 | tf_op jit(solution)/shard_map/all_to_all | solution.py:752
  31.6 8.0 %collective-permute-start.10 = (f32[1,384,128]{2,1,0:T(8,128)S(1)}, f32[1,384,128]{2,1,0:T(8,128)S(1)}, u32[]{:S(2)}, u32[]{:S(2)}) collective-permute-start(f32[1,384,128]{2,1,0:T(8,128)S(1)} %get-tuple-element.63), channel_id=1, source_target_pairs={{0,1},{1,0},{2,3},{3,2},{4,5},{5,4},{6,7},{7,6},{8,9},{9,8},{10,11... | collective-permute-start | bytes 589832 | tf_op jit(solution)/shard_map/ppermute | solution.py:661
  31.9 6.8 %collective-permute-start.8 = (f32[128,128]{1,0:T(8,128)S(1)}, f32[128,128]{1,0:T(8,128)S(1)}, u32[]{:S(2)}, u32[]{:S(2)}) collective-permute-start(f32[128,128]{1,0:T(8,128)S(1)} %get-tuple-element.61), channel_id=1, source_target_pairs={{0,8},{8,16},{16,24},{24,0},{1,9},{9,17},{17,25},{25,1},{2,10},{10... | collective-permute-start | bytes 196616 | tf_op jit(solution)/shard_map/ppermute | solution.py:661
  33.6 6.0 %collective-permute-start.9 = (f32[128,128]{1,0:T(8,128)S(1)}, f32[128,128]{1,0:T(8,128)S(1)}, u32[]{:S(2)}, u32[]{:S(2)}) collective-permute-start(f32[128,128]{1,0:T(8,128)S(1)} %get-tuple-element.62), channel_id=1, source_target_pairs={{0,24},{8,0},{16,8},{24,16},{1,25},{9,1},{17,9},{25,17},{2,26},{10... | collective-permute-start | bytes 196616 | tf_op jit(solution)/shard_map/ppermute | solution.py:661
  34.8 9.2 %collective-permute-start.6 = (f32[1,240,128]{2,1,0:T(8,128)S(1)}, f32[1,240,128]{2,1,0:T(8,128)S(1)}, u32[]{:S(2)}, u32[]{:S(2)}) collective-permute-start(f32[1,240,128]{2,1,0:T(8,128)S(1)} %get-tuple-element.59), channel_id=1, source_target_pairs={{0,2},{2,4},{4,6},{6,0},{1,3},{3,5},{5,7},{7,1},{8,10},{10,12},{12... | collective-permute-start | bytes 368648 | tf_op jit(solution)/shard_map/ppermute | solution.py:661
  36.5 7.6 %collective-permute-start.7 = (f32[1,240,128]{2,1,0:T(8,128)S(1)}, f32[1,240,128]{2,1,0:T(8,128)S(1)}, u32[]{:S(2)}, u32[]{:S(2)}) collective-permute-start(f32[1,240,128]{2,1,0:T(8,128)S(1)} %get-tuple-element.60), channel_id=1, source_target_pairs={{0,6},{2,0},{4,2},{6,4},{1,7},{3,1},{5,3},{7,5},{8,14},{10,8},{12,... | collective-permute-start | bytes 368648 | tf_op jit(solution)/shard_map/ppermute | solution.py:661
  46.4 6.2 %collective-permute-start.11 = (f32[240,128]{1,0:T(8,128)S(1)}, f32[240,128]{1,0:T(8,128)S(1)}, u32[]{:S(2)}, u32[]{:S(2)}) collective-permute-start(f32[240,128]{1,0:T(8,128)S(1)} %get-tuple-element.70), channel_id=1, source_target_pairs={{0,8},{8,0},{16,24},{24,16},{1,9},{9,1},{17,25},{25,17},{2,10},{10... | collective-permute-start | bytes 368648 | tf_op jit(solution)/shard_map/ppermute | solution.py:665
  47.8 7.3 %collective-permute-start.12 = (f32[240,128]{1,0:T(8,128)S(1)}, f32[240,128]{1,0:T(8,128)S(1)}, u32[]{:S(2)}, u32[]{:S(2)}) collective-permute-start(f32[240,128]{1,0:T(8,128)S(1)} %get-tuple-element.71), channel_id=1, source_target_pairs={{0,16},{8,24},{16,0},{24,8},{1,17},{9,25},{17,1},{25,9},{2,18},{10... | collective-permute-start | bytes 368648 | tf_op jit(solution)/shard_map/ppermute | solution.py:665
  48.5 6.6 %collective-permute-start.13 = (f32[240,128]{1,0:T(8,128)S(1)}, f32[240,128]{1,0:T(8,128)S(1)}, u32[]{:S(2)}, u32[]{:S(2)}) collective-permute-start(f32[240,128]{1,0:T(8,128)S(1)} %get-tuple-element.72), channel_id=1, source_target_pairs={{0,24},{8,16},{16,8},{24,0},{1,25},{9,17},{17,9},{25,1},{2,26},{10... | collective-permute-start | bytes 368648 | tf_op jit(solution)/shard_map/ppermute | solution.py:665

commit v11 on v10

--- a/solution.py
+++ b/solution.py
@@ -204,7 +204,7 @@
     def row(self, c, i, t):
         if i < self.per:
             return c * self.nz + (i * self.ny + t)
-        return (self.comps + c // 2) * self.nz + lax.rem(c, 2) * self.half + ((i - self.per) * self.ny + t)
+        return (self.comps + c // 2) * self.nz + (c % 2) * self.half + ((i - self.per) * self.ny + t)
 
 
 def depth_fluxes(blocks, read, write):
@@ -234,7 +234,7 @@
         depth_fluxes(blocks, read, write)
         return carry
 
-    lax.fori_loop(0, nodes, node, 0, unroll=2)
+    lax.fori_loop(0, nodes, node, 0, unroll=True)
 
 
 def write_edges(read, nx, ny, comps, lo_ref, hi_ref, side_ref):
@@ -259,7 +259,7 @@
         speeds = signal_speeds([read(c, i) for c in range(comps)])
         return tuple(jnp.maximum(b, s) for b, s in zip(best, speeds))
 
-    return lax.fori_loop(first, first + count, step, best, unroll=4 if count % 4 == 0 else count)
+    return lax.fori_loop(first, first + count, step, best, unroll=True)
 
 
 def speed_row(best, width):
@@ -379,7 +379,7 @@
     write_edges(lambda c, i: nat_ref[c, i], nx, ny, comps, lo_ref, hi_ref, side_ref)
 
 
-def along_second(nat_ref, side_ref, alpha, fy, yp, ym, gp, gm):
+def along_second(nat_ref, side_ref, alpha, fy, yp, ym, gp, gm, beside=None):
     comps, nx, ny, nz = nat_ref.shape
     rows = gp.shape[0] // (2 * HALO)
 
@@ -417,6 +417,8 @@
         def store(i, value):
             fy[pl.ds(i * rows + first, TILE), :] = value
 
+        if beside is not None:
+            beside(b)
         stream(load, store, ny)
         return carry
 
@@ -452,7 +454,7 @@
     return jnp.concatenate([zf[rows_at((m * blocks.count + b) * size, width), :] for m in range(nodes)], axis=0)
 
 
-def along_first(u, alphas, lo_ref, hi_ref, fy, rate, xp, xm, extra, after):
+def along_first(u, alphas, lo_ref, hi_ref, fy, rate, xp, xm, extra, after, unrolled=False):
     comps, nx, ny, nz = rate.shape
     rows = -(-comps * nx // TILE) * TILE
     every = range(comps)
@@ -477,8 +479,7 @@
 
         lax.fori_loop(0, HALO, ghost, 0, unroll=HALO)
 
-    def along(c, carry):
-        after(jnp.maximum(c - 1, 0))
+    def component(c):
         for t in range(0, ny, TILE):
 
             def load(j, t=t):
@@ -490,10 +491,21 @@
                 rate[c, i, pl.ds(t, TILE), :] = value if extra is None else value + extra(c, i, t)
 
             stream(load, store, nx)
+
+    def along(c, carry):
+        after(jnp.maximum(c - 1, 0))
+        component(c)
         return carry
 
-    lax.fori_loop(0, comps, along, 0)
-    after(jnp.int32(comps - 1))
+    if unrolled:
+        for c in every:
+            if c:
+                after(c - 1)
+            component(c)
+        after(comps - 1)
+    else:
+        lax.fori_loop(0, comps, along, 0)
+        after(jnp.int32(comps - 1))
 
 
 def tile_rows(tile):
@@ -540,9 +552,12 @@
     write_halves(blocks, nodes, zu, zf)
     tile = speeds_of(al_ref, al_out, alphas, nodes)
     along_last(blocks, nodes, zf, zu, alphas)
-    for b in range(blocks.count):
-        fz[pl.ds(b * nz, nz), :] = block_rates(blocks, nodes, zf, b).T
-    along_second(nat_ref, side_ref, tile[1:2], fy, *scratch)
+
+    def turn(b):
+        fz[rows_at(b * nz, nz), :] = block_rates(blocks, nodes, zf, b).T
+
+    assert blocks.count == scratch[2].shape[0] // (2 * HALO) // TILE
+    along_second(nat_ref, side_ref, tile[1:2], fy, *scratch, beside=turn)
 
 
 def first_rows_kernel(nat_in, lo_in, hi_in, al_in, zf, fy, start_ref, *refs, nodes):
@@ -567,10 +582,11 @@
 
     def after(c):
         blocks.put_whole(nat_ref, c, state(blocks.whole(rate, c), c))
-        b = blocks.comps + c // 2
-        blocks.put_leftovers(nat_ref, b, state(blocks.leftovers(rate, *blocks.pair(b)), b))
-
-    along_first(lambda c, i: nat_in[c, i], tile_rows(al_in), lo_in, hi_in, fy, rate, xp, xm, None, after)
+        if c % 2 == 1 or c == comps - 1:
+            b = comps + c // 2
+            blocks.put_leftovers(nat_ref, b, state(blocks.leftovers(rate, *blocks.pair(b)), b))
+
+    along_first(lambda c, i: nat_in[c, i], tile_rows(al_in), lo_in, hi_in, fy, rate, xp, xm, None, after, True)
 
     def read(c, i):
         return nat_ref[c, i]
@@ -613,7 +629,7 @@
                         value = value + weights[k][j] * rates[j]
                     outs[k][at, :] = value
 
-    along_first(lambda c, i: nat_ref[c, i], tile_rows(al_ref), lo_ref, hi_ref, fy, rate, xp, xm, extra, after)
+    along_first(lambda c, i: nat_ref[c, i], tile_rows(al_ref), lo_ref, hi_ref, fy, rate, xp, xm, extra, after, True)
 
 
 def close_kernel(*refs):

time: 56.3 us -> 55.4 us (0.984)
  Pallas kernels: 17.1 us -> 15.8 us
    pallas_call x9, Pallas kernels: 17.1 us -> 15.8 us  [call(): pl.pallas_call(kernel, out_shape=[jax.ShapeDtypeStruct(shape, jnp.float32...]
  transfers between devices with their start and end apart: 16 -> 16, of which waited for: 6 -> 7; matrix products, arithmetic and copies ran while one was open for 0% -> 0% of each run, Pallas kernels for 16% -> 16%
where the time goes in v11:
time: 55.4 us; the launch traced here: 55.1 us
  starting transfers between devices  28.8 us (52%)
  Pallas kernels  15.8 us (29%)
  waiting for transfers between devices  8.61 us (16%)
  local copies, waits for them, and re-layouts  1.81 us (3%)
    pallas_call x9, Pallas kernels, call(): pl.pallas_call(kernel, out_shape=[jax.ShapeDtypeStruct(shape, jnp.float32...  15.8 us
    ppermute x8, starting transfers between devices, shifted(): lax.ppermute(value, axis, [(i, (i + by) % count) for i in range(count)])  11 us
    all_to_all x2, starting transfers between devices, local(): speeds = lax.all_to_all(speeds, everyone, 0, 0)  9.65 us
    ppermute x6, starting transfers between devices, swapped(): lax.ppermute(value, 'node', [(i, i ^ by) for i in range(lax.axis_size('no...  8.1 us
    ppermute x6, waiting for transfers between devices, swapped(): lax.ppermute(value, 'node', [(i, i ^ by) for i in range(lax.axis_size('no...  5.81 us
    unnamed x4, local copies, waits for them, and re-layouts  1.81 us
    all_to_all x2, waiting for transfers between devices, local(): speeds = lax.all_to_all(speeds, everyone, 0, 0)  1.66 us
    ppermute x8, waiting for transfers between devices, shifted(): lax.ppermute(value, axis, [(i, (i + by) % count) for i in range(count)])  1.14 us
  transfers between devices with their start and end apart: 16, of which 7 were waited for; matrix products, arithmetic and copies ran while one was open for 0% of the time, Pallas kernels for 16%

profile of v11, /device:TPU:0, one launch (start us, length us, event | category | flops | bytes accessed | tf_op | source)
XLA Modules:
  0.0 55.1 jit_solution(5583611118097254372)
XLA Ops:
  0.0 0.0 copy-start
  0.0 1.0 %copy-done = f32[1,5,12,16,128]{4,3,2,1,0:T(8,128)S(1)} copy-done((f32[1,5,12,16,128]{4,3,2,1,0:T(8,128)S(1)}, f32[1,5,12,16,128]{4,3,2,1,0:T(8,128)}, u32[]{:S(2)}) %copy-start) | copy-done | bytes 491544
  1.0 1.2 %open_kernel.1 = (f32[288,128]{1,0:T(8,128)S(1)}, f32[288,128]{1,0:T(8,128)S(1)}, f32[288,128]{1,0:T(8,128)S(1)}, f32[288,128]{1,0:T(8,128)S(1)}, f32[32,8,128]{2,1,0:T(8,128)}) custom-call(f32[1,5,12,16,128]{4,3,2,1,0:T(8,128)S(1)} %copy-done), custom_call_target="tpu_custom_call" | custom-call | flops 500000000 | bytes 983040 | tf_op jit(solution)/shard_map/open_kernel/pallas_call | solution.py:662
  2.3 3.0 %collective-permute-start = (f32[288,128]{1,0:T(8,128)S(1)}, f32[288,128]{1,0:T(8,128)S(1)}, u32[]{:S(2)}, u32[]{:S(2)}) collective-permute-start(f32[288,128]{1,0:T(8,128)S(1)} %get-tuple-element.40), channel_id=1, source_target_pairs={{0,8},{8,0},{16,24},{24,16},{1,9},{9,1},{17,25},{25,17},{2,10},{10... | collective-permute-start | bytes 442376 | tf_op jit(solution)/shard_map/ppermute | solution.py:681
  5.3 1.5 %collective-permute-start.1 = (f32[288,128]{1,0:T(8,128)S(1)}, f32[288,128]{1,0:T(8,128)S(1)}, u32[]{:S(2)}, u32[]{:S(2)}) collective-permute-start(f32[288,128]{1,0:T(8,128)S(1)} %get-tuple-element.41), channel_id=1, source_target_pairs={{0,16},{8,24},{16,0},{24,8},{1,17},{9,25},{17,1},{25,9},{2,18},{10... | collective-permute-start | bytes 442376 | tf_op jit(solution)/shard_map/ppermute | solution.py:681
  6.8 0.0 collective-permute-start.2
  6.8 6.3 %all-to-all-start = ((f32[32,8,128]{2,1,0:T(8,128)}), f32[32,8,128]{2,1,0:T(8,128)S(1)}, u32[]{:S(2)}, u32[]{:S(2)}) async-start(f32[32,8,128]{2,1,0:T(8,128)} %get-tuple-element.53), calls=%async_computation | async-start | bytes 262144 | tf_op jit(solution)/shard_map/all_to_all | solution.py:730
  13.1 0.0 collective-permute-done.refs_1_
  13.1 0.6 %collective-permute-done.1.refs_2_ = f32[288,128]{1,0:T(8,128)S(1)} collective-permute-done((f32[288,128]{1,0:T(8,128)S(1)}, f32[288,128]{1,0:T(8,128)S(1)}, u32[]{:S(2)}, u32[]{:S(2)}) %collective-permute-start.1) | collective-permute-done | bytes 147488 | tf_op jit(solution)/shard_map/ppermute | solution.py:681
  13.7 0.0 collective-permute-done.2.refs_3_
  13.7 0.4 gather_kernel.1
  14.2 0.1 collective-permute-start.5
  14.2 1.6 %collective-permute-start.3 = (f32[1,240,128]{2,1,0:T(8,128)S(1)}, f32[1,240,128]{2,1,0:T(8,128)S(1)}, u32[]{:S(2)}, u32[]{:S(2)}) collective-permute-start(f32[1,240,128]{2,1,0:T(8,128)S(1)} %get-tuple-element.44), channel_id=1, source_target_pairs={{0,2},{2,4},{4,6},{6,0},{1,3},{3,5},{5,7},{7,1},{8,10},{10,12},{12... | collective-permute-start | bytes 368648 | tf_op jit(solution)/shard_map/ppermute | solution.py:677
  15.9 2.2 %collective-permute-start.4 = (f32[1,240,128]{2,1,0:T(8,128)S(1)}, f32[1,240,128]{2,1,0:T(8,128)S(1)}, u32[]{:S(2)}, u32[]{:S(2)}) collective-permute-start(f32[1,240,128]{2,1,0:T(8,128)S(1)} %get-tuple-element.45), channel_id=1, source_target_pairs={{0,6},{2,0},{4,2},{6,4},{1,7},{3,1},{5,3},{7,5},{8,14},{10,8},{12,... | collective-permute-start | bytes 368648 | tf_op jit(solution)/shard_map/ppermute | solution.py:677
  18.1 0.0 copy-start.1
  18.1 0.2 halves_kernel.1.zf_in
  18.4 0.0 collective-permute-done.5.side_ref
  18.4 0.8 %copy-done.1 = f32[5,12,16,128]{3,2,1,0:T(8,128)S(1)} copy-done((f32[5,12,16,128]{3,2,1,0:T(8,128)S(1)}, f32[5,12,16,128]{3,2,1,0:T(8,128)}, u32[]{:S(2)}) %copy-start.1) | copy-done | bytes 491544
  19.2 0.6 %start_kernel.1 = (f32[256,128]{1,0:T(8,128)S(1)}, f32[240,128]{1,0:T(8,128)S(1)}) custom-call(f32[5,12,16,128]{3,2,1,0:T(8,128)S(1)} %copy-done.1), custom_call_target="tpu_custom_call" | custom-call | flops 500000000 | bytes 983040 | tf_op jit(solution)/shard_map/start_kernel/pallas_call | solution.py:662
  19.8 1.5 %all-to-all-done.al_ref = f32[32,8,128]{2,1,0:T(8,128)S(1)} async-done(((f32[32,8,128]{2,1,0:T(8,128)}), f32[32,8,128]{2,1,0:T(8,128)S(1)}, u32[]{:S(2)}, u32[]{:S(2)}) %all-to-all-start) | async-done | bytes 131104 | tf_op jit(solution)/shard_map/all_to_all | solution.py:730
  21.3 3.5 %first_lanes_kernel.1 = (f32[1024,128]{1,0:T(8,128)S(1)}, f32[1280,128]{1,0:T(8,128)S(1)}, f32[8,128]{1,0:T(8,128)S(1)}) custom-call(f32[5,12,16,128]{3,2,1,0:T(8,128)S(1)} %get-tuple-element.43.nat_ref.nat_in, f32[1280,128]{1,0:T(8,128)S(1)} %get-tuple-element.46.rows_ref.zu, f32[1280,128]{1,0:T(8,128)S(1)} %halves_kernel.1.zf_in, ...), custom_call_target="tpu_custom_call", output_to_operand_aliasing={{1}: (2, {})} | custom-call | flops 4000000000 | bytes 4259840 | tf_op jit(solution)/shard_map/first_lanes_kernel/pallas_call | solution.py:662
  24.8 0.0 collective-permute-done.3.lo_in
  24.8 0.0 collective-permute-done.4.hi_in
  24.8 2.9 %first_rows_kernel.1 = (f32[5,12,16,128]{3,2,1,0:T(8,128)S(1)}, f32[1,240,128]{2,1,0:T(8,128)S(1)}, f32[1,240,128]{2,1,0:T(8,128)S(1)}, f32[1,384,128]{2,1,0:T(8...) custom-call(f32[5,12,16,128]{3,2,1,0:T(8,128)S(1)} %get-tuple-elemen, ...), custom_call_target="tpu_custom_call", output_to_operand_aliasing={{0}: (0, {}), {1}: (1, {}), {2}: (2, {})} | custom-call | flops 2500000000 | bytes 4104192 | tf_op jit(solution)/shard_map/first_rows_kernel/pallas_call | solution.py:662
  27.7 3.3 %all-to-all-start.1 = ((f32[32,8,128]{2,1,0:T(8,128)}), f32[32,8,128]{2,1,0:T(8,128)S(1)}, u32[]{:S(2)}, u32[]{:S(2)}) async-start(f32[32,8,128]{2,1,0:T(8,128)} %get-tuple-element.64), calls=%async_computation.1 | async-start | bytes 262144 | tf_op jit(solution)/shard_map/all_to_all | solution.py:768
  31.1 0.3 collective-permute-start.10
  31.4 1.7 %collective-permute-start.8 = (f32[128,128]{1,0:T(8,128)S(1)}, f32[128,128]{1,0:T(8,128)S(1)}, u32[]{:S(2)}, u32[]{:S(2)}) collective-permute-start(f32[128,128]{1,0:T(8,128)S(1)} %get-tuple-element.61), channel_id=1, source_target_pairs={{0,8},{8,16},{16,24},{24,0},{1,9},{9,17},{17,25},{25,1},{2,10},{10... | collective-permute-start | bytes 196616 | tf_op jit(solution)/shard_map/ppermute | solution.py:677
  33.1 1.2 %collective-permute-start.9 = (f32[128,128]{1,0:T(8,128)S(1)}, f32[128,128]{1,0:T(8,128)S(1)}, u32[]{:S(2)}, u32[]{:S(2)}) collective-permute-start(f32[128,128]{1,0:T(8,128)S(1)} %get-tuple-element.62), channel_id=1, source_target_pairs={{0,24},{8,0},{16,8},{24,16},{1,25},{9,1},{17,9},{25,17},{2,26},{10... | collective-permute-start | bytes 196616 | tf_op jit(solution)/shard_map/ppermute | solution.py:677
  34.3 1.7 %collective-permute-start.6 = (f32[1,240,128]{2,1,0:T(8,128)S(1)}, f32[1,240,128]{2,1,0:T(8,128)S(1)}, u32[]{:S(2)}, u32[]{:S(2)}) collective-permute-start(f32[1,240,128]{2,1,0:T(8,128)S(1)} %get-tuple-element.59), channel_id=1, source_target_pairs={{0,2},{2,4},{4,6},{6,0},{1,3},{3,5},{5,7},{7,1},{8,10},{10,12},{12... | collective-permute-start | bytes 368648 | tf_op jit(solution)/shard_map/ppermute | solution.py:677
  36.0 2.1 %collective-permute-start.7 = (f32[1,240,128]{2,1,0:T(8,128)S(1)}, f32[1,240,128]{2,1,0:T(8,128)S(1)}, u32[]{:S(2)}, u32[]{:S(2)}) collective-permute-start(f32[1,240,128]{2,1,0:T(8,128)S(1)} %get-tuple-element.60), channel_id=1, source_target_pairs={{0,6},{2,0},{4,2},{6,4},{1,7},{3,1},{5,3},{7,5},{8,14},{10,8},{12,... | collective-permute-start | bytes 368648 | tf_op jit(solution)/shard_map/ppermute | solution.py:677
  38.2 0.0 collective-permute-done.8.before_ref
  38.2 0.9 %collective-permute-done.9.behind_ref = f32[128,128]{1,0:T(8,128)S(1)} collective-permute-done((f32[128,128]{1,0:T(8,128)S(1)}, f32[128,128]{1,0:T(8,128)S(1)}, u32[]{:S(2)}, u32[]{:S(2)}) %collective-permute-start.9) | collective-permute-done | bytes 65568 | tf_op jit(solution)/shard_map/ppermute | solution.py:677
  39.1 0.0 collective-permute-done.10.side_ref
  39.1 0.2 all-to-all-done.1.al_ref
  39.3 3.9 %second_lanes_kernel.1 = (f32[1024,128]{1,0:T(8,128)S(1)}, f32[1024,128]{1,0:T(8,128)S(1)}, f32[8,128]{1,0:T(8,128)S(1)}) custom-call(f32[5,12,16,128]{3,2,1,0:T(8,128)S(1)} %get-tuple-element.58.nat_ref, f32[128,128]{1,0:T(8,128)S(1)} %collective-permute-done.8.before_ref, f32[128,128]{1,0:T(8,128)S(1)} %collective-permute-done.9.behind_ref, ...), custom_call_target="tpu_custom_call" | custom-call | flops 4000000000 | bytes 1900544 | tf_op jit(solution)/shard_map/second_lanes_kernel/pallas_call | solution.py:662
  43.2 0.0 collective-permute-done.6.lo_ref
  43.2 0.2 collective-permute-done.7.hi_ref
  43.4 2.0 %second_rows_kernel.1 = (f32[240,128]{1,0:T(8,128)S(1)}, f32[240,128]{1,0:T(8,128)S(1)}, f32[240,128]{1,0:T(8,128)S(1)}, f32[240,128]{1,0:T(8,128)S(1)}) custom-call(f32[5,12,16,128]{3,2,1,0:T(8,128)S(1)} %get-tuple-element.58.nat_ref, f32[1,240,128]{2,1,0:T(8,128)S(1)} %collective-permute-done.6.lo_ref, f32[1,240,128]{2,1,0:T(8,128)S(1)} %collective-permute-done.7.hi_ref, ...), custom_call_target="tpu_custom_call" | custom-call | flops 2500000000 | bytes 3825664 | tf_op jit(solution)/shard_map/second_rows_kernel/pallas_call | solution.py:662
  45.4 1.2 %collective-permute-start.11 = (f32[240,128]{1,0:T(8,128)S(1)}, f32[240,128]{1,0:T(8,128)S(1)}, u32[]{:S(2)}, u32[]{:S(2)}) collective-permute-start(f32[240,128]{1,0:T(8,128)S(1)} %get-tuple-element.70), channel_id=1, source_target_pairs={{0,8},{8,0},{16,24},{24,16},{1,9},{9,1},{17,25},{25,17},{2,10},{10... | collective-permute-start | bytes 368648 | tf_op jit(solution)/shard_map/ppermute | solution.py:681
  46.7 1.1 %collective-permute-start.12 = (f32[240,128]{1,0:T(8,128)S(1)}, f32[240,128]{1,0:T(8,128)S(1)}, u32[]{:S(2)}, u32[]{:S(2)}) collective-permute-start(f32[240,128]{1,0:T(8,128)S(1)} %get-tuple-element.71), channel_id=1, source_target_pairs={{0,16},{8,24},{16,0},{24,8},{1,17},{9,25},{17,1},{25,9},{2,18},{10... | collective-permute-start | bytes 368648 | tf_op jit(solution)/shard_map/ppermute | solution.py:681
  47.8 1.2 %collective-permute-start.13 = (f32[240,128]{1,0:T(8,128)S(1)}, f32[240,128]{1,0:T(8,128)S(1)}, u32[]{:S(2)}, u32[]{:S(2)}) collective-permute-start(f32[240,128]{1,0:T(8,128)S(1)} %get-tuple-element.72), channel_id=1, source_target_pairs={{0,24},{8,16},{16,8},{24,0},{1,25},{9,17},{17,9},{25,1},{2,26},{10... | collective-permute-start | bytes 368648 | tf_op jit(solution)/shard_map/ppermute | solution.py:681
  49.0 2.7 %collective-permute-done.11.refs_1_ = f32[240,128]{1,0:T(8,128)S(1)} collective-permute-done((f32[240,128]{1,0:T(8,128)S(1)}, f32[240,128]{1,0:T(8,128)S(1)}, u32[]{:S(2)}, u32[]{:S(2)}) %collective-permute-start.11) | collective-permute-done | bytes 122912 | tf_op jit(solution)/shard_map/ppermute | solution.py:681
  51.6 2.5 %collective-permute-done.12.refs_2_ = f32[240,128]{1,0:T(8,128)S(1)} collective-permute-done((f32[240,128]{1,0:T(8,128)S(1)}, f32[240,128]{1,0:T(8,128)S(1)}, u32[]{:S(2)}, u32[]{:S(2)}) %collective-permute-start.12) | collective-permute-done | bytes 122912 | tf_op jit(solution)/shard_map/ppermute | solution.py:681
  54.2 0.0 collective-permute-done.13.refs_3_
  54.2 0.9 %close_kernel.1 = f32[1,5,12,16,128]{4,3,2,1,0:T(8,128)} custom-call(f32[240,128]{1,0:T(8,128)S(1)} %get-tuple-element.69.refs_0_, f32[240,128]{1,0:T(8,128)S(1)} %collective-permute-done.11.refs_1_, f32[240,128]{1,0:T(8,128)S(1)} %collective-permute-done.12.refs_2_, f32[240,128]{1,0:T(8,128)S(1)} %collective-permute-done.13.refs_3_), custom_call_target="tpu_custom_call" | custom-call | flops 500000000 | bytes 983040 | tf_op jit(solution)/shard_map/close_kernel/pallas_call | solution.py:662
Async XLA Ops:
  0.0 1.0 %copy-start = (f32[1,5,12,16,128]{4,3,2,1,0:T(8,128)S(1)}, f32[1,5,12,16,128]{4,3,2,1,0:T(8,128)}, u32[]{:S(2)}) copy-start(f32[1,5,12,16,128]{4,3,2,1,0:T(8,128)} %u_ref.1) | copy-start | bytes 1474564
  2.3 10.9 %collective-permute-start = (f32[288,128]{1,0:T(8,128)S(1)}, f32[288,128]{1,0:T(8,128)S(1)}, u32[]{:S(2)}, u32[]{:S(2)}) collective-permute-start(f32[288,128]{1,0:T(8,128)S(1)} %get-tuple-element.40), channel_id=1, source_target_pairs={{0,8},{8,0},{16,24},{24,16},{1,9},{9,1},{17,25},{25,17},{2,10},{10... | collective-permute-start | bytes 442376 | tf_op jit(solution)/shard_map/ppermute | solution.py:681
  5.3 8.5 %collective-permute-start.1 = (f32[288,128]{1,0:T(8,128)S(1)}, f32[288,128]{1,0:T(8,128)S(1)}, u32[]{:S(2)}, u32[]{:S(2)}) collective-permute-start(f32[288,128]{1,0:T(8,128)S(1)} %get-tuple-element.41), channel_id=1, source_target_pairs={{0,16},{8,24},{16,0},{24,8},{1,17},{9,25},{17,1},{25,9},{2,18},{10... | collective-permute-start | bytes 442376 | tf_op jit(solution)/shard_map/ppermute | solution.py:681
  6.8 7.0 %collective-permute-start.2 = (f32[288,128]{1,0:T(8,128)S(1)}, f32[288,128]{1,0:T(8,128)S(1)}, u32[]{:S(2)}, u32[]{:S(2)}) collective-permute-start(f32[288,128]{1,0:T(8,128)S(1)} %get-tuple-element.42), channel_id=1, source_target_pairs={{0,24},{8,16},{16,8},{24,0},{1,25},{9,17},{17,9},{25,1},{2,26},{10... | collective-permute-start | bytes 442376 | tf_op jit(solution)/shard_map/ppermute | solution.py:681
  6.8 14.5 %all-to-all-start = ((f32[32,8,128]{2,1,0:T(8,128)}), f32[32,8,128]{2,1,0:T(8,128)S(1)}, u32[]{:S(2)}, u32[]{:S(2)}) async-start(f32[32,8,128]{2,1,0:T(8,128)} %get-tuple-element.53), calls=%async_computation | async-start | bytes 262144 | tf_op jit(solution)/shard_map/all_to_all | solution.py:730
  14.2 4.2 %collective-permute-start.5 = (f32[1,384,128]{2,1,0:T(8,128)S(1)}, f32[1,384,128]{2,1,0:T(8,128)S(1)}, u32[]{:S(2)}, u32[]{:S(2)}) collective-permute-start(f32[1,384,128]{2,1,0:T(8,128)S(1)} %get-tuple-element.47), channel_id=1, source_target_pairs={{0,1},{1,0},{2,3},{3,2},{4,5},{5,4},{6,7},{7,6},{8,9},{9,8},{10,11... | collective-permute-start | bytes 589832 | tf_op jit(solution)/shard_map/ppermute | solution.py:677
  14.2 10.6 %collective-permute-start.3 = (f32[1,240,128]{2,1,0:T(8,128)S(1)}, f32[1,240,128]{2,1,0:T(8,128)S(1)}, u32[]{:S(2)}, u32[]{:S(2)}) collective-permute-start(f32[1,240,128]{2,1,0:T(8,128)S(1)} %get-tuple-element.44), channel_id=1, source_target_pairs={{0,2},{2,4},{4,6},{6,0},{1,3},{3,5},{5,7},{7,1},{8,10},{10,12},{12... | collective-permute-start | bytes 368648 | tf_op jit(solution)/shard_map/ppermute | solution.py:677
  15.9 9.0 %collective-permute-start.4 = (f32[1,240,128]{2,1,0:T(8,128)S(1)}, f32[1,240,128]{2,1,0:T(8,128)S(1)}, u32[]{:S(2)}, u32[]{:S(2)}) collective-permute-start(f32[1,240,128]{2,1,0:T(8,128)S(1)} %get-tuple-element.45), channel_id=1, source_target_pairs={{0,6},{2,0},{4,2},{6,4},{1,7},{3,1},{5,3},{7,5},{8,14},{10,8},{12,... | collective-permute-start | bytes 368648 | tf_op jit(solution)/shard_map/ppermute | solution.py:677
  18.1 1.0 %copy-start.1 = (f32[5,12,16,128]{3,2,1,0:T(8,128)S(1)}, f32[5,12,16,128]{3,2,1,0:T(8,128)}, u32[]{:S(2)}) copy-start(f32[5,12,16,128]{3,2,1,0:T(8,128)} %init_ref) | copy-start | bytes 1474564
  27.7 11.5 %all-to-all-start.1 = ((f32[32,8,128]{2,1,0:T(8,128)}), f32[32,8,128]{2,1,0:T(8,128)S(1)}, u32[]{:S(2)}, u32[]{:S(2)}) async-start(f32[32,8,128]{2,1,0:T(8,128)} %get-tuple-element.64), calls=%async_computation.1 | async-start | bytes 262144 | tf_op jit(solution)/shard_map/all_to_all | solution.py:768
  31.1 8.0 %collective-permute-start.10 = (f32[1,384,128]{2,1,0:T(8,128)S(1)}, f32[1,384,128]{2,1,0:T(8,128)S(1)}, u32[]{:S(2)}, u32[]{:S(2)}) collective-permute-start(f32[1,384,128]{2,1,0:T(8,128)S(1)} %get-tuple-element.63), channel_id=1, source_target_pairs={{0,1},{1,0},{2,3},{3,2},{4,5},{5,4},{6,7},{7,6},{8,9},{9,8},{10,11... | collective-permute-start | bytes 589832 | tf_op jit(solution)/shard_map/ppermute | solution.py:677
  31.4 6.8 %collective-permute-start.8 = (f32[128,128]{1,0:T(8,128)S(1)}, f32[128,128]{1,0:T(8,128)S(1)}, u32[]{:S(2)}, u32[]{:S(2)}) collective-permute-start(f32[128,128]{1,0:T(8,128)S(1)} %get-tuple-element.61), channel_id=1, source_target_pairs={{0,8},{8,16},{16,24},{24,0},{1,9},{9,17},{17,25},{25,1},{2,10},{10... | collective-permute-start | bytes 196616 | tf_op jit(solution)/shard_map/ppermute | solution.py:677
  33.1 6.0 %collective-permute-start.9 = (f32[128,128]{1,0:T(8,128)S(1)}, f32[128,128]{1,0:T(8,128)S(1)}, u32[]{:S(2)}, u32[]{:S(2)}) collective-permute-start(f32[128,128]{1,0:T(8,128)S(1)} %get-tuple-element.62), channel_id=1, source_target_pairs={{0,24},{8,0},{16,8},{24,16},{1,25},{9,1},{17,9},{25,17},{2,26},{10... | collective-permute-start | bytes 196616 | tf_op jit(solution)/shard_map/ppermute | solution.py:677
  34.3 8.9 %collective-permute-start.6 = (f32[1,240,128]{2,1,0:T(8,128)S(1)}, f32[1,240,128]{2,1,0:T(8,128)S(1)}, u32[]{:S(2)}, u32[]{:S(2)}) collective-permute-start(f32[1,240,128]{2,1,0:T(8,128)S(1)} %get-tuple-element.59), channel_id=1, source_target_pairs={{0,2},{2,4},{4,6},{6,0},{1,3},{3,5},{5,7},{7,1},{8,10},{10,12},{12... | collective-permute-start | bytes 368648 | tf_op jit(solution)/shard_map/ppermute | solution.py:677
  36.0 7.4 %collective-permute-start.7 = (f32[1,240,128]{2,1,0:T(8,128)S(1)}, f32[1,240,128]{2,1,0:T(8,128)S(1)}, u32[]{:S(2)}, u32[]{:S(2)}) collective-permute-start(f32[1,240,128]{2,1,0:T(8,128)S(1)} %get-tuple-element.60), channel_id=1, source_target_pairs={{0,6},{2,0},{4,2},{6,4},{1,7},{3,1},{5,3},{7,5},{8,14},{10,8},{12,... | collective-permute-start | bytes 368648 | tf_op jit(solution)/shard_map/ppermute | solution.py:677
  45.4 6.2 %collective-permute-start.11 = (f32[240,128]{1,0:T(8,128)S(1)}, f32[240,128]{1,0:T(8,128)S(1)}, u32[]{:S(2)}, u32[]{:S(2)}) collective-permute-start(f32[240,128]{1,0:T(8,128)S(1)} %get-tuple-element.70), channel_id=1, source_target_pairs={{0,8},{8,0},{16,24},{24,16},{1,9},{9,1},{17,25},{25,17},{2,10},{10... | collective-permute-start | bytes 368648 | tf_op jit(solution)/shard_map/ppermute | solution.py:681
  46.7 7.5 %collective-permute-start.12 = (f32[240,128]{1,0:T(8,128)S(1)}, f32[240,128]{1,0:T(8,128)S(1)}, u32[]{:S(2)}, u32[]{:S(2)}) collective-permute-start(f32[240,128]{1,0:T(8,128)S(1)} %get-tuple-element.71), channel_id=1, source_target_pairs={{0,16},{8,24},{16,0},{24,8},{1,17},{9,25},{17,1},{25,9},{2,18},{10... | collective-permute-start | bytes 368648 | tf_op jit(solution)/shard_map/ppermute | solution.py:681
  47.8 6.4 %collective-permute-start.13 = (f32[240,128]{1,0:T(8,128)S(1)}, f32[240,128]{1,0:T(8,128)S(1)}, u32[]{:S(2)}, u32[]{:S(2)}) collective-permute-start(f32[240,128]{1,0:T(8,128)S(1)} %get-tuple-element.72), channel_id=1, source_target_pairs={{0,24},{8,16},{16,8},{24,0},{1,25},{9,17},{17,9},{25,1},{2,26},{10... | collective-permute-start | bytes 368648 | tf_op jit(solution)/shard_map/ppermute | solution.py:681

commit v12 on v11

--- a/solution.py
+++ b/solution.py
@@ -262,31 +262,21 @@
     return lax.fori_loop(first, first + count, step, best, unroll=True)
 
 
-def speed_row(best, width):
-    rows = [jnp.max(b, axis=0, keepdims=True) for b in best]
-    size = width
-    while size > TILE:
-        size //= 2
-        rows = [jnp.maximum(r, turned(r, -size)) for r in rows]
-    rows = [turned(r, TILE * k) for k, r in enumerate(rows)]
-    return merged(rows, lane_index(rows[0].shape) % width // TILE)
-
-
-def speed_tile(row, nodes):
-    nz = row.shape[-1]
+def speed_tile(best, nodes):
+    nz = best.shape[-1]
     width = nz // nodes
     shape = (3 * nodes, nz)
-    lane = lane_index(shape)
     place = lax.broadcasted_iota(jnp.int32, shape, 0)
-    mine = (lane // width == place % nodes) & (lane % width // TILE == place // nodes)
-    spots = jnp.max(jnp.where(mine, row, 0.0), axis=1, keepdims=True)
+    rows = jnp.where(place < nodes, best[:1], jnp.where(place < 2 * nodes, best[1:2], best[2:3]))
+    spots = jnp.max(jnp.where(lane_index(shape) // width == place % nodes, rows, 0.0), axis=1, keepdims=True)
     group = lane_index((1, nz)) // width
     rows = [merged([spots[k * nodes + m : k * nodes + m + 1] for m in range(nodes)], group) for k in range(3)]
     return jnp.concatenate(rows + [jnp.zeros((TILE - 3, nz), jnp.float32)], axis=0), spots
 
 
-def send_speeds(row, tiles_ref, out_hbm, sem):
-    tiles_ref[...] = jnp.broadcast_to(row[None], tiles_ref.shape)
+def send_speeds(rows, tiles_ref, out_hbm, sem):
+    tile = jnp.concatenate(rows + [jnp.zeros((TILE - 3, rows[0].shape[-1]), jnp.float32)], axis=0)
+    tiles_ref[...] = jnp.broadcast_to(tile[None], tiles_ref.shape)
     copy = pltpu.make_async_copy(tiles_ref, out_hbm, sem)
     copy.start()
     return copy
@@ -303,9 +293,8 @@
     width = nz // nodes
     rows = [jnp.max(b, axis=0, keepdims=True) for b in best]
     rows = [functools.reduce(jnp.maximum, [turned(r, width * k) for k in range(nodes)]) for r in rows]
-    row = speed_row(rows, width)
-    row = jnp.where(lane_index(row.shape) // width == me, row, 0.0)
-    copy = send_speeds(row, tiles_ref, speeds_hbm, sem)
+    mine = lane_index(rows[0].shape) // width == me
+    copy = send_speeds([jnp.where(mine, r, 0.0) for r in rows], tiles_ref, speeds_hbm, sem)
     quarters = [me ^ k for k in range(nodes)]
     for b in range(blocks.count):
         send_quarter(blocks, blocks.natural(u_ref.at[0], b).T, ring, b, parts, quarters, width)
@@ -513,7 +502,7 @@
 
 
 def speeds_of(al_ref, al_out, alphas, nodes):
-    tile, spots = speed_tile(jnp.max(al_ref[...], axis=0)[:1], nodes)
+    tile, spots = speed_tile(jnp.max(al_ref[...], axis=0), nodes)
     al_out[...] = tile
     for m in range(nodes):
         at = 2 * nodes + m
@@ -592,8 +581,8 @@
         return nat_ref[c, i]
 
     best = tuple(jnp.zeros((ny, nz), jnp.float32) for _ in range(3))
-    row = speed_row(faster(best, read, 0, nx, comps), width)
-    copy = send_speeds(row, tiles_ref, speeds_hbm, sem)
+    best = faster(best, read, 0, nx, comps)
+    copy = send_speeds([jnp.max(b, axis=0, keepdims=True) for b in best], tiles_ref, speeds_hbm, sem)
     write_edges(read, nx, ny, comps, lo_ref, hi_ref, side_ref)
     copy.wait()
 

time: 55.4 us -> 55 us (level)
  no operation moved by 1% of the time
where the time goes in v12:
time: 55 us; the launch traced here: 54.7 us
  starting transfers between devices  28.8 us (52%)
  Pallas kernels  15.4 us (28%)
  waiting for transfers between devices  8.61 us (16%)
  local copies, waits for them, and re-layouts  1.81 us (3%)
    pallas_call x9, Pallas kernels, call(): pl.pallas_call(kernel, out_shape=[jax.ShapeDtypeStruct(shape, jnp.float32...  15.4 us
    ppermute x8, starting transfers between devices, shifted(): lax.ppermute(value, axis, [(i, (i + by) % count) for i in range(count)])  11 us
    all_to_all x2, starting transfers between devices, local(): speeds = lax.all_to_all(speeds, everyone, 0, 0)  9.65 us
    ppermute x6, starting transfers between devices, swapped(): lax.ppermute(value, 'node', [(i, i ^ by) for i in range(lax.axis_size('no...  8.1 us
    ppermute x6, waiting for transfers between devices, swapped(): lax.ppermute(value, 'node', [(i, i ^ by) for i in range(lax.axis_size('no...  5.81 us
    unnamed x4, local copies, waits for them, and re-layouts  1.81 us
    all_to_all x2, waiting for transfers between devices, local(): speeds = lax.all_to_all(speeds, everyone, 0, 0)  1.66 us
    ppermute x8, waiting for transfers between devices, shifted(): lax.ppermute(value, axis, [(i, (i + by) % count) for i in range(count)])  1.14 us
  transfers between devices with their start and end apart: 16, of which 7 were waited for; matrix products, arithmetic and copies ran while one was open for 0% of the time, Pallas kernels for 16%

profile of v12, /device:TPU:0, one launch (start us, length us, event | category | flops | bytes accessed | tf_op | source)
XLA Modules:
  0.0 54.7 jit_solution(12949937430285903971)
XLA Ops:
  0.0 0.0 copy-start
  0.0 1.0 %copy-done = f32[1,5,12,16,128]{4,3,2,1,0:T(8,128)S(1)} copy-done((f32[1,5,12,16,128]{4,3,2,1,0:T(8,128)S(1)}, f32[1,5,12,16,128]{4,3,2,1,0:T(8,128)}, u32[]{:S(2)}) %copy-start) | copy-done | bytes 491544
  1.0 1.0 %open_kernel.1 = (f32[288,128]{1,0:T(8,128)S(1)}, f32[288,128]{1,0:T(8,128)S(1)}, f32[288,128]{1,0:T(8,128)S(1)}, f32[288,128]{1,0:T(8,128)S(1)}, f32[32,8,128]{2,1,0:T(8,128)}) custom-call(f32[1,5,12,16,128]{4,3,2,1,0:T(8,128)S(1)} %copy-done), custom_call_target="tpu_custom_call" | custom-call | flops 500000000 | bytes 983040 | tf_op jit(solution)/shard_map/open_kernel/pallas_call | solution.py:651
  2.0 3.0 %collective-permute-start = (f32[288,128]{1,0:T(8,128)S(1)}, f32[288,128]{1,0:T(8,128)S(1)}, u32[]{:S(2)}, u32[]{:S(2)}) collective-permute-start(f32[288,128]{1,0:T(8,128)S(1)} %get-tuple-element.40), channel_id=1, source_target_pairs={{0,8},{8,0},{16,24},{24,16},{1,9},{9,1},{17,25},{25,17},{2,10},{10... | collective-permute-start | bytes 442376 | tf_op jit(solution)/shard_map/ppermute | solution.py:670
  5.0 1.5 %collective-permute-start.1 = (f32[288,128]{1,0:T(8,128)S(1)}, f32[288,128]{1,0:T(8,128)S(1)}, u32[]{:S(2)}, u32[]{:S(2)}) collective-permute-start(f32[288,128]{1,0:T(8,128)S(1)} %get-tuple-element.41), channel_id=1, source_target_pairs={{0,16},{8,24},{16,0},{24,8},{1,17},{9,25},{17,1},{25,9},{2,18},{10... | collective-permute-start | bytes 442376 | tf_op jit(solution)/shard_map/ppermute | solution.py:670
  6.5 0.0 collective-permute-start.2
  6.6 6.3 %all-to-all-start = ((f32[32,8,128]{2,1,0:T(8,128)}), f32[32,8,128]{2,1,0:T(8,128)S(1)}, u32[]{:S(2)}, u32[]{:S(2)}) async-start(f32[32,8,128]{2,1,0:T(8,128)} %get-tuple-element.53), calls=%async_computation | async-start | bytes 262144 | tf_op jit(solution)/shard_map/all_to_all | solution.py:719
  12.9 0.0 collective-permute-done.refs_1_
  12.9 0.6 %collective-permute-done.1.refs_2_ = f32[288,128]{1,0:T(8,128)S(1)} collective-permute-done((f32[288,128]{1,0:T(8,128)S(1)}, f32[288,128]{1,0:T(8,128)S(1)}, u32[]{:S(2)}, u32[]{:S(2)}) %collective-permute-start.1) | collective-permute-done | bytes 147488 | tf_op jit(solution)/shard_map/ppermute | solution.py:670
  13.5 0.0 collective-permute-done.2.refs_3_
  13.5 0.4 gather_kernel.1
  13.9 0.1 collective-permute-start.5
  14.0 1.6 %collective-permute-start.3 = (f32[1,240,128]{2,1,0:T(8,128)S(1)}, f32[1,240,128]{2,1,0:T(8,128)S(1)}, u32[]{:S(2)}, u32[]{:S(2)}) collective-permute-start(f32[1,240,128]{2,1,0:T(8,128)S(1)} %get-tuple-element.44), channel_id=1, source_target_pairs={{0,2},{2,4},{4,6},{6,0},{1,3},{3,5},{5,7},{7,1},{8,10},{10,12},{12... | collective-permute-start | bytes 368648 | tf_op jit(solution)/shard_map/ppermute | solution.py:666
  15.6 2.2 %collective-permute-start.4 = (f32[1,240,128]{2,1,0:T(8,128)S(1)}, f32[1,240,128]{2,1,0:T(8,128)S(1)}, u32[]{:S(2)}, u32[]{:S(2)}) collective-permute-start(f32[1,240,128]{2,1,0:T(8,128)S(1)} %get-tuple-element.45), channel_id=1, source_target_pairs={{0,6},{2,0},{4,2},{6,4},{1,7},{3,1},{5,3},{7,5},{8,14},{10,8},{12,... | collective-permute-start | bytes 368648 | tf_op jit(solution)/shard_map/ppermute | solution.py:666
  17.9 0.0 copy-start.1
  17.9 0.2 halves_kernel.1.zf_in
  18.1 0.0 collective-permute-done.5.side_ref
  18.1 0.8 %copy-done.1 = f32[5,12,16,128]{3,2,1,0:T(8,128)S(1)} copy-done((f32[5,12,16,128]{3,2,1,0:T(8,128)S(1)}, f32[5,12,16,128]{3,2,1,0:T(8,128)}, u32[]{:S(2)}) %copy-start.1) | copy-done | bytes 491544
  18.9 0.6 %start_kernel.1 = (f32[256,128]{1,0:T(8,128)S(1)}, f32[240,128]{1,0:T(8,128)S(1)}) custom-call(f32[5,12,16,128]{3,2,1,0:T(8,128)S(1)} %copy-done.1), custom_call_target="tpu_custom_call" | custom-call | flops 500000000 | bytes 983040 | tf_op jit(solution)/shard_map/start_kernel/pallas_call | solution.py:651
  19.6 1.5 %all-to-all-done.al_ref = f32[32,8,128]{2,1,0:T(8,128)S(1)} async-done(((f32[32,8,128]{2,1,0:T(8,128)}), f32[32,8,128]{2,1,0:T(8,128)S(1)}, u32[]{:S(2)}, u32[]{:S(2)}) %all-to-all-start) | async-done | bytes 131104 | tf_op jit(solution)/shard_map/all_to_all | solution.py:719
  21.1 3.5 %first_lanes_kernel.1 = (f32[1024,128]{1,0:T(8,128)S(1)}, f32[1280,128]{1,0:T(8,128)S(1)}, f32[8,128]{1,0:T(8,128)S(1)}) custom-call(f32[5,12,16,128]{3,2,1,0:T(8,128)S(1)} %get-tuple-element.43.nat_ref.nat_in, f32[1280,128]{1,0:T(8,128)S(1)} %get-tuple-element.46.rows_ref.zu, f32[1280,128]{1,0:T(8,128)S(1)} %halves_kernel.1.zf_in, ...), custom_call_target="tpu_custom_call", output_to_operand_aliasing={{1}: (2, {})} | custom-call | flops 4000000000 | bytes 4259840 | tf_op jit(solution)/shard_map/first_lanes_kernel/pallas_call | solution.py:651
  24.6 0.0 collective-permute-done.3.lo_in
  24.6 0.0 collective-permute-done.4.hi_in
  24.6 2.7 %first_rows_kernel.1 = (f32[5,12,16,128]{3,2,1,0:T(8,128)S(1)}, f32[1,240,128]{2,1,0:T(8,128)S(1)}, f32[1,240,128]{2,1,0:T(8,128)S(1)}, f32[1,384,128]{2,1,0:T(8...) custom-call(f32[5,12,16,128]{3,2,1,0:T(8,128)S(1)} %get-tuple-elemen, ...), custom_call_target="tpu_custom_call", output_to_operand_aliasing={{0}: (0, {}), {1}: (1, {}), {2}: (2, {})} | custom-call | flops 2500000000 | bytes 4104192 | tf_op jit(solution)/shard_map/first_rows_kernel/pallas_call | solution.py:651
  27.3 3.3 %all-to-all-start.1 = ((f32[32,8,128]{2,1,0:T(8,128)}), f32[32,8,128]{2,1,0:T(8,128)S(1)}, u32[]{:S(2)}, u32[]{:S(2)}) async-start(f32[32,8,128]{2,1,0:T(8,128)} %get-tuple-element.64), calls=%async_computation.1 | async-start | bytes 262144 | tf_op jit(solution)/shard_map/all_to_all | solution.py:757
  30.7 0.3 collective-permute-start.10
  31.0 1.7 %collective-permute-start.8 = (f32[128,128]{1,0:T(8,128)S(1)}, f32[128,128]{1,0:T(8,128)S(1)}, u32[]{:S(2)}, u32[]{:S(2)}) collective-permute-start(f32[128,128]{1,0:T(8,128)S(1)} %get-tuple-element.61), channel_id=1, source_target_pairs={{0,8},{8,16},{16,24},{24,0},{1,9},{9,17},{17,25},{25,1},{2,10},{10... | collective-permute-start | bytes 196616 | tf_op jit(solution)/shard_map/ppermute | solution.py:666
  32.7 1.2 %collective-permute-start.9 = (f32[128,128]{1,0:T(8,128)S(1)}, f32[128,128]{1,0:T(8,128)S(1)}, u32[]{:S(2)}, u32[]{:S(2)}) collective-permute-start(f32[128,128]{1,0:T(8,128)S(1)} %get-tuple-element.62), channel_id=1, source_target_pairs={{0,24},{8,0},{16,8},{24,16},{1,25},{9,1},{17,9},{25,17},{2,26},{10... | collective-permute-start | bytes 196616 | tf_op jit(solution)/shard_map/ppermute | solution.py:666
  33.9 1.7 %collective-permute-start.6 = (f32[1,240,128]{2,1,0:T(8,128)S(1)}, f32[1,240,128]{2,1,0:T(8,128)S(1)}, u32[]{:S(2)}, u32[]{:S(2)}) collective-permute-start(f32[1,240,128]{2,1,0:T(8,128)S(1)} %get-tuple-element.59), channel_id=1, source_target_pairs={{0,2},{2,4},{4,6},{6,0},{1,3},{3,5},{5,7},{7,1},{8,10},{10,12},{12... | collective-permute-start | bytes 368648 | tf_op jit(solution)/shard_map/ppermute | solution.py:666
  35.6 2.1 %collective-permute-start.7 = (f32[1,240,128]{2,1,0:T(8,128)S(1)}, f32[1,240,128]{2,1,0:T(8,128)S(1)}, u32[]{:S(2)}, u32[]{:S(2)}) collective-permute-start(f32[1,240,128]{2,1,0:T(8,128)S(1)} %get-tuple-element.60), channel_id=1, source_target_pairs={{0,6},{2,0},{4,2},{6,4},{1,7},{3,1},{5,3},{7,5},{8,14},{10,8},{12,... | collective-permute-start | bytes 368648 | tf_op jit(solution)/shard_map/ppermute | solution.py:666
  37.7 0.0 collective-permute-done.8.before_ref
  37.7 0.9 %collective-permute-done.9.behind_ref = f32[128,128]{1,0:T(8,128)S(1)} collective-permute-done((f32[128,128]{1,0:T(8,128)S(1)}, f32[128,128]{1,0:T(8,128)S(1)}, u32[]{:S(2)}, u32[]{:S(2)}) %collective-permute-start.9) | collective-permute-done | bytes 65568 | tf_op jit(solution)/shard_map/ppermute | solution.py:666
  38.7 0.0 collective-permute-done.10.side_ref
  38.7 0.2 all-to-all-done.1.al_ref
  38.8 3.9 %second_lanes_kernel.1 = (f32[1024,128]{1,0:T(8,128)S(1)}, f32[1024,128]{1,0:T(8,128)S(1)}, f32[8,128]{1,0:T(8,128)S(1)}) custom-call(f32[5,12,16,128]{3,2,1,0:T(8,128)S(1)} %get-tuple-element.58.nat_ref, f32[128,128]{1,0:T(8,128)S(1)} %collective-permute-done.8.before_ref, f32[128,128]{1,0:T(8,128)S(1)} %collective-permute-done.9.behind_ref, ...), custom_call_target="tpu_custom_call" | custom-call | flops 4000000000 | bytes 1900544 | tf_op jit(solution)/shard_map/second_lanes_kernel/pallas_call | solution.py:651
  42.8 0.0 collective-permute-done.6.lo_ref
  42.8 0.2 collective-permute-done.7.hi_ref
  43.0 2.0 %second_rows_kernel.1 = (f32[240,128]{1,0:T(8,128)S(1)}, f32[240,128]{1,0:T(8,128)S(1)}, f32[240,128]{1,0:T(8,128)S(1)}, f32[240,128]{1,0:T(8,128)S(1)}) custom-call(f32[5,12,16,128]{3,2,1,0:T(8,128)S(1)} %get-tuple-element.58.nat_ref, f32[1,240,128]{2,1,0:T(8,128)S(1)} %collective-permute-done.6.lo_ref, f32[1,240,128]{2,1,0:T(8,128)S(1)} %collective-permute-done.7.hi_ref, ...), custom_call_target="tpu_custom_call" | custom-call | flops 2500000000 | bytes 3825664 | tf_op jit(solution)/shard_map/second_rows_kernel/pallas_call | solution.py:651
  45.0 1.2 %collective-permute-start.11 = (f32[240,128]{1,0:T(8,128)S(1)}, f32[240,128]{1,0:T(8,128)S(1)}, u32[]{:S(2)}, u32[]{:S(2)}) collective-permute-start(f32[240,128]{1,0:T(8,128)S(1)} %get-tuple-element.70), channel_id=1, source_target_pairs={{0,8},{8,0},{16,24},{24,16},{1,9},{9,1},{17,25},{25,17},{2,10},{10... | collective-permute-start | bytes 368648 | tf_op jit(solution)/shard_map/ppermute | solution.py:670
  46.2 1.1 %collective-permute-start.12 = (f32[240,128]{1,0:T(8,128)S(1)}, f32[240,128]{1,0:T(8,128)S(1)}, u32[]{:S(2)}, u32[]{:S(2)}) collective-permute-start(f32[240,128]{1,0:T(8,128)S(1)} %get-tuple-element.71), channel_id=1, source_target_pairs={{0,16},{8,24},{16,0},{24,8},{1,17},{9,25},{17,1},{25,9},{2,18},{10... | collective-permute-start | bytes 368648 | tf_op jit(solution)/shard_map/ppermute | solution.py:670
  47.3 1.2 %collective-permute-start.13 = (f32[240,128]{1,0:T(8,128)S(1)}, f32[240,128]{1,0:T(8,128)S(1)}, u32[]{:S(2)}, u32[]{:S(2)}) collective-permute-start(f32[240,128]{1,0:T(8,128)S(1)} %get-tuple-element.72), channel_id=1, source_target_pairs={{0,24},{8,16},{16,8},{24,0},{1,25},{9,17},{17,9},{25,1},{2,26},{10... | collective-permute-start | bytes 368648 | tf_op jit(solution)/shard_map/ppermute | solution.py:670
  48.5 2.7 %collective-permute-done.11.refs_1_ = f32[240,128]{1,0:T(8,128)S(1)} collective-permute-done((f32[240,128]{1,0:T(8,128)S(1)}, f32[240,128]{1,0:T(8,128)S(1)}, u32[]{:S(2)}, u32[]{:S(2)}) %collective-permute-start.11) | collective-permute-done | bytes 122912 | tf_op jit(solution)/shard_map/ppermute | solution.py:670
  51.2 2.5 %collective-permute-done.12.refs_2_ = f32[240,128]{1,0:T(8,128)S(1)} collective-permute-done((f32[240,128]{1,0:T(8,128)S(1)}, f32[240,128]{1,0:T(8,128)S(1)}, u32[]{:S(2)}, u32[]{:S(2)}) %collective-permute-start.12) | collective-permute-done | bytes 122912 | tf_op jit(solution)/shard_map/ppermute | solution.py:670
  53.7 0.0 collective-permute-done.13.refs_3_
  53.7 0.9 %close_kernel.1 = f32[1,5,12,16,128]{4,3,2,1,0:T(8,128)} custom-call(f32[240,128]{1,0:T(8,128)S(1)} %get-tuple-element.69.refs_0_, f32[240,128]{1,0:T(8,128)S(1)} %collective-permute-done.11.refs_1_, f32[240,128]{1,0:T(8,128)S(1)} %collective-permute-done.12.refs_2_, f32[240,128]{1,0:T(8,128)S(1)} %collective-permute-done.13.refs_3_), custom_call_target="tpu_custom_call" | custom-call | flops 500000000 | bytes 983040 | tf_op jit(solution)/shard_map/close_kernel/pallas_call | solution.py:651
Async XLA Ops:
  0.0 1.0 %copy-start = (f32[1,5,12,16,128]{4,3,2,1,0:T(8,128)S(1)}, f32[1,5,12,16,128]{4,3,2,1,0:T(8,128)}, u32[]{:S(2)}) copy-start(f32[1,5,12,16,128]{4,3,2,1,0:T(8,128)} %u_ref.1) | copy-start | bytes 1474564
  2.0 10.9 %collective-permute-start = (f32[288,128]{1,0:T(8,128)S(1)}, f32[288,128]{1,0:T(8,128)S(1)}, u32[]{:S(2)}, u32[]{:S(2)}) collective-permute-start(f32[288,128]{1,0:T(8,128)S(1)} %get-tuple-element.40), channel_id=1, source_target_pairs={{0,8},{8,0},{16,24},{24,16},{1,9},{9,1},{17,25},{25,17},{2,10},{10... | collective-permute-start | bytes 442376 | tf_op jit(solution)/shard_map/ppermute | solution.py:670
  5.0 8.5 %collective-permute-start.1 = (f32[288,128]{1,0:T(8,128)S(1)}, f32[288,128]{1,0:T(8,128)S(1)}, u32[]{:S(2)}, u32[]{:S(2)}) collective-permute-start(f32[288,128]{1,0:T(8,128)S(1)} %get-tuple-element.41), channel_id=1, source_target_pairs={{0,16},{8,24},{16,0},{24,8},{1,17},{9,25},{17,1},{25,9},{2,18},{10... | collective-permute-start | bytes 442376 | tf_op jit(solution)/shard_map/ppermute | solution.py:670
  6.5 7.0 %collective-permute-start.2 = (f32[288,128]{1,0:T(8,128)S(1)}, f32[288,128]{1,0:T(8,128)S(1)}, u32[]{:S(2)}, u32[]{:S(2)}) collective-permute-start(f32[288,128]{1,0:T(8,128)S(1)} %get-tuple-element.42), channel_id=1, source_target_pairs={{0,24},{8,16},{16,8},{24,0},{1,25},{9,17},{17,9},{25,1},{2,26},{10... | collective-permute-start | bytes 442376 | tf_op jit(solution)/shard_map/ppermute | solution.py:670
  6.6 14.5 %all-to-all-start = ((f32[32,8,128]{2,1,0:T(8,128)}), f32[32,8,128]{2,1,0:T(8,128)S(1)}, u32[]{:S(2)}, u32[]{:S(2)}) async-start(f32[32,8,128]{2,1,0:T(8,128)} %get-tuple-element.53), calls=%async_computation | async-start | bytes 262144 | tf_op jit(solution)/shard_map/all_to_all | solution.py:719
  13.9 4.2 %collective-permute-start.5 = (f32[1,384,128]{2,1,0:T(8,128)S(1)}, f32[1,384,128]{2,1,0:T(8,128)S(1)}, u32[]{:S(2)}, u32[]{:S(2)}) collective-permute-start(f32[1,384,128]{2,1,0:T(8,128)S(1)} %get-tuple-element.47), channel_id=1, source_target_pairs={{0,1},{1,0},{2,3},{3,2},{4,5},{5,4},{6,7},{7,6},{8,9},{9,8},{10,11... | collective-permute-start | bytes 589832 | tf_op jit(solution)/shard_map/ppermute | solution.py:666
  14.0 10.6 %collective-permute-start.3 = (f32[1,240,128]{2,1,0:T(8,128)S(1)}, f32[1,240,128]{2,1,0:T(8,128)S(1)}, u32[]{:S(2)}, u32[]{:S(2)}) collective-permute-start(f32[1,240,128]{2,1,0:T(8,128)S(1)} %get-tuple-element.44), channel_id=1, source_target_pairs={{0,2},{2,4},{4,6},{6,0},{1,3},{3,5},{5,7},{7,1},{8,10},{10,12},{12... | collective-permute-start | bytes 368648 | tf_op jit(solution)/shard_map/ppermute | solution.py:666
  15.6 9.0 %collective-permute-start.4 = (f32[1,240,128]{2,1,0:T(8,128)S(1)}, f32[1,240,128]{2,1,0:T(8,128)S(1)}, u32[]{:S(2)}, u32[]{:S(2)}) collective-permute-start(f32[1,240,128]{2,1,0:T(8,128)S(1)} %get-tuple-element.45), channel_id=1, source_target_pairs={{0,6},{2,0},{4,2},{6,4},{1,7},{3,1},{5,3},{7,5},{8,14},{10,8},{12,... | collective-permute-start | bytes 368648 | tf_op jit(solution)/shard_map/ppermute | solution.py:666
  17.9 1.0 %copy-start.1 = (f32[5,12,16,128]{3,2,1,0:T(8,128)S(1)}, f32[5,12,16,128]{3,2,1,0:T(8,128)}, u32[]{:S(2)}) copy-start(f32[5,12,16,128]{3,2,1,0:T(8,128)} %init_ref) | copy-start | bytes 1474564
  27.3 11.5 %all-to-all-start.1 = ((f32[32,8,128]{2,1,0:T(8,128)}), f32[32,8,128]{2,1,0:T(8,128)S(1)}, u32[]{:S(2)}, u32[]{:S(2)}) async-start(f32[32,8,128]{2,1,0:T(8,128)} %get-tuple-element.64), calls=%async_computation.1 | async-start | bytes 262144 | tf_op jit(solution)/shard_map/all_to_all | solution.py:757
  30.7 8.0 %collective-permute-start.10 = (f32[1,384,128]{2,1,0:T(8,128)S(1)}, f32[1,384,128]{2,1,0:T(8,128)S(1)}, u32[]{:S(2)}, u32[]{:S(2)}) collective-permute-start(f32[1,384,128]{2,1,0:T(8,128)S(1)} %get-tuple-element.63), channel_id=1, source_target_pairs={{0,1},{1,0},{2,3},{3,2},{4,5},{5,4},{6,7},{7,6},{8,9},{9,8},{10,11... | collective-permute-start | bytes 589832 | tf_op jit(solution)/shard_map/ppermute | solution.py:666
  31.0 6.8 %collective-permute-start.8 = (f32[128,128]{1,0:T(8,128)S(1)}, f32[128,128]{1,0:T(8,128)S(1)}, u32[]{:S(2)}, u32[]{:S(2)}) collective-permute-start(f32[128,128]{1,0:T(8,128)S(1)} %get-tuple-element.61), channel_id=1, source_target_pairs={{0,8},{8,16},{16,24},{24,0},{1,9},{9,17},{17,25},{25,1},{2,10},{10... | collective-permute-start | bytes 196616 | tf_op jit(solution)/shard_map/ppermute | solution.py:666
  32.7 6.0 %collective-permute-start.9 = (f32[128,128]{1,0:T(8,128)S(1)}, f32[128,128]{1,0:T(8,128)S(1)}, u32[]{:S(2)}, u32[]{:S(2)}) collective-permute-start(f32[128,128]{1,0:T(8,128)S(1)} %get-tuple-element.62), channel_id=1, source_target_pairs={{0,24},{8,0},{16,8},{24,16},{1,25},{9,1},{17,9},{25,17},{2,26},{10... | collective-permute-start | bytes 196616 | tf_op jit(solution)/shard_map/ppermute | solution.py:666
  33.9 8.9 %collective-permute-start.6 = (f32[1,240,128]{2,1,0:T(8,128)S(1)}, f32[1,240,128]{2,1,0:T(8,128)S(1)}, u32[]{:S(2)}, u32[]{:S(2)}) collective-permute-start(f32[1,240,128]{2,1,0:T(8,128)S(1)} %get-tuple-element.59), channel_id=1, source_target_pairs={{0,2},{2,4},{4,6},{6,0},{1,3},{3,5},{5,7},{7,1},{8,10},{10,12},{12... | collective-permute-start | bytes 368648 | tf_op jit(solution)/shard_map/ppermute | solution.py:666
  35.6 7.4 %collective-permute-start.7 = (f32[1,240,128]{2,1,0:T(8,128)S(1)}, f32[1,240,128]{2,1,0:T(8,128)S(1)}, u32[]{:S(2)}, u32[]{:S(2)}) collective-permute-start(f32[1,240,128]{2,1,0:T(8,128)S(1)} %get-tuple-element.60), channel_id=1, source_target_pairs={{0,6},{2,0},{4,2},{6,4},{1,7},{3,1},{5,3},{7,5},{8,14},{10,8},{12,... | collective-permute-start | bytes 368648 | tf_op jit(solution)/shard_map/ppermute | solution.py:666
  45.0 6.2 %collective-permute-start.11 = (f32[240,128]{1,0:T(8,128)S(1)}, f32[240,128]{1,0:T(8,128)S(1)}, u32[]{:S(2)}, u32[]{:S(2)}) collective-permute-start(f32[240,128]{1,0:T(8,128)S(1)} %get-tuple-element.70), channel_id=1, source_target_pairs={{0,8},{8,0},{16,24},{24,16},{1,9},{9,1},{17,25},{25,17},{2,10},{10... | collective-permute-start | bytes 368648 | tf_op jit(solution)/shard_map/ppermute | solution.py:670
  46.2 7.5 %collective-permute-start.12 = (f32[240,128]{1,0:T(8,128)S(1)}, f32[240,128]{1,0:T(8,128)S(1)}, u32[]{:S(2)}, u32[]{:S(2)}) collective-permute-start(f32[240,128]{1,0:T(8,128)S(1)} %get-tuple-element.71), channel_id=1, source_target_pairs={{0,16},{8,24},{16,0},{24,8},{1,17},{9,25},{17,1},{25,9},{2,18},{10... | collective-permute-start | bytes 368648 | tf_op jit(solution)/shard_map/ppermute | solution.py:670
  47.3 6.4 %collective-permute-start.13 = (f32[240,128]{1,0:T(8,128)S(1)}, f32[240,128]{1,0:T(8,128)S(1)}, u32[]{:S(2)}, u32[]{:S(2)}) collective-permute-start(f32[240,128]{1,0:T(8,128)S(1)} %get-tuple-element.72), channel_id=1, source_target_pairs={{0,24},{8,16},{16,8},{24,0},{1,25},{9,17},{17,9},{25,1},{2,26},{10... | collective-permute-start | bytes 368648 | tf_op jit(solution)/shard_map/ppermute | solution.py:670

commit v13 on v12

--- a/solution.py
+++ b/solution.py
@@ -414,7 +414,7 @@
     lax.fori_loop(0, rows // TILE, along, 0)
 
 
-def along_last(blocks, nodes, zf, zu, alphas):
+def along_last(blocks, nodes, flux, zu, alphas, zf):
     width = blocks.nz // nodes
     size = width + 8
     each = width // CHUNK
@@ -426,7 +426,7 @@
 
         def load(j):
             at = pl.ds(start + j, TILE, stride=size)
-            return split(zf[at, :], zu[at, :], alpha)
+            return split(flux[at, :], zu[at, :], alpha)
 
         def store(i, value):
             zf[pl.ds(start + i, TILE, stride=size), :] = value
@@ -515,10 +515,9 @@
 
 
 def first_lanes_kernel(nat_ref, zu, zf_in, side_ref, al_ref, fy, zf, al_out, *scratch, nodes):
-    del zf_in
     *scratch, alphas = scratch
     tile = speeds_of(al_ref, al_out, alphas, nodes)
-    along_last(Blocks(*nat_ref.shape), nodes, zf, zu, alphas)
+    along_last(Blocks(*nat_ref.shape), nodes, zf_in, zu, alphas, zf)
     along_second(nat_ref, side_ref, tile[1:2], fy, *scratch)
 
 
@@ -540,7 +539,7 @@
             zu[pl.ds(start + HALO + width, HALO), :] = behind_ref[ghost, :]
     write_halves(blocks, nodes, zu, zf)
     tile = speeds_of(al_ref, al_out, alphas, nodes)
-    along_last(blocks, nodes, zf, zu, alphas)
+    along_last(blocks, nodes, zf, zu, alphas, zf)
 
     def turn(b):
         fz[rows_at(b * nz, nz), :] = block_rates(blocks, nodes, zf, b).T

time: 55 us -> 57.1 us (1.038)
  Pallas kernels: 15.4 us -> 18.3 us
    pallas_call x9, Pallas kernels: 15.4 us -> 18.3 us  [call(): pl.pallas_call(kernel, out_shape=[jax.ShapeDtypeStruct(shape, jnp.float32...]
    all_to_all x2, starting transfers between devices: 9.65 us -> 8.89 us  [local(): speeds = lax.all_to_all(speeds, everyone, 0, 0)]
  transfers between devices with their start and end apart: 16 -> 16, of which waited for: 7 -> 7; matrix products, arithmetic and copies ran while one was open for 0% -> 0% of each run, Pallas kernels for 16% -> 20%
where the time goes in v13:
time: 57.1 us; the launch traced here: 56.8 us
  starting transfers between devices  28.3 us (50%)
  Pallas kernels  18.3 us (32%)
  waiting for transfers between devices  8.26 us (14%)
  local copies, waits for them, and re-layouts  1.81 us (3%)
    pallas_call x9, Pallas kernels, call(): pl.pallas_call(kernel, out_shape=[jax.ShapeDtypeStruct(shape, jnp.float32...  18.3 us
    ppermute x8, starting transfers between devices, shifted(): lax.ppermute(value, axis, [(i, (i + by) % count) for i in range(count)])  11.3 us
    all_to_all x2, starting transfers between devices, local(): speeds = lax.all_to_all(speeds, everyone, 0, 0)  8.89 us
    ppermute x6, starting transfers between devices, swapped(): lax.ppermute(value, 'node', [(i, i ^ by) for i in range(lax.axis_size('no...  8.1 us
    ppermute x6, waiting for transfers between devices, swapped(): lax.ppermute(value, 'node', [(i, i ^ by) for i in range(lax.axis_size('no...  5.85 us
    unnamed x4, local copies, waits for them, and re-layouts  1.81 us
    all_to_all x2, waiting for transfers between devices, local(): speeds = lax.all_to_all(speeds, everyone, 0, 0)  1.77 us
  transfers between devices with their start and end apart: 16, of which 7 were waited for; matrix products, arithmetic and copies ran while one was open for 0% of the time, Pallas kernels for 20%

profile of v13, /device:TPU:0, one launch (start us, length us, event | category | flops | bytes accessed | tf_op | source)
XLA Modules:
  0.0 56.8 jit_solution(14910255840867298964)
XLA Ops:
  0.0 0.0 copy-start
  0.0 1.0 %copy-done = f32[1,5,12,16,128]{4,3,2,1,0:T(8,128)S(1)} copy-done((f32[1,5,12,16,128]{4,3,2,1,0:T(8,128)S(1)}, f32[1,5,12,16,128]{4,3,2,1,0:T(8,128)}, u32[]{:S(2)}) %copy-start) | copy-done | bytes 491544
  1.0 1.0 %open_kernel.1 = (f32[288,128]{1,0:T(8,128)S(1)}, f32[288,128]{1,0:T(8,128)S(1)}, f32[288,128]{1,0:T(8,128)S(1)}, f32[288,128]{1,0:T(8,128)S(1)}, f32[32,8,128]{2,1,0:T(8,128)}) custom-call(f32[1,5,12,16,128]{4,3,2,1,0:T(8,128)S(1)} %copy-done), custom_call_target="tpu_custom_call" | custom-call | flops 500000000 | bytes 983040 | tf_op jit(solution)/shard_map/open_kernel/pallas_call | solution.py:650
  2.0 3.0 %collective-permute-start = (f32[288,128]{1,0:T(8,128)S(1)}, f32[288,128]{1,0:T(8,128)S(1)}, u32[]{:S(2)}, u32[]{:S(2)}) collective-permute-start(f32[288,128]{1,0:T(8,128)S(1)} %get-tuple-element.40), channel_id=1, source_target_pairs={{0,8},{8,0},{16,24},{24,16},{1,9},{9,1},{17,25},{25,17},{2,10},{10... | collective-permute-start | bytes 442376 | tf_op jit(solution)/shard_map/ppermute | solution.py:669
  5.0 1.5 %collective-permute-start.1 = (f32[288,128]{1,0:T(8,128)S(1)}, f32[288,128]{1,0:T(8,128)S(1)}, u32[]{:S(2)}, u32[]{:S(2)}) collective-permute-start(f32[288,128]{1,0:T(8,128)S(1)} %get-tuple-element.41), channel_id=1, source_target_pairs={{0,16},{8,24},{16,0},{24,8},{1,17},{9,25},{17,1},{25,9},{2,18},{10... | collective-permute-start | bytes 442376 | tf_op jit(solution)/shard_map/ppermute | solution.py:669
  6.5 0.0 collective-permute-start.2
  6.6 6.3 %all-to-all-start = ((f32[32,8,128]{2,1,0:T(8,128)}), f32[32,8,128]{2,1,0:T(8,128)S(1)}, u32[]{:S(2)}, u32[]{:S(2)}) async-start(f32[32,8,128]{2,1,0:T(8,128)} %get-tuple-element.53), calls=%async_computation | async-start | bytes 262144 | tf_op jit(solution)/shard_map/all_to_all | solution.py:718
  12.9 0.0 collective-permute-done.refs_1_
  12.9 0.6 %collective-permute-done.1.refs_2_ = f32[288,128]{1,0:T(8,128)S(1)} collective-permute-done((f32[288,128]{1,0:T(8,128)S(1)}, f32[288,128]{1,0:T(8,128)S(1)}, u32[]{:S(2)}, u32[]{:S(2)}) %collective-permute-start.1) | collective-permute-done | bytes 147488 | tf_op jit(solution)/shard_map/ppermute | solution.py:669
  13.5 0.0 collective-permute-done.2.refs_3_
  13.5 0.4 gather_kernel.1
  13.9 0.1 collective-permute-start.5
  14.0 1.6 %collective-permute-start.3 = (f32[1,240,128]{2,1,0:T(8,128)S(1)}, f32[1,240,128]{2,1,0:T(8,128)S(1)}, u32[]{:S(2)}, u32[]{:S(2)}) collective-permute-start(f32[1,240,128]{2,1,0:T(8,128)S(1)} %get-tuple-element.44), channel_id=1, source_target_pairs={{0,2},{2,4},{4,6},{6,0},{1,3},{3,5},{5,7},{7,1},{8,10},{10,12},{12... | collective-permute-start | bytes 368648 | tf_op jit(solution)/shard_map/ppermute | solution.py:665
  15.6 2.2 %collective-permute-start.4 = (f32[1,240,128]{2,1,0:T(8,128)S(1)}, f32[1,240,128]{2,1,0:T(8,128)S(1)}, u32[]{:S(2)}, u32[]{:S(2)}) collective-permute-start(f32[1,240,128]{2,1,0:T(8,128)S(1)} %get-tuple-element.45), channel_id=1, source_target_pairs={{0,6},{2,0},{4,2},{6,4},{1,7},{3,1},{5,3},{7,5},{8,14},{10,8},{12,... | collective-permute-start | bytes 368648 | tf_op jit(solution)/shard_map/ppermute | solution.py:665
  17.9 0.0 copy-start.1
  17.9 0.2 halves_kernel.1.zf_in
  18.1 0.0 collective-permute-done.5.side_ref
  18.1 0.8 %copy-done.1 = f32[5,12,16,128]{3,2,1,0:T(8,128)S(1)} copy-done((f32[5,12,16,128]{3,2,1,0:T(8,128)S(1)}, f32[5,12,16,128]{3,2,1,0:T(8,128)}, u32[]{:S(2)}) %copy-start.1) | copy-done | bytes 491544
  18.9 0.6 %start_kernel.1 = (f32[256,128]{1,0:T(8,128)S(1)}, f32[240,128]{1,0:T(8,128)S(1)}) custom-call(f32[5,12,16,128]{3,2,1,0:T(8,128)S(1)} %copy-done.1), custom_call_target="tpu_custom_call" | custom-call | flops 500000000 | bytes 983040 | tf_op jit(solution)/shard_map/start_kernel/pallas_call | solution.py:650
  19.6 1.5 %all-to-all-done.al_ref = f32[32,8,128]{2,1,0:T(8,128)S(1)} async-done(((f32[32,8,128]{2,1,0:T(8,128)}), f32[32,8,128]{2,1,0:T(8,128)S(1)}, u32[]{:S(2)}, u32[]{:S(2)}) %all-to-all-start) | async-done | bytes 131104 | tf_op jit(solution)/shard_map/all_to_all | solution.py:718
  21.1 6.4 %first_lanes_kernel.1 = (f32[1024,128]{1,0:T(8,128)S(1)}, f32[1280,128]{1,0:T(8,128)S(1)}, f32[8,128]{1,0:T(8,128)S(1)}) custom-call(f32[5,12,16,128]{3,2,1,0:T(8,128)S(1)} %get-tuple-element.43.nat_ref.nat_in, f32[1280,128]{1,0:T(8,128)S(1)} %get-tuple-element.46.rows_ref.zu, f32[1280,128]{1,0:T(8,128)S(1)} %halves_kernel.1.zf_in, ...), custom_call_target="tpu_custom_call", output_to_operand_aliasing={{1}: (2, {})} | custom-call | flops 4000000000 | bytes 4259840 | tf_op jit(solution)/shard_map/first_lanes_kernel/pallas_call | solution.py:650
  27.5 0.0 collective-permute-done.3.lo_in
  27.5 0.0 collective-permute-done.4.hi_in
  27.5 2.7 %first_rows_kernel.1 = (f32[5,12,16,128]{3,2,1,0:T(8,128)S(1)}, f32[1,240,128]{2,1,0:T(8,128)S(1)}, f32[1,240,128]{2,1,0:T(8,128)S(1)}, f32[1,384,128]{2,1,0:T(8...) custom-call(f32[5,12,16,128]{3,2,1,0:T(8,128)S(1)} %get-tuple-elemen, ...), custom_call_target="tpu_custom_call", output_to_operand_aliasing={{0}: (0, {}), {1}: (1, {}), {2}: (2, {})} | custom-call | flops 2500000000 | bytes 4104192 | tf_op jit(solution)/shard_map/first_rows_kernel/pallas_call | solution.py:650
  30.2 2.6 %all-to-all-start.1 = ((f32[32,8,128]{2,1,0:T(8,128)}), f32[32,8,128]{2,1,0:T(8,128)S(1)}, u32[]{:S(2)}, u32[]{:S(2)}) async-start(f32[32,8,128]{2,1,0:T(8,128)} %get-tuple-element.64), calls=%async_computation.1 | async-start | bytes 262144 | tf_op jit(solution)/shard_map/all_to_all | solution.py:756
  32.8 0.6 %collective-permute-start.10 = (f32[1,384,128]{2,1,0:T(8,128)S(1)}, f32[1,384,128]{2,1,0:T(8,128)S(1)}, u32[]{:S(2)}, u32[]{:S(2)}) collective-permute-start(f32[1,384,128]{2,1,0:T(8,128)S(1)} %get-tuple-element.63), channel_id=1, source_target_pairs={{0,1},{1,0},{2,3},{3,2},{4,5},{5,4},{6,7},{7,6},{8,9},{9,8},{10,11... | collective-permute-start | bytes 589832 | tf_op jit(solution)/shard_map/ppermute | solution.py:665
  33.4 1.2 %collective-permute-start.8 = (f32[128,128]{1,0:T(8,128)S(1)}, f32[128,128]{1,0:T(8,128)S(1)}, u32[]{:S(2)}, u32[]{:S(2)}) collective-permute-start(f32[128,128]{1,0:T(8,128)S(1)} %get-tuple-element.61), channel_id=1, source_target_pairs={{0,8},{8,16},{16,24},{24,0},{1,9},{9,17},{17,25},{25,1},{2,10},{10... | collective-permute-start | bytes 196616 | tf_op jit(solution)/shard_map/ppermute | solution.py:665
  34.7 1.7 %collective-permute-start.9 = (f32[128,128]{1,0:T(8,128)S(1)}, f32[128,128]{1,0:T(8,128)S(1)}, u32[]{:S(2)}, u32[]{:S(2)}) collective-permute-start(f32[128,128]{1,0:T(8,128)S(1)} %get-tuple-element.62), channel_id=1, source_target_pairs={{0,24},{8,0},{16,8},{24,16},{1,25},{9,1},{17,9},{25,17},{2,26},{10... | collective-permute-start | bytes 196616 | tf_op jit(solution)/shard_map/ppermute | solution.py:665
  36.4 1.3 %collective-permute-start.6 = (f32[1,240,128]{2,1,0:T(8,128)S(1)}, f32[1,240,128]{2,1,0:T(8,128)S(1)}, u32[]{:S(2)}, u32[]{:S(2)}) collective-permute-start(f32[1,240,128]{2,1,0:T(8,128)S(1)} %get-tuple-element.59), channel_id=1, source_target_pairs={{0,2},{2,4},{4,6},{6,0},{1,3},{3,5},{5,7},{7,1},{8,10},{10,12},{12... | collective-permute-start | bytes 368648 | tf_op jit(solution)/shard_map/ppermute | solution.py:665
  37.7 2.5 %collective-permute-start.7 = (f32[1,240,128]{2,1,0:T(8,128)S(1)}, f32[1,240,128]{2,1,0:T(8,128)S(1)}, u32[]{:S(2)}, u32[]{:S(2)}) collective-permute-start(f32[1,240,128]{2,1,0:T(8,128)S(1)} %get-tuple-element.60), channel_id=1, source_target_pairs={{0,6},{2,0},{4,2},{6,4},{1,7},{3,1},{5,3},{7,5},{8,14},{10,8},{12,... | collective-permute-start | bytes 368648 | tf_op jit(solution)/shard_map/ppermute | solution.py:665
  40.2 0.0 collective-permute-done.8.before_ref
  40.2 0.5 collective-permute-done.9.behind_ref
  40.7 0.0 collective-permute-done.10.side_ref
  40.7 0.3 all-to-all-done.1.al_ref
  41.0 3.9 %second_lanes_kernel.1 = (f32[1024,128]{1,0:T(8,128)S(1)}, f32[1024,128]{1,0:T(8,128)S(1)}, f32[8,128]{1,0:T(8,128)S(1)}) custom-call(f32[5,12,16,128]{3,2,1,0:T(8,128)S(1)} %get-tuple-element.58.nat_ref, f32[128,128]{1,0:T(8,128)S(1)} %collective-permute-done.8.before_ref, f32[128,128]{1,0:T(8,128)S(1)} %collective-permute-done.9.behind_ref, ...), custom_call_target="tpu_custom_call" | custom-call | flops 4000000000 | bytes 1900544 | tf_op jit(solution)/shard_map/second_lanes_kernel/pallas_call | solution.py:650
  44.9 0.0 collective-permute-done.6.lo_ref
  44.9 0.1 collective-permute-done.7.hi_ref
  45.0 2.0 %second_rows_kernel.1 = (f32[240,128]{1,0:T(8,128)S(1)}, f32[240,128]{1,0:T(8,128)S(1)}, f32[240,128]{1,0:T(8,128)S(1)}, f32[240,128]{1,0:T(8,128)S(1)}) custom-call(f32[5,12,16,128]{3,2,1,0:T(8,128)S(1)} %get-tuple-element.58.nat_ref, f32[1,240,128]{2,1,0:T(8,128)S(1)} %collective-permute-done.6.lo_ref, f32[1,240,128]{2,1,0:T(8,128)S(1)} %collective-permute-done.7.hi_ref, ...), custom_call_target="tpu_custom_call" | custom-call | flops 2500000000 | bytes 3825664 | tf_op jit(solution)/shard_map/second_rows_kernel/pallas_call | solution.py:650
  47.1 1.3 %collective-permute-start.11 = (f32[240,128]{1,0:T(8,128)S(1)}, f32[240,128]{1,0:T(8,128)S(1)}, u32[]{:S(2)}, u32[]{:S(2)}) collective-permute-start(f32[240,128]{1,0:T(8,128)S(1)} %get-tuple-element.70), channel_id=1, source_target_pairs={{0,8},{8,0},{16,24},{24,16},{1,9},{9,1},{17,25},{25,17},{2,10},{10... | collective-permute-start | bytes 368648 | tf_op jit(solution)/shard_map/ppermute | solution.py:669
  48.4 1.1 %collective-permute-start.12 = (f32[240,128]{1,0:T(8,128)S(1)}, f32[240,128]{1,0:T(8,128)S(1)}, u32[]{:S(2)}, u32[]{:S(2)}) collective-permute-start(f32[240,128]{1,0:T(8,128)S(1)} %get-tuple-element.71), channel_id=1, source_target_pairs={{0,16},{8,24},{16,0},{24,8},{1,17},{9,25},{17,1},{25,9},{2,18},{10... | collective-permute-start | bytes 368648 | tf_op jit(solution)/shard_map/ppermute | solution.py:669
  49.5 1.1 %collective-permute-start.13 = (f32[240,128]{1,0:T(8,128)S(1)}, f32[240,128]{1,0:T(8,128)S(1)}, u32[]{:S(2)}, u32[]{:S(2)}) collective-permute-start(f32[240,128]{1,0:T(8,128)S(1)} %get-tuple-element.72), channel_id=1, source_target_pairs={{0,24},{8,16},{16,8},{24,0},{1,25},{9,17},{17,9},{25,1},{2,26},{10... | collective-permute-start | bytes 368648 | tf_op jit(solution)/shard_map/ppermute | solution.py:669
  50.6 2.6 %collective-permute-done.11.refs_1_ = f32[240,128]{1,0:T(8,128)S(1)} collective-permute-done((f32[240,128]{1,0:T(8,128)S(1)}, f32[240,128]{1,0:T(8,128)S(1)}, u32[]{:S(2)}, u32[]{:S(2)}) %collective-permute-start.11) | collective-permute-done | bytes 122912 | tf_op jit(solution)/shard_map/ppermute | solution.py:669
  53.2 2.6 %collective-permute-done.12.refs_2_ = f32[240,128]{1,0:T(8,128)S(1)} collective-permute-done((f32[240,128]{1,0:T(8,128)S(1)}, f32[240,128]{1,0:T(8,128)S(1)}, u32[]{:S(2)}, u32[]{:S(2)}) %collective-permute-start.12) | collective-permute-done | bytes 122912 | tf_op jit(solution)/shard_map/ppermute | solution.py:669
  55.8 0.0 collective-permute-done.13.refs_3_
  55.9 0.9 %close_kernel.1 = f32[1,5,12,16,128]{4,3,2,1,0:T(8,128)} custom-call(f32[240,128]{1,0:T(8,128)S(1)} %get-tuple-element.69.refs_0_, f32[240,128]{1,0:T(8,128)S(1)} %collective-permute-done.11.refs_1_, f32[240,128]{1,0:T(8,128)S(1)} %collective-permute-done.12.refs_2_, f32[240,128]{1,0:T(8,128)S(1)} %collective-permute-done.13.refs_3_), custom_call_target="tpu_custom_call" | custom-call | flops 500000000 | bytes 983040 | tf_op jit(solution)/shard_map/close_kernel/pallas_call | solution.py:650
Async XLA Ops:
  0.0 1.0 %copy-start = (f32[1,5,12,16,128]{4,3,2,1,0:T(8,128)S(1)}, f32[1,5,12,16,128]{4,3,2,1,0:T(8,128)}, u32[]{:S(2)}) copy-start(f32[1,5,12,16,128]{4,3,2,1,0:T(8,128)} %u_ref.1) | copy-start | bytes 1474564
  2.0 10.9 %collective-permute-start = (f32[288,128]{1,0:T(8,128)S(1)}, f32[288,128]{1,0:T(8,128)S(1)}, u32[]{:S(2)}, u32[]{:S(2)}) collective-permute-start(f32[288,128]{1,0:T(8,128)S(1)} %get-tuple-element.40), channel_id=1, source_target_pairs={{0,8},{8,0},{16,24},{24,16},{1,9},{9,1},{17,25},{25,17},{2,10},{10... | collective-permute-start | bytes 442376 | tf_op jit(solution)/shard_map/ppermute | solution.py:669
  5.0 8.5 %collective-permute-start.1 = (f32[288,128]{1,0:T(8,128)S(1)}, f32[288,128]{1,0:T(8,128)S(1)}, u32[]{:S(2)}, u32[]{:S(2)}) collective-permute-start(f32[288,128]{1,0:T(8,128)S(1)} %get-tuple-element.41), channel_id=1, source_target_pairs={{0,16},{8,24},{16,0},{24,8},{1,17},{9,25},{17,1},{25,9},{2,18},{10... | collective-permute-start | bytes 442376 | tf_op jit(solution)/shard_map/ppermute | solution.py:669
  6.5 7.0 %collective-permute-start.2 = (f32[288,128]{1,0:T(8,128)S(1)}, f32[288,128]{1,0:T(8,128)S(1)}, u32[]{:S(2)}, u32[]{:S(2)}) collective-permute-start(f32[288,128]{1,0:T(8,128)S(1)} %get-tuple-element.42), channel_id=1, source_target_pairs={{0,24},{8,16},{16,8},{24,0},{1,25},{9,17},{17,9},{25,1},{2,26},{10... | collective-permute-start | bytes 442376 | tf_op jit(solution)/shard_map/ppermute | solution.py:669
  6.6 14.5 %all-to-all-start = ((f32[32,8,128]{2,1,0:T(8,128)}), f32[32,8,128]{2,1,0:T(8,128)S(1)}, u32[]{:S(2)}, u32[]{:S(2)}) async-start(f32[32,8,128]{2,1,0:T(8,128)} %get-tuple-element.53), calls=%async_computation | async-start | bytes 262144 | tf_op jit(solution)/shard_map/all_to_all | solution.py:718
  13.9 4.2 %collective-permute-start.5 = (f32[1,384,128]{2,1,0:T(8,128)S(1)}, f32[1,384,128]{2,1,0:T(8,128)S(1)}, u32[]{:S(2)}, u32[]{:S(2)}) collective-permute-start(f32[1,384,128]{2,1,0:T(8,128)S(1)} %get-tuple-element.47), channel_id=1, source_target_pairs={{0,1},{1,0},{2,3},{3,2},{4,5},{5,4},{6,7},{7,6},{8,9},{9,8},{10,11... | collective-permute-start | bytes 589832 | tf_op jit(solution)/shard_map/ppermute | solution.py:665
  14.0 13.5 %collective-permute-start.3 = (f32[1,240,128]{2,1,0:T(8,128)S(1)}, f32[1,240,128]{2,1,0:T(8,128)S(1)}, u32[]{:S(2)}, u32[]{:S(2)}) collective-permute-start(f32[1,240,128]{2,1,0:T(8,128)S(1)} %get-tuple-element.44), channel_id=1, source_target_pairs={{0,2},{2,4},{4,6},{6,0},{1,3},{3,5},{5,7},{7,1},{8,10},{10,12},{12... | collective-permute-start | bytes 368648 | tf_op jit(solution)/shard_map/ppermute | solution.py:665
  15.6 11.9 %collective-permute-start.4 = (f32[1,240,128]{2,1,0:T(8,128)S(1)}, f32[1,240,128]{2,1,0:T(8,128)S(1)}, u32[]{:S(2)}, u32[]{:S(2)}) collective-permute-start(f32[1,240,128]{2,1,0:T(8,128)S(1)} %get-tuple-element.45), channel_id=1, source_target_pairs={{0,6},{2,0},{4,2},{6,4},{1,7},{3,1},{5,3},{7,5},{8,14},{10,8},{12,... | collective-permute-start | bytes 368648 | tf_op jit(solution)/shard_map/ppermute | solution.py:665
  17.9 1.0 %copy-start.1 = (f32[5,12,16,128]{3,2,1,0:T(8,128)S(1)}, f32[5,12,16,128]{3,2,1,0:T(8,128)}, u32[]{:S(2)}) copy-start(f32[5,12,16,128]{3,2,1,0:T(8,128)} %init_ref) | copy-start | bytes 1474564
  30.2 10.8 %all-to-all-start.1 = ((f32[32,8,128]{2,1,0:T(8,128)}), f32[32,8,128]{2,1,0:T(8,128)S(1)}, u32[]{:S(2)}, u32[]{:S(2)}) async-start(f32[32,8,128]{2,1,0:T(8,128)} %get-tuple-element.64), calls=%async_computation.1 | async-start | bytes 262144 | tf_op jit(solution)/shard_map/all_to_all | solution.py:756
  32.8 7.9 %collective-permute-start.10 = (f32[1,384,128]{2,1,0:T(8,128)S(1)}, f32[1,384,128]{2,1,0:T(8,128)S(1)}, u32[]{:S(2)}, u32[]{:S(2)}) collective-permute-start(f32[1,384,128]{2,1,0:T(8,128)S(1)} %get-tuple-element.63), channel_id=1, source_target_pairs={{0,1},{1,0},{2,3},{3,2},{4,5},{5,4},{6,7},{7,6},{8,9},{9,8},{10,11... | collective-permute-start | bytes 589832 | tf_op jit(solution)/shard_map/ppermute | solution.py:665
  33.4 6.8 %collective-permute-start.8 = (f32[128,128]{1,0:T(8,128)S(1)}, f32[128,128]{1,0:T(8,128)S(1)}, u32[]{:S(2)}, u32[]{:S(2)}) collective-permute-start(f32[128,128]{1,0:T(8,128)S(1)} %get-tuple-element.61), channel_id=1, source_target_pairs={{0,8},{8,16},{16,24},{24,0},{1,9},{9,17},{17,25},{25,1},{2,10},{10... | collective-permute-start | bytes 196616 | tf_op jit(solution)/shard_map/ppermute | solution.py:665
  34.7 6.0 %collective-permute-start.9 = (f32[128,128]{1,0:T(8,128)S(1)}, f32[128,128]{1,0:T(8,128)S(1)}, u32[]{:S(2)}, u32[]{:S(2)}) collective-permute-start(f32[128,128]{1,0:T(8,128)S(1)} %get-tuple-element.62), channel_id=1, source_target_pairs={{0,24},{8,0},{16,8},{24,16},{1,25},{9,1},{17,9},{25,17},{2,26},{10... | collective-permute-start | bytes 196616 | tf_op jit(solution)/shard_map/ppermute | solution.py:665
  36.4 8.6 %collective-permute-start.6 = (f32[1,240,128]{2,1,0:T(8,128)S(1)}, f32[1,240,128]{2,1,0:T(8,128)S(1)}, u32[]{:S(2)}, u32[]{:S(2)}) collective-permute-start(f32[1,240,128]{2,1,0:T(8,128)S(1)} %get-tuple-element.59), channel_id=1, source_target_pairs={{0,2},{2,4},{4,6},{6,0},{1,3},{3,5},{5,7},{7,1},{8,10},{10,12},{12... | collective-permute-start | bytes 368648 | tf_op jit(solution)/shard_map/ppermute | solution.py:665
  37.7 7.4 %collective-permute-start.7 = (f32[1,240,128]{2,1,0:T(8,128)S(1)}, f32[1,240,128]{2,1,0:T(8,128)S(1)}, u32[]{:S(2)}, u32[]{:S(2)}) collective-permute-start(f32[1,240,128]{2,1,0:T(8,128)S(1)} %get-tuple-element.60), channel_id=1, source_target_pairs={{0,6},{2,0},{4,2},{6,4},{1,7},{3,1},{5,3},{7,5},{8,14},{10,8},{12,... | collective-permute-start | bytes 368648 | tf_op jit(solution)/shard_map/ppermute | solution.py:665
  47.1 6.2 %collective-permute-start.11 = (f32[240,128]{1,0:T(8,128)S(1)}, f32[240,128]{1,0:T(8,128)S(1)}, u32[]{:S(2)}, u32[]{:S(2)}) collective-permute-start(f32[240,128]{1,0:T(8,128)S(1)} %get-tuple-element.70), channel_id=1, source_target_pairs={{0,8},{8,0},{16,24},{24,16},{1,9},{9,1},{17,25},{25,17},{2,10},{10... | collective-permute-start | bytes 368648 | tf_op jit(solution)/shard_map/ppermute | solution.py:669
  48.4 7.5 %collective-permute-start.12 = (f32[240,128]{1,0:T(8,128)S(1)}, f32[240,128]{1,0:T(8,128)S(1)}, u32[]{:S(2)}, u32[]{:S(2)}) collective-permute-start(f32[240,128]{1,0:T(8,128)S(1)} %get-tuple-element.71), channel_id=1, source_target_pairs={{0,16},{8,24},{16,0},{24,8},{1,17},{9,25},{17,1},{25,9},{2,18},{10... | collective-permute-start | bytes 368648 | tf_op jit(solution)/shard_map/ppermute | solution.py:669
  49.5 6.4 %collective-permute-start.13 = (f32[240,128]{1,0:T(8,128)S(1)}, f32[240,128]{1,0:T(8,128)S(1)}, u32[]{:S(2)}, u32[]{:S(2)}) collective-permute-start(f32[240,128]{1,0:T(8,128)S(1)} %get-tuple-element.72), channel_id=1, source_target_pairs={{0,24},{8,16},{16,8},{24,0},{1,25},{9,17},{17,9},{25,1},{2,26},{10... | collective-permute-start | bytes 368648 | tf_op jit(solution)/shard_map/ppermute | solution.py:669
